TPU v7x, 32 devices: a whole 2x2x4 slice. The times are simulated.
32 devices in a mesh: frag: 2 (over y), vir: 4 (over z), occ: 2 (over x), rep: 2 (over core).
Axes of the slice: x: 2, y: 2, z: 4, core: 2. Of those that a mesh axis runs over, the one named last changes fastest.
Arguments:
- amplitudes: bfloat16 [16, 4, 1024, 1024], P('frag', 'rep', 'vir'), parts along dimension 0, may hold values from -6 to 6
- integrals: bfloat16 [8, 4, 1024, 1024], P(('frag', 'rep'), 'occ', 'vir'), parts along dimension 0, may hold values from -0.09375 to 0.09375
- amp_mask: int32 [8, 16, 16], P('frag'), parts along dimension 0, may hold values 0 or 1
- int_mask: int32 [8, 4, 16, 16], P('frag'), parts along dimension 0, may hold values 0 or 1
- eps_slab: float32 [16], P('frag'), parts along dimension 0, may hold values from -1.6 to -0.4
- eps_pair: float32 [8], P(('frag', 'occ', 'rep')), parts along dimension 0, may hold values from -1.6 to -0.4
- eps_vir: float32 [2048], P('frag'), parts along dimension 0, may hold values from 0.3 to 3
Outputs:
- update: float32 [16, 1024, 4, 1024], P('frag', 'vir', ('occ', 'rep')), parts along dimension 0
There are 2 independent parts, one for each index of `frag`. A program takes and returns all parts, laid end to end along the dimension named above; each array names one. Nothing has to cross between parts.
All inputs are finite; a program needn't handle non-finite values.
Results may differ from a plain program's by a relative error of at most 0.0022.
Values may be sent and summed in bfloat16 or wider, within the bound.
No kernel may reach another device: no remote copies, remote signals or barrier semaphores. Data moves between devices by JAX's collectives and lax.ppermute only.
A program may use at most 192 MiB of HBM per device.

v0:
```python
import jax
import jax.numpy as jnp
from jax import lax
from jax.sharding import PartitionSpec as P

TILE = 64


def tile_mask(mask_tiles, row_start, row_count, tile_size):
    tile_count = mask_tiles.shape[-1]
    row_tiles = (row_start + jnp.arange(row_count, dtype=jnp.int32)) // tile_size
    select = (row_tiles[:, None] == jnp.arange(tile_count, dtype=jnp.int32)[None, :]).astype(
        jnp.float32
    )
    picked = jnp.einsum("ra,...ac->...rc", select, mask_tiles.astype(jnp.float32))
    return jnp.repeat(picked, tile_size, axis=-1)


def cycle_terms(combined, gathered):
    direct_term = jnp.einsum(
        "ikac,kjcb->iajb", combined, gathered, preferred_element_type=jnp.float32
    )
    swapped_term = jnp.einsum(
        "ikac,kjbc->iajb", combined, gathered, preferred_element_type=jnp.float32
    )
    return 2.0 * direct_term - swapped_term


def shards(amplitudes, integrals, amp_mask, int_mask, eps_slab, eps_pair, eps_vir):
    row_count = amplitudes.shape[2]
    half_count = amplitudes.shape[1]
    pair_count = integrals.shape[1]
    row_start = lax.axis_index("vir") * row_count
    k_start = lax.axis_index("rep") * half_count
    j_start = lax.axis_index("occ") * pair_count
    zero_index = jnp.zeros((), jnp.int32)
    k_masks = lax.dynamic_slice_in_dim(amp_mask, k_start, half_count, 0)
    screened = (
        amplitudes.astype(jnp.float32) * tile_mask(k_masks, row_start, row_count, TILE)[None]
    ).astype(jnp.bfloat16)
    received = lax.all_to_all(screened, "vir", split_axis=3, concat_axis=2, tiled=True)
    combined = (
        2.0 * screened.astype(jnp.float32) - jnp.swapaxes(received, 2, 3).astype(jnp.float32)
    ).astype(jnp.bfloat16)
    pair_masks = lax.dynamic_slice(
        int_mask,
        (k_start, j_start, zero_index, zero_index),
        (half_count, pair_count, int_mask.shape[2], int_mask.shape[3]),
    )
    kept_local = (
        integrals.astype(jnp.float32) * tile_mask(pair_masks, row_start, row_count, TILE)
    ).astype(jnp.bfloat16)
    gathered = lax.all_gather(kept_local, "vir", axis=2, tiled=True)
    partial_cycle = cycle_terms(combined, gathered)
    cycle = lax.psum_scatter(partial_cycle, "rep", scatter_dimension=2, tiled=True)
    row_energy = lax.dynamic_slice_in_dim(eps_vir, row_start, row_count, 0)
    denominator = (
        row_energy[None, :, None, None]
        + eps_vir[None, None, None, :]
        - eps_slab[:, None, None, None]
        - eps_pair[None, None, :, None]
    )
    return cycle / denominator


def solution(mesh):
    in_specs = (
        P("frag", "rep", "vir", None),
        P(("frag", "rep"), "occ", "vir", None),
        P("frag", None, None),
        P("frag", None, None, None),
        P("frag"),
        P(("frag", "occ", "rep")),
        P("frag"),
    )
    out_specs = P("frag", "vir", ("occ", "rep"), None)
    return jax.shard_map(shards, mesh=mesh, in_specs=in_specs, out_specs=out_specs, check_vma=False)
```

profile of v0, /device:TPU:9, one launch (start us, length us, event | category | flops | bytes accessed | tf_op | source)
XLA Modules:
  0.0 533.0 jit_solution(882104660842064005)
XLA Ops:
  6.5 0.0 copy-start
  6.5 0.8 constant_dynamic-slice_fusion.1
  7.3 0.1 copy.53
  7.4 0.1 convolution_bitcast_fusion.1
  7.5 0.2 broadcast_in_dim.4
  7.7 1.6 copy.34
  9.3 12.5 %copy.32 = bf16[8,2,256,1024]{2,0,1,3:T(8,128)(2,1)} copy(bf16[8,2,256,1024]{3,2,1,0:T(8,128)(2,1)} %param.7) | data formatting | bytes 16777216 | tf_op args[0]
  21.8 7.6 %multiply_convert_fusion = bf16[8,2,256,1024]{2,0,1,3:T(8,128)(2,1)} fusion(bf16[8,2,256,1024]{2,0,1,3:T(8,128)(2,1)} %copy.32, f32[2,256,1024]{1,0,2:T(2,128)S(1)} %copy.34), kind=kLoop, calls=%fused_computation.4 | loop fusion | flops 12582912 | bytes 18874368 | tf_op jit(solution)/shard_map/convert_element_type | solution.py:40
  29.4 5.6 %all-to-all-start = ((bf16[8,2,256,1024]{2,0,1,3:T(8,128)(2,1)}), bf16[8,2,256,1024]{2,0,1,3:T(8,128)(2,1)}, u32[]{:S(2)}, u32[]{:S(2)}) async-start(bf16[8,2,256,1024]{2,0,1,3:T(8,128)(2,1)} %multiply_convert_fusion), calls=%async_computation | async-start | bytes 16777216 | tf_op jit(solution)/shard_map/all_to_all | solution.py:41
  35.0 0.0 all-gather.2.cloned.1.call-start
  35.1 0.0 copy-done
  35.1 0.1 copy.54
  35.2 0.1 convolution_bitcast_fusion
  35.3 2.3 broadcast_in_dim.5
  37.6 5.4 %copy.38 = f32[2,2,256,1024]{3,2,0,1:T(8,128)} copy(f32[2,2,256,1024]{2,3,1,0:T(8,128)} %bitcast.53) | data formatting | bytes 8388608 | tf_op jit(solution)/shard_map/reshape | solution.py:16
  43.0 5.0 multiply_convert_fusion.1
  48.0 0.0 all-gather.2.cloned.1.call-update
  48.0 0.2 all-reduce.3.cloned.1.call-start
  48.3 297.9 %all-to-all-done = bf16[8,2,256,1024]{2,0,1,3:T(8,128)(2,1)} async-done(((bf16[8,2,256,1024]{2,0,1,3:T(8,128)(2,1)}), bf16[8,2,256,1024]{2,0,1,3:T(8,128)(2,1)}, u32[]{:S(2)}, u32[]{:S(2)}) %all-to-all-start) | async-done | bytes 8388640 | tf_op jit(solution)/shard_map/all_to_all | solution.py:41
  346.2 17.0 %copy.35 = f32[8,2,256,4,256]{4,0,1,2,3:T(8,128)} copy(bf16[8,2,256,4,256]{2,0,1,4,3:T(8,128)(2,1)} %bitcast.27) | data formatting | bytes 25165824 | tf_op jit(solution)/shard_map/convert_element_type | solution.py:43
  363.3 12.1 %fusion = bf16[8,2,256,1024]{2,0,1,3:T(8,128)(2,1)} fusion(f32[8,2,256,4,256]{4,0,1,2,3:T(8,128)} %copy.35, f32[2,256,1024]{1,0,2:T(2,128)S(1)} %copy.34, bf16[8,2,256,1024]{2,0,1,3:T(8,128)(2,1)} %copy.32), kind=kLoop, calls=%fused_computation.1 | loop fusion | flops 29360128 | bytes 35651584 | tf_op jit(solution)/shard_map/convert_element_type | solution.py:44
  375.3 12.3 %copy.43 = bf16[8,2,256,1024,1]{3,2,1,4,0:T(8,128)(2,1)} copy(bf16[8,2,256,1024,1]{2,0,1,3,4:T(8,128)(2,1)} %bitcast.52) | data formatting | bytes 16777216 | tf_op jit(solution)/shard_map/convert_element_type | solution.py:44
  387.6 24.2 %fusion.2 = f32[8,256,2,1024,1]{3,1,4,2,0:T(8,128)} fusion(bf16[8,2,256,1024,1]{3,2,1,4,0:T(8,128)(2,1)} %copy.43, bf16[2,2,1024,1024]{3,2,0,1:T(8,128)(2,1)} %all-gather.2.cloned.1.call-done), kind=kOutput, calls=%fused_computation.7 | convolution fusion | flops 17179869184 | bytes 33554432 | tf_op jit(solution)/shard_map/ikac,kjcb->iajb/dot_general | solution.py:20
  411.8 26.8 %bitcast_subtract_fusion.1 = f32[8,256,2,1024]{3,1,2,0:T(8,128)} fusion(f32[8,256,2,1024,1]{3,1,4,2,0:T(8,128)} %fusion.2, bf16[8,2,256,1024,1]{3,2,1,4,0:T(8,128)(2,1)} %copy.43, bf16[2,2,1024,1024]{3,2,0,1:T(8,128)(2,1)} %all-gather.2.cloned.1.call-done), kind=kOutput, calls=%fused_computation.2 | convolution fusion | flops 17188257792 | bytes 50331648 | tf_op jit(solution)/shard_map/ikac,kjbc->iajb/dot_general | solution.py:23
  438.6 0.0 all-reduce.3.cloned.1.call-update
  439.3 0.0 copy-done.2
  439.3 0.1 dynamic_slice.11
  439.4 0.6 dynamic-slice
  439.9 0.1 broadcast_add_fusion
  440.1 64.5 %all-reduce.3.cloned.1.call-done = f32[8,256,2,1024]{3,1,2,0:T(8,128)} async-done(((f32[8,256,2,1024]{3,1,2,0:T(8,128)}), f32[8,256,2,1024]{3,1,2,0:T(8,128)}) %all-reduce.3.cloned.1.call-update) | async-done | bytes 16777232
  504.6 5.3 dynamic-slice_divide_fusion
  509.9 16.3 %copy.41 = f32[8,256,1,1024]{3,2,1,0:T(1,128)} copy(f32[8,256,1,1024]{3,1,2,0:T(8,128)S(1)} %dynamic-slice_divide_fusion) | data formatting | bytes 16777216 | tf_op jit(solution)/shard_map/div | solution.py:63
  (10 shorter events, 0.0 us)
Async XLA Ops:
  6.5 28.5 %copy-start = (s32[4,4,16,16]{3,2,1,0:T(8,128)S(1)}, s32[4,4,16,16]{3,2,1,0:T(8,128)}, u32[]{:S(2)}) copy-start(s32[4,4,16,16]{3,2,1,0:T(8,128)} %param.10) | copy-start | bytes 49156
  29.4 316.8 %all-to-all-start = ((bf16[8,2,256,1024]{2,0,1,3:T(8,128)(2,1)}), bf16[8,2,256,1024]{2,0,1,3:T(8,128)(2,1)}, u32[]{:S(2)}, u32[]{:S(2)}) async-start(bf16[8,2,256,1024]{2,0,1,3:T(8,128)(2,1)} %multiply_convert_fusion), calls=%async_computation | async-start | bytes 16777216 | tf_op jit(solution)/shard_map/all_to_all | solution.py:41
  35.0 352.6 %all-gather.2.cloned.1.call-start = ((), (), s32[]{:S(2)}) async-start(), calls=%async_computation.1 | async-start | bytes 10485760 | tf_op jit(solution)/shard_map/all_gather | solution.py:53
  48.0 456.6 %all-reduce.3.cloned.1.call-start = ((), (), s32[]{:S(2)}) async-start(), calls=%async_computation.2 | async-start | bytes 33554432
  438.6 0.7 copy-start.2
  438.6 0.8 copy-start.4
  438.6 66.0 %copy-start.3 = (f32[8]{0:T(128)S(1)}, f32[8]{0:T(128)}, u32[]{:S(2)}) copy-start(f32[8]{0:T(128)} %param.11) | copy-start | bytes 100
  504.6 21.6 %copy-start.1 = (s32[4,4,16,16]{3,2,1,0:T(8,128)S(1)}, s32[4,4,16,16]{3,2,1,0:T(8,128)}, u32[]{:S(2)}) copy-start(s32[4,4,16,16]{3,2,1,0:T(8,128)} %param.10) | copy-start | bytes 49156
Sparse Core Ops, SparseCore 0:
  48.2 302.1 all-gather.1
  438.7 65.8 all-reduce.2
where the time goes:
time: 535 us; the launch traced here: 533 us
  waiting for transfers between devices  363 us (68%)
  local copies, waits for them, and re-layouts  69.2 us (13%)
  matrix products  51.2 us (10%)
  other arithmetic  30.1 us (6%)
  between operations  14.2 us (3%)
  starting transfers between devices  5.88 us (1%)
    all_to_all x1, waiting for transfers between devices, shards(): lax.all_to_all(screened, 'vir', split_axis=3, concat_axis=2, tiled=True)  298 us
    unnamed x3, waiting for transfers between devices  64.6 us
    dot_general x1, matrix products, cycle_terms(): jnp.einsum('ikac,kjbc->iajb', combined, gathered, preferred_element_type=...  26.8 us
    dot_general x1, matrix products, cycle_terms(): jnp.einsum('ikac,kjcb->iajb', combined, gathered, preferred_element_type=...  24.2 us
    convert_element_type x1, local copies, waits for them, and re-layouts, shards(): jnp.swapaxes(received, 2, 3).astype(jnp.float32)  17 us
    div x1, local copies, waits for them, and re-layouts, shards(): return cycle / denominator  16.3 us
    unnamed x14, local copies, waits for them, and re-layouts  13.3 us
    convert_element_type x1, local copies, waits for them, and re-layouts, shards(): combined = (2.0 * screened.astype(jnp.float32) - jnp.swapaxes(received, 2...  12.3 us
  transfers between devices with their start and end apart: 3, of which 2 were waited for; matrix products, arithmetic and copies ran while one was open for 10% of the time, Pallas kernels for 0%

commit v1 on v0

--- a/solution.py
+++ b/solution.py
@@ -1,9 +1,17 @@
+import functools
+
 import jax
 import jax.numpy as jnp
 from jax import lax
+from jax.experimental import pallas as pl
+from jax.experimental.pallas import tpu as pltpu
 from jax.sharding import PartitionSpec as P
 
 TILE = 64
+LANES = 128
+AMP_SLOTS = 46
+INT_SLOTS = 160
+VMEM_LIMIT = 60 * 1024 * 1024
 
 
 def tile_mask(mask_tiles, row_start, row_count, tile_size):
@@ -26,7 +34,7 @@
     return 2.0 * direct_term - swapped_term
 
 
-def shards(amplitudes, integrals, amp_mask, int_mask, eps_slab, eps_pair, eps_vir):
+def dense_shards(amplitudes, integrals, amp_mask, int_mask, eps_slab, eps_pair, eps_vir):
     row_count = amplitudes.shape[2]
     half_count = amplitudes.shape[1]
     pair_count = integrals.shape[1]
@@ -63,6 +71,468 @@
     return cycle / denominator
 
 
+def low_lanes(rows):
+    return lax.broadcasted_iota(jnp.int32, (rows, LANES), 1) < TILE
+
+
+def swap_halves(block):
+    return pltpu.roll(block, TILE, 1)
+
+
+def pack_int_kernel(meta, mask, own_ref, oth_ref, out_ref):
+    v, r, j = meta[0], meta[2], meta[3]
+    low = low_lanes(32)
+    count = jnp.int32(0)
+    for kk in range(4):
+        k = lax.rem(kk + 2 * r, 4)
+
+        def body(n, count, kk=kk, k=k):
+            ap, cp = n // 8, n % 8
+            col = pl.multiple_of(cp * LANES, LANES)
+            for a2 in range(2):
+                row = pl.multiple_of(ap * 128 + a2 * TILE, TILE)
+                if kk < 2:
+                    block = own_ref[kk, r, pl.ds(row, TILE), pl.ds(col, LANES)]
+                else:
+                    block = oth_ref[kk - 2, pl.ds(row, TILE), pl.ds(col, LANES)]
+                top, bottom = block[:32], block[32:]
+                turned_top, turned_bottom = swap_halves(top), swap_halves(bottom)
+                at_row = 4 * v + 2 * ap + a2
+                out_ref[jnp.minimum(count, INT_SLOTS - 1)] = jnp.where(low, top, turned_bottom)
+                count = count + mask[k, j, at_row, 2 * cp]
+                out_ref[jnp.minimum(count, INT_SLOTS - 1)] = jnp.where(low, turned_top, bottom)
+                count = count + mask[k, j, at_row, 2 * cp + 1]
+            return count
+
+        count = lax.fori_loop(0, 16, body, count)
+
+
+def pack_amp_kernel(meta, mask, own_ref, oth_ref, out_ref):
+    v, r = meta[0], meta[2]
+    low = low_lanes(TILE)
+    for d in range(1, 4):
+        dest = lax.rem(v + d, 4)
+        count = jnp.int32(0)
+        for kk in range(4):
+            k = lax.rem(kk + 2 * r, 4)
+            ref = own_ref if kk < 2 else oth_ref
+
+            def body(n, count, d=d, kk=kk, k=k, ref=ref, dest=dest):
+                ap, cp = n // 2, n % 2
+                col = pl.multiple_of(dest * 256 + cp * LANES, LANES)
+                tiles = []
+                for a2 in range(2):
+                    row = pl.multiple_of(ap * 128 + a2 * TILE, TILE)
+                    x0 = ref[0, 0, 0, kk % 2, pl.ds(row, TILE), pl.ds(col, LANES)]
+                    x1 = ref[0, 0, 1, kk % 2, pl.ds(row, TILE), pl.ds(col, LANES)]
+                    tiles.append(
+                        (jnp.where(low, x0, swap_halves(x1)), jnp.where(low, swap_halves(x0), x1))
+                    )
+                for c2 in range(2):
+                    for a2 in range(2):
+                        out_ref[d - 1, jnp.minimum(count, AMP_SLOTS - 1)] = tiles[a2][c2]
+                        count = count + mask[k, 4 * v + 2 * ap + a2, 4 * dest + 2 * cp + c2]
+                return count
+
+            count = lax.fori_loop(0, 4, body, count)
+
+
+def unpack_int_kernel(d, meta, mask, buf_ref, d_ref, t_ref, count_ref):
+    v, r, j = meta[0], meta[2], meta[3]
+    kk = pl.program_id(0)
+    k = lax.rem(kk + 2 * r, 4)
+    s = lax.rem(v + 4 - d, 4)
+    low = low_lanes(32)
+    zero = jnp.zeros((32, LANES), jnp.bfloat16)
+
+    @pl.when(kk == 0)
+    def _():
+        count_ref[0] = 0
+
+    def body(n, count):
+        ap, cp = n // 8, n % 8
+        parts = []
+        for a2 in range(2):
+            at_row = 4 * s + 2 * ap + a2
+            m0, m1 = mask[k, j, at_row, 2 * cp], mask[k, j, at_row, 2 * cp + 1]
+            y0 = buf_ref[jnp.minimum(count, INT_SLOTS - 1)]
+            count = count + m0
+            y1 = buf_ref[jnp.minimum(count, INT_SLOTS - 1)]
+            count = count + m1
+            y0 = jnp.where(m0 > 0, y0, zero)
+            y1 = jnp.where(m1 > 0, y1, zero)
+            parts.append(jnp.where(low, y0, swap_halves(y1)))
+            parts.append(jnp.where(low, swap_halves(y0), y1))
+        block = jnp.concatenate(parts, axis=0)
+        row = pl.multiple_of(ap * 128, 128)
+        col = pl.multiple_of(cp * LANES, LANES)
+        d_ref[0, pl.ds(row, 128), pl.ds(col, LANES)] = block
+        t_ref[0, pl.ds(col, LANES), pl.ds(row, 128)] = block.T
+        return count
+
+    count_ref[0] = lax.fori_loop(0, 16, body, count_ref[0])
+
+
+def own_int_kernel(meta, mask, own_ref, oth_ref, d_ref, t_ref):
+    v, r, j = meta[0], meta[2], meta[3]
+    kk = pl.program_id(0)
+    k = lax.rem(kk + 2 * r, 4)
+    low = low_lanes(TILE)
+    zero = jnp.zeros((TILE, LANES), jnp.bfloat16)
+
+    def body(n, carry):
+        ap, cp = n // 8, n % 8
+        col = pl.multiple_of(cp * LANES, LANES)
+        parts = []
+        for a2 in range(2):
+            at_row = 4 * v + 2 * ap + a2
+            row = pl.multiple_of(ap * 128 + a2 * TILE, TILE)
+            m0, m1 = mask[k, j, at_row, 2 * cp], mask[k, j, at_row, 2 * cp + 1]
+            block = jnp.where(
+                kk < 2,
+                own_ref[0, 0, pl.ds(row, TILE), pl.ds(col, LANES)],
+                oth_ref[0, pl.ds(row, TILE), pl.ds(col, LANES)],
+            )
+            parts.append(
+                jnp.where(low, jnp.where(m0 > 0, block, zero), jnp.where(m1 > 0, block, zero))
+            )
+        block = jnp.concatenate(parts, axis=0)
+        row = pl.multiple_of(ap * 128, 128)
+        d_ref[0, pl.ds(row, 128), pl.ds(col, LANES)] = block
+        t_ref[0, pl.ds(col, LANES), pl.ds(row, 128)] = block.T
+        return carry
+
+    lax.fori_loop(0, 16, body, 0)
+
+
+def lane_scale(m0, m1, value):
+    lane = lax.broadcasted_iota(jnp.int32, (1, LANES), 1)
+    return value * jnp.where(lane < TILE, m0, m1).astype(jnp.float32)
+
+
+def combine_kernel(d, meta, mask, own_ref, oth_ref, near_ref, far_ref, out_ref, count_ref):
+    v, x, r = meta[0], meta[1], meta[2]
+    kk = pl.program_id(0)
+    k = lax.rem(kk + 2 * r, 4)
+    s = lax.rem(v + 4 - d, 4)
+    zero = jnp.zeros((TILE, LANES), jnp.bfloat16)
+
+    @pl.when(kk == 0)
+    def _():
+        count_ref[0] = 0
+
+    def body(n, count):
+        ap, c = n // 4, n % 4
+        arow = pl.multiple_of(c * TILE, TILE)
+        ccol = pl.multiple_of(ap * 128, 128)
+        slots, kept = [], []
+        for a2 in range(2):
+            m = mask[k, 4 * s + 2 * ap + a2, 4 * v + c]
+            slots.append(jnp.minimum(count, AMP_SLOTS - 1))
+            kept.append(m)
+            count = count + m
+        own_scale = lane_scale(
+            mask[k, 4 * v + c, 4 * s + 2 * ap], mask[k, 4 * v + c, 4 * s + 2 * ap + 1], 2.0
+        )
+        for xx, buf in ((x, near_ref), (1 - x, far_ref)):
+            stacked = jnp.concatenate(
+                [jnp.where(kept[a2] > 0, buf[slots[a2]], zero) for a2 in range(2)], axis=0
+            )
+            turned = stacked.T.astype(jnp.float32)
+            for ii in range(2):
+                local = jnp.where(
+                    kk < 2,
+                    own_ref[xx, 0, ii, 0, pl.ds(arow, TILE), pl.ds(ccol, 128)],
+                    oth_ref[xx, 0, ii, 0, pl.ds(arow, TILE), pl.ds(ccol, 128)],
+                ).astype(jnp.float32)
+                value = own_scale * local - turned[ii * TILE : (ii + 1) * TILE]
+                out_ref[xx, ii, pl.ds(arow, TILE), pl.ds(ccol, 128)] = value.astype(jnp.bfloat16)
+        return count
+
+    count_ref[0] = lax.fori_loop(0, 8, body, count_ref[0])
+
+
+def diagonal_kernel(meta, mask, own_ref, oth_ref, out_ref):
+    v, r = meta[0], meta[2]
+    kk = pl.program_id(0)
+    k = lax.rem(kk + 2 * r, 4)
+
+    def screened(xx, ii, a0, c0):
+        rows = []
+        for a2 in range(2):
+            start = a0 * 128 + a2 * TILE
+            block = jnp.where(
+                kk < 2,
+                own_ref[xx, 0, ii, 0, start : start + TILE, c0 * 128 : (c0 + 1) * 128],
+                oth_ref[xx, 0, ii, 0, start : start + TILE, c0 * 128 : (c0 + 1) * 128],
+            ).astype(jnp.float32)
+            at_row = 4 * v + 2 * a0 + a2
+            rows.append(
+                block
+                * lane_scale(
+                    mask[k, at_row, 4 * v + 2 * c0], mask[k, at_row, 4 * v + 2 * c0 + 1], 1.0
+                )
+            )
+        return jnp.concatenate(rows, axis=0)
+
+    for xx in range(2):
+        for ii in range(2):
+            for a0 in range(2):
+                for c0 in range(2):
+                    value = 2.0 * screened(xx, ii, a0, c0) - screened(xx, ii, c0, a0).T
+                    out_ref[xx, ii, a0 * 128 : (a0 + 1) * 128, c0 * 128 : (c0 + 1) * 128] = (
+                        value.astype(jnp.bfloat16)
+                    )
+
+
+def contract_kernel(
+    meta, eps_slab, eps_pair, eps_rows, eps_cols, *refs
+):
+    ints, own, oth, out_ref, w_ref = refs[:8], refs[8:12], refs[12:16], refs[16], refs[17]
+    v, r = meta[0], meta[2]
+    g = pl.program_id(0)
+
+    @pl.when(g == 0)
+    def _():
+        for q in range(4):
+            sq = lax.rem(v + 4 - q, 4)
+            for p in range(4):
+                sp = lax.rem(v + 4 - p, 4)
+                col = pl.multiple_of(sp * 256, 256)
+                row = pl.multiple_of(sq * 256, 256)
+
+                def body(k, carry, q=q, p=p, col=col, row=row):
+                    direct = ints[q][k, :, pl.ds(col, 256)].astype(jnp.float32)
+                    swapped = ints[4 + p][k, pl.ds(row, 256), :].astype(jnp.float32)
+                    w_ref[q, pl.ds(pl.multiple_of(k * 256, 256), 256), pl.ds(col, 256)] = (
+                        2.0 * direct - swapped
+                    ).astype(jnp.bfloat16)
+                    return carry
+
+                lax.fori_loop(0, 4, body, 0)
+
+    def work(blocks, i):
+        total = jnp.dot(blocks[0][0, 0], w_ref[0], preferred_element_type=jnp.float32)
+        for q in range(1, 4):
+            total += jnp.dot(blocks[q][0, 0], w_ref[q], preferred_element_type=jnp.float32)
+        value = total / ((eps_rows[...] + eps_cols[...]) - eps_slab[i] - eps_pair[0])
+        for n in range(8):
+            out_ref[pl.ds(n, 256, stride=8), :] = value[:, n * 128 : (n + 1) * 128]
+
+    @pl.when(g < 4)
+    def _():
+        work(own, 4 * (g // 2) + 2 * r + g % 2)
+
+    @pl.when(g >= 4)
+    def _():
+        work(oth, 4 * ((g - 4) // 2) + 2 * (1 - r) + g % 2)
+
+
+def smem():
+    return pl.BlockSpec(memory_space=pltpu.SMEM)
+
+
+def whole():
+    return pl.BlockSpec(memory_space=pltpu.VMEM)
+
+
+def params():
+    return pltpu.CompilerParams(vmem_limit_bytes=VMEM_LIMIT)
+
+
+def packed_shards(amplitudes, integrals, amp_mask, int_mask, eps_slab, eps_pair, eps_vir):
+    v, x, r = lax.axis_index("vir"), lax.axis_index("occ"), lax.axis_index("rep")
+    meta = jnp.stack([v, x, r, 2 * x + r]).astype(jnp.int32)
+    swap = [(0, 1), (1, 0)]
+    bf16 = jnp.bfloat16
+
+    pairs = amp_mask.reshape(4, 4, 4, 4, 4).sum((0, 2, 4))
+    pairs = jnp.where(jnp.eye(4, dtype=bool), 0, pairs)
+    pieces = int_mask.reshape(4, 4, 4, 4, 16).sum((0, 3, 4))
+    over = jnp.logical_or(jnp.max(pairs) > AMP_SLOTS - 1, jnp.max(pieces) > INT_SLOTS - 1)
+    over = over.astype(jnp.int32).reshape(1)
+    over = over + lax.ppermute(over, "frag", swap)
+
+    int_oth = lax.ppermute(
+        lax.dynamic_index_in_dim(integrals, 1 - r, 1, keepdims=False), "rep", swap
+    )
+    amps = amplitudes.reshape(2, 2, 2, 2, 256, 1024)
+    amp_oth = lax.ppermute(lax.dynamic_slice_in_dim(amps, 1 - r, 1, 1), "rep", swap)
+
+    packed_int = pl.pallas_call(
+        pack_int_kernel,
+        out_shape=jax.ShapeDtypeStruct((INT_SLOTS, 32, LANES), bf16),
+        in_specs=[smem(), smem(), whole(), whole()],
+        out_specs=whole(),
+        compiler_params=params(),
+        name="pack_int",
+    )(meta, int_mask, integrals, int_oth)
+
+    packed_amp = pl.pallas_call(
+        pack_amp_kernel,
+        grid_spec=pltpu.PrefetchScalarGridSpec(
+            num_scalar_prefetch=2,
+            grid=(1,),
+            in_specs=[
+                pl.BlockSpec((1, 1, 2, 2, 256, 1024), lambda g, meta, mask: (meta[1], meta[2], 0, 0, 0, 0)),
+                pl.BlockSpec((1, 1, 2, 2, 256, 1024), lambda g, meta, mask: (meta[1], 0, 0, 0, 0, 0)),
+            ],
+            out_specs=pl.BlockSpec((3, AMP_SLOTS, TILE, LANES), lambda g, meta, mask: (0, 0, 0, 0)),
+        ),
+        out_shape=jax.ShapeDtypeStruct((3, AMP_SLOTS, TILE, LANES), bf16),
+        compiler_params=params(),
+        name="pack_amp",
+    )(meta, amp_mask, amps, amp_oth)
+
+    near = [
+        lax.ppermute(packed_amp[d - 1], "vir", [(s, (s + d) % 4) for s in range(4)])
+        for d in (1, 2, 3)
+    ]
+    far = [lax.ppermute(a, "occ", swap) for a in near]
+
+    up1 = lax.ppermute(packed_int, "vir", [(0, 1), (1, 2), (2, 3)])
+    down1 = lax.ppermute(packed_int, "vir", [(1, 0), (2, 1), (3, 2)])
+    up2 = lax.ppermute(up1, "vir", [(1, 2), (2, 3)])
+    down2 = lax.ppermute(down1, "vir", [(1, 0), (2, 1)])
+    second = jnp.where(v < 2, down2, up2)
+    third = lax.ppermute(second, "vir", [(1, 0), (2, 3)])
+    arrived = {1: jnp.where(v == 0, third, up1), 2: second, 3: jnp.where(v == 3, third, down1)}
+
+    def k_place(kk, r):
+        return lax.rem(kk + 2 * r, 4)
+
+    int_shapes = [
+        jax.ShapeDtypeStruct((4, 256, 1024), bf16),
+        jax.ShapeDtypeStruct((4, 1024, 256), bf16),
+    ]
+    int_outs = [
+        pl.BlockSpec((1, 256, 1024), lambda kk, meta, mask: (k_place(kk, meta[2]), 0, 0)),
+        pl.BlockSpec((1, 1024, 256), lambda kk, meta, mask: (k_place(kk, meta[2]), 0, 0)),
+    ]
+    rows, cols = [], []
+    for d in range(4):
+        if d == 0:
+            kernel, scratch = own_int_kernel, []
+            specs = [
+                pl.BlockSpec((1, 1, 256, 1024), lambda kk, meta, mask: (jnp.minimum(kk, 1), meta[2], 0, 0)),
+                pl.BlockSpec((1, 256, 1024), lambda kk, meta, mask: (jnp.maximum(kk - 2, 0), 0, 0)),
+            ]
+            operands = (integrals, int_oth)
+        else:
+            kernel, scratch = functools.partial(unpack_int_kernel, d), [pltpu.SMEM((1,), jnp.int32)]
+            specs = [pl.BlockSpec((INT_SLOTS, 32, LANES), lambda kk, meta, mask: (0, 0, 0))]
+            operands = (arrived[d],)
+        direct, swapped = pl.pallas_call(
+            kernel,
+            grid_spec=pltpu.PrefetchScalarGridSpec(
+                num_scalar_prefetch=2, grid=(4,), in_specs=specs, out_specs=int_outs, scratch_shapes=scratch
+            ),
+            out_shape=int_shapes,
+            compiler_params=params(),
+            name=f"ints_{d}",
+        )(meta, int_mask, *operands)
+        rows.append(direct)
+        cols.append(swapped)
+
+    combined = []
+    for d in range(4):
+        local_specs = [
+            pl.BlockSpec(
+                (2, 1, 2, 1, 256, 256),
+                lambda kk, meta, mask, d=d: (0, meta[2], 0, jnp.minimum(kk, 1), 0, lax.rem(meta[0] + 4 - d, 4)),
+            ),
+            pl.BlockSpec(
+                (2, 1, 2, 1, 256, 256),
+                lambda kk, meta, mask, d=d: (0, 0, 0, jnp.maximum(kk - 2, 0), 0, lax.rem(meta[0] + 4 - d, 4)),
+            ),
+        ]
+        if d == 0:
+            kernel, scratch, specs, operands = diagonal_kernel, [], [], ()
+        else:
+            kernel, scratch = functools.partial(combine_kernel, d), [pltpu.SMEM((1,), jnp.int32)]
+            specs = [pl.BlockSpec((AMP_SLOTS, TILE, LANES), lambda kk, meta, mask: (0, 0, 0))] * 2
+            operands = (near[d - 1], far[d - 1])
+        combined.append(
+            pl.pallas_call(
+                kernel,
+                grid_spec=pltpu.PrefetchScalarGridSpec(
+                    num_scalar_prefetch=2,
+                    grid=(4,),
+                    in_specs=local_specs + specs,
+                    out_specs=pl.BlockSpec(
+                        (2, 2, 256, 256), lambda kk, meta, mask: (0, 0, 0, k_place(kk, meta[2]))
+                    ),
+                    scratch_shapes=scratch,
+                ),
+                out_shape=jax.ShapeDtypeStruct((2, 2, 256, 1024), bf16),
+                compiler_params=params(),
+                name=f"combine_{d}",
+            )(meta, amp_mask, amps, amp_oth, *operands)
+        )
+    combined_oth = [lax.ppermute(c, "rep", swap) for c in combined]
+
+    row_energy = lax.dynamic_slice_in_dim(eps_vir, v * 256, 256, 0).reshape(256, 1)
+    col_energy = eps_vir.reshape(1, 1024)
+
+    def contract(ops):
+        rows, cols, own, oth = ops
+        resident = [
+            pl.BlockSpec((4, 256, 1024), lambda g, *_: (0, 0, 0), pipeline_mode=pl.Buffered(1))
+        ] * 4 + [
+            pl.BlockSpec((4, 1024, 256), lambda g, *_: (0, 0, 0), pipeline_mode=pl.Buffered(1))
+        ] * 4
+
+        def own_at(g, *_):
+            g = jnp.minimum(g, 3)
+            return (g // 2, g % 2, 0, 0)
+
+        def oth_at(g, *_):
+            g = jnp.maximum(g - 4, 0)
+            return (g // 2, g % 2, 0, 0)
+
+        def out_at(g, meta, *_):
+            r = jnp.where(g < 4, meta[2], 1 - meta[2])
+            return (4 * ((g % 4) // 2) + 2 * r + g % 2, 0)
+
+        out = pl.pallas_call(
+            contract_kernel,
+            grid_spec=pltpu.PrefetchScalarGridSpec(
+                num_scalar_prefetch=3,
+                grid=(8,),
+                in_specs=[
+                    pl.BlockSpec((256, 1), lambda g, *_: (0, 0)),
+                    pl.BlockSpec((1, 1024), lambda g, *_: (0, 0)),
+                ]
+                + resident
+                + [pl.BlockSpec((1, 1, 256, 1024), own_at)] * 4
+                + [pl.BlockSpec((1, 1, 256, 1024), oth_at)] * 4,
+                out_specs=pl.BlockSpec((2048, 128), out_at),
+                scratch_shapes=[pltpu.VMEM((4, 1024, 1024), bf16)],
+            ),
+            out_shape=jax.ShapeDtypeStruct((8 * 2048, 128), jnp.float32),
+            compiler_params=params(),
+            name="contract",
+        )(meta, eps_slab, eps_pair, row_energy, col_energy, *rows, *cols, *own, *oth)
+        return out.reshape(8, 256, 1, 1024)
+
+    def dense(ops):
+        return dense_shards(amplitudes, integrals, amp_mask, int_mask, eps_slab, eps_pair, eps_vir)
+
+    return lax.cond(over[0] > 0, dense, contract, (rows, cols, combined, combined_oth))
+
+
+def shards(sizes, *args):
+    amplitudes, integrals, amp_mask, int_mask = args[:4]
+    fits = (
+        sizes == {"frag": 2, "vir": 4, "occ": 2, "rep": 2}
+        and amplitudes.shape == (8, 2, 256, 1024)
+        and integrals.shape == (2, 2, 256, 1024)
+        and amp_mask.shape == (4, 16, 16)
+        and int_mask.shape == (4, 4, 16, 16)
+    )
+    return packed_shards(*args) if fits else dense_shards(*args)
+
+
 def solution(mesh):
     in_specs = (
         P("frag", "rep", "vir", None),
@@ -74,4 +544,10 @@
         P("frag"),
     )
     out_specs = P("frag", "vir", ("occ", "rep"), None)
-    return jax.shard_map(shards, mesh=mesh, in_specs=in_specs, out_specs=out_specs, check_vma=False)
+    return jax.shard_map(
+        functools.partial(shards, dict(mesh.shape)),
+        mesh=mesh,
+        in_specs=in_specs,
+        out_specs=out_specs,
+        check_vma=False,
+    )

time: 535 us -> 309 us (0.58)
  waiting for transfers between devices: 363 us -> 78.6 us
  Pallas kernels: 0 us -> 134 us
  matrix products: 51.2 us -> 0 us
  local copies, waits for them, and re-layouts: 69.2 us -> 32.8 us
  starting transfers between devices: 5.88 us -> 35.2 us
  other arithmetic: 30.1 us -> 7.09 us
    all_to_all x1 -> x0, waiting for transfers between devices: 298 us -> none  [shards(): lax.all_to_all(screened, 'vir', split_axis=3, concat_axis=2, tiled=True)]
    pallas_call x0 -> x11, Pallas kernels: none -> 134 us  [the longest x8 83.1 us: packed_shards(): pl.pallas_call(kernel, grid_spec=pltpu.PrefetchScalarGridSpec(num_scalar_...]
    ppermute x0 -> x18, waiting for transfers between devices: none -> 78.6 us  [the longest x3 56.9 us: packed_shards(): lax.ppermute(packed_amp[d - 1], 'vir', [(s, (s + d) % 4) for s in range(4)])]
    unnamed x3 -> x0, waiting for transfers between devices: 64.6 us -> none
    dot_general x4 -> x0, matrix products: 51.2 us -> none  [the longest x1 26.8 us: cycle_terms(): jnp.einsum('ikac,kjbc->iajb', combined, gathered, preferred_element_type=...]
    ppermute x0 -> x18, starting transfers between devices: none -> 35.2 us  [the longest x4 11.2 us: packed_shards(): combined_oth = [lax.ppermute(c, 'rep', swap) for c in combined]]
    convert_element_type x2 -> x0, local copies, waits for them, and re-layouts: 29.3 us -> none  [the longest x1 17 us: shards(): jnp.swapaxes(received, 2, 3).astype(jnp.float32)]
    convert_element_type x3 -> x0, other arithmetic: 24.6 us -> none  [the longest x1 12.1 us: shards(): combined = (2.0 * screened.astype(jnp.float32) - jnp.swapaxes(received, 2...]
  transfers between devices with their start and end apart: 3 -> 18, of which waited for: 2 -> 5; matrix products, arithmetic and copies ran while one was open for 10% -> 3% of each run, Pallas kernels for 0% -> 33%
where the time goes in v1:
time: 309 us; the launch traced here: 303 us
  Pallas kernels  134 us (43%)
  waiting for transfers between devices  78.6 us (25%)
  starting transfers between devices  35.2 us (11%)
  local copies, waits for them, and re-layouts  32.8 us (11%)
  between operations  15.5 us (5%)
  other arithmetic  7.09 us (2%)
    pallas_call x8, Pallas kernels, packed_shards(): pl.pallas_call(kernel, grid_spec=pltpu.PrefetchScalarGridSpec(num_scalar_...  83.1 us
    ppermute x3, waiting for transfers between devices, packed_shards(): lax.ppermute(packed_amp[d - 1], 'vir', [(s, (s + d) % 4) for s in range(4)])  56.9 us
    pallas_call x1, Pallas kernels, contract(): pl.pallas_call(contract_kernel, grid_spec=pltpu.PrefetchScalarGridSpec(nu...  32.6 us
    ppermute x1, waiting for transfers between devices, packed_shards(): down1 = lax.ppermute(packed_int, 'vir', [(1, 0), (2, 1), (3, 2)])  12.1 us
    ppermute x4, starting transfers between devices, packed_shards(): combined_oth = [lax.ppermute(c, 'rep', swap) for c in combined]  11.2 us
    cond x1, local copies, waits for them, and re-layouts  10.1 us
    reshape x1, local copies, waits for them, and re-layouts, contract(): return out.reshape(8, 256, 1, 1024)  9.32 us
    pallas_call x1, Pallas kernels, packed_shards(): pl.pallas_call(pack_amp_kernel, grid_spec=pltpu.PrefetchScalarGridSpec(nu...  9.09 us
  transfers between devices with their start and end apart: 18, of which 5 were waited for; matrix products, arithmetic and copies ran while one was open for 3% of the time, Pallas kernels for 33%

profile of v1, /device:TPU:9, one launch (start us, length us, event | category | flops | bytes accessed | tf_op | source)
XLA Modules:
  0.0 303.2 jit_solution(4252449021077588188)
XLA Ops:
  6.5 4.8 %constant_dynamic-slice_fusion = bf16[2,1,2,2,256,1024]{5,4,3,2,1,0:T(8,128)(2,1)} fusion(bf16[2,2,2,2,256,1024]{5,4,3,2,1,0:T(8,128)(2,1)} %bitcast.69, s32[]{:T(128)S(6)} %select_n.54), kind=kLoop, calls=%fused_computation.38 | loop fusion | bytes 8388612 | tf_op jit(solution)/shard_map/dynamic_slice | solution.py:360
  13.2 7.3 %collective-permute-done.1.oth_ref = bf16[2,256,1024]{2,1,0:T(8,128)(2,1)S(1)} collective-permute-done((bf16[2,256,1024]{2,1,0:T(8,128)(2,1)}, bf16[2,256,1024]{2,1,0:T(8,128)(2,1)S(1)}, u32[]{:S(2)}, u32[]{:S(2)}) %collective-permute-start.1) | collective-permute-done | bytes 1048608 | tf_op jit(solution)/shard_map/ppermute | solution.py:356
  21.5 8.9 %pack_int.1 = bf16[160,32,128]{2,1,0:T(8,128)(2,1)} custom-call(s32[4]{0:T(128)S(1)} %pad_add_fusion.meta, s32[4,4,16,16]{3,2,1,0:T(8,128)S(1)} %copy-done.3, bf16[2,2,256,1024]{3,2,1,0:T(8,128)(2,1)S(1)} %copy-done, bf16[2,256,1024]{2,1,0:T(8,128)(2,1)} %copy-done.5), custom_call_target="tpu_custom_call" | custom-call | tf_op jit(solution)/shard_map/pack_int/pallas_call | solution.py:362
  32.4 3.4 %collective-permute-start.4 = (bf16[160,32,128]{2,1,0:T(8,128)(2,1)}, bf16[160,32,128]{2,1,0:T(8,128)(2,1)}, u32[]{:S(2)}, u32[]{:S(2)}) collective-permute-start(bf16[160,32,128]{2,1,0:T(8,128)(2,1)} %pack_int.1), channel_id=1, source_target_pairs={{0,4},{4,8},{8,12},{1,5},{5,9},{9,13},{2,6},{6,10},{10,14},{3,7},{... | collective-permute-start | bytes 3932168 | tf_op jit(solution)/shard_map/ppermute | solution.py:393
  35.8 9.1 %pack_amp.1 = bf16[3,46,64,128]{3,2,1,0:T(8,128)(2,1)} custom-call(s32[4]{0:T(128)S(1)} %pad_add_fusion.meta, s32[4,16,16]{2,1,0:T(8,128)S(1)} %copy-done.6, bf16[2,2,2,2,256,1024]{5,4,3,2,1,0:T(8,128)(2,1)} %bitcast.70, bf16[2,1,2,2,256,1024]{5,4,3,2,1,0:T(8,128)(2,1)} %collective-permute-done.7.oth_ref), custom_call_target="tpu_custom_call" | custom-call | tf_op jit(solution)/shard_map/pack_amp/pallas_call | solution.py:371
  44.8 2.0 slice_bitcast_fusion
  46.9 2.4 collective-permute-start.8
  50.6 12.1 %collective-permute-done.2 = bf16[160,32,128]{2,1,0:T(8,128)(2,1)} collective-permute-done((bf16[160,32,128]{2,1,0:T(8,128)(2,1)}, bf16[160,32,128]{2,1,0:T(8,128)(2,1)}, u32[]{:S(2)}, u32[]{:S(2)}) %collective-permute-start.2) | collective-permute-done | bytes 1310752 | tf_op jit(solution)/shard_map/ppermute | solution.py:394
  62.6 2.2 collective-permute-start.3
  64.9 5.2 %collective-permute-start.5 = (bf16[160,32,128]{2,1,0:T(8,128)(2,1)}, bf16[160,32,128]{2,1,0:T(8,128)(2,1)}, u32[]{:S(2)}, u32[]{:S(2)}) collective-permute-start(bf16[160,32,128]{2,1,0:T(8,128)(2,1)} %collective-permute-done.4), channel_id=1, source_target_pairs={{4,8},{8,12},{5,9},{9,13},{6,10},{10,14},{7,11},{11,15},{20,24},{2... | collective-permute-start | bytes 3932168 | tf_op jit(solution)/shard_map/ppermute | solution.py:395
  70.1 10.6 %collective-permute-done.8.near_ref = bf16[46,64,128]{2,1,0:T(8,128)(2,1)} collective-permute-done((bf16[46,64,128]{2,1,0:T(8,128)(2,1)S(1)}, bf16[46,64,128]{2,1,0:T(8,128)(2,1)}, u32[]{:S(2)}, u32[]{:S(2)}) %collective-permute-start.8) | collective-permute-done | bytes 753696 | tf_op jit(solution)/shard_map/ppermute | solution.py:388
  81.8 46.3 %collective-permute-done.10.near_ref = bf16[46,64,128]{2,1,0:T(8,128)(2,1)} collective-permute-done((bf16[46,64,128]{2,1,0:T(8,128)(2,1)S(1)}, bf16[46,64,128]{2,1,0:T(8,128)(2,1)}, u32[]{:S(2)}, u32[]{:S(2)}) %collective-permute-start.10) | collective-permute-done | bytes 753696 | tf_op jit(solution)/shard_map/ppermute | solution.py:388
  130.2 5.8 %combine_0.1 = bf16[2,2,256,1024]{3,2,1,0:T(8,128)(2,1)} custom-call(s32[4]{0:T(128)S(1)} %pad_add_fusion.meta, s32[4,16,16]{2,1,0:T(8,128)S(1)} %copy-done.6, bf16[2,2,2,2,256,1024]{5,4,3,2,1,0:T(8,128)(2,1)} %bitcast.71, bf16[2,1,2,2,256,1024]{5,4,3,2,1,0:T(8,128)(2,1)} %collective-permute-done.7.oth_ref), custom_call_target="tpu_custom_call" | custom-call | tf_op jit(solution)/shard_map/combine_0/pallas_call | solution.py:456
  136.0 3.2 %collective-permute-start.14 = (bf16[2,2,256,1024]{3,2,1,0:T(8,128)(2,1)}, bf16[2,2,256,1024]{3,2,1,0:T(8,128)(2,1)}, u32[]{:S(2)}, u32[]{:S(2)}) collective-permute-start(bf16[2,2,256,1024]{3,2,1,0:T(8,128)(2,1)} %combine_0.1), channel_id=1, source_target_pairs={{0,1},{1,0},{2,3},{3,2},{4,5},{5,4},{6,7},{7,6},{8,9},{9,8},{10,11... | collective-permute-start | bytes 6291464 | tf_op jit(solution)/shard_map/ppermute | solution.py:472
  139.2 7.2 %combine_1.1 = bf16[2,2,256,1024]{3,2,1,0:T(8,128)(2,1)} custom-call(s32[4]{0:T(128)S(1)} %pad_add_fusion.meta, s32[4,16,16]{2,1,0:T(8,128)S(1)} %copy-done.6, bf16[2,2,2,2,256,1024]{5,4,3,2,1,0:T(8,128)(2,1)} %bitcast.72, bf16[2,1,2,2,256,1024]{5,4,3,2,1,0:T(8,128)(2,1)} %collective-permute-done.7.oth_ref, ...), custom_call_target="tpu_custom_call" | custom-call | tf_op jit(solution)/shard_map/combine_1/pallas_call | solution.py:456
  146.4 4.4 %collective-permute-start.15 = (bf16[2,2,256,1024]{3,2,1,0:T(8,128)(2,1)}, bf16[2,2,256,1024]{3,2,1,0:T(8,128)(2,1)}, u32[]{:S(2)}, u32[]{:S(2)}) collective-permute-start(bf16[2,2,256,1024]{3,2,1,0:T(8,128)(2,1)} %combine_1.1), channel_id=1, source_target_pairs={{0,1},{1,0},{2,3},{3,2},{4,5},{5,4},{6,7},{7,6},{8,9},{9,8},{10,11... | collective-permute-start | bytes 6291464 | tf_op jit(solution)/shard_map/ppermute | solution.py:472
  150.8 7.2 %combine_2.1 = bf16[2,2,256,1024]{3,2,1,0:T(8,128)(2,1)} custom-call(s32[4]{0:T(128)S(1)} %pad_add_fusion.meta, s32[4,16,16]{2,1,0:T(8,128)S(1)} %copy-done.6, bf16[2,2,2,2,256,1024]{5,4,3,2,1,0:T(8,128)(2,1)} %bitcast.73, bf16[2,1,2,2,256,1024]{5,4,3,2,1,0:T(8,128)(2,1)} %collective-permute-done.7.oth_ref, ...), custom_call_target="tpu_custom_call" | custom-call | tf_op jit(solution)/shard_map/combine_2/pallas_call | solution.py:456
  158.0 2.2 collective-permute-done.13.far_ref
  160.2 3.6 %collective-permute-start.16 = (bf16[2,2,256,1024]{3,2,1,0:T(8,128)(2,1)}, bf16[2,2,256,1024]{3,2,1,0:T(8,128)(2,1)}, u32[]{:S(2)}, u32[]{:S(2)}) collective-permute-start(bf16[2,2,256,1024]{3,2,1,0:T(8,128)(2,1)} %combine_2.1), channel_id=1, source_target_pairs={{0,1},{1,0},{2,3},{3,2},{4,5},{5,4},{6,7},{7,6},{8,9},{9,8},{10,11... | collective-permute-start | bytes 6291464 | tf_op jit(solution)/shard_map/ppermute | solution.py:472
  163.8 7.2 %combine_3.1 = bf16[2,2,256,1024]{3,2,1,0:T(8,128)(2,1)} custom-call(s32[4]{0:T(128)S(1)} %pad_add_fusion.meta, s32[4,16,16]{2,1,0:T(8,128)S(1)} %copy-done.6, bf16[2,2,2,2,256,1024]{5,4,3,2,1,0:T(8,128)(2,1)} %bitcast.74, bf16[2,1,2,2,256,1024]{5,4,3,2,1,0:T(8,128)(2,1)} %collective-permute-done.7.oth_ref, bf16[46,64,128]{2,1,0:T(8,128)(2,1)} %copy-done.8, ...), custom_call_target="tpu_custom_call" | custom-call | tf_op jit(solution)/shard_map/combine_3/pallas_call | solution.py:456
  173.6 2.0 collective-permute-start
  177.1 2.4 collective-permute-start.6
  180.1 10.4 %ints_0.1 = (bf16[4,256,1024]{2,1,0:T(8,128)(2,1)}, bf16[4,1024,256]{2,1,0:T(8,128)(2,1)}) custom-call(s32[4]{0:T(128)S(1)} %pad_add_fusion.meta, s32[4,4,16,16]{3,2,1,0:T(8,128)S(1)} %copy-done.3, bf16[2,2,256,1024]{3,2,1,0:T(8,128)(2,1)S(1)} %copy-done, bf16[2,256,1024]{2,1,0:T(8,128)(2,1)} %copy-done.5), custom_call_target="tpu_custom_call" | custom-call | tf_op jit(solution)/shard_map/ints_0/pallas_call | solution.py:425
  190.5 15.1 %ints_2.1 = (bf16[4,256,1024]{2,1,0:T(8,128)(2,1)}, bf16[4,1024,256]{2,1,0:T(8,128)(2,1)}) custom-call(s32[4]{0:T(128)S(1)} %pad_add_fusion.meta, s32[4,4,16,16]{3,2,1,0:T(8,128)S(1)} %copy-done.3, bf16[160,32,128]{2,1,0:T(8,128)(2,1)} %copy-done.4), custom_call_target="tpu_custom_call" | custom-call | tf_op jit(solution)/shard_map/ints_2/pallas_call | solution.py:425
  205.6 3.8 %broadcast_select_fusion = (bf16[160,32,128]{2,1,0:T(8,128)(2,1)}, bf16[160,32,128]{2,1,0:T(8,128)(2,1)}) fusion(bf16[160,32,128]{2,1,0:T(8,128)(2,1)} %collective-permute-done.6, bf16[160,32,128]{2,1,0:T(8,128)(2,1)} %collective-permute-done.2, pred[]{:T(512)S(6)} %eq.14, bf16[160,32,128]{2,1,0:T(8,128)(2,1)} %collective-permute-done.4, pred[]{:T(512)S(6)} %eq.13), kind=kLoop, calls=%fused_computation.28 | loop fusion | flops 1310720 | bytes 6553602 | tf_op jit(solution)/shard_map/jit(_where)/select_n | solution.py:399
  209.5 15.2 %ints_3.1 = (bf16[4,256,1024]{2,1,0:T(8,128)(2,1)}, bf16[4,1024,256]{2,1,0:T(8,128)(2,1)}) custom-call(s32[4]{0:T(128)S(1)} %pad_add_fusion.meta, s32[4,4,16,16]{3,2,1,0:T(8,128)S(1)} %copy-done.3, bf16[160,32,128]{2,1,0:T(8,128)(2,1)} %get-tuple-element.166.buf_ref), custom_call_target="tpu_custom_call" | custom-call | tf_op jit(solution)/shard_map/ints_3/pallas_call | solution.py:425
  224.6 15.1 %ints_1.1 = (bf16[4,256,1024]{2,1,0:T(8,128)(2,1)}, bf16[4,1024,256]{2,1,0:T(8,128)(2,1)}) custom-call(s32[4]{0:T(128)S(1)} %pad_add_fusion.meta, s32[4,4,16,16]{3,2,1,0:T(8,128)S(1)} %copy-done.3, bf16[160,32,128]{2,1,0:T(8,128)(2,1)} %get-tuple-element.167.buf_ref), custom_call_target="tpu_custom_call" | custom-call | tf_op jit(solution)/shard_map/ints_1/pallas_call | solution.py:425
  239.8 53.1 %conditional.1 = (f32[8,256,1,1024]{3,2,1,0:T(1,128)S(1)}) conditional(s32[]{:T(128)} %bitcast.23, (s32[]{:T(128)}, f32[1024]{0:T(1024)S(1)}, s32[4]{0:T(128)S(1)}, f32[8]{0:T(128)S(1)}, f32[1]{0:T(128)}, /*index=5*/bf16[4,256,1024]{2,1,0:T(8,128)(2,1)}, bf16[4,256,1024]{2,1,0:T(8,128)(2,1)}, bf16[4,256,1024]{2,1,0:T(8,128)(2,1)}, ...), branch_computations={%region_6.7_spmd, %region_7.9_spmd} | conditional | flops 34424766464 | bytes 426019776 | solution.py:521
  240.7 32.6 %contract.1 = f32[16384,128]{1,0:T(8,128)} custom-call(s32[4]{0:T(128)S(1)} %get-tuple-element.77.meta, f32[8]{0:T(128)S(1)} %get-tuple-element.78.eps_slab, f32[1]{0:T(128)} %get-tuple-element.79.eps_pair, f32[256,1]{1,0:T(8,128)} %copy.51.eps_rows, f32[1,1024]{1,0:T(1,128)S(1)} %bitcast.79, bf16[4,256,1024]{2,1,0:T(8,128)(2,1)} %get-tuple-element.82.refs_0_, ...), custom_call_target="tpu_custom_call" | custom-call | tf_op jit(solution)/shard_map/cond/branch_0_fun/contract/pallas_call | solution.py:497
  273.3 9.3 %reshape.98 = f32[8,256,1,1024]{3,1,0,2:T(8,128)} reshape(f32[16384,128]{1,0:T(8,128)} %contract.1) | data formatting | bytes 16777216 | tf_op jit(solution)/shard_map/cond/branch_0_fun/reshape | solution.py:516
  282.7 10.1 %copy.74 = f32[8,256,1,1024]{3,2,1,0:T(1,128)S(1)} copy(f32[8,256,1,1024]{3,1,2,0:T(8,128)} %bitcast.76) | data formatting | bytes 16777216 | tf_op jit(solution)/shard_map/cond
  293.0 3.4 %copy-done.2 = f32[8,256,1,1024]{3,2,1,0:T(1,128)} copy-done((f32[8,256,1,1024]{3,2,1,0:T(1,128)}, f32[8,256,1,1024]{3,2,1,0:T(1,128)S(1)}, u32[]{:S(2)}) %copy-start.2) | copy-done | bytes 8388632
  (54 shorter events, 12.8 us)
Async XLA Ops:
  6.5 5.5 %copy-start = (bf16[2,2,256,1024]{3,2,1,0:T(8,128)(2,1)S(1)}, bf16[2,2,256,1024]{3,2,1,0:T(8,128)(2,1)}, u32[]{:S(2)}) copy-start(bf16[2,2,256,1024]{3,2,1,0:T(8,128)(2,1)} %own_ref.3) | copy-start | bytes 6291460
  6.5 15.0 %copy-start.3 = (s32[4,4,16,16]{3,2,1,0:T(8,128)S(1)}, s32[4,4,16,16]{3,2,1,0:T(8,128)}, u32[]{:S(2)}) copy-start(s32[4,4,16,16]{3,2,1,0:T(8,128)} %mask.14) | copy-start | bytes 49156
  6.5 29.2 %copy-start.6 = (s32[4,16,16]{2,1,0:T(8,128)S(1)}, s32[4,16,16]{2,1,0:T(8,128)}, u32[]{:S(2)}) copy-start(s32[4,16,16]{2,1,0:T(8,128)} %mask.19) | copy-start | bytes 12292
  11.3 24.4 %collective-permute-start.7 = (bf16[2,1,2,2,256,1024]{5,4,3,2,1,0:T(8,128)(2,1)}, bf16[2,1,2,2,256,1024]{5,4,3,2,1,0:T(8,128)(2,1)}, u32[]{:S(2)}, u32[]{:S(2)}) collective-permute-start(bf16[2,1,2,2,256,1024]{5,4,3,2,1,0:T(8,128)(2,1)} %constant_dynamic-slice_fusion), channel_id=1, source_target_pairs={{0,1},{1,0},{2,3},{3,2},{4,5},{5,4},{6,7},{7,6},{8,9},{9,8},{10,11... | collective-permute-start | bytes 12582920 | tf_op jit(solution)/shard_map/ppermute | solution.py:360
  13.1 7.4 %collective-permute-start.1 = (bf16[2,256,1024]{2,1,0:T(8,128)(2,1)}, bf16[2,256,1024]{2,1,0:T(8,128)(2,1)S(1)}, u32[]{:S(2)}, u32[]{:S(2)}) collective-permute-start(bf16[2,256,1024]{2,1,0:T(8,128)(2,1)} %dynamic-slice_bitcast_fusion), channel_id=1, source_target_pairs={{0,1},{1,0},{2,3},{3,2},{4,5},{5,4},{6,7},{7,6},{8,9},{9,8},{10,11... | collective-permute-start | bytes 3145736 | tf_op jit(solution)/shard_map/ppermute | solution.py:356
  20.5 1.0 copy-start.5
  30.4 32.2 %collective-permute-start.2 = (bf16[160,32,128]{2,1,0:T(8,128)(2,1)}, bf16[160,32,128]{2,1,0:T(8,128)(2,1)}, u32[]{:S(2)}, u32[]{:S(2)}) collective-permute-start(bf16[160,32,128]{2,1,0:T(8,128)(2,1)} %pack_int.1), channel_id=1, source_target_pairs={{4,0},{8,4},{12,8},{5,1},{9,5},{13,9},{6,2},{10,6},{14,10},{7,3},{... | collective-permute-start | bytes 3932168 | tf_op jit(solution)/shard_map/ppermute | solution.py:394
  32.4 32.5 %collective-permute-start.4 = (bf16[160,32,128]{2,1,0:T(8,128)(2,1)}, bf16[160,32,128]{2,1,0:T(8,128)(2,1)}, u32[]{:S(2)}, u32[]{:S(2)}) collective-permute-start(bf16[160,32,128]{2,1,0:T(8,128)(2,1)} %pack_int.1), channel_id=1, source_target_pairs={{0,4},{4,8},{8,12},{1,5},{5,9},{9,13},{2,6},{6,10},{10,14},{3,7},{... | collective-permute-start | bytes 3932168 | tf_op jit(solution)/shard_map/ppermute | solution.py:393
  46.9 33.8 %collective-permute-start.8 = (bf16[46,64,128]{2,1,0:T(8,128)(2,1)S(1)}, bf16[46,64,128]{2,1,0:T(8,128)(2,1)}, u32[]{:S(2)}, u32[]{:S(2)}) collective-permute-start(bf16[46,64,128]{2,1,0:T(8,128)(2,1)S(1)} %get-tuple-element.165), channel_id=1, source_target_pairs={{0,4},{4,8},{8,12},{12,0},{1,5},{5,9},{9,13},{13,1},{2,6},{6,10},{... | collective-permute-start | bytes 2261000 | tf_op jit(solution)/shard_map/ppermute | solution.py:388
  49.3 78.7 %collective-permute-start.10 = (bf16[46,64,128]{2,1,0:T(8,128)(2,1)S(1)}, bf16[46,64,128]{2,1,0:T(8,128)(2,1)}, u32[]{:S(2)}, u32[]{:S(2)}) collective-permute-start(bf16[46,64,128]{2,1,0:T(8,128)(2,1)S(1)} %get-tuple-element.164), channel_id=1, source_target_pairs={{0,8},{4,12},{8,0},{12,4},{1,9},{5,13},{9,1},{13,5},{2,10},{6,14},... | collective-permute-start | bytes 2261000 | tf_op jit(solution)/shard_map/ppermute | solution.py:388
  50.1 79.2 %collective-permute-start.12 = (bf16[46,64,128]{2,1,0:T(8,128)(2,1)S(1)}, bf16[46,64,128]{2,1,0:T(8,128)(2,1)S(1)}, u32[]{:S(2)}, u32[]{:S(2)}) collective-permute-start(bf16[46,64,128]{2,1,0:T(8,128)(2,1)S(1)} %get-tuple-element.163), channel_id=1, source_target_pairs={{0,12},{4,0},{8,4},{12,8},{1,13},{5,1},{9,5},{13,9},{2,14},{6,2},{... | collective-permute-start | bytes 2261000 | tf_op jit(solution)/shard_map/ppermute | solution.py:388
  62.6 108.3 %collective-permute-start.3 = (bf16[160,32,128]{2,1,0:T(8,128)(2,1)}, bf16[160,32,128]{2,1,0:T(8,128)(2,1)}, u32[]{:S(2)}, u32[]{:S(2)}) collective-permute-start(bf16[160,32,128]{2,1,0:T(8,128)(2,1)} %collective-permute-done.2), channel_id=1, source_target_pairs={{4,0},{8,4},{5,1},{9,5},{6,2},{10,6},{7,3},{11,7},{20,16},{24,20},... | collective-permute-start | bytes 3932168 | tf_op jit(solution)/shard_map/ppermute | solution.py:396
  64.9 108.7 %collective-permute-start.5 = (bf16[160,32,128]{2,1,0:T(8,128)(2,1)}, bf16[160,32,128]{2,1,0:T(8,128)(2,1)}, u32[]{:S(2)}, u32[]{:S(2)}) collective-permute-start(bf16[160,32,128]{2,1,0:T(8,128)(2,1)} %collective-permute-done.4), channel_id=1, source_target_pairs={{4,8},{8,12},{5,9},{9,13},{6,10},{10,14},{7,11},{11,15},{20,24},{2... | collective-permute-start | bytes 3932168 | tf_op jit(solution)/shard_map/ppermute | solution.py:395
  80.7 55.2 %collective-permute-start.9 = (bf16[46,64,128]{2,1,0:T(8,128)(2,1)}, bf16[46,64,128]{2,1,0:T(8,128)(2,1)}, u32[]{:S(2)}, u32[]{:S(2)}) collective-permute-start(bf16[46,64,128]{2,1,0:T(8,128)(2,1)} %collective-permute-done.8.near_ref), channel_id=1, source_target_pairs={{0,2},{2,0},{1,3},{3,1},{4,6},{6,4},{5,7},{7,5},{8,10},{10,8},{9,1... | collective-permute-start | bytes 2261000 | tf_op jit(solution)/shard_map/ppermute | solution.py:391
  128.0 18.3 %collective-permute-start.11 = (bf16[46,64,128]{2,1,0:T(8,128)(2,1)}, bf16[46,64,128]{2,1,0:T(8,128)(2,1)}, u32[]{:S(2)}, u32[]{:S(2)}) collective-permute-start(bf16[46,64,128]{2,1,0:T(8,128)(2,1)} %collective-permute-done.10.near_ref), channel_id=1, source_target_pairs={{0,2},{2,0},{1,3},{3,1},{4,6},{6,4},{5,7},{7,5},{8,10},{10,8},{9,1... | collective-permute-start | bytes 2261000 | tf_op jit(solution)/shard_map/ppermute | solution.py:391
  129.3 17.1 %copy-start.8 = (bf16[46,64,128]{2,1,0:T(8,128)(2,1)}, bf16[46,64,128]{2,1,0:T(8,128)(2,1)S(1)}, u32[]{:S(2)}) copy-start(bf16[46,64,128]{2,1,0:T(8,128)(2,1)S(1)} %collective-permute-done.12.near_ref) | copy-start | bytes 2260996
  129.3 30.9 %collective-permute-start.13 = (bf16[46,64,128]{2,1,0:T(8,128)(2,1)S(1)}, bf16[46,64,128]{2,1,0:T(8,128)(2,1)}, u32[]{:S(2)}, u32[]{:S(2)}) collective-permute-start(bf16[46,64,128]{2,1,0:T(8,128)(2,1)S(1)} %collective-permute-done.12.near_ref), channel_id=1, source_target_pairs={{0,2},{2,0},{1,3},{3,1},{4,6},{6,4},{5,7},{7,5},{8,10},{10,8},{9,1... | collective-permute-start | bytes 2261000 | tf_op jit(solution)/shard_map/ppermute | solution.py:391
  136.0 103.8 %collective-permute-start.14 = (bf16[2,2,256,1024]{3,2,1,0:T(8,128)(2,1)}, bf16[2,2,256,1024]{3,2,1,0:T(8,128)(2,1)}, u32[]{:S(2)}, u32[]{:S(2)}) collective-permute-start(bf16[2,2,256,1024]{3,2,1,0:T(8,128)(2,1)} %combine_0.1), channel_id=1, source_target_pairs={{0,1},{1,0},{2,3},{3,2},{4,5},{5,4},{6,7},{7,6},{8,9},{9,8},{10,11... | collective-permute-start | bytes 6291464 | tf_op jit(solution)/shard_map/ppermute | solution.py:472
  146.4 93.4 %collective-permute-start.15 = (bf16[2,2,256,1024]{3,2,1,0:T(8,128)(2,1)}, bf16[2,2,256,1024]{3,2,1,0:T(8,128)(2,1)}, u32[]{:S(2)}, u32[]{:S(2)}) collective-permute-start(bf16[2,2,256,1024]{3,2,1,0:T(8,128)(2,1)} %combine_1.1), channel_id=1, source_target_pairs={{0,1},{1,0},{2,3},{3,2},{4,5},{5,4},{6,7},{7,6},{8,9},{9,8},{10,11... | collective-permute-start | bytes 6291464 | tf_op jit(solution)/shard_map/ppermute | solution.py:472
  160.2 79.6 %collective-permute-start.16 = (bf16[2,2,256,1024]{3,2,1,0:T(8,128)(2,1)}, bf16[2,2,256,1024]{3,2,1,0:T(8,128)(2,1)}, u32[]{:S(2)}, u32[]{:S(2)}) collective-permute-start(bf16[2,2,256,1024]{3,2,1,0:T(8,128)(2,1)} %combine_2.1), channel_id=1, source_target_pairs={{0,1},{1,0},{2,3},{3,2},{4,5},{5,4},{6,7},{7,6},{8,9},{9,8},{10,11... | collective-permute-start | bytes 6291464 | tf_op jit(solution)/shard_map/ppermute | solution.py:472
  170.9 68.8 %collective-permute-start.17 = (bf16[2,2,256,1024]{3,2,1,0:T(8,128)(2,1)}, bf16[2,2,256,1024]{3,2,1,0:T(8,128)(2,1)}, u32[]{:S(2)}, u32[]{:S(2)}) collective-permute-start(bf16[2,2,256,1024]{3,2,1,0:T(8,128)(2,1)} %combine_3.1), channel_id=1, source_target_pairs={{0,1},{1,0},{2,3},{3,2},{4,5},{5,4},{6,7},{7,6},{8,9},{9,8},{10,11... | collective-permute-start | bytes 6291464 | tf_op jit(solution)/shard_map/ppermute | solution.py:472
  173.6 66.2 %copy-start.9 = (f32[1024]{0:T(1024)S(1)}, f32[1024]{0:T(1024)}, u32[]{:S(2)}) copy-start(f32[1024]{0:T(1024)} %param.15) | copy-start | bytes 12292
  173.6 66.2 %copy-start.10 = (f32[8]{0:T(128)S(1)}, f32[8]{0:T(128)}, u32[]{:S(2)}) copy-start(f32[8]{0:T(128)} %param.13) | copy-start | bytes 100
  173.6 3.5 %collective-permute-start = (s32[1]{0:T(128)}, s32[1]{0:T(128)}, u32[]{:S(2)}, u32[]{:S(2)}) collective-permute-start(s32[1]{0:T(128)} %bitcast.22), channel_id=1, source_target_pairs={{0,16},{16,0},{1,17},{17,1},{2,18},{18,2},{3,19},{19,3},{4,20},{20... | collective-permute-start | bytes 20 | tf_op jit(solution)/shard_map/ppermute | solution.py:354
  177.1 13.5 %copy-start.4 = (bf16[160,32,128]{2,1,0:T(8,128)(2,1)}, bf16[160,32,128]{2,1,0:T(8,128)(2,1)S(1)}, u32[]{:S(2)}) copy-start(bf16[160,32,128]{2,1,0:T(8,128)(2,1)S(1)} %broadcast_select_fusion.1.buf_ref) | copy-start | bytes 3932164
  177.1 28.6 %collective-permute-start.6 = (bf16[160,32,128]{2,1,0:T(8,128)(2,1)S(1)}, bf16[160,32,128]{2,1,0:T(8,128)(2,1)}, u32[]{:S(2)}, u32[]{:S(2)}) collective-permute-start(bf16[160,32,128]{2,1,0:T(8,128)(2,1)S(1)} %broadcast_select_fusion.1.buf_ref), channel_id=1, source_target_pairs={{4,0},{8,12},{5,1},{9,13},{6,2},{10,14},{7,3},{11,15},{20,16},{24,... | collective-permute-start | bytes 3932168 | tf_op jit(solution)/shard_map/ppermute | solution.py:398
  205.6 34.2 %copy-start.7 = (s32[4,16,16]{2,1,0:T(8,128)S(1)}, s32[4,16,16]{2,1,0:T(8,128)}, u32[]{:S(2)}) copy-start(s32[4,16,16]{2,1,0:T(8,128)} %mask.19) | copy-start | bytes 12292
  293.0 3.4 %copy-start.2 = (f32[8,256,1,1024]{3,2,1,0:T(1,128)}, f32[8,256,1,1024]{3,2,1,0:T(1,128)S(1)}, u32[]{:S(2)}) copy-start(f32[8,256,1,1024]{3,2,1,0:T(1,128)S(1)} %get-tuple-element.179) | copy-start | bytes 25165828

commit v2 on v0

--- a/solution.py
+++ b/solution.py
@@ -1,9 +1,18 @@
+import functools
+
 import jax
 import jax.numpy as jnp
 from jax import lax
+from jax.experimental import pallas as pl
+from jax.experimental.pallas import tpu as pltpu
 from jax.sharding import PartitionSpec as P
 
 TILE = 64
+LANES = 128
+AMP_SLOTS = 46
+INT_SLOTS = 160
+VMEM_LIMIT = 60 * 1024 * 1024
+NO_COST = pl.CostEstimate(flops=1024, bytes_accessed=1024, transcendentals=0)
 
 
 def tile_mask(mask_tiles, row_start, row_count, tile_size):
@@ -26,7 +35,7 @@
     return 2.0 * direct_term - swapped_term
 
 
-def shards(amplitudes, integrals, amp_mask, int_mask, eps_slab, eps_pair, eps_vir):
+def dense_shards(amplitudes, integrals, amp_mask, int_mask, eps_slab, eps_pair, eps_vir):
     row_count = amplitudes.shape[2]
     half_count = amplitudes.shape[1]
     pair_count = integrals.shape[1]
@@ -63,6 +72,612 @@
     return cycle / denominator
 
 
+def low_lanes(rows):
+    return lax.broadcasted_iota(jnp.int32, (rows, LANES), 1) < TILE
+
+
+def swap_halves(block):
+    return pltpu.roll(block, TILE, 1)
+
+
+def fill(buf, choices):
+    for chosen, ref in choices:
+
+        @pl.when(chosen)
+        def _(ref=ref):
+            pltpu.sync_copy(ref, buf)
+
+
+def pack_int_kernel(meta, mask, own_ref, oth_ref, out_ref):
+    v, r, j = meta[0], meta[2], meta[3]
+    low = low_lanes(32)
+    count = jnp.int32(0)
+    for half in range(2):
+
+        def body(n, count, half=half):
+            kk, ap = n // 2, n % 2
+            k = lax.rem(kk + 2 * half + 2 * r, 4)
+            for cp in range(8):
+                for a2 in range(2):
+                    row = pl.multiple_of(ap * 128 + a2 * TILE, TILE)
+                    if half == 0:
+                        block = own_ref[kk, r, pl.ds(row, TILE), cp * LANES : (cp + 1) * LANES]
+                    else:
+                        block = oth_ref[kk, r, pl.ds(row, TILE), cp * LANES : (cp + 1) * LANES]
+                    top, bottom = block[:32], block[32:]
+                    turned_top, turned_bottom = swap_halves(top), swap_halves(bottom)
+                    at_row = 4 * v + 2 * ap + a2
+                    out_ref[jnp.minimum(count, INT_SLOTS - 1)] = jnp.where(low, top, turned_bottom)
+                    count = count + mask[k, j, at_row, 2 * cp]
+                    out_ref[jnp.minimum(count, INT_SLOTS - 1)] = jnp.where(low, turned_top, bottom)
+                    count = count + mask[k, j, at_row, 2 * cp + 1]
+            return count
+
+        count = lax.fori_loop(0, 4, body, count)
+
+
+def pack_amp_kernel(meta, mask, own_ref, oth_ref, *out_refs):
+    v, r = meta[0], meta[2]
+    low = low_lanes(TILE)
+    for d in range(1, 4):
+        dest = v ^ d
+        count = jnp.int32(0)
+        for half in range(2):
+            ref = own_ref if half == 0 else oth_ref
+
+            def body(kk, count, d=d, dest=dest, half=half, ref=ref):
+                k = lax.rem(kk + 2 * half + 2 * r, 4)
+                for ap in range(2):
+                    for cp in range(2):
+                        col = pl.multiple_of(dest * 256 + cp * LANES, LANES)
+                        tiles = []
+                        for a2 in range(2):
+                            row = ap * 128 + a2 * TILE
+                            x0 = ref[0, 0, 0, kk, row : row + TILE, pl.ds(col, LANES)]
+                            x1 = ref[0, 0, 1, kk, row : row + TILE, pl.ds(col, LANES)]
+                            tiles.append(
+                                (jnp.where(low, x0, swap_halves(x1)), jnp.where(low, swap_halves(x0), x1))
+                            )
+                        for c2 in range(2):
+                            for a2 in range(2):
+                                out_refs[d - 1][jnp.minimum(count, AMP_SLOTS - 1)] = tiles[a2][c2]
+                                count = count + mask[k, 4 * v + 2 * ap + a2, 4 * dest + 2 * cp + c2]
+                return count
+
+            count = lax.fori_loop(0, 2, body, count)
+
+
+def unpack_group(buf_ref, mask, k, j, s, ap, count, d_ref, t_ref, at):
+    low = low_lanes(32)
+    zero = jnp.zeros((32, LANES), jnp.bfloat16)
+    row = pl.multiple_of(ap * 128, 128)
+    for cp in range(8):
+        parts = []
+        for a2 in range(2):
+            at_row = 4 * s + 2 * ap + a2
+            m0, m1 = mask[k, j, at_row, 2 * cp], mask[k, j, at_row, 2 * cp + 1]
+            y0 = buf_ref[jnp.minimum(count, INT_SLOTS - 1)]
+            count = count + m0
+            y1 = buf_ref[jnp.minimum(count, INT_SLOTS - 1)]
+            count = count + m1
+            y0 = jnp.where(m0 > 0, y0, zero)
+            y1 = jnp.where(m1 > 0, y1, zero)
+            parts.append(jnp.where(low, y0, swap_halves(y1)))
+            parts.append(jnp.where(low, swap_halves(y0), y1))
+        block = jnp.concatenate(parts, axis=0)
+        d_ref[at, pl.ds(row, 128), cp * LANES : (cp + 1) * LANES] = block
+        t_ref[at, cp * LANES : (cp + 1) * LANES, pl.ds(row, 128)] = block.T
+    return count
+
+
+def unpack_int_kernel(d, meta, mask, down_ref, up_ref, d_ref, t_ref, buf_ref, count_ref):
+    v, r, j = meta[0], meta[2], meta[3]
+    kk = pl.program_id(0)
+    k = lax.rem(kk + 2 * r, 4)
+    s = v ^ d
+
+    @pl.when(kk == 0)
+    def _():
+        count_ref[0] = 0
+        fill(buf_ref, [(s > v, down_ref), (s < v, up_ref)])
+
+    count_ref[0] = lax.fori_loop(
+        0,
+        2,
+        lambda ap, count: unpack_group(buf_ref, mask, k, j, s, ap, count, d_ref, t_ref, 0),
+        count_ref[0],
+    )
+
+
+def own_int_kernel(meta, mask, own_ref, oth_ref, d_ref, t_ref):
+    v, r, j = meta[0], meta[2], meta[3]
+    kk = pl.program_id(0)
+    k = lax.rem(kk + 2 * r, 4)
+    low = low_lanes(TILE)
+    zero = jnp.zeros((TILE, LANES), jnp.bfloat16)
+
+    def body(ap, carry):
+        for cp in range(8):
+            parts = []
+            for a2 in range(2):
+                at_row = 4 * v + 2 * ap + a2
+                row = pl.multiple_of(ap * 128 + a2 * TILE, TILE)
+                m0, m1 = mask[k, j, at_row, 2 * cp], mask[k, j, at_row, 2 * cp + 1]
+                block = jnp.where(
+                    kk < 2,
+                    own_ref[0, 0, pl.ds(row, TILE), cp * LANES : (cp + 1) * LANES],
+                    oth_ref[0, 0, pl.ds(row, TILE), cp * LANES : (cp + 1) * LANES],
+                )
+                parts.append(
+                    jnp.where(low, jnp.where(m0 > 0, block, zero), jnp.where(m1 > 0, block, zero))
+                )
+            block = jnp.concatenate(parts, axis=0)
+            row = pl.multiple_of(ap * 128, 128)
+            d_ref[0, pl.ds(row, 128), cp * LANES : (cp + 1) * LANES] = block
+            t_ref[0, cp * LANES : (cp + 1) * LANES, pl.ds(row, 128)] = block.T
+        return carry
+
+    lax.fori_loop(0, 2, body, 0)
+
+
+def lane_scale(m0, m1, value):
+    lane = lax.broadcasted_iota(jnp.int32, (1, LANES), 1)
+    return value * jnp.where(lane < TILE, m0, m1).astype(jnp.float32)
+
+
+def combine_kernel(d, base, meta, mask, own_ref, oth_ref, near_ref, far_ref, *refs):
+    if d == 3:
+        out_ref, count_ref = refs[-2:]
+    else:
+        out_ref, count_ref = refs[1:]
+    v, x, r = meta[0], meta[1], meta[2]
+    kk = pl.program_id(0) + base
+    k = lax.rem(kk + 2 * r, 4)
+    s = v ^ d
+    zero = jnp.zeros((TILE, LANES), jnp.bfloat16)
+
+    @pl.when(pl.program_id(0) == 0)
+    def _():
+        count_ref[0] = 0 if base == 0 else refs[0][0]
+
+    def body(ap, count):
+        ccol = pl.multiple_of(ap * 128, 128)
+        for c in range(4):
+            arow = c * TILE
+            slots, kept = [], []
+            for a2 in range(2):
+                m = mask[k, 4 * s + 2 * ap + a2, 4 * v + c]
+                slots.append(jnp.minimum(count, AMP_SLOTS - 1))
+                kept.append(m)
+                count = count + m
+            own_scale = lane_scale(
+                mask[k, 4 * v + c, 4 * s + 2 * ap], mask[k, 4 * v + c, 4 * s + 2 * ap + 1], 2.0
+            )
+            for xx, buf in ((x, near_ref), (1 - x, far_ref)):
+                stacked = jnp.concatenate(
+                    [jnp.where(kept[a2] > 0, buf[slots[a2]], zero) for a2 in range(2)], axis=0
+                )
+                turned = stacked.T.astype(jnp.float32)
+                for ii in range(2):
+                    local = jnp.where(
+                        kk < 2,
+                        own_ref[xx, 0, ii, 0, pl.ds(arow, TILE), pl.ds(ccol, 128)],
+                        oth_ref[xx, 0, ii, 0, pl.ds(arow, TILE), pl.ds(ccol, 128)],
+                    ).astype(jnp.float32)
+                    value = own_scale * local - turned[ii * TILE : (ii + 1) * TILE]
+                    out_ref[0, xx, ii, pl.ds(arow, TILE), pl.ds(ccol, 128)] = value.astype(jnp.bfloat16)
+        return count
+
+    count_ref[0] = lax.fori_loop(0, 2, body, count_ref[0])
+
+
+def diagonal_kernel(meta, mask, own_ref, oth_ref, out_ref):
+    v, r = meta[0], meta[2]
+    kk = pl.program_id(0)
+    k = lax.rem(kk + 2 * r, 4)
+
+    def screened(xx, ii, a0, c0):
+        rows = []
+        for a2 in range(2):
+            start = a0 * 128 + a2 * TILE
+            block = jnp.where(
+                kk < 2,
+                own_ref[xx, 0, ii, 0, start : start + TILE, c0 * 128 : (c0 + 1) * 128],
+                oth_ref[xx, 0, ii, 0, start : start + TILE, c0 * 128 : (c0 + 1) * 128],
+            ).astype(jnp.float32)
+            at_row = 4 * v + 2 * a0 + a2
+            rows.append(
+                block
+                * lane_scale(
+                    mask[k, at_row, 4 * v + 2 * c0], mask[k, at_row, 4 * v + 2 * c0 + 1], 1.0
+                )
+            )
+        return jnp.concatenate(rows, axis=0)
+
+    for xx in range(2):
+        for ii in range(2):
+            for a0 in range(2):
+                for c0 in range(2):
+                    value = 2.0 * screened(xx, ii, a0, c0) - screened(xx, ii, c0, a0).T
+                    out_ref[0, xx, ii, a0 * 128 : (a0 + 1) * 128, c0 * 128 : (c0 + 1) * 128] = (
+                        value.astype(jnp.bfloat16)
+                    )
+
+
+def folded(direct, swapped):
+    return (2.0 * direct.astype(jnp.float32) - swapped.astype(jnp.float32)).astype(jnp.bfloat16)
+
+
+def early_kernel(meta, *refs):
+    direct, swapped, own, oth, out_ref, w_ref = (
+        refs[:3], refs[3:6], refs[6:9], refs[9:12], refs[12], refs[13]
+    )
+    v = meta[0]
+    g = pl.program_id(0)
+
+    @pl.when(g == 0)
+    def _():
+        for q in range(3):
+            for p in range(3):
+                col = pl.multiple_of((v ^ p) * 256, 256)
+                row = pl.multiple_of((v ^ q) * 256, 256)
+                for k in range(4):
+                    w_ref[q, k * 256 : (k + 1) * 256, p * 256 : (p + 1) * 256] = folded(
+                        direct[q][k, :, pl.ds(col, 256)], swapped[p][k, pl.ds(row, 256), :]
+                    )
+
+    def work(blocks):
+        total = jnp.dot(
+            blocks[0][...].reshape(512, 1024), w_ref[0], preferred_element_type=jnp.float32
+        )
+        for q in range(1, 3):
+            total += jnp.dot(
+                blocks[q][...].reshape(512, 1024), w_ref[q], preferred_element_type=jnp.float32
+            )
+        out_ref[...] = total
+
+    @pl.when(g < 2)
+    def _():
+        work(own)
+
+    @pl.when(g >= 2)
+    def _():
+        work(oth)
+
+
+def tail_kernel(meta, mask, eps_slab, eps_pair, eps_rows, eps_cols, part_ref, *refs):
+    direct, swapped, own, oth = refs[:3], refs[3:6], refs[6:11], refs[11:16]
+    end_down, end_up, down, up, out_ref = refs[16:21]
+    buf_ref, d_ref, t_ref, row_ref, col_ref = refs[21:]
+    v, r, j = meta[0], meta[2], meta[3]
+    g = pl.program_id(0)
+    last = v ^ 3
+
+    @pl.when(g == 0)
+    def _():
+        fill(buf_ref, [(v == 0, end_down), (v == 1, down), (v == 2, up), (v == 3, end_up)])
+
+        def body(n, count):
+            k = lax.rem(n // 2 + 2 * r, 4)
+            return unpack_group(buf_ref, mask, k, j, last, n % 2, count, d_ref, t_ref, k)
+
+        lax.fori_loop(0, 8, body, jnp.int32(0))
+        last_at = pl.multiple_of(last * 256, 256)
+        for p in range(4):
+            at = pl.multiple_of((v ^ p) * 256, 256)
+            for k in range(4):
+                ks = slice(k * 256, (k + 1) * 256)
+                row_ref[ks, p * 256 : (p + 1) * 256] = folded(
+                    d_ref[k, :, pl.ds(at, 256)],
+                    swapped[p][k] if p < 3 else t_ref[k, pl.ds(last_at, 256), :],
+                )
+                if p < 3:
+                    col_ref[p, ks, :] = folded(direct[p][k], t_ref[k, pl.ds(at, 256), :])
+
+    def work(blocks, i, k0):
+        flat = [b[...].reshape(512, b.shape[-1]) for b in blocks]
+        total = jnp.float32(0)
+        for half in range(2):
+            at = pl.multiple_of(256 * lax.rem(k0 + 2 * half, 4), 512)
+            total += jnp.dot(flat[3 + half], row_ref[pl.ds(at, 512), :], preferred_element_type=jnp.float32)
+        late = total[:, 768:]
+        for q in range(3):
+            late += jnp.dot(flat[q], col_ref[q], preferred_element_type=jnp.float32)
+        for p in range(4):
+            s = v ^ p
+            value = late if p == 3 else total[:, p * 256 : (p + 1) * 256] + part_ref[:, p * 256 : (p + 1) * 256]
+            cols = eps_cols[:, pl.ds(pl.multiple_of(s * 256, 256), 256)]
+            for ii in range(2):
+                energy = (eps_rows[...] + cols) - eps_slab[i + ii] - eps_pair[0]
+                done = value[ii * 256 : (ii + 1) * 256] / energy
+                for n in range(2):
+                    at = pl.multiple_of(s * 256 + n * 128, 128)
+                    out_ref[ii, :, 0, pl.ds(at, 128)] = done[:, n * 128 : (n + 1) * 128]
+
+    @pl.when(g < 2)
+    def _():
+        work(own, 4 * g + 2 * r, 2 * r)
+
+    @pl.when(g >= 2)
+    def _():
+        work(oth, 4 * (g - 2) + 2 * (1 - r), 2 * (1 - r))
+
+
+def smem():
+    return pl.BlockSpec(memory_space=pltpu.SMEM)
+
+
+def whole():
+    return pl.BlockSpec(memory_space=pltpu.VMEM)
+
+
+def anywhere():
+    return pl.BlockSpec(memory_space=pl.ANY)
+
+
+def params():
+    return pltpu.CompilerParams(vmem_limit_bytes=VMEM_LIMIT)
+
+
+def k_place(kk, r):
+    return lax.rem(kk + 2 * r, 4)
+
+
+def packed_shards(amplitudes, integrals, amp_mask, int_mask, eps_slab, eps_pair, eps_vir):
+    v, x, r = lax.axis_index("vir"), lax.axis_index("occ"), lax.axis_index("rep")
+    meta = jnp.stack([v, x, r, 2 * x + r]).astype(jnp.int32)
+    swap = [(0, 1), (1, 0)]
+    bf16 = jnp.bfloat16
+
+    pairs = amp_mask.reshape(4, 4, 4, 4, 4).sum((0, 2, 4))
+    pairs = jnp.where(jnp.eye(4, dtype=bool), 0, pairs)
+    pieces = int_mask.reshape(4, 4, 4, 4, 16).sum((0, 3, 4))
+    over = jnp.logical_or(jnp.max(pairs) > AMP_SLOTS - 1, jnp.max(pieces) > INT_SLOTS - 1)
+    over = over.astype(jnp.int32).reshape(1)
+    over = over + lax.ppermute(over, "frag", swap)
+
+    int_oth = lax.ppermute(integrals, "rep", swap)
+    amps = amplitudes.reshape(2, 2, 2, 2, 256, 1024)
+    amp_oth = lax.ppermute(amps, "rep", swap)
+    amp_oth, over = lax.optimization_barrier((amp_oth, over))
+
+    packed_int = pl.pallas_call(
+        pack_int_kernel,
+        out_shape=jax.ShapeDtypeStruct((INT_SLOTS, 32, LANES), bf16),
+        in_specs=[smem(), smem(), whole(), whole()],
+        out_specs=whole(),
+        compiler_params=params(),
+        cost_estimate=NO_COST,
+        name="pack_int",
+    )(meta, int_mask, integrals, int_oth)
+
+    up1 = lax.ppermute(packed_int, "vir", [(0, 1), (1, 2), (2, 3)])
+    down1 = lax.ppermute(packed_int, "vir", [(1, 0), (2, 1), (3, 2)])
+
+    packed_amp = pl.pallas_call(
+        pack_amp_kernel,
+        grid_spec=pltpu.PrefetchScalarGridSpec(
+            num_scalar_prefetch=2,
+            grid=(1,),
+            in_specs=[
+                pl.BlockSpec((1, 1, 2, 2, 256, 1024), lambda g, meta, mask: (meta[1], meta[2], 0, 0, 0, 0)),
+                pl.BlockSpec((1, 1, 2, 2, 256, 1024), lambda g, meta, mask: (meta[1], meta[2], 0, 0, 0, 0)),
+            ],
+            out_specs=[pl.BlockSpec((AMP_SLOTS, TILE, LANES), lambda g, meta, mask: (0, 0, 0))] * 3,
+        ),
+        out_shape=[jax.ShapeDtypeStruct((AMP_SLOTS, TILE, LANES), bf16)] * 3,
+        compiler_params=params(),
+        cost_estimate=NO_COST,
+        name="pack_amp",
+    )(meta, amp_mask, amps, amp_oth)
+
+    near = [lax.ppermute(packed_amp[d - 1], "vir", [(s, s ^ d) for s in range(4)]) for d in (1, 2, 3)]
+    far = [lax.ppermute(a, "occ", swap) for a in near]
+    far[0], far[1], near[2] = lax.optimization_barrier((far[0], far[1], near[2]))
+
+    up2 = lax.ppermute(up1, "vir", [(1, 2), (2, 3)])
+    down2 = lax.ppermute(down1, "vir", [(1, 0), (2, 1)])
+
+    int_shapes = [
+        jax.ShapeDtypeStruct((4, 256, 1024), bf16),
+        jax.ShapeDtypeStruct((4, 1024, 256), bf16),
+    ]
+    int_outs = [
+        pl.BlockSpec((1, 256, 1024), lambda kk, meta, mask: (k_place(kk, meta[2]), 0, 0)),
+        pl.BlockSpec((1, 1024, 256), lambda kk, meta, mask: (k_place(kk, meta[2]), 0, 0)),
+    ]
+    rows, cols = [], []
+    for d in range(3):
+        if d == 0:
+            kernel, scratch = own_int_kernel, []
+            specs = [
+                pl.BlockSpec((1, 1, 256, 1024), lambda kk, meta, mask: (jnp.minimum(kk, 1), meta[2], 0, 0)),
+                pl.BlockSpec((1, 1, 256, 1024), lambda kk, meta, mask: (jnp.maximum(kk - 2, 0), meta[2], 0, 0)),
+            ]
+            operands = (integrals, int_oth)
+        else:
+            kernel = functools.partial(unpack_int_kernel, d)
+            scratch = [pltpu.VMEM((INT_SLOTS, 32, LANES), bf16), pltpu.SMEM((1,), jnp.int32)]
+            specs = [anywhere(), anywhere()]
+            operands = (down1, up1) if d == 1 else (down2, up2)
+        direct, swapped = pl.pallas_call(
+            kernel,
+            grid_spec=pltpu.PrefetchScalarGridSpec(
+                num_scalar_prefetch=2, grid=(4,), in_specs=specs, out_specs=int_outs, scratch_shapes=scratch
+            ),
+            out_shape=int_shapes,
+            compiler_params=params(),
+            cost_estimate=NO_COST,
+            name=f"ints_{d}",
+        )(meta, int_mask, *operands)
+        rows.append(direct)
+        cols.append(swapped)
+
+    def local_specs(d, base):
+        def at(side):
+            def place(kk, meta, mask):
+                k = jnp.minimum(kk + base, 1) if side == 0 else jnp.maximum(kk + base - 2, 0)
+                return (0, meta[2], 0, k, 0, meta[0] ^ d)
+
+            return place
+
+        return [pl.BlockSpec((2, 1, 2, 1, 256, 256), at(side)) for side in range(2)]
+
+    def combine(d, base, steps, extra_specs, extra, out_specs, out_shape, aliases, scratch):
+        kernel = diagonal_kernel if d == 0 else functools.partial(combine_kernel, d, base)
+        specs, operands = [], ()
+        if d > 0:
+            specs = [pl.BlockSpec((AMP_SLOTS, TILE, LANES), lambda kk, meta, mask: (0, 0, 0))] * 2
+            operands = (near[d - 1], far[d - 1])
+        return pl.pallas_call(
+            kernel,
+            grid_spec=pltpu.PrefetchScalarGridSpec(
+                num_scalar_prefetch=2,
+                grid=(steps,),
+                in_specs=local_specs(d, base) + specs + extra_specs,
+                out_specs=out_specs,
+                scratch_shapes=scratch,
+            ),
+            out_shape=out_shape,
+            input_output_aliases=aliases,
+            compiler_params=params(),
+            cost_estimate=NO_COST,
+            name=f"combine_{d}_{base}",
+        )(meta, amp_mask, amps, amp_oth, *operands, *extra)
+
+    counter = pltpu.SMEM((1,), jnp.int32)
+    first = None
+    for d in range(3):
+        first = combine(
+            d,
+            0,
+            4,
+            [] if d == 0 else [anywhere()],
+            () if d == 0 else (first,),
+            pl.BlockSpec(
+                (1, 2, 2, 256, 256), lambda kk, meta, mask, d=d: (d, 0, 0, 0, k_place(kk, meta[2]))
+            ),
+            jax.ShapeDtypeStruct((3, 2, 2, 256, 1024), bf16),
+            {} if d == 0 else {6: 0},
+            [] if d == 0 else [counter],
+        )
+    halves, count = [], None
+    for base in (0, 2):
+        half, count = combine(
+            3,
+            base,
+            2,
+            [] if base == 0 else [smem()],
+            () if base == 0 else (count,),
+            [pl.BlockSpec((1, 2, 2, 256, 256), lambda kk, meta, mask: (0, 0, 0, 0, kk)), smem()],
+            [jax.ShapeDtypeStruct((1, 2, 2, 256, 512), bf16), jax.ShapeDtypeStruct((1,), jnp.int32)],
+            {},
+            [],
+        )
+        halves.append(half)
+    first, up2, down2 = lax.optimization_barrier((first, up2, down2))
+    first_oth = lax.ppermute(first, "rep", swap)
+    halves_oth = [lax.ppermute(h, "rep", swap) for h in halves]
+    end_down = lax.ppermute(down2, "vir", [(1, 0)])
+    end_up = lax.ppermute(up2, "vir", [(2, 3)])
+
+    def own_at(d, width=1024):
+        return pl.BlockSpec((1, 1, 2, 256, width), lambda g, *_: (d % 3, jnp.minimum(g, 1), 0, 0, 0))
+
+    def oth_at(d, width=1024):
+        return pl.BlockSpec((1, 1, 2, 256, width), lambda g, *_: (d % 3, jnp.maximum(g - 2, 0), 0, 0, 0))
+
+    def place(g, meta, *_):
+        return (2 * (g % 2) + jnp.where(g < 2, meta[2], 1 - meta[2]), 0)
+
+    once = pl.Buffered(1)
+    part = pl.pallas_call(
+        early_kernel,
+        grid_spec=pltpu.PrefetchScalarGridSpec(
+            num_scalar_prefetch=1,
+            grid=(4,),
+            in_specs=[pl.BlockSpec((4, 256, 1024), lambda g, *_: (0, 0, 0), pipeline_mode=once)] * 3
+            + [pl.BlockSpec((4, 1024, 256), lambda g, *_: (0, 0, 0), pipeline_mode=once)] * 3
+            + [own_at(d) for d in range(3)]
+            + [oth_at(d) for d in range(3)],
+            out_specs=pl.BlockSpec((512, 768), place),
+            scratch_shapes=[pltpu.VMEM((3, 1024, 768), bf16)],
+        ),
+        out_shape=jax.ShapeDtypeStruct((2048, 768), jnp.float32),
+        compiler_params=params(),
+        cost_estimate=NO_COST,
+        name="early",
+    )(meta, *rows, *cols, *[first] * 3, *[first_oth] * 3)
+
+    row_energy = lax.dynamic_slice_in_dim(eps_vir, v * 256, 256, 0).reshape(256, 1)
+    col_energy = eps_vir.reshape(1, 1024)
+
+    def finish(ops):
+        part, rows, cols, own, oth, last = ops
+        return pl.pallas_call(
+            tail_kernel,
+            grid_spec=pltpu.PrefetchScalarGridSpec(
+                num_scalar_prefetch=4,
+                grid=(4,),
+                in_specs=[
+                    pl.BlockSpec((256, 1), lambda g, *_: (0, 0)),
+                    pl.BlockSpec((1, 1024), lambda g, *_: (0, 0)),
+                    pl.BlockSpec((512, 768), place),
+                ]
+                + [pl.BlockSpec((4, 256, 256), lambda g, meta, *_: (0, 0, meta[0] ^ 3), pipeline_mode=once)] * 3
+                + [pl.BlockSpec((4, 256, 256), lambda g, meta, *_: (0, meta[0] ^ 3, 0), pipeline_mode=once)] * 3
+                + [own_at(d) for d in range(3)]
+                + [own_at(3, 512)] * 2
+                + [oth_at(d) for d in range(3)]
+                + [oth_at(3, 512)] * 2
+                + [anywhere()] * 4,
+                out_specs=pl.BlockSpec((2, 256, 1, 1024), lambda g, meta, *_: (*place(g, meta), 0, 0)),
+                scratch_shapes=[
+                    pltpu.VMEM((INT_SLOTS, 32, LANES), bf16),
+                    pltpu.VMEM((4, 256, 1024), bf16),
+                    pltpu.VMEM((4, 1024, 256), bf16),
+                    pltpu.VMEM((1024, 1024), bf16),
+                    pltpu.VMEM((3, 1024, 256), bf16),
+                ],
+            ),
+            out_shape=jax.ShapeDtypeStruct((8, 256, 1, 1024), jnp.float32),
+            compiler_params=params(),
+            cost_estimate=NO_COST,
+            name="tail",
+        )(meta, int_mask, eps_slab, eps_pair, row_energy, col_energy, part, *rows, *cols, *own, *oth, *last)
+
+    def dense(ops):
+        return dense_shards(
+            amplitudes, integrals, amp_mask, int_mask, eps_slab, eps_pair, eps_vir
+        )
+
+    return lax.cond(
+        over[0] > 0,
+        dense,
+        finish,
+        (
+            part,
+            rows,
+            cols,
+            (first, first, first, *halves),
+            (first_oth, first_oth, first_oth, *halves_oth),
+            (end_down, end_up, down1, up1),
+        ),
+    )
+
+
+def shards(sizes, *args):
+    amplitudes, integrals, amp_mask, int_mask = args[:4]
+    fits = (
+        sizes == {"frag": 2, "vir": 4, "occ": 2, "rep": 2}
+        and amplitudes.shape == (8, 2, 256, 1024)
+        and integrals.shape == (2, 2, 256, 1024)
+        and amp_mask.shape == (4, 16, 16)
+        and int_mask.shape == (4, 4, 16, 16)
+    )
+    return packed_shards(*args) if fits else dense_shards(*args)
+
+
 def solution(mesh):
     in_specs = (
         P("frag", "rep", "vir", None),
@@ -74,4 +689,10 @@
         P("frag"),
     )
     out_specs = P("frag", "vir", ("occ", "rep"), None)
-    return jax.shard_map(shards, mesh=mesh, in_specs=in_specs, out_specs=out_specs, check_vma=False)
+    return jax.shard_map(
+        functools.partial(shards, dict(mesh.shape)),
+        mesh=mesh,
+        in_specs=in_specs,
+        out_specs=out_specs,
+        check_vma=False,
+    )

time: 535 us -> 277 us (0.52)
  waiting for transfers between devices: 363 us -> 114 us
  Pallas kernels: 0 us -> 110 us
  local copies, waits for them, and re-layouts: 69.2 us -> 3.27 us
  matrix products: 51.2 us -> 0 us
  other arithmetic: 30.1 us -> 3.43 us
  starting transfers between devices: 5.88 us -> 27.7 us
    all_to_all x1 -> x0, waiting for transfers between devices: 298 us -> none  [shards(): lax.all_to_all(screened, 'vir', split_axis=3, concat_axis=2, tiled=True)]
    ppermute x0 -> x18, waiting for transfers between devices: none -> 114 us  [the longest x3 78.4 us: packed_shards(): lax.ppermute(packed_amp[d - 1], 'vir', [(s, s ^ d) for s in range(4)])]
    pallas_call x0 -> x12, Pallas kernels: none -> 110 us  [the longest x1 28 us: finish(): pl.pallas_call(tail_kernel, grid_spec=pltpu.PrefetchScalarGridSpec(num_sc...]
    unnamed x3 -> x0, waiting for transfers between devices: 64.6 us -> none
    dot_general x4 -> x0, matrix products: 51.2 us -> none  [the longest x1 26.8 us: cycle_terms(): jnp.einsum('ikac,kjbc->iajb', combined, gathered, preferred_element_type=...]
    convert_element_type x2 -> x0, local copies, waits for them, and re-layouts: 29.3 us -> none  [the longest x1 17 us: shards(): jnp.swapaxes(received, 2, 3).astype(jnp.float32)]
    ppermute x0 -> x18, starting transfers between devices: none -> 27.7 us  [the longest x1 5.29 us: packed_shards(): up2 = lax.ppermute(up1, 'vir', [(1, 2), (2, 3)])]
    convert_element_type x3 -> x0, other arithmetic: 24.6 us -> none  [the longest x1 12.1 us: shards(): combined = (2.0 * screened.astype(jnp.float32) - jnp.swapaxes(received, 2...]
  transfers between devices with their start and end apart: 3 -> 18, of which waited for: 2 -> 6; matrix products, arithmetic and copies ran while one was open for 10% -> 1% of each run, Pallas kernels for 0% -> 30%
where the time goes in v2:
time: 277 us; the launch traced here: 274 us
  waiting for transfers between devices  114 us (41%)
  Pallas kernels  110 us (40%)
  starting transfers between devices  27.7 us (10%)
  between operations  15.3 us (6%)
  other arithmetic  3.43 us (1%)
  local copies, waits for them, and re-layouts  3.27 us (1%)
    ppermute x3, waiting for transfers between devices, packed_shards(): lax.ppermute(packed_amp[d - 1], 'vir', [(s, s ^ d) for s in range(4)])  78.4 us
    pallas_call x1, Pallas kernels, finish(): pl.pallas_call(tail_kernel, grid_spec=pltpu.PrefetchScalarGridSpec(num_sc...  28 us
    pallas_call x5, Pallas kernels, combine(): pl.pallas_call(kernel, grid_spec=pltpu.PrefetchScalarGridSpec(num_scalar_...  27.6 us
    pallas_call x3, Pallas kernels, packed_shards(): pl.pallas_call(kernel, grid_spec=pltpu.PrefetchScalarGridSpec(num_scalar_...  23.1 us
    pallas_call x1, Pallas kernels, packed_shards(): pl.pallas_call(early_kernel, grid_spec=pltpu.PrefetchScalarGridSpec(num_s...  20.1 us
    ppermute x3, waiting for transfers between devices, packed_shards(): far = [lax.ppermute(a, 'occ', swap) for a in near]  13 us
    ppermute x1, waiting for transfers between devices, packed_shards(): int_oth = lax.ppermute(integrals, 'rep', swap)  11.9 us
    ppermute x1, waiting for transfers between devices, packed_shards(): down1 = lax.ppermute(packed_int, 'vir', [(1, 0), (2, 1), (3, 2)])  9.96 us
  transfers between devices with their start and end apart: 18, of which 6 were waited for; matrix products, arithmetic and copies ran while one was open for 1% of the time, Pallas kernels for 30%

profile of v2, /device:TPU:9, one launch (start us, length us, event | category | flops | bytes accessed | tf_op | source)
XLA Modules:
  0.0 274.5 jit_solution(9898616004563686449)
XLA Ops:
  7.3 11.9 %collective-permute-done.2.oth_ref = bf16[2,2,256,1024]{3,2,1,0:T(8,128)(2,1)S(1)} collective-permute-done((bf16[2,2,256,1024]{3,2,1,0:T(8,128)(2,1)}, bf16[2,2,256,1024]{3,2,1,0:T(8,128)(2,1)S(1)}, u32[]{:S(2)}, u32[]{:S(2)}) %collective-permute-start.2) | collective-permute-done | bytes 2097184 | tf_op jit(solution)/shard_map/ppermute | solution.py:439
  19.2 1.3 copy-done
  20.5 5.1 %pack_int.1 = bf16[160,32,128]{2,1,0:T(8,128)(2,1)} custom-call(s32[4]{0:T(128)S(1)} %pad_add_fusion.meta, s32[4,4,16,16]{3,2,1,0:T(8,128)} %mask.13, bf16[2,2,256,1024]{3,2,1,0:T(8,128)(2,1)} %own_ref.3, bf16[2,2,256,1024]{3,2,1,0:T(8,128)(2,1)} %copy-done), custom_call_target="tpu_custom_call" | custom-call | flops 1024 | bytes 1024 | tf_op jit(solution)/shard_map/pack_int/pallas_call | solution.py:444
  25.6 1.9 collective-permute-start.3
  27.5 3.4 %collective-permute-start.4 = (bf16[160,32,128]{2,1,0:T(8,128)(2,1)}, bf16[160,32,128]{2,1,0:T(8,128)(2,1)S(1)}, u32[]{:S(2)}, u32[]{:S(2)}) collective-permute-start(bf16[160,32,128]{2,1,0:T(8,128)(2,1)} %pack_int.1), channel_id=1, source_target_pairs={{0,4},{4,8},{8,12},{1,5},{5,9},{9,13},{2,6},{6,10},{10,14},{3,7},{... | collective-permute-start | bytes 3932168 | tf_op jit(solution)/shard_map/ppermute | solution.py:454
  30.9 1.1 reduce_sum.29
  35.5 2.0 collective-permute-start.1
  38.9 6.5 %pack_amp.1 = (bf16[46,64,128]{2,1,0:T(8,128)(2,1)}, bf16[46,64,128]{2,1,0:T(8,128)(2,1)}, bf16[46,64,128]{2,1,0:T(8,128)(2,1)}) custom-call(s32[4]{0:T(128)S(1)} %pad_add_fusion.meta, s32[4,16,16]{2,1,0:T(8,128)} %mask.19, bf16[2,2,2,2,256,1024]{5,4,3,2,1,0:T(8,128)(2,1)} %bitcast.61, bf16[2,2,2,2,256,1024]{5,4,3,2,1,0:T(8,128)(2,1)} %collective-permute-done.oth_ref), custom_call_target="tpu_custom_call" | custom-call | flops 1024 | bytes 1024 | tf_op jit(solution)/shard_map/pack_amp/pallas_call | solution.py:457
  45.9 2.1 collective-permute-start.8
  48.0 10.0 %collective-permute-done.3.down_ref = bf16[160,32,128]{2,1,0:T(8,128)(2,1)S(1)} collective-permute-done((bf16[160,32,128]{2,1,0:T(8,128)(2,1)}, bf16[160,32,128]{2,1,0:T(8,128)(2,1)S(1)}, u32[]{:S(2)}, u32[]{:S(2)}) %collective-permute-start.3) | collective-permute-done | bytes 1310752 | tf_op jit(solution)/shard_map/ppermute | solution.py:455
  57.9 2.2 collective-permute-start.5
  60.1 5.3 %collective-permute-start.6 = (bf16[160,32,128]{2,1,0:T(8,128)(2,1)S(1)}, bf16[160,32,128]{2,1,0:T(8,128)(2,1)}, u32[]{:S(2)}, u32[]{:S(2)}) collective-permute-start(bf16[160,32,128]{2,1,0:T(8,128)(2,1)S(1)} %collective-permute-done.4.up_ref), channel_id=1, source_target_pairs={{4,8},{8,12},{5,9},{9,13},{6,10},{10,14},{7,11},{11,15},{20,24},{2... | collective-permute-start | bytes 3932168 | tf_op jit(solution)/shard_map/ppermute | solution.py:478
  65.4 25.8 %collective-permute-done.7.near_ref = bf16[46,64,128]{2,1,0:T(8,128)(2,1)} collective-permute-done((bf16[46,64,128]{2,1,0:T(8,128)(2,1)}, bf16[46,64,128]{2,1,0:T(8,128)(2,1)}, u32[]{:S(2)}, u32[]{:S(2)}) %collective-permute-start.7) | collective-permute-done | bytes 753696 | tf_op jit(solution)/shard_map/ppermute | solution.py:474
  91.2 1.2 collective-permute-start.10
  92.4 0.9 collective-permute-start.9
  93.3 5.7 %combine_0_0.1.refs_0_ = bf16[3,2,2,256,1024]{4,3,2,1,0:T(8,128)(2,1)} custom-call(s32[4]{0:T(128)S(1)} %pad_add_fusion.meta, s32[4,16,16]{2,1,0:T(8,128)S(1)} %copy-done.5, bf16[2,2,2,2,256,1024]{5,4,3,2,1,0:T(8,128)(2,1)} %bitcast.62, bf16[2,2,2,2,256,1024]{5,4,3,2,1,0:T(8,128)(2,1)} %collective-permute-done.oth_ref), custom_call_target="tpu_custom_call" | custom-call | flops 1024 | bytes 1024 | tf_op jit(solution)/shard_map/combine_0_0/pallas_call | solution.py:532
  99.1 52.5 %collective-permute-done.11.near_ref = bf16[46,64,128]{2,1,0:T(8,128)(2,1)S(1)} collective-permute-done((bf16[46,64,128]{2,1,0:T(8,128)(2,1)}, bf16[46,64,128]{2,1,0:T(8,128)(2,1)S(1)}, u32[]{:S(2)}, u32[]{:S(2)}) %collective-permute-start.11) | collective-permute-done | bytes 753696 | tf_op jit(solution)/shard_map/ppermute | solution.py:474
  151.6 6.2 %combine_1_0.1.refs_0_ = bf16[3,2,2,256,1024]{4,3,2,1,0:T(8,128)(2,1)} custom-call(s32[4]{0:T(128)S(1)} %pad_add_fusion.meta, s32[4,16,16]{2,1,0:T(8,128)S(1)} %copy-done.5, bf16[2,2,2,2,256,1024]{5,4,3,2,1,0:T(8,128)(2,1)} %bitcast.63, bf16[2,2,2,2,256,1024]{5,4,3,2,1,0:T(8,128)(2,1)} %collective-permute-done.oth_ref, ...), custom_call_target="tpu_custom_call", output_to_operand_aliasing={{}: (6, {})} | custom-call | flops 1024 | bytes 1024 | tf_op jit(solution)/shard_map/combine_1_0/pallas_call | solution.py:532
  157.9 6.2 %combine_2_0.1.refs_6_.refs_7_.refs_8_ = bf16[3,2,2,256,1024]{4,3,2,1,0:T(8,128)(2,1)} custom-call(s32[4]{0:T(128)S(1)} %pad_add_fusion.meta, s32[4,16,16]{2,1,0:T(8,128)S(1)} %copy-done.5, bf16[2,2,2,2,256,1024]{5,4,3,2,1,0:T(8,128)(2,1)} %bitcast.64, ...), custom_call_target="tpu_custom_call", output_to_operand_aliasing={{}: (6, {})} | custom-call | flops 1024 | bytes 1024 | tf_op jit(solution)/shard_map/combine_2_0/pallas_call | solution.py:532
  164.1 1.3 collective-permute-start.12
  165.4 1.2 collective-permute-start.13
  166.6 2.4 collective-permute-start.16
  169.0 1.7 collective-permute-start.17
  170.8 13.0 %collective-permute-done.13.far_ref = bf16[46,64,128]{2,1,0:T(8,128)(2,1)S(1)} collective-permute-done((bf16[46,64,128]{2,1,0:T(8,128)(2,1)S(1)}, bf16[46,64,128]{2,1,0:T(8,128)(2,1)S(1)}, u32[]{:S(2)}, u32[]{:S(2)}) %collective-permute-start.13) | collective-permute-done | bytes 753696 | tf_op jit(solution)/shard_map/ppermute | solution.py:475
  184.7 4.4 %combine_3_0.1 = (bf16[1,2,2,256,512]{4,3,2,1,0:T(8,128)(2,1)}, s32[1]{0:T(128)}) custom-call(s32[4]{0:T(128)S(1)} %pad_add_fusion.meta, s32[4,16,16]{2,1,0:T(8,128)S(1)} %copy-done.5, bf16[2,2,2,2,256,1024]{5,4,3,2,1,0:T(8,128)(2,1)} %bitcast.65, bf16[2,2,2,2,256,1024]{5,4,3,2,1,0:T(8,128)(2,1)} %collective-permute-done.oth_ref, ...), custom_call_target="tpu_custom_call" | custom-call | flops 1024 | bytes 1024 | tf_op jit(solution)/shard_map/combine_3_0/pallas_call | solution.py:532
  189.1 5.0 %combine_3_2.1 = (bf16[1,2,2,256,512]{4,3,2,1,0:T(8,128)(2,1)}, s32[1]{0:T(128)}) custom-call(s32[4]{0:T(128)S(1)} %pad_add_fusion.meta, s32[4,16,16]{2,1,0:T(8,128)S(1)} %copy-done.5, bf16[2,2,2,2,256,1024]{5,4,3,2,1,0:T(8,128)(2,1)} %bitcast.66, bf16[2,2,2,2,256,1024]{5,4,3,2,1,0:T(8,128)(2,1)} %collective-permute-done.oth_ref, ...), custom_call_target="tpu_custom_call" | custom-call | flops 1024 | bytes 1024 | tf_op jit(solution)/shard_map/combine_3_2/pallas_call | solution.py:532
  195.0 7.3 %ints_0.1 = (bf16[4,256,1024]{2,1,0:T(8,128)(2,1)S(1)}, bf16[4,1024,256]{2,1,0:T(8,128)(2,1)}) custom-call(s32[4]{0:T(128)S(1)} %pad_add_fusion.meta, s32[4,4,16,16]{3,2,1,0:T(8,128)S(1)} %copy-done.1, bf16[2,2,256,1024]{3,2,1,0:T(8,128)(2,1)} %own_ref.3, bf16[2,2,256,1024]{3,2,1,0:T(8,128)(2,1)} %copy-done), custom_call_target="tpu_custom_call" | custom-call | flops 1024 | bytes 1024 | tf_op jit(solution)/shard_map/ints_0/pallas_call | solution.py:503
  202.3 7.9 %ints_1.1 = (bf16[4,256,1024]{2,1,0:T(8,128)(2,1)}, bf16[4,1024,256]{2,1,0:T(8,128)(2,1)}) custom-call(s32[4]{0:T(128)S(1)} %pad_add_fusion.meta, s32[4,4,16,16]{3,2,1,0:T(8,128)S(1)} %copy-done.1, bf16[160,32,128]{2,1,0:T(8,128)(2,1)S(1)} %collective-permute-done.3.down_ref, bf16[160,32,128]{2,1,0:T(8,128)(2,1)} %copy-done.2), custom_call_target="tpu_custom_call" | custom-call | flops 1024 | bytes 1024 | tf_op jit(solution)/shard_map/ints_1/pallas_call | solution.py:503
  210.2 7.9 %ints_2.1 = (bf16[4,256,1024]{2,1,0:T(8,128)(2,1)}, bf16[4,1024,256]{2,1,0:T(8,128)(2,1)}) custom-call(s32[4]{0:T(128)S(1)} %pad_add_fusion.meta, s32[4,4,16,16]{3,2,1,0:T(8,128)S(1)} %copy-done.1, bf16[160,32,128]{2,1,0:T(8,128)(2,1)} %collective-permute-done.5.down_ref, bf16[160,32,128]{2,1,0:T(8,128)(2,1)} %collective-permute-done.6.up_ref), custom_call_target="tpu_custom_call" | custom-call | flops 1024 | bytes 1024 | tf_op jit(solution)/shard_map/ints_2/pallas_call | solution.py:503
  218.1 20.1 %early.1 = f32[2048,768]{1,0:T(8,128)} custom-call(s32[4]{0:T(128)S(1)} %pad_add_fusion.meta, bf16[4,256,1024]{2,1,0:T(8,128)(2,1)S(1)} %get-tuple-element.132.refs_0_, bf16[4,256,1024]{2,1,0:T(8,128)(2,1)} %get-tuple-element.133.refs_1_, bf16[4,256,1024]{2,1,0:T(8,128)(2,1)} %get-tuple-element.134.refs_2_, ...), custom_call_target="tpu_custom_call" | custom-call | flops 1024 | bytes 1024 | tf_op jit(solution)/shard_map/early/pallas_call | solution.py:594
  238.2 29.4 %conditional.1 = (f32[8,256,1,1024]{3,2,1,0:T(1,128)}) conditional(s32[]{:T(128)} %bitcast.23, (s32[]{:T(128)}, f32[1024]{0:T(1024)S(1)}, s32[4]{0:T(128)S(1)}, s32[4,4,16,16]{3,2,1,0:T(8,128)S(1)}, f32[8]{0:T(128)S(1)}, /*index=5*/f32[1]{0:T(128)}, f32[2048,768]{1,0:T(8,128)}, bf16[4,256,1024]{2,1,0:T(8,128)(2,1)S(1)}, ...), branch_computations={%region_6.7_spmd, %region_7.9_spmd} | conditional | flops 34424766464 | bytes 417631168 | solution.py:654
  239.4 28.0 %tail.1 = f32[8,256,1,1024]{3,2,1,0:T(1,128)} custom-call(s32[4]{0:T(128)S(1)} %get-tuple-element.81.meta, s32[4,4,16,16]{3,2,1,0:T(8,128)S(1)} %get-tuple-element.82.mask, f32[8]{0:T(128)S(1)} %get-tuple-element.83.eps_slab, f32[1]{0:T(128)} %get-tuple-element.84.eps_pair, f32[256,1]{1,0:T(8,128)} %copy.53.eps_rows, f32[1,1024]{1,0:T(1,128)S(1)} %bitcast.70, ...), custom_call_target="tpu_custom_call" | custom-call | flops 1024 | bytes 1024 | tf_op jit(solution)/shard_map/cond/branch_0_fun/tail/pallas_call | solution.py:617
  (44 shorter events, 7.1 us)
Async XLA Ops:
  6.5 32.4 %collective-permute-start = (bf16[2,2,2,2,256,1024]{5,4,3,2,1,0:T(8,128)(2,1)}, bf16[2,2,2,2,256,1024]{5,4,3,2,1,0:T(8,128)(2,1)}, u32[]{:S(2)}, u32[]{:S(2)}) collective-permute-start(bf16[2,2,2,2,256,1024]{5,4,3,2,1,0:T(8,128)(2,1)} %bitcast.60), channel_id=1, source_target_pairs={{0,1},{1,0},{2,3},{3,2},{4,5},{5,4},{6,7},{7,6},{8,9},{9,8},{10,11... | collective-permute-start | bytes 25165832 | tf_op jit(solution)/shard_map/ppermute | solution.py:441
  7.2 11.9 %collective-permute-start.2 = (bf16[2,2,256,1024]{3,2,1,0:T(8,128)(2,1)}, bf16[2,2,256,1024]{3,2,1,0:T(8,128)(2,1)S(1)}, u32[]{:S(2)}, u32[]{:S(2)}) collective-permute-start(bf16[2,2,256,1024]{3,2,1,0:T(8,128)(2,1)} %own_ref.3), channel_id=1, source_target_pairs={{0,1},{1,0},{2,3},{3,2},{4,5},{5,4},{6,7},{7,6},{8,9},{9,8},{10,11... | collective-permute-start | bytes 6291464 | tf_op jit(solution)/shard_map/ppermute | solution.py:439
  19.2 1.3 copy-start
  25.6 32.3 %collective-permute-start.3 = (bf16[160,32,128]{2,1,0:T(8,128)(2,1)}, bf16[160,32,128]{2,1,0:T(8,128)(2,1)S(1)}, u32[]{:S(2)}, u32[]{:S(2)}) collective-permute-start(bf16[160,32,128]{2,1,0:T(8,128)(2,1)} %pack_int.1), channel_id=1, source_target_pairs={{4,0},{8,4},{12,8},{5,1},{9,5},{13,9},{6,2},{10,6},{14,10},{7,3},{... | collective-permute-start | bytes 3932168 | tf_op jit(solution)/shard_map/ppermute | solution.py:455
  27.5 32.6 %collective-permute-start.4 = (bf16[160,32,128]{2,1,0:T(8,128)(2,1)}, bf16[160,32,128]{2,1,0:T(8,128)(2,1)S(1)}, u32[]{:S(2)}, u32[]{:S(2)}) collective-permute-start(bf16[160,32,128]{2,1,0:T(8,128)(2,1)} %pack_int.1), channel_id=1, source_target_pairs={{0,4},{4,8},{8,12},{1,5},{5,9},{9,13},{2,6},{6,10},{10,14},{3,7},{... | collective-permute-start | bytes 3932168 | tf_op jit(solution)/shard_map/ppermute | solution.py:454
  35.5 2.8 %collective-permute-start.1 = (s32[1]{0:T(128)}, s32[1]{0:T(128)}, u32[]{:S(2)}, u32[]{:S(2)}) collective-permute-start(s32[1]{0:T(128)} %bitcast.22), channel_id=1, source_target_pairs={{0,16},{16,0},{1,17},{17,1},{2,18},{18,2},{3,19},{19,3},{4,20},{20... | collective-permute-start | bytes 20 | tf_op jit(solution)/shard_map/ppermute | solution.py:437
  38.9 54.5 %copy-start.5 = (s32[4,16,16]{2,1,0:T(8,128)S(1)}, s32[4,16,16]{2,1,0:T(8,128)}, u32[]{:S(2)}) copy-start(s32[4,16,16]{2,1,0:T(8,128)} %mask.19) | copy-start | bytes 12292
  45.4 45.8 %collective-permute-start.7 = (bf16[46,64,128]{2,1,0:T(8,128)(2,1)}, bf16[46,64,128]{2,1,0:T(8,128)(2,1)}, u32[]{:S(2)}, u32[]{:S(2)}) collective-permute-start(bf16[46,64,128]{2,1,0:T(8,128)(2,1)} %get-tuple-element.139), channel_id=1, source_target_pairs={{0,8},{4,12},{8,0},{12,4},{1,9},{5,13},{9,1},{13,5},{2,10},{6,14},... | collective-permute-start | bytes 2261000 | tf_op jit(solution)/shard_map/ppermute | solution.py:474
  45.9 46.6 %collective-permute-start.8 = (bf16[46,64,128]{2,1,0:T(8,128)(2,1)}, bf16[46,64,128]{2,1,0:T(8,128)(2,1)}, u32[]{:S(2)}, u32[]{:S(2)}) collective-permute-start(bf16[46,64,128]{2,1,0:T(8,128)(2,1)} %get-tuple-element.140), channel_id=1, source_target_pairs={{0,4},{4,0},{8,12},{12,8},{1,5},{5,1},{9,13},{13,9},{2,6},{6,2},{1... | collective-permute-start | bytes 2261000 | tf_op jit(solution)/shard_map/ppermute | solution.py:474
  57.9 106.1 %collective-permute-start.5 = (bf16[160,32,128]{2,1,0:T(8,128)(2,1)S(1)}, bf16[160,32,128]{2,1,0:T(8,128)(2,1)}, u32[]{:S(2)}, u32[]{:S(2)}) collective-permute-start(bf16[160,32,128]{2,1,0:T(8,128)(2,1)S(1)} %collective-permute-done.3.down_ref), channel_id=1, source_target_pairs={{4,0},{8,4},{5,1},{9,5},{6,2},{10,6},{7,3},{11,7},{20,16},{24,20},... | collective-permute-start | bytes 3932168 | tf_op jit(solution)/shard_map/ppermute | solution.py:479
  60.1 39.0 %copy-start.2 = (bf16[160,32,128]{2,1,0:T(8,128)(2,1)}, bf16[160,32,128]{2,1,0:T(8,128)(2,1)S(1)}, u32[]{:S(2)}) copy-start(bf16[160,32,128]{2,1,0:T(8,128)(2,1)S(1)} %collective-permute-done.4.up_ref) | copy-start | bytes 3932164
  60.1 104.0 %collective-permute-start.6 = (bf16[160,32,128]{2,1,0:T(8,128)(2,1)S(1)}, bf16[160,32,128]{2,1,0:T(8,128)(2,1)}, u32[]{:S(2)}, u32[]{:S(2)}) collective-permute-start(bf16[160,32,128]{2,1,0:T(8,128)(2,1)S(1)} %collective-permute-done.4.up_ref), channel_id=1, source_target_pairs={{4,8},{8,12},{5,9},{9,13},{6,10},{10,14},{7,11},{11,15},{20,24},{2... | collective-permute-start | bytes 3932168 | tf_op jit(solution)/shard_map/ppermute | solution.py:478
  65.4 86.2 %collective-permute-start.11 = (bf16[46,64,128]{2,1,0:T(8,128)(2,1)}, bf16[46,64,128]{2,1,0:T(8,128)(2,1)S(1)}, u32[]{:S(2)}, u32[]{:S(2)}) collective-permute-start(bf16[46,64,128]{2,1,0:T(8,128)(2,1)} %get-tuple-element.141), channel_id=1, source_target_pairs={{0,12},{4,8},{8,4},{12,0},{1,13},{5,9},{9,5},{13,1},{2,14},{6,10},... | collective-permute-start | bytes 2261000 | tf_op jit(solution)/shard_map/ppermute | solution.py:474
  91.2 60.4 %collective-permute-start.10 = (bf16[46,64,128]{2,1,0:T(8,128)(2,1)}, bf16[46,64,128]{2,1,0:T(8,128)(2,1)}, u32[]{:S(2)}, u32[]{:S(2)}) collective-permute-start(bf16[46,64,128]{2,1,0:T(8,128)(2,1)} %collective-permute-done.7.near_ref), channel_id=1, source_target_pairs={{0,2},{2,0},{1,3},{3,1},{4,6},{6,4},{5,7},{7,5},{8,10},{10,8},{9,1... | collective-permute-start | bytes 2261000 | tf_op jit(solution)/shard_map/ppermute | solution.py:475
  92.4 59.2 %collective-permute-start.9 = (bf16[46,64,128]{2,1,0:T(8,128)(2,1)}, bf16[46,64,128]{2,1,0:T(8,128)(2,1)}, u32[]{:S(2)}, u32[]{:S(2)}) collective-permute-start(bf16[46,64,128]{2,1,0:T(8,128)(2,1)} %collective-permute-done.8.near_ref), channel_id=1, source_target_pairs={{0,2},{2,0},{1,3},{3,1},{4,6},{6,4},{5,7},{7,5},{8,10},{10,8},{9,1... | collective-permute-start | bytes 2261000 | tf_op jit(solution)/shard_map/ppermute | solution.py:475
  151.6 13.8 %copy-start.3 = (bf16[46,64,128]{2,1,0:T(8,128)(2,1)}, bf16[46,64,128]{2,1,0:T(8,128)(2,1)S(1)}, u32[]{:S(2)}) copy-start(bf16[46,64,128]{2,1,0:T(8,128)(2,1)S(1)} %collective-permute-done.11.near_ref) | copy-start | bytes 2260996
  164.1 54.0 %collective-permute-start.12 = (bf16[3,2,2,256,1024]{4,3,2,1,0:T(8,128)(2,1)}, bf16[3,2,2,256,1024]{4,3,2,1,0:T(8,128)(2,1)}, u32[]{:S(2)}, u32[]{:S(2)}) collective-permute-start(bf16[3,2,2,256,1024]{4,3,2,1,0:T(8,128)(2,1)} %combine_2_0.1.refs_6_.refs_7_.refs_8_), channel_id=1, source_target_pairs={{0,1},{1,0},{2,3},{3,2},{4,5},{5,4},{6,7},{7,6},{8,9},{9,8},{10,11... | collective-permute-start | bytes 18874376 | tf_op jit(solution)/shard_map/ppermute | solution.py:579
  165.4 18.4 %collective-permute-start.13 = (bf16[46,64,128]{2,1,0:T(8,128)(2,1)S(1)}, bf16[46,64,128]{2,1,0:T(8,128)(2,1)S(1)}, u32[]{:S(2)}, u32[]{:S(2)}) collective-permute-start(bf16[46,64,128]{2,1,0:T(8,128)(2,1)S(1)} %collective-permute-done.11.near_ref), channel_id=1, source_target_pairs={{0,2},{2,0},{1,3},{3,1},{4,6},{6,4},{5,7},{7,5},{8,10},{10,8},{9,1... | collective-permute-start | bytes 2261000 | tf_op jit(solution)/shard_map/ppermute | solution.py:475
  166.6 71.6 %collective-permute-start.16 = (bf16[160,32,128]{2,1,0:T(8,128)(2,1)}, bf16[160,32,128]{2,1,0:T(8,128)(2,1)}, u32[]{:S(2)}, u32[]{:S(2)}) collective-permute-start(bf16[160,32,128]{2,1,0:T(8,128)(2,1)} %collective-permute-done.5.down_ref), channel_id=1, source_target_pairs={{4,0},{5,1},{6,2},{7,3},{20,16},{21,17},{22,18},{23,19}} | collective-permute-start | bytes 3932168 | tf_op jit(solution)/shard_map/ppermute | solution.py:581
  169.0 69.2 %collective-permute-start.17 = (bf16[160,32,128]{2,1,0:T(8,128)(2,1)}, bf16[160,32,128]{2,1,0:T(8,128)(2,1)}, u32[]{:S(2)}, u32[]{:S(2)}) collective-permute-start(bf16[160,32,128]{2,1,0:T(8,128)(2,1)} %collective-permute-done.6.up_ref), channel_id=1, source_target_pairs={{8,12},{9,13},{10,14},{11,15},{24,28},{25,29},{26,30},{27,31}} | collective-permute-start | bytes 3932168 | tf_op jit(solution)/shard_map/ppermute | solution.py:582
  183.8 0.9 copy-start.4
  189.1 5.9 %copy-start.1 = (s32[4,4,16,16]{3,2,1,0:T(8,128)S(1)}, s32[4,4,16,16]{3,2,1,0:T(8,128)}, u32[]{:S(2)}) copy-start(s32[4,4,16,16]{3,2,1,0:T(8,128)} %mask.13) | copy-start | bytes 49156
  194.1 44.0 %collective-permute-start.15 = (bf16[1,2,2,256,512]{4,3,2,1,0:T(8,128)(2,1)}, bf16[1,2,2,256,512]{4,3,2,1,0:T(8,128)(2,1)}, u32[]{:S(2)}, u32[]{:S(2)}) collective-permute-start(bf16[1,2,2,256,512]{4,3,2,1,0:T(8,128)(2,1)} %get-tuple-element.148), channel_id=1, source_target_pairs={{0,1},{1,0},{2,3},{3,2},{4,5},{5,4},{6,7},{7,6},{8,9},{9,8},{10,11... | collective-permute-start | bytes 3145736 | tf_op jit(solution)/shard_map/ppermute | solution.py:580
  195.0 43.2 %collective-permute-start.14 = (bf16[1,2,2,256,512]{4,3,2,1,0:T(8,128)(2,1)}, bf16[1,2,2,256,512]{4,3,2,1,0:T(8,128)(2,1)}, u32[]{:S(2)}, u32[]{:S(2)}) collective-permute-start(bf16[1,2,2,256,512]{4,3,2,1,0:T(8,128)(2,1)} %get-tuple-element.146), channel_id=1, source_target_pairs={{0,1},{1,0},{2,3},{3,2},{4,5},{5,4},{6,7},{7,6},{8,9},{9,8},{10,11... | collective-permute-start | bytes 3145736 | tf_op jit(solution)/shard_map/ppermute | solution.py:580
  218.1 20.1 %copy-start.6 = (f32[1024]{0:T(1024)S(1)}, f32[1024]{0:T(1024)}, u32[]{:S(2)}) copy-start(f32[1024]{0:T(1024)} %param.15) | copy-start | bytes 12292
  218.1 20.1 %copy-start.7 = (f32[8]{0:T(128)S(1)}, f32[8]{0:T(128)}, u32[]{:S(2)}) copy-start(f32[8]{0:T(128)} %param.13) | copy-start | bytes 100

commit v3 on v2

--- a/solution.py
+++ b/solution.py
@@ -170,7 +170,8 @@
     return count
 
 
-def unpack_int_kernel(d, meta, mask, down_ref, up_ref, d_ref, t_ref, buf_ref, count_ref):
+def unpack_int_kernel(d, meta, mask, *refs):
+    sources, (d_ref, t_ref, buf_ref, count_ref) = refs[:-4], refs[-4:]
     v, r, j = meta[0], meta[2], meta[3]
     kk = pl.program_id(0)
     k = lax.rem(kk + 2 * r, 4)
@@ -179,7 +180,10 @@
     @pl.when(kk == 0)
     def _():
         count_ref[0] = 0
-        fill(buf_ref, [(s > v, down_ref), (s < v, up_ref)])
+        if d < 3:
+            fill(buf_ref, [(s > v, sources[0]), (s < v, sources[1])])
+        else:
+            fill(buf_ref, [(v == n, source) for n, source in enumerate(sources)])
 
     count_ref[0] = lax.fori_loop(
         0,
@@ -345,34 +349,28 @@
         work(oth)
 
 
-def tail_kernel(meta, mask, eps_slab, eps_pair, eps_rows, eps_cols, part_ref, *refs):
-    direct, swapped, own, oth = refs[:3], refs[3:6], refs[6:11], refs[11:16]
-    end_down, end_up, down, up, out_ref = refs[16:21]
-    buf_ref, d_ref, t_ref, row_ref, col_ref = refs[21:]
-    v, r, j = meta[0], meta[2], meta[3]
+def tail_kernel(meta, eps_slab, eps_pair, eps_rows, eps_cols, part_ref, *refs):
+    direct, swapped, own, oth, out_ref = refs[:4], refs[4:8], refs[8:13], refs[13:18], refs[18]
+    row_ref, col_ref = refs[19:]
+    v, r = meta[0], meta[2]
     g = pl.program_id(0)
     last = v ^ 3
 
     @pl.when(g == 0)
     def _():
-        fill(buf_ref, [(v == 0, end_down), (v == 1, down), (v == 2, up), (v == 3, end_up)])
-
-        def body(n, count):
-            k = lax.rem(n // 2 + 2 * r, 4)
-            return unpack_group(buf_ref, mask, k, j, last, n % 2, count, d_ref, t_ref, k)
-
-        lax.fori_loop(0, 8, body, jnp.int32(0))
         last_at = pl.multiple_of(last * 256, 256)
         for p in range(4):
             at = pl.multiple_of((v ^ p) * 256, 256)
             for k in range(4):
                 ks = slice(k * 256, (k + 1) * 256)
                 row_ref[ks, p * 256 : (p + 1) * 256] = folded(
-                    d_ref[k, :, pl.ds(at, 256)],
-                    swapped[p][k] if p < 3 else t_ref[k, pl.ds(last_at, 256), :],
+                    direct[3][k, :, pl.ds(at, 256)],
+                    swapped[p][k] if p < 3 else swapped[3][k, pl.ds(last_at, 256), :],
                 )
                 if p < 3:
-                    col_ref[p, ks, :] = folded(direct[p][k], t_ref[k, pl.ds(at, 256), :])
+                    col_ref[p, ks, :] = folded(
+                        direct[p][k], swapped[3][k, pl.ds(at, 256), :]
+                    )
 
     def work(blocks, i, k0):
         flat = [b[...].reshape(512, b.shape[-1]) for b in blocks]
@@ -471,9 +469,8 @@
         name="pack_amp",
     )(meta, amp_mask, amps, amp_oth)
 
-    near = [lax.ppermute(packed_amp[d - 1], "vir", [(s, s ^ d) for s in range(4)]) for d in (1, 2, 3)]
-    far = [lax.ppermute(a, "occ", swap) for a in near]
-    far[0], far[1], near[2] = lax.optimization_barrier((far[0], far[1], near[2]))
+    def across(d, packed):
+        return lax.ppermute(packed, "vir", [(s, s ^ d) for s in range(4)])
 
     up2 = lax.ppermute(up1, "vir", [(1, 2), (2, 3)])
     down2 = lax.ppermute(down1, "vir", [(1, 0), (2, 1)])
@@ -486,21 +483,18 @@
         pl.BlockSpec((1, 256, 1024), lambda kk, meta, mask: (k_place(kk, meta[2]), 0, 0)),
         pl.BlockSpec((1, 1024, 256), lambda kk, meta, mask: (k_place(kk, meta[2]), 0, 0)),
     ]
-    rows, cols = [], []
-    for d in range(3):
+    def unpack(d, *operands):
         if d == 0:
             kernel, scratch = own_int_kernel, []
             specs = [
                 pl.BlockSpec((1, 1, 256, 1024), lambda kk, meta, mask: (jnp.minimum(kk, 1), meta[2], 0, 0)),
                 pl.BlockSpec((1, 1, 256, 1024), lambda kk, meta, mask: (jnp.maximum(kk - 2, 0), meta[2], 0, 0)),
             ]
-            operands = (integrals, int_oth)
         else:
             kernel = functools.partial(unpack_int_kernel, d)
             scratch = [pltpu.VMEM((INT_SLOTS, 32, LANES), bf16), pltpu.SMEM((1,), jnp.int32)]
-            specs = [anywhere(), anywhere()]
-            operands = (down1, up1) if d == 1 else (down2, up2)
-        direct, swapped = pl.pallas_call(
+            specs = [anywhere() for _ in operands]
+        return pl.pallas_call(
             kernel,
             grid_spec=pltpu.PrefetchScalarGridSpec(
                 num_scalar_prefetch=2, grid=(4,), in_specs=specs, out_specs=int_outs, scratch_shapes=scratch
@@ -510,8 +504,6 @@
             cost_estimate=NO_COST,
             name=f"ints_{d}",
         )(meta, int_mask, *operands)
-        rows.append(direct)
-        cols.append(swapped)
 
     def local_specs(d, base):
         def at(side):
@@ -523,12 +515,12 @@
 
         return [pl.BlockSpec((2, 1, 2, 1, 256, 256), at(side)) for side in range(2)]
 
-    def combine(d, base, steps, extra_specs, extra, out_specs, out_shape, aliases, scratch):
+    def combine(d, base, near, far, steps, extra_specs, extra, out_specs, out_shape, aliases, scratch):
         kernel = diagonal_kernel if d == 0 else functools.partial(combine_kernel, d, base)
         specs, operands = [], ()
         if d > 0:
             specs = [pl.BlockSpec((AMP_SLOTS, TILE, LANES), lambda kk, meta, mask: (0, 0, 0))] * 2
-            operands = (near[d - 1], far[d - 1])
+            operands = (near, far)
         return pl.pallas_call(
             kernel,
             grid_spec=pltpu.PrefetchScalarGridSpec(
@@ -545,41 +537,54 @@
             name=f"combine_{d}_{base}",
         )(meta, amp_mask, amps, amp_oth, *operands, *extra)
 
-    counter = pltpu.SMEM((1,), jnp.int32)
-    first = None
-    for d in range(3):
-        first = combine(
+    def combine_first(d, near, far, sofar):
+        return combine(
             d,
             0,
+            near,
+            far,
             4,
             [] if d == 0 else [anywhere()],
-            () if d == 0 else (first,),
+            () if d == 0 else (sofar,),
             pl.BlockSpec(
-                (1, 2, 2, 256, 256), lambda kk, meta, mask, d=d: (d, 0, 0, 0, k_place(kk, meta[2]))
+                (1, 2, 2, 256, 256), lambda kk, meta, mask: (d, 0, 0, 0, k_place(kk, meta[2]))
             ),
             jax.ShapeDtypeStruct((3, 2, 2, 256, 1024), bf16),
             {} if d == 0 else {6: 0},
-            [] if d == 0 else [counter],
+            [] if d == 0 else [pltpu.SMEM((1,), jnp.int32)],
         )
-    halves, count = [], None
-    for base in (0, 2):
-        half, count = combine(
+
+    def combine_half(base, near, far, *count):
+        return combine(
             3,
             base,
+            near,
+            far,
             2,
-            [] if base == 0 else [smem()],
-            () if base == 0 else (count,),
+            [smem() for _ in count],
+            count,
             [pl.BlockSpec((1, 2, 2, 256, 256), lambda kk, meta, mask: (0, 0, 0, 0, kk)), smem()],
             [jax.ShapeDtypeStruct((1, 2, 2, 256, 512), bf16), jax.ShapeDtypeStruct((1,), jnp.int32)],
             {},
             [],
         )
-        halves.append(half)
-    first, up2, down2 = lax.optimization_barrier((first, up2, down2))
-    first_oth = lax.ppermute(first, "rep", swap)
-    halves_oth = [lax.ppermute(h, "rep", swap) for h in halves]
+
+    ready = lax.optimization_barrier
+    ints = [unpack(0, integrals, int_oth)]
+    first = combine_first(0, None, None, None)
+    near1, near2 = across(1, packed_amp[0]), across(2, packed_amp[1])
+    near1, ints[0], first = ready((near1, ints[0], first))
+    far1, far2 = lax.ppermute(near1, "occ", swap), lax.ppermute(near2, "occ", swap)
+    ints.append(unpack(1, down1, up1))
+    ints[1], far1 = ready((ints[1], far1))
+    first = combine_first(1, near1, far1, first)
+    first = combine_first(2, near2, far2, first)
+    up2, down2, first, packed3 = ready((up2, down2, first, packed_amp[2]))
+    near3 = across(3, packed3)
     end_down = lax.ppermute(down2, "vir", [(1, 0)])
     end_up = lax.ppermute(up2, "vir", [(2, 3)])
+    ints.append(unpack(2, down2, up2))
+    first_oth = lax.ppermute(first, "rep", swap)
 
     def own_at(d, width=1024):
         return pl.BlockSpec((1, 1, 2, 256, width), lambda g, *_: (d % 3, jnp.minimum(g, 1), 0, 0, 0))
@@ -607,17 +612,27 @@
         compiler_params=params(),
         cost_estimate=NO_COST,
         name="early",
-    )(meta, *rows, *cols, *[first] * 3, *[first_oth] * 3)
+    )(meta, *[d for d, _ in ints], *[t for _, t in ints], *[first] * 3, *[first_oth] * 3)
+
+    near3, end_down, end_up, part = ready((near3, end_down, end_up, part))
+    far3 = lax.ppermute(near3, "occ", swap)
+    ints.append(unpack(3, end_down, down1, up1, end_up))
+    far3, ints[3] = ready((far3, ints[3]))
+    half0, count = combine_half(0, near3, far3)
+    half1, _ = combine_half(2, near3, far3, count)
+    halves = (half0, half1)
+    halves_oth = tuple(lax.ppermute(h, "rep", swap) for h in halves)
+    rows, cols = [d for d, _ in ints], [t for _, t in ints]
 
     row_energy = lax.dynamic_slice_in_dim(eps_vir, v * 256, 256, 0).reshape(256, 1)
     col_energy = eps_vir.reshape(1, 1024)
 
     def finish(ops):
-        part, rows, cols, own, oth, last = ops
+        part, rows, cols, own, oth = ops
         return pl.pallas_call(
             tail_kernel,
             grid_spec=pltpu.PrefetchScalarGridSpec(
-                num_scalar_prefetch=4,
+                num_scalar_prefetch=3,
                 grid=(4,),
                 in_specs=[
                     pl.BlockSpec((256, 1), lambda g, *_: (0, 0)),
@@ -625,17 +640,15 @@
                     pl.BlockSpec((512, 768), place),
                 ]
                 + [pl.BlockSpec((4, 256, 256), lambda g, meta, *_: (0, 0, meta[0] ^ 3), pipeline_mode=once)] * 3
+                + [pl.BlockSpec((4, 256, 1024), lambda g, meta, *_: (0, 0, 0), pipeline_mode=once)]
                 + [pl.BlockSpec((4, 256, 256), lambda g, meta, *_: (0, meta[0] ^ 3, 0), pipeline_mode=once)] * 3
+                + [pl.BlockSpec((4, 1024, 256), lambda g, meta, *_: (0, 0, 0), pipeline_mode=once)]
                 + [own_at(d) for d in range(3)]
                 + [own_at(3, 512)] * 2
                 + [oth_at(d) for d in range(3)]
-                + [oth_at(3, 512)] * 2
-                + [anywhere()] * 4,
+                + [oth_at(3, 512)] * 2,
                 out_specs=pl.BlockSpec((2, 256, 1, 1024), lambda g, meta, *_: (*place(g, meta), 0, 0)),
                 scratch_shapes=[
-                    pltpu.VMEM((INT_SLOTS, 32, LANES), bf16),
-                    pltpu.VMEM((4, 256, 1024), bf16),
-                    pltpu.VMEM((4, 1024, 256), bf16),
                     pltpu.VMEM((1024, 1024), bf16),
                     pltpu.VMEM((3, 1024, 256), bf16),
                 ],
@@ -644,7 +657,7 @@
             compiler_params=params(),
             cost_estimate=NO_COST,
             name="tail",
-        )(meta, int_mask, eps_slab, eps_pair, row_energy, col_energy, part, *rows, *cols, *own, *oth, *last)
+        )(meta, eps_slab, eps_pair, row_energy, col_energy, part, *rows, *cols, *own, *oth)
 
     def dense(ops):
         return dense_shards(
@@ -661,7 +674,6 @@
             cols,
             (first, first, first, *halves),
             (first_oth, first_oth, first_oth, *halves_oth),
-            (end_down, end_up, down1, up1),
         ),
     )
 

time: 277 us -> 254 us (0.917)
  waiting for transfers between devices: 114 us -> 77.1 us
  starting transfers between devices: 27.7 us -> 33.3 us
  Pallas kernels: 110 us -> 115 us
    ppermute x8, waiting for transfers between devices: 91.4 us -> 47.9 us  [the longest x3 21.9 us: across(): return lax.ppermute(packed, 'vir', [(s, s ^ d) for s in range(4)])]
    ppermute x1, waiting for transfers between devices: 9.96 us -> 0.01 us  [packed_shards(): down1 = lax.ppermute(packed_int, 'vir', [(1, 0), (2, 1), (3, 2)])]
    ppermute x1, waiting for transfers between devices: 0.01 us -> 8.82 us  [packed_shards(): up1 = lax.ppermute(packed_int, 'vir', [(0, 1), (1, 2), (2, 3)])]
    pallas_call x3 -> x4, Pallas kernels: 23.1 us -> 30.9 us  [unpack(): pl.pallas_call(kernel, grid_spec=pltpu.PrefetchScalarGridSpec(num_scalar_...]
    ppermute x1, waiting for transfers between devices: 0.01 us -> 7.67 us  [packed_shards(): end_down = lax.ppermute(down2, 'vir', [(1, 0)])]
    pallas_call x1, Pallas kernels: 28 us -> 24.3 us  [finish(): pl.pallas_call(tail_kernel, grid_spec=pltpu.PrefetchScalarGridSpec(num_sc...]
  transfers between devices with their start and end apart: 18 -> 18, of which waited for: 6 -> 12; matrix products, arithmetic and copies ran while one was open for 1% -> 1% of each run, Pallas kernels for 30% -> 33%
where the time goes in v3:
time: 254 us; the launch traced here: 249 us
  Pallas kernels  115 us (45%)
  waiting for transfers between devices  77.1 us (30%)
  starting transfers between devices  33.3 us (13%)
  between operations  15.4 us (6%)
  local copies, waits for them, and re-layouts  4.4 us (2%)
  other arithmetic  3.54 us (1%)
    pallas_call x4, Pallas kernels, unpack(): pl.pallas_call(kernel, grid_spec=pltpu.PrefetchScalarGridSpec(num_scalar_...  30.9 us
    pallas_call x5, Pallas kernels, combine(): pl.pallas_call(kernel, grid_spec=pltpu.PrefetchScalarGridSpec(num_scalar_...  28.3 us
    pallas_call x1, Pallas kernels, finish(): pl.pallas_call(tail_kernel, grid_spec=pltpu.PrefetchScalarGridSpec(num_sc...  24.3 us
    ppermute x3, waiting for transfers between devices, across(): return lax.ppermute(packed, 'vir', [(s, s ^ d) for s in range(4)])  21.9 us
    pallas_call x1, Pallas kernels, packed_shards(): pl.pallas_call(early_kernel, grid_spec=pltpu.PrefetchScalarGridSpec(num_s...  20.1 us
    ppermute x1, waiting for transfers between devices, packed_shards(): int_oth = lax.ppermute(integrals, 'rep', swap)  11.9 us
    ppermute x1, waiting for transfers between devices, packed_shards(): lax.ppermute(near2, 'occ', swap)  9.78 us
    ppermute x1, waiting for transfers between devices, packed_shards(): up1 = lax.ppermute(packed_int, 'vir', [(0, 1), (1, 2), (2, 3)])  8.82 us
  transfers between devices with their start and end apart: 18, of which 12 were waited for; matrix products, arithmetic and copies ran while one was open for 1% of the time, Pallas kernels for 33%

profile of v3, /device:TPU:9, one launch (start us, length us, event | category | flops | bytes accessed | tf_op | source)
XLA Modules:
  0.0 249.3 jit_solution(12431826014939460084)
XLA Ops:
  7.3 11.9 %collective-permute-done.2.oth_ref = bf16[2,2,256,1024]{3,2,1,0:T(8,128)(2,1)S(1)} collective-permute-done((bf16[2,2,256,1024]{3,2,1,0:T(8,128)(2,1)}, bf16[2,2,256,1024]{3,2,1,0:T(8,128)(2,1)S(1)}, u32[]{:S(2)}, u32[]{:S(2)}) %collective-permute-start.2) | collective-permute-done | bytes 2097184 | tf_op jit(solution)/shard_map/ppermute | solution.py:437
  20.5 5.1 %pack_int.1 = bf16[160,32,128]{2,1,0:T(8,128)(2,1)} custom-call(s32[4]{0:T(128)S(1)} %pad_add_fusion.meta, s32[4,4,16,16]{3,2,1,0:T(8,128)} %mask.19, bf16[2,2,256,1024]{3,2,1,0:T(8,128)(2,1)} %own_ref.3, bf16[2,2,256,1024]{3,2,1,0:T(8,128)(2,1)} %copy-done), custom_call_target="tpu_custom_call" | custom-call | flops 1024 | bytes 1024 | tf_op jit(solution)/shard_map/pack_int/pallas_call | solution.py:442
  25.6 3.2 %collective-permute-start.3 = (bf16[160,32,128]{2,1,0:T(8,128)(2,1)}, bf16[160,32,128]{2,1,0:T(8,128)(2,1)S(1)}, u32[]{:S(2)}, u32[]{:S(2)}) collective-permute-start(bf16[160,32,128]{2,1,0:T(8,128)(2,1)} %pack_int.1), channel_id=1, source_target_pairs={{0,4},{4,8},{8,12},{1,5},{5,9},{9,13},{2,6},{6,10},{10,14},{3,7},{... | collective-permute-start | bytes 3932168 | tf_op jit(solution)/shard_map/ppermute | solution.py:452
  28.8 2.2 collective-permute-start.5
  35.9 2.0 collective-permute-start.1
  39.4 6.6 %pack_amp.1 = (bf16[46,64,128]{2,1,0:T(8,128)(2,1)}, bf16[46,64,128]{2,1,0:T(8,128)(2,1)}, bf16[46,64,128]{2,1,0:T(8,128)(2,1)}) custom-call(s32[4]{0:T(128)S(1)} %pad_add_fusion.meta, s32[4,16,16]{2,1,0:T(8,128)} %mask.21, bf16[2,2,2,2,256,1024]{5,4,3,2,1,0:T(8,128)(2,1)} %bitcast.61, bf16[2,2,2,2,256,1024]{5,4,3,2,1,0:T(8,128)(2,1)} %collective-permute-done.oth_ref), custom_call_target="tpu_custom_call" | custom-call | flops 1024 | bytes 1024 | tf_op jit(solution)/shard_map/pack_amp/pallas_call | solution.py:455
  46.0 3.2 %collective-permute-start.7 = (bf16[46,64,128]{2,1,0:T(8,128)(2,1)}, bf16[46,64,128]{2,1,0:T(8,128)(2,1)}, u32[]{:S(2)}, u32[]{:S(2)}) collective-permute-start(bf16[46,64,128]{2,1,0:T(8,128)(2,1)} %get-tuple-element.138), channel_id=1, source_target_pairs={{0,8},{4,12},{8,0},{12,4},{1,9},{5,13},{9,1},{13,5},{2,10},{6,14},... | collective-permute-start | bytes 2261000 | tf_op jit(solution)/shard_map/ppermute | solution.py:473
  49.2 8.8 %collective-permute-done.3.refs_1_.refs_2_ = bf16[160,32,128]{2,1,0:T(8,128)(2,1)S(1)} collective-permute-done((bf16[160,32,128]{2,1,0:T(8,128)(2,1)}, bf16[160,32,128]{2,1,0:T(8,128)(2,1)S(1)}, u32[]{:S(2)}, u32[]{:S(2)}) %collective-permute-start.3) | collective-permute-done | bytes 1310752 | tf_op jit(solution)/shard_map/ppermute | solution.py:452
  58.0 4.3 %collective-permute-start.4 = (bf16[160,32,128]{2,1,0:T(8,128)(2,1)S(1)}, bf16[160,32,128]{2,1,0:T(8,128)(2,1)}, u32[]{:S(2)}, u32[]{:S(2)}) collective-permute-start(bf16[160,32,128]{2,1,0:T(8,128)(2,1)S(1)} %collective-permute-done.3.refs_1_.refs_2_), channel_id=1, source_target_pairs={{4,8},{8,12},{5,9},{9,13},{6,10},{10,14},{7,11},{11,15},{20,24},{2... | collective-permute-start | bytes 3932168 | tf_op jit(solution)/shard_map/ppermute | solution.py:475
  62.3 1.9 collective-permute-start.6
  64.2 7.3 %ints_0.1 = (bf16[4,256,1024]{2,1,0:T(8,128)(2,1)S(1)}, bf16[4,1024,256]{2,1,0:T(8,128)(2,1)}) custom-call(s32[4]{0:T(128)S(1)} %pad_add_fusion.meta, s32[4,4,16,16]{3,2,1,0:T(8,128)S(1)} %copy-done.1, bf16[2,2,256,1024]{3,2,1,0:T(8,128)(2,1)} %own_ref.3, bf16[2,2,256,1024]{3,2,1,0:T(8,128)(2,1)} %copy-done), custom_call_target="tpu_custom_call" | custom-call | flops 1024 | bytes 1024 | tf_op jit(solution)/shard_map/ints_0/pallas_call | solution.py:497
  71.5 5.9 %combine_0_0.1.refs_0_ = bf16[3,2,2,256,1024]{4,3,2,1,0:T(8,128)(2,1)} custom-call(s32[4]{0:T(128)S(1)} %pad_add_fusion.meta, s32[4,16,16]{2,1,0:T(8,128)} %mask.21, bf16[2,2,2,2,256,1024]{5,4,3,2,1,0:T(8,128)(2,1)} %bitcast.62, bf16[2,2,2,2,256,1024]{5,4,3,2,1,0:T(8,128)(2,1)} %collective-permute-done.oth_ref), custom_call_target="tpu_custom_call" | custom-call | flops 1024 | bytes 1024 | tf_op jit(solution)/shard_map/combine_0_0/pallas_call | solution.py:524
  77.4 13.9 %collective-permute-done.9.near_ref = bf16[46,64,128]{2,1,0:T(8,128)(2,1)} collective-permute-done((bf16[46,64,128]{2,1,0:T(8,128)(2,1)}, bf16[46,64,128]{2,1,0:T(8,128)(2,1)}, u32[]{:S(2)}, u32[]{:S(2)}) %collective-permute-start.9) | collective-permute-done | bytes 753696 | tf_op jit(solution)/shard_map/ppermute | solution.py:473
  92.5 1.8 collective-permute-done.7.near_ref
  95.5 7.9 %ints_1.1 = (bf16[4,256,1024]{2,1,0:T(8,128)(2,1)}, bf16[4,1024,256]{2,1,0:T(8,128)(2,1)}) custom-call(s32[4]{0:T(128)S(1)} %pad_add_fusion.meta, s32[4,4,16,16]{3,2,1,0:T(8,128)S(1)} %copy-done.1, bf16[160,32,128]{2,1,0:T(8,128)(2,1)} %collective-permute-done.5.refs_0_.refs_1_, bf16[160,32,128]{2,1,0:T(8,128)(2,1)} %copy-done.2), custom_call_target="tpu_custom_call" | custom-call | flops 1024 | bytes 1024 | tf_op jit(solution)/shard_map/ints_1/pallas_call | solution.py:497
  103.4 4.0 %collective-permute-done.10.far_ref = bf16[46,64,128]{2,1,0:T(8,128)(2,1)} collective-permute-done((bf16[46,64,128]{2,1,0:T(8,128)(2,1)}, bf16[46,64,128]{2,1,0:T(8,128)(2,1)}, u32[]{:S(2)}, u32[]{:S(2)}) %collective-permute-start.10) | collective-permute-done | bytes 753696 | tf_op jit(solution)/shard_map/ppermute | solution.py:577
  107.4 6.4 %combine_1_0.1.refs_0_ = bf16[3,2,2,256,1024]{4,3,2,1,0:T(8,128)(2,1)} custom-call(s32[4]{0:T(128)S(1)} %pad_add_fusion.meta, s32[4,16,16]{2,1,0:T(8,128)} %mask.21, bf16[2,2,2,2,256,1024]{5,4,3,2,1,0:T(8,128)(2,1)} %bitcast.63, bf16[2,2,2,2,256,1024]{5,4,3,2,1,0:T(8,128)(2,1)} %collective-permute-done.oth_ref, ...), custom_call_target="tpu_custom_call", output_to_operand_aliasing={{}: (6, {})} | custom-call | flops 1024 | bytes 1024 | tf_op jit(solution)/shard_map/combine_1_0/pallas_call | solution.py:524
  113.8 9.8 %collective-permute-done.8.far_ref = bf16[46,64,128]{2,1,0:T(8,128)(2,1)} collective-permute-done((bf16[46,64,128]{2,1,0:T(8,128)(2,1)}, bf16[46,64,128]{2,1,0:T(8,128)(2,1)}, u32[]{:S(2)}, u32[]{:S(2)}) %collective-permute-start.8) | collective-permute-done | bytes 753696 | tf_op jit(solution)/shard_map/ppermute | solution.py:577
  123.6 6.3 %combine_2_0.1.refs_6_.refs_7_.refs_8_ = bf16[3,2,2,256,1024]{4,3,2,1,0:T(8,128)(2,1)} custom-call(s32[4]{0:T(128)S(1)} %pad_add_fusion.meta, s32[4,16,16]{2,1,0:T(8,128)} %mask.21, bf16[2,2,2,2,256,1024]{5,4,3,2,1,0:T(8,128)(2,1)} %bitcast.64, bf16[2,2,2,2,256,1024]{5,4,3,2,1,0:T(8,128)(2,1)} %collective-permute-done.oth_ref, ...), custom_call_target="tpu_custom_call", output_to_operand_aliasing={{}: (6, {})} | custom-call | flops 1024 | bytes 1024 | tf_op jit(solution)/shard_map/combine_2_0/pallas_call | solution.py:524
  129.9 3.5 %collective-permute-start.14 = (bf16[3,2,2,256,1024]{4,3,2,1,0:T(8,128)(2,1)}, bf16[3,2,2,256,1024]{4,3,2,1,0:T(8,128)(2,1)}, u32[]{:S(2)}, u32[]{:S(2)}) collective-permute-start(bf16[3,2,2,256,1024]{4,3,2,1,0:T(8,128)(2,1)} %combine_2_0.1.refs_6_.refs_7_.refs_8_), channel_id=1, source_target_pairs={{0,1},{1,0},{2,3},{3,2},{4,5},{5,4},{6,7},{7,6},{8,9},{9,8},{10,11... | collective-permute-start | bytes 18874376 | tf_op jit(solution)/shard_map/ppermute | solution.py:587
  133.4 5.2 %collective-permute-start.12 = (bf16[160,32,128]{2,1,0:T(8,128)(2,1)}, bf16[160,32,128]{2,1,0:T(8,128)(2,1)}, u32[]{:S(2)}, u32[]{:S(2)}) collective-permute-start(bf16[160,32,128]{2,1,0:T(8,128)(2,1)} %collective-permute-done.6.refs_0_), channel_id=1, source_target_pairs={{4,0},{5,1},{6,2},{7,3},{20,16},{21,17},{22,18},{23,19}} | collective-permute-start | bytes 3932168 | tf_op jit(solution)/shard_map/ppermute | solution.py:584
  140.3 7.9 %ints_2.1 = (bf16[4,256,1024]{2,1,0:T(8,128)(2,1)}, bf16[4,1024,256]{2,1,0:T(8,128)(2,1)}) custom-call(s32[4]{0:T(128)S(1)} %pad_add_fusion.meta, s32[4,4,16,16]{3,2,1,0:T(8,128)S(1)} %copy-done.1, bf16[160,32,128]{2,1,0:T(8,128)(2,1)} %collective-permute-done.6.refs_0_, bf16[160,32,128]{2,1,0:T(8,128)(2,1)} %collective-permute-done.4.refs_1_), custom_call_target="tpu_custom_call" | custom-call | flops 1024 | bytes 1024 | tf_op jit(solution)/shard_map/ints_2/pallas_call | solution.py:497
  148.2 20.1 %early.1 = f32[2048,768]{1,0:T(8,128)} custom-call(s32[4]{0:T(128)S(1)} %pad_add_fusion.meta, bf16[4,256,1024]{2,1,0:T(8,128)(2,1)S(1)} %get-tuple-element.151.refs_0_, bf16[4,256,1024]{2,1,0:T(8,128)(2,1)} %get-tuple-element.152.refs_1_, bf16[4,256,1024]{2,1,0:T(8,128)(2,1)} %get-tuple-element.153.refs_2_, ...), custom_call_target="tpu_custom_call" | custom-call | flops 1024 | bytes 1024 | tf_op jit(solution)/shard_map/early/pallas_call | solution.py:599
  168.3 6.2 %collective-permute-done.11.near_ref = bf16[46,64,128]{2,1,0:T(8,128)(2,1)S(1)} collective-permute-done((bf16[46,64,128]{2,1,0:T(8,128)(2,1)}, bf16[46,64,128]{2,1,0:T(8,128)(2,1)S(1)}, u32[]{:S(2)}, u32[]{:S(2)}) %collective-permute-start.11) | collective-permute-done | bytes 753696 | tf_op jit(solution)/shard_map/ppermute | solution.py:473
  174.5 7.7 %collective-permute-done.12.refs_0_ = bf16[160,32,128]{2,1,0:T(8,128)(2,1)} collective-permute-done((bf16[160,32,128]{2,1,0:T(8,128)(2,1)}, bf16[160,32,128]{2,1,0:T(8,128)(2,1)}, u32[]{:S(2)}, u32[]{:S(2)}) %collective-permute-start.12) | collective-permute-done | bytes 1310752 | tf_op jit(solution)/shard_map/ppermute | solution.py:584
  183.4 7.9 %ints_3.1 = (bf16[4,256,1024]{2,1,0:T(8,128)(2,1)}, bf16[4,1024,256]{2,1,0:T(8,128)(2,1)}) custom-call(s32[4]{0:T(128)S(1)} %pad_add_fusion.meta, s32[4,4,16,16]{3,2,1,0:T(8,128)S(1)} %copy-done.1, bf16[160,32,128]{2,1,0:T(8,128)(2,1)} %collective-permute-done.12.refs_0_, bf16[160,32,128]{2,1,0:T(8,128)(2,1)} %collective-permute-done.5.refs_0_.refs_1_, ...), custom_call_target="tpu_custom_call" | custom-call | flops 1024 | bytes 1024 | tf_op jit(solution)/shard_map/ints_3/pallas_call | solution.py:497
  191.3 8.5 %collective-permute-done.15.far_ref = bf16[46,64,128]{2,1,0:T(8,128)(2,1)} collective-permute-done((bf16[46,64,128]{2,1,0:T(8,128)(2,1)S(1)}, bf16[46,64,128]{2,1,0:T(8,128)(2,1)}, u32[]{:S(2)}, u32[]{:S(2)}) %collective-permute-start.15) | collective-permute-done | bytes 753696 | tf_op jit(solution)/shard_map/ppermute | solution.py:618
  199.8 4.5 %combine_3_0.1 = (bf16[1,2,2,256,512]{4,3,2,1,0:T(8,128)(2,1)}, s32[1]{0:T(128)}) custom-call(s32[4]{0:T(128)S(1)} %pad_add_fusion.meta, s32[4,16,16]{2,1,0:T(8,128)} %mask.21, bf16[2,2,2,2,256,1024]{5,4,3,2,1,0:T(8,128)(2,1)} %bitcast.65, bf16[2,2,2,2,256,1024]{5,4,3,2,1,0:T(8,128)(2,1)} %collective-permute-done.oth_ref, bf16[46,64,128]{2,1,0:T(8,128)(2,1)} %copy-done.3, ...), custom_call_target="tpu_custom_call" | custom-call | flops 1024 | bytes 1024 | tf_op jit(solution)/shard_map/combine_3_0/pallas_call | solution.py:524
  204.3 5.2 %combine_3_2.1 = (bf16[1,2,2,256,512]{4,3,2,1,0:T(8,128)(2,1)}, s32[1]{0:T(128)}) custom-call(s32[4]{0:T(128)S(1)} %pad_add_fusion.meta, s32[4,16,16]{2,1,0:T(8,128)} %mask.21, bf16[2,2,2,2,256,1024]{5,4,3,2,1,0:T(8,128)(2,1)} %bitcast.66, bf16[2,2,2,2,256,1024]{5,4,3,2,1,0:T(8,128)(2,1)} %collective-permute-done.oth_ref, bf16[46,64,128]{2,1,0:T(8,128)(2,1)} %copy-done.3, ...), custom_call_target="tpu_custom_call" | custom-call | flops 1024 | bytes 1024 | tf_op jit(solution)/shard_map/combine_3_2/pallas_call | solution.py:524
  211.3 3.2 %collective-permute-done.17 = bf16[1,2,2,256,512]{4,3,2,1,0:T(8,128)(2,1)S(1)} collective-permute-done((bf16[1,2,2,256,512]{4,3,2,1,0:T(8,128)(2,1)}, bf16[1,2,2,256,512]{4,3,2,1,0:T(8,128)(2,1)S(1)}, u32[]{:S(2)}, u32[]{:S(2)}) %collective-permute-start.17) | collective-permute-done | bytes 1048608 | tf_op jit(solution)/shard_map/ppermute | solution.py:624
  215.0 27.4 %conditional.1 = (f32[8,256,1,1024]{3,2,1,0:T(1,128)}) conditional(s32[]{:T(128)} %bitcast.23, (s32[]{:T(128)}, f32[1024]{0:T(1024)S(1)}, s32[4]{0:T(128)S(1)}, f32[8]{0:T(128)S(1)}, f32[1]{0:T(128)}, /*index=5*/f32[2048,768]{1,0:T(8,128)}, bf16[4,256,1024]{2,1,0:T(8,128)(2,1)S(1)}, bf16[4,256,1024]{2,1,0:T(8,128)(2,1)}, ...), branch_computations={%region_6.7_spmd, %region_7.9_spmd} | conditional | flops 34424766464 | bytes 417631168 | solution.py:667
  217.9 24.3 %tail.1 = f32[8,256,1,1024]{3,2,1,0:T(1,128)} custom-call(s32[4]{0:T(128)S(1)} %get-tuple-element.75.meta, f32[8]{0:T(128)S(1)} %get-tuple-element.76.eps_slab, f32[1]{0:T(128)} %get-tuple-element.77.eps_pair, f32[256,1]{1,0:T(8,128)} %copy.53.eps_rows, f32[1,1024]{1,0:T(1,128)S(1)} %bitcast.70, f32[2048,768]{1,0:T(8,128)} %get-tuple-element.80.part_ref, ...), custom_call_target="tpu_custom_call" | custom-call | flops 1024 | bytes 1024 | tf_op jit(solution)/shard_map/cond/branch_0_fun/tail/pallas_call | solution.py:632
  (47 shorter events, 17.1 us)
Async XLA Ops:
  6.5 32.8 %collective-permute-start = (bf16[2,2,2,2,256,1024]{5,4,3,2,1,0:T(8,128)(2,1)}, bf16[2,2,2,2,256,1024]{5,4,3,2,1,0:T(8,128)(2,1)}, u32[]{:S(2)}, u32[]{:S(2)}) collective-permute-start(bf16[2,2,2,2,256,1024]{5,4,3,2,1,0:T(8,128)(2,1)} %bitcast.60), channel_id=1, source_target_pairs={{0,1},{1,0},{2,3},{3,2},{4,5},{5,4},{6,7},{7,6},{8,9},{9,8},{10,11... | collective-permute-start | bytes 25165832 | tf_op jit(solution)/shard_map/ppermute | solution.py:439
  7.2 11.9 %collective-permute-start.2 = (bf16[2,2,256,1024]{3,2,1,0:T(8,128)(2,1)}, bf16[2,2,256,1024]{3,2,1,0:T(8,128)(2,1)S(1)}, u32[]{:S(2)}, u32[]{:S(2)}) collective-permute-start(bf16[2,2,256,1024]{3,2,1,0:T(8,128)(2,1)} %own_ref.3), channel_id=1, source_target_pairs={{0,1},{1,0},{2,3},{3,2},{4,5},{5,4},{6,7},{7,6},{8,9},{9,8},{10,11... | collective-permute-start | bytes 6291464 | tf_op jit(solution)/shard_map/ppermute | solution.py:437
  19.2 1.3 copy-start
  25.6 32.4 %collective-permute-start.3 = (bf16[160,32,128]{2,1,0:T(8,128)(2,1)}, bf16[160,32,128]{2,1,0:T(8,128)(2,1)S(1)}, u32[]{:S(2)}, u32[]{:S(2)}) collective-permute-start(bf16[160,32,128]{2,1,0:T(8,128)(2,1)} %pack_int.1), channel_id=1, source_target_pairs={{0,4},{4,8},{8,12},{1,5},{5,9},{9,13},{2,6},{6,10},{10,14},{3,7},{... | collective-permute-start | bytes 3932168 | tf_op jit(solution)/shard_map/ppermute | solution.py:452
  28.8 33.5 %collective-permute-start.5 = (bf16[160,32,128]{2,1,0:T(8,128)(2,1)}, bf16[160,32,128]{2,1,0:T(8,128)(2,1)}, u32[]{:S(2)}, u32[]{:S(2)}) collective-permute-start(bf16[160,32,128]{2,1,0:T(8,128)(2,1)} %pack_int.1), channel_id=1, source_target_pairs={{4,0},{8,4},{12,8},{5,1},{9,5},{13,9},{6,2},{10,6},{14,10},{7,3},{... | collective-permute-start | bytes 3932168 | tf_op jit(solution)/shard_map/ppermute | solution.py:453
  35.9 2.9 %collective-permute-start.1 = (s32[1]{0:T(128)}, s32[1]{0:T(128)}, u32[]{:S(2)}, u32[]{:S(2)}) collective-permute-start(s32[1]{0:T(128)} %bitcast.22), channel_id=1, source_target_pairs={{0,16},{16,0},{1,17},{17,1},{2,18},{18,2},{3,19},{19,3},{4,20},{20... | collective-permute-start | bytes 20 | tf_op jit(solution)/shard_map/ppermute | solution.py:435
  39.3 24.9 %copy-start.1 = (s32[4,4,16,16]{3,2,1,0:T(8,128)S(1)}, s32[4,4,16,16]{3,2,1,0:T(8,128)}, u32[]{:S(2)}) copy-start(s32[4,4,16,16]{3,2,1,0:T(8,128)} %mask.19) | copy-start | bytes 49156
  46.0 45.3 %collective-permute-start.9 = (bf16[46,64,128]{2,1,0:T(8,128)(2,1)}, bf16[46,64,128]{2,1,0:T(8,128)(2,1)}, u32[]{:S(2)}, u32[]{:S(2)}) collective-permute-start(bf16[46,64,128]{2,1,0:T(8,128)(2,1)} %get-tuple-element.139), channel_id=1, source_target_pairs={{0,4},{4,0},{8,12},{12,8},{1,5},{5,1},{9,13},{13,9},{2,6},{6,2},{1... | collective-permute-start | bytes 2261000 | tf_op jit(solution)/shard_map/ppermute | solution.py:473
  46.0 48.3 %collective-permute-start.7 = (bf16[46,64,128]{2,1,0:T(8,128)(2,1)}, bf16[46,64,128]{2,1,0:T(8,128)(2,1)}, u32[]{:S(2)}, u32[]{:S(2)}) collective-permute-start(bf16[46,64,128]{2,1,0:T(8,128)(2,1)} %get-tuple-element.138), channel_id=1, source_target_pairs={{0,8},{4,12},{8,0},{12,4},{1,9},{5,13},{9,1},{13,5},{2,10},{6,14},... | collective-permute-start | bytes 2261000 | tf_op jit(solution)/shard_map/ppermute | solution.py:473
  58.0 19.4 %copy-start.2 = (bf16[160,32,128]{2,1,0:T(8,128)(2,1)}, bf16[160,32,128]{2,1,0:T(8,128)(2,1)S(1)}, u32[]{:S(2)}) copy-start(bf16[160,32,128]{2,1,0:T(8,128)(2,1)S(1)} %collective-permute-done.3.refs_1_.refs_2_) | copy-start | bytes 3932164
  58.0 71.9 %collective-permute-start.4 = (bf16[160,32,128]{2,1,0:T(8,128)(2,1)S(1)}, bf16[160,32,128]{2,1,0:T(8,128)(2,1)}, u32[]{:S(2)}, u32[]{:S(2)}) collective-permute-start(bf16[160,32,128]{2,1,0:T(8,128)(2,1)S(1)} %collective-permute-done.3.refs_1_.refs_2_), channel_id=1, source_target_pairs={{4,8},{8,12},{5,9},{9,13},{6,10},{10,14},{7,11},{11,15},{20,24},{2... | collective-permute-start | bytes 3932168 | tf_op jit(solution)/shard_map/ppermute | solution.py:475
  62.3 67.6 %collective-permute-start.6 = (bf16[160,32,128]{2,1,0:T(8,128)(2,1)}, bf16[160,32,128]{2,1,0:T(8,128)(2,1)}, u32[]{:S(2)}, u32[]{:S(2)}) collective-permute-start(bf16[160,32,128]{2,1,0:T(8,128)(2,1)} %collective-permute-done.5.refs_0_.refs_1_), channel_id=1, source_target_pairs={{4,0},{8,4},{5,1},{9,5},{6,2},{10,6},{7,3},{11,7},{20,16},{24,20},... | collective-permute-start | bytes 3932168 | tf_op jit(solution)/shard_map/ppermute | solution.py:476
  91.3 16.1 %collective-permute-start.10 = (bf16[46,64,128]{2,1,0:T(8,128)(2,1)}, bf16[46,64,128]{2,1,0:T(8,128)(2,1)}, u32[]{:S(2)}, u32[]{:S(2)}) collective-permute-start(bf16[46,64,128]{2,1,0:T(8,128)(2,1)} %collective-permute-done.9.near_ref), channel_id=1, source_target_pairs={{0,2},{2,0},{1,3},{3,1},{4,6},{6,4},{5,7},{7,5},{8,10},{10,8},{9,1... | collective-permute-start | bytes 2261000 | tf_op jit(solution)/shard_map/ppermute | solution.py:577
  94.3 29.3 %collective-permute-start.8 = (bf16[46,64,128]{2,1,0:T(8,128)(2,1)}, bf16[46,64,128]{2,1,0:T(8,128)(2,1)}, u32[]{:S(2)}, u32[]{:S(2)}) collective-permute-start(bf16[46,64,128]{2,1,0:T(8,128)(2,1)} %collective-permute-done.7.near_ref), channel_id=1, source_target_pairs={{0,2},{2,0},{1,3},{3,1},{4,6},{6,4},{5,7},{7,5},{8,10},{10,8},{9,1... | collective-permute-start | bytes 2261000 | tf_op jit(solution)/shard_map/ppermute | solution.py:577
  129.9 18.3 %collective-permute-start.14 = (bf16[3,2,2,256,1024]{4,3,2,1,0:T(8,128)(2,1)}, bf16[3,2,2,256,1024]{4,3,2,1,0:T(8,128)(2,1)}, u32[]{:S(2)}, u32[]{:S(2)}) collective-permute-start(bf16[3,2,2,256,1024]{4,3,2,1,0:T(8,128)(2,1)} %combine_2_0.1.refs_6_.refs_7_.refs_8_), channel_id=1, source_target_pairs={{0,1},{1,0},{2,3},{3,2},{4,5},{5,4},{6,7},{7,6},{8,9},{9,8},{10,11... | collective-permute-start | bytes 18874376 | tf_op jit(solution)/shard_map/ppermute | solution.py:587
  133.4 48.7 %collective-permute-start.12 = (bf16[160,32,128]{2,1,0:T(8,128)(2,1)}, bf16[160,32,128]{2,1,0:T(8,128)(2,1)}, u32[]{:S(2)}, u32[]{:S(2)}) collective-permute-start(bf16[160,32,128]{2,1,0:T(8,128)(2,1)} %collective-permute-done.6.refs_0_), channel_id=1, source_target_pairs={{4,0},{5,1},{6,2},{7,3},{20,16},{21,17},{22,18},{23,19}} | collective-permute-start | bytes 3932168 | tf_op jit(solution)/shard_map/ppermute | solution.py:584
  138.6 43.6 %collective-permute-start.13 = (bf16[160,32,128]{2,1,0:T(8,128)(2,1)}, bf16[160,32,128]{2,1,0:T(8,128)(2,1)}, u32[]{:S(2)}, u32[]{:S(2)}) collective-permute-start(bf16[160,32,128]{2,1,0:T(8,128)(2,1)} %collective-permute-done.4.refs_1_), channel_id=1, source_target_pairs={{8,12},{9,13},{10,14},{11,15},{24,28},{25,29},{26,30},{27,31}} | collective-permute-start | bytes 3932168 | tf_op jit(solution)/shard_map/ppermute | solution.py:585
  140.3 34.1 %collective-permute-start.11 = (bf16[46,64,128]{2,1,0:T(8,128)(2,1)}, bf16[46,64,128]{2,1,0:T(8,128)(2,1)S(1)}, u32[]{:S(2)}, u32[]{:S(2)}) collective-permute-start(bf16[46,64,128]{2,1,0:T(8,128)(2,1)} %get-tuple-element.148), channel_id=1, source_target_pairs={{0,12},{4,8},{8,4},{12,0},{1,13},{5,9},{9,5},{13,1},{2,14},{6,10},... | collective-permute-start | bytes 2261000 | tf_op jit(solution)/shard_map/ppermute | solution.py:473
  174.5 25.3 %copy-start.3 = (bf16[46,64,128]{2,1,0:T(8,128)(2,1)}, bf16[46,64,128]{2,1,0:T(8,128)(2,1)S(1)}, u32[]{:S(2)}) copy-start(bf16[46,64,128]{2,1,0:T(8,128)(2,1)S(1)} %collective-permute-done.11.near_ref) | copy-start | bytes 2260996
  182.1 17.7 %collective-permute-start.15 = (bf16[46,64,128]{2,1,0:T(8,128)(2,1)S(1)}, bf16[46,64,128]{2,1,0:T(8,128)(2,1)}, u32[]{:S(2)}, u32[]{:S(2)}) collective-permute-start(bf16[46,64,128]{2,1,0:T(8,128)(2,1)S(1)} %collective-permute-done.11.near_ref), channel_id=1, source_target_pairs={{0,2},{2,0},{1,3},{3,1},{4,6},{6,4},{5,7},{7,5},{8,10},{10,8},{9,1... | collective-permute-start | bytes 2261000 | tf_op jit(solution)/shard_map/ppermute | solution.py:618
  204.3 6.9 %copy-start.4 = (bf16[1,2,2,256,512]{4,3,2,1,0:T(8,128)(2,1)S(1)}, bf16[1,2,2,256,512]{4,3,2,1,0:T(8,128)(2,1)}, u32[]{:S(2)}) copy-start(bf16[1,2,2,256,512]{4,3,2,1,0:T(8,128)(2,1)} %get-tuple-element.167) | copy-start | bytes 3145732
  204.3 10.7 %copy-start.7 = (f32[1024]{0:T(1024)S(1)}, f32[1024]{0:T(1024)}, u32[]{:S(2)}) copy-start(f32[1024]{0:T(1024)} %param.15) | copy-start | bytes 12292
  204.3 10.7 %copy-start.8 = (f32[8]{0:T(128)S(1)}, f32[8]{0:T(128)}, u32[]{:S(2)}) copy-start(f32[8]{0:T(128)} %param.13) | copy-start | bytes 100
  209.5 5.0 %collective-permute-start.17 = (bf16[1,2,2,256,512]{4,3,2,1,0:T(8,128)(2,1)}, bf16[1,2,2,256,512]{4,3,2,1,0:T(8,128)(2,1)S(1)}, u32[]{:S(2)}, u32[]{:S(2)}) collective-permute-start(bf16[1,2,2,256,512]{4,3,2,1,0:T(8,128)(2,1)} %get-tuple-element.169), channel_id=1, source_target_pairs={{0,1},{1,0},{2,3},{3,2},{4,5},{5,4},{6,7},{7,6},{8,9},{9,8},{10,11... | collective-permute-start | bytes 3145736 | tf_op jit(solution)/shard_map/ppermute | solution.py:624
  211.2 3.8 %collective-permute-start.16 = (bf16[1,2,2,256,512]{4,3,2,1,0:T(8,128)(2,1)S(1)}, bf16[1,2,2,256,512]{4,3,2,1,0:T(8,128)(2,1)S(1)}, u32[]{:S(2)}, u32[]{:S(2)}) collective-permute-start(bf16[1,2,2,256,512]{4,3,2,1,0:T(8,128)(2,1)S(1)} %copy-done.4), channel_id=1, source_target_pairs={{0,1},{1,0},{2,3},{3,2},{4,5},{5,4},{6,7},{7,6},{8,9},{9,8},{10,11... | collective-permute-start | bytes 3145736 | tf_op jit(solution)/shard_map/ppermute | solution.py:624
  215.0 1.0 copy-start.5
  216.0 1.0 copy-start.6

commit v4 on v3

--- a/solution.py
+++ b/solution.py
@@ -349,41 +349,66 @@
         work(oth)
 
 
-def tail_kernel(meta, eps_slab, eps_pair, eps_rows, eps_cols, part_ref, *refs):
-    direct, swapped, own, oth, out_ref = refs[:4], refs[4:8], refs[8:13], refs[13:18], refs[18]
-    row_ref, col_ref = refs[19:]
+def late_kernel(meta, *refs):
+    direct, swapped, own, oth = refs[:4], refs[4:8], refs[8:11], refs[11:14]
+    row_ref, out_ref, col_ref = refs[14:]
+    v = meta[0]
+    g = pl.program_id(0)
+    last_at = pl.multiple_of((v ^ 3) * 256, 256)
+
+    for p in range(4):
+        at = pl.multiple_of((v ^ p) * 256, 256)
+        row_ref[:, p * 256 : (p + 1) * 256] = folded(
+            direct[3][g, :, pl.ds(at, 256)],
+            swapped[p][g] if p < 3 else swapped[3][g, pl.ds(last_at, 256), :],
+        )
+
+    @pl.when(g == 0)
+    def _():
+        for p in range(3):
+            at = pl.multiple_of((v ^ p) * 256, 256)
+            for k in range(4):
+                col_ref[p, k * 256 : (k + 1) * 256, :] = folded(
+                    direct[p][k], swapped[3][k, pl.ds(at, 256), :]
+                )
+
+    def work(blocks):
+        total = jnp.dot(
+            blocks[0][...].reshape(512, 1024), col_ref[0], preferred_element_type=jnp.float32
+        )
+        for q in range(1, 3):
+            total += jnp.dot(
+                blocks[q][...].reshape(512, 1024), col_ref[q], preferred_element_type=jnp.float32
+            )
+        out_ref[...] = total
+
+    @pl.when(g < 2)
+    def _():
+        work(own)
+
+    @pl.when(g >= 2)
+    def _():
+        work(oth)
+
+
+def tail_kernel(meta, eps_slab, eps_pair, eps_rows, eps_cols, part_ref, late_ref, row_ref, *refs):
+    own, oth, out_ref = refs[:2], refs[2:4], refs[4]
     v, r = meta[0], meta[2]
     g = pl.program_id(0)
-    last = v ^ 3
-
-    @pl.when(g == 0)
-    def _():
-        last_at = pl.multiple_of(last * 256, 256)
-        for p in range(4):
-            at = pl.multiple_of((v ^ p) * 256, 256)
-            for k in range(4):
-                ks = slice(k * 256, (k + 1) * 256)
-                row_ref[ks, p * 256 : (p + 1) * 256] = folded(
-                    direct[3][k, :, pl.ds(at, 256)],
-                    swapped[p][k] if p < 3 else swapped[3][k, pl.ds(last_at, 256), :],
-                )
-                if p < 3:
-                    col_ref[p, ks, :] = folded(
-                        direct[p][k], swapped[3][k, pl.ds(at, 256), :]
-                    )
 
     def work(blocks, i, k0):
-        flat = [b[...].reshape(512, b.shape[-1]) for b in blocks]
         total = jnp.float32(0)
         for half in range(2):
             at = pl.multiple_of(256 * lax.rem(k0 + 2 * half, 4), 512)
-            total += jnp.dot(flat[3 + half], row_ref[pl.ds(at, 512), :], preferred_element_type=jnp.float32)
-        late = total[:, 768:]
-        for q in range(3):
-            late += jnp.dot(flat[q], col_ref[q], preferred_element_type=jnp.float32)
+            total += jnp.dot(
+                blocks[half][...].reshape(512, 512),
+                row_ref[pl.ds(at, 512), :],
+                preferred_element_type=jnp.float32,
+            )
         for p in range(4):
             s = v ^ p
-            value = late if p == 3 else total[:, p * 256 : (p + 1) * 256] + part_ref[:, p * 256 : (p + 1) * 256]
+            before = late_ref[...] if p == 3 else part_ref[:, p * 256 : (p + 1) * 256]
+            value = total[:, p * 256 : (p + 1) * 256] + before
             cols = eps_cols[:, pl.ds(pl.multiple_of(s * 256, 256), 256)]
             for ii in range(2):
                 energy = (eps_rows[...] + cols) - eps_slab[i + ii] - eps_pair[0]
@@ -432,12 +457,11 @@
     pieces = int_mask.reshape(4, 4, 4, 4, 16).sum((0, 3, 4))
     over = jnp.logical_or(jnp.max(pairs) > AMP_SLOTS - 1, jnp.max(pieces) > INT_SLOTS - 1)
     over = over.astype(jnp.int32).reshape(1)
-    over = over + lax.ppermute(over, "frag", swap)
 
     int_oth = lax.ppermute(integrals, "rep", swap)
     amps = amplitudes.reshape(2, 2, 2, 2, 256, 1024)
-    amp_oth = lax.ppermute(amps, "rep", swap)
-    amp_oth, over = lax.optimization_barrier((amp_oth, over))
+    int_oth, later = lax.optimization_barrier((int_oth, amps))
+    amp_oth = lax.ppermute(later, "rep", swap)
 
     packed_int = pl.pallas_call(
         pack_int_kernel,
@@ -574,9 +598,11 @@
     first = combine_first(0, None, None, None)
     near1, near2 = across(1, packed_amp[0]), across(2, packed_amp[1])
     near1, ints[0], first = ready((near1, ints[0], first))
+    near2, over = ready((near2, over))
     far1, far2 = lax.ppermute(near1, "occ", swap), lax.ppermute(near2, "occ", swap)
     ints.append(unpack(1, down1, up1))
-    ints[1], far1 = ready((ints[1], far1))
+    over = over + lax.ppermute(over, "frag", swap)
+    ints[1], far1, over = ready((ints[1], far1, over))
     first = combine_first(1, near1, far1, first)
     first = combine_first(2, near2, far2, first)
     up2, down2, first, packed3 = ready((up2, down2, first, packed_amp[2]))
@@ -614,21 +640,45 @@
         name="early",
     )(meta, *[d for d, _ in ints], *[t for _, t in ints], *[first] * 3, *[first_oth] * 3)
 
-    near3, end_down, end_up, part = ready((near3, end_down, end_up, part))
+    near3, part = ready((near3, part))
     far3 = lax.ppermute(near3, "occ", swap)
     ints.append(unpack(3, end_down, down1, up1, end_up))
-    far3, ints[3] = ready((far3, ints[3]))
+    rows, cols = [d for d, _ in ints], [t for _, t in ints]
+    last_row, late = pl.pallas_call(
+        late_kernel,
+        grid_spec=pltpu.PrefetchScalarGridSpec(
+            num_scalar_prefetch=1,
+            grid=(4,),
+            in_specs=[pl.BlockSpec((4, 256, 256), lambda g, meta: (0, 0, meta[0] ^ 3), pipeline_mode=once)] * 3
+            + [pl.BlockSpec((4, 256, 1024), lambda g, meta: (0, 0, 0), pipeline_mode=once)]
+            + [pl.BlockSpec((4, 256, 256), lambda g, meta: (0, meta[0] ^ 3, 0), pipeline_mode=once)] * 3
+            + [pl.BlockSpec((4, 1024, 256), lambda g, meta: (0, 0, 0), pipeline_mode=once)]
+            + [own_at(d) for d in range(3)]
+            + [oth_at(d) for d in range(3)],
+            out_specs=[
+                pl.BlockSpec((256, 1024), lambda g, meta: (g, 0)),
+                pl.BlockSpec((512, 256), place),
+            ],
+            scratch_shapes=[pltpu.VMEM((3, 1024, 256), bf16)],
+        ),
+        out_shape=[
+            jax.ShapeDtypeStruct((1024, 1024), bf16),
+            jax.ShapeDtypeStruct((2048, 256), jnp.float32),
+        ],
+        compiler_params=params(),
+        cost_estimate=NO_COST,
+        name="late",
+    )(meta, *rows, *cols, *[first] * 3, *[first_oth] * 3)
+    far3, late = ready((far3, late))
     half0, count = combine_half(0, near3, far3)
     half1, _ = combine_half(2, near3, far3, count)
     halves = (half0, half1)
     halves_oth = tuple(lax.ppermute(h, "rep", swap) for h in halves)
-    rows, cols = [d for d, _ in ints], [t for _, t in ints]
-
     row_energy = lax.dynamic_slice_in_dim(eps_vir, v * 256, 256, 0).reshape(256, 1)
     col_energy = eps_vir.reshape(1, 1024)
 
     def finish(ops):
-        part, rows, cols, own, oth = ops
+        part, late, last_row, own, oth = ops
         return pl.pallas_call(
             tail_kernel,
             grid_spec=pltpu.PrefetchScalarGridSpec(
@@ -638,26 +688,18 @@
                     pl.BlockSpec((256, 1), lambda g, *_: (0, 0)),
                     pl.BlockSpec((1, 1024), lambda g, *_: (0, 0)),
                     pl.BlockSpec((512, 768), place),
+                    pl.BlockSpec((512, 256), place),
+                    pl.BlockSpec((1024, 1024), lambda g, *_: (0, 0), pipeline_mode=once),
                 ]
-                + [pl.BlockSpec((4, 256, 256), lambda g, meta, *_: (0, 0, meta[0] ^ 3), pipeline_mode=once)] * 3
-                + [pl.BlockSpec((4, 256, 1024), lambda g, meta, *_: (0, 0, 0), pipeline_mode=once)]
-                + [pl.BlockSpec((4, 256, 256), lambda g, meta, *_: (0, meta[0] ^ 3, 0), pipeline_mode=once)] * 3
-                + [pl.BlockSpec((4, 1024, 256), lambda g, meta, *_: (0, 0, 0), pipeline_mode=once)]
-                + [own_at(d) for d in range(3)]
                 + [own_at(3, 512)] * 2
-                + [oth_at(d) for d in range(3)]
                 + [oth_at(3, 512)] * 2,
                 out_specs=pl.BlockSpec((2, 256, 1, 1024), lambda g, meta, *_: (*place(g, meta), 0, 0)),
-                scratch_shapes=[
-                    pltpu.VMEM((1024, 1024), bf16),
-                    pltpu.VMEM((3, 1024, 256), bf16),
-                ],
             ),
             out_shape=jax.ShapeDtypeStruct((8, 256, 1, 1024), jnp.float32),
             compiler_params=params(),
             cost_estimate=NO_COST,
             name="tail",
-        )(meta, eps_slab, eps_pair, row_energy, col_energy, part, *rows, *cols, *own, *oth)
+        )(meta, eps_slab, eps_pair, row_energy, col_energy, part, late, last_row, *own, *oth)
 
     def dense(ops):
         return dense_shards(
@@ -668,13 +710,7 @@
         over[0] > 0,
         dense,
         finish,
-        (
-            part,
-            rows,
-            cols,
-            (first, first, first, *halves),
-            (first_oth, first_oth, first_oth, *halves_oth),
-        ),
+        (part, late, last_row, halves, halves_oth),
     )
 
 

time: 254 us -> 253 us (level); the launches traced: 249 us -> 252 us
  waiting for transfers between devices: 77.1 us -> 50.6 us
  loops' own time: 0.23 us -> 15.7 us
  Pallas kernels: 115 us -> 122 us
  starting transfers between devices: 33.3 us -> 39.3 us
    another operation x1, loops' own time: 0.23 us -> 15.7 us  [packed_shards(): lax.cond(over[0] > 0, dense, finish, (part, late, last_row, halves, halve...]
    pallas_call x0 -> x1, Pallas kernels: none -> 13 us  [packed_shards(): pl.pallas_call(late_kernel, grid_spec=pltpu.PrefetchScalarGridSpec(num_sc...]
    ppermute x3, waiting for transfers between devices: 21.9 us -> 9.1 us  [across(): return lax.ppermute(packed, 'vir', [(s, s ^ d) for s in range(4)])]
    ppermute x1, waiting for transfers between devices: 8.55 us -> 0.01 us  [packed_shards(): far3 = lax.ppermute(near3, 'occ', swap)]
    ppermute x1, waiting for transfers between devices: 11.9 us -> 4 us  [packed_shards(): int_oth = lax.ppermute(integrals, 'rep', swap)]
    ppermute x1, waiting for transfers between devices: 8.82 us -> 16.3 us  [packed_shards(): up1 = lax.ppermute(packed_int, 'vir', [(0, 1), (1, 2), (2, 3)])]
    ppermute x1, starting transfers between devices: 3.51 us -> 10.7 us  [packed_shards(): first_oth = lax.ppermute(first, 'rep', swap)]
    pallas_call x1, Pallas kernels: 24.3 us -> 17.2 us  [finish(): pl.pallas_call(tail_kernel, grid_spec=pltpu.PrefetchScalarGridSpec(num_sc...]
  transfers between devices with their start and end apart: 18 -> 18, of which waited for: 12 -> 9; matrix products, arithmetic and copies ran while one was open for 1% -> 2% of each run, Pallas kernels for 33% -> 38%
where the time goes in v4:
time: 253 us; the launch traced here: 252 us
  Pallas kernels  122 us (48%)
  waiting for transfers between devices  50.6 us (20%)
  starting transfers between devices  39.3 us (16%)
  loops' own time  15.7 us (6%)
  between operations  15.6 us (6%)
  other arithmetic  4.51 us (2%)
  local copies, waits for them, and re-layouts  4.46 us (2%)
    pallas_call x4, Pallas kernels, unpack(): pl.pallas_call(kernel, grid_spec=pltpu.PrefetchScalarGridSpec(num_scalar_...  31.3 us
    pallas_call x5, Pallas kernels, combine(): pl.pallas_call(kernel, grid_spec=pltpu.PrefetchScalarGridSpec(num_scalar_...  27.8 us
    pallas_call x1, Pallas kernels, packed_shards(): pl.pallas_call(early_kernel, grid_spec=pltpu.PrefetchScalarGridSpec(num_s...  20.8 us
    pallas_call x1, Pallas kernels, finish(): pl.pallas_call(tail_kernel, grid_spec=pltpu.PrefetchScalarGridSpec(num_sc...  17.2 us
    ppermute x1, waiting for transfers between devices, packed_shards(): up1 = lax.ppermute(packed_int, 'vir', [(0, 1), (1, 2), (2, 3)])  16.3 us
    another operation x1, loops' own time, packed_shards(): lax.cond(over[0] > 0, dense, finish, (part, late, last_row, halves, halve...  15.7 us
    pallas_call x1, Pallas kernels, packed_shards(): pl.pallas_call(late_kernel, grid_spec=pltpu.PrefetchScalarGridSpec(num_sc...  13 us
    ppermute x1, waiting for transfers between devices, packed_shards(): end_down = lax.ppermute(down2, 'vir', [(1, 0)])  11.8 us
  transfers between devices with their start and end apart: 18, of which 9 were waited for; matrix products, arithmetic and copies ran while one was open for 2% of the time, Pallas kernels for 38%

profile of v4, /device:TPU:9, one launch (start us, length us, event | category | flops | bytes accessed | tf_op | source)
XLA Modules:
  0.0 251.7 jit_solution(16647288606578069873)
XLA Ops:
  7.2 4.0 %collective-permute-done.oth_ref = bf16[2,2,256,1024]{3,2,1,0:T(8,128)(2,1)S(1)} collective-permute-done((bf16[2,2,256,1024]{3,2,1,0:T(8,128)(2,1)}, bf16[2,2,256,1024]{3,2,1,0:T(8,128)(2,1)S(1)}, u32[]{:S(2)}, u32[]{:S(2)}) %collective-permute-start) | collective-permute-done | bytes 2097184 | tf_op jit(solution)/shard_map/ppermute | solution.py:461
  12.5 5.1 %pack_int.1 = bf16[160,32,128]{2,1,0:T(8,128)(2,1)} custom-call(s32[4]{0:T(128)S(1)} %pad_add_fusion.meta, s32[4,4,16,16]{3,2,1,0:T(8,128)} %mask.19, bf16[2,2,256,1024]{3,2,1,0:T(8,128)(2,1)} %own_ref.3, bf16[2,2,256,1024]{3,2,1,0:T(8,128)(2,1)} %copy-done.2), custom_call_target="tpu_custom_call" | custom-call | flops 1024 | bytes 1024 | tf_op jit(solution)/shard_map/pack_int/pallas_call | solution.py:466
  17.6 3.3 %collective-permute-start.2 = (bf16[160,32,128]{2,1,0:T(8,128)(2,1)}, bf16[160,32,128]{2,1,0:T(8,128)(2,1)S(1)}, u32[]{:S(2)}, u32[]{:S(2)}) collective-permute-start(bf16[160,32,128]{2,1,0:T(8,128)(2,1)} %pack_int.1), channel_id=1, source_target_pairs={{0,4},{4,8},{8,12},{1,5},{5,9},{9,13},{2,6},{6,10},{10,14},{3,7},{... | collective-permute-start | bytes 3932168 | tf_op jit(solution)/shard_map/ppermute | solution.py:476
  21.0 2.2 collective-permute-start.1
  23.1 1.6 collective-permute-done.3.oth_ref
  24.7 6.5 %pack_amp.1 = (bf16[46,64,128]{2,1,0:T(8,128)(2,1)}, bf16[46,64,128]{2,1,0:T(8,128)(2,1)}, bf16[46,64,128]{2,1,0:T(8,128)(2,1)}) custom-call(s32[4]{0:T(128)S(1)} %pad_add_fusion.meta, s32[4,16,16]{2,1,0:T(8,128)} %mask.21, bf16[2,2,2,2,256,1024]{5,4,3,2,1,0:T(8,128)(2,1)} %bitcast.61, bf16[2,2,2,2,256,1024]{5,4,3,2,1,0:T(8,128)(2,1)} %collective-permute-done.3.oth_ref), custom_call_target="tpu_custom_call" | custom-call | flops 1024 | bytes 1024 | tf_op jit(solution)/shard_map/pack_amp/pallas_call | solution.py:479
  31.2 2.5 collective-permute-start.6
  33.7 16.3 %collective-permute-done.2.refs_1_.refs_2_ = bf16[160,32,128]{2,1,0:T(8,128)(2,1)S(1)} collective-permute-done((bf16[160,32,128]{2,1,0:T(8,128)(2,1)}, bf16[160,32,128]{2,1,0:T(8,128)(2,1)S(1)}, u32[]{:S(2)}, u32[]{:S(2)}) %collective-permute-start.2) | collective-permute-done | bytes 1310752 | tf_op jit(solution)/shard_map/ppermute | solution.py:476
  50.0 4.3 %collective-permute-start.8 = (bf16[160,32,128]{2,1,0:T(8,128)(2,1)S(1)}, bf16[160,32,128]{2,1,0:T(8,128)(2,1)}, u32[]{:S(2)}, u32[]{:S(2)}) collective-permute-start(bf16[160,32,128]{2,1,0:T(8,128)(2,1)S(1)} %collective-permute-done.2.refs_1_.refs_2_), channel_id=1, source_target_pairs={{4,8},{8,12},{5,9},{9,13},{6,10},{10,14},{7,11},{11,15},{20,24},{2... | collective-permute-start | bytes 3932168 | tf_op jit(solution)/shard_map/ppermute | solution.py:499
  54.3 1.9 collective-permute-start.9
  62.6 7.5 %ints_0.1 = (bf16[4,256,1024]{2,1,0:T(8,128)(2,1)}, bf16[4,1024,256]{2,1,0:T(8,128)(2,1)}) custom-call(s32[4]{0:T(128)S(1)} %pad_add_fusion.meta, s32[4,4,16,16]{3,2,1,0:T(8,128)S(1)} %copy-done.3, bf16[2,2,256,1024]{3,2,1,0:T(8,128)(2,1)S(1)} %copy-done, bf16[2,2,256,1024]{3,2,1,0:T(8,128)(2,1)} %copy-done.2), custom_call_target="tpu_custom_call" | custom-call | flops 1024 | bytes 1024 | tf_op jit(solution)/shard_map/ints_0/pallas_call | solution.py:521
  70.1 5.8 %combine_0_0.1.refs_0_ = bf16[3,2,2,256,1024]{4,3,2,1,0:T(8,128)(2,1)} custom-call(s32[4]{0:T(128)S(1)} %pad_add_fusion.meta, s32[4,16,16]{2,1,0:T(8,128)} %mask.21, bf16[2,2,2,2,256,1024]{5,4,3,2,1,0:T(8,128)(2,1)} %bitcast.62, bf16[2,2,2,2,256,1024]{5,4,3,2,1,0:T(8,128)(2,1)} %collective-permute-done.3.oth_ref), custom_call_target="tpu_custom_call" | custom-call | flops 1024 | bytes 1024 | tf_op jit(solution)/shard_map/combine_0_0/pallas_call | solution.py:548
  75.9 7.3 %collective-permute-done.4.near_ref = bf16[46,64,128]{2,1,0:T(8,128)(2,1)} collective-permute-done((bf16[46,64,128]{2,1,0:T(8,128)(2,1)}, bf16[46,64,128]{2,1,0:T(8,128)(2,1)}, u32[]{:S(2)}, u32[]{:S(2)}) %collective-permute-start.4) | collective-permute-done | bytes 753696 | tf_op jit(solution)/shard_map/ppermute | solution.py:497
  84.4 1.8 collective-permute-done.6.near_ref
  87.4 7.9 %ints_1.1 = (bf16[4,256,1024]{2,1,0:T(8,128)(2,1)}, bf16[4,1024,256]{2,1,0:T(8,128)(2,1)}) custom-call(s32[4]{0:T(128)S(1)} %pad_add_fusion.meta, s32[4,4,16,16]{3,2,1,0:T(8,128)S(1)} %copy-done.3, bf16[160,32,128]{2,1,0:T(8,128)(2,1)} %collective-permute-done.1.refs_0_.refs_1_, bf16[160,32,128]{2,1,0:T(8,128)(2,1)} %copy-done.4), custom_call_target="tpu_custom_call" | custom-call | flops 1024 | bytes 1024 | tf_op jit(solution)/shard_map/ints_1/pallas_call | solution.py:521
  95.3 2.0 collective-permute-start.7
  98.8 6.3 %combine_1_0.1.refs_0_ = bf16[3,2,2,256,1024]{4,3,2,1,0:T(8,128)(2,1)} custom-call(s32[4]{0:T(128)S(1)} %pad_add_fusion.meta, s32[4,16,16]{2,1,0:T(8,128)} %mask.21, bf16[2,2,2,2,256,1024]{5,4,3,2,1,0:T(8,128)(2,1)} %bitcast.63, bf16[2,2,2,2,256,1024]{5,4,3,2,1,0:T(8,128)(2,1)} %collective-permute-done.3.oth_ref, ...), custom_call_target="tpu_custom_call", output_to_operand_aliasing={{}: (6, {})} | custom-call | flops 1024 | bytes 1024 | tf_op jit(solution)/shard_map/combine_1_0/pallas_call | solution.py:548
  105.1 3.2 %collective-permute-done.10.far_ref = bf16[46,64,128]{2,1,0:T(8,128)(2,1)} collective-permute-done((bf16[46,64,128]{2,1,0:T(8,128)(2,1)}, bf16[46,64,128]{2,1,0:T(8,128)(2,1)}, u32[]{:S(2)}, u32[]{:S(2)}) %collective-permute-start.10) | collective-permute-done | bytes 753696 | tf_op jit(solution)/shard_map/ppermute | solution.py:602
  108.2 6.3 %combine_2_0.1.refs_6_.refs_7_.refs_8_.refs_9_.refs_10_ = bf16[3,2,2,256,1024]{4,3,2,1,0:T(8,128)(2,1)} custom-call(s32[4]{0:T(128)S(1)} %pad_add_fusion.meta, s32[4,16,16]{2,1,0:T(8,128)} %mask.21, bf16[2,2,2,2,256,1024]{5,4,3,2,1,0:T(8,128)(2,1)} %bitcast.64, ...), custom_call_target="tpu_custom_call", output_to_operand_aliasing={{}: (6, {})} | custom-call | flops 1024 | bytes 1024 | tf_op jit(solution)/shard_map/combine_2_0/pallas_call | solution.py:548
  114.5 10.7 %collective-permute-start.12 = (bf16[3,2,2,256,1024]{4,3,2,1,0:T(8,128)(2,1)}, bf16[3,2,2,256,1024]{4,3,2,1,0:T(8,128)(2,1)}, u32[]{:S(2)}, u32[]{:S(2)}) collective-permute-start(bf16[3,2,2,256,1024]{4,3,2,1,0:T(8,128)(2,1)} %combine_2_0.1.refs_6_.refs_7_.refs_8_.refs_9_.refs_10_), channel_id=1, source_target_pairs={{0,1},{1,0},{2,3},{3,2},{4,5},{5,4},{6,7},{7,6},{8,9},{9,8},{10,11... | collective-permute-start | bytes 18874376 | tf_op jit(solution)/shard_map/ppermute | solution.py:613
  125.2 5.2 %collective-permute-start.14 = (bf16[160,32,128]{2,1,0:T(8,128)(2,1)}, bf16[160,32,128]{2,1,0:T(8,128)(2,1)}, u32[]{:S(2)}, u32[]{:S(2)}) collective-permute-start(bf16[160,32,128]{2,1,0:T(8,128)(2,1)} %collective-permute-done.9.refs_0_), channel_id=1, source_target_pairs={{4,0},{5,1},{6,2},{7,3},{20,16},{21,17},{22,18},{23,19}} | collective-permute-start | bytes 3932168 | tf_op jit(solution)/shard_map/ppermute | solution.py:610
  130.4 2.0 collective-permute-start.15
  132.4 8.0 %ints_2.1 = (bf16[4,256,1024]{2,1,0:T(8,128)(2,1)}, bf16[4,1024,256]{2,1,0:T(8,128)(2,1)}) custom-call(s32[4]{0:T(128)S(1)} %pad_add_fusion.meta, s32[4,4,16,16]{3,2,1,0:T(8,128)S(1)} %copy-done.3, bf16[160,32,128]{2,1,0:T(8,128)(2,1)} %collective-permute-done.9.refs_0_, bf16[160,32,128]{2,1,0:T(8,128)(2,1)} %collective-permute-done.8.refs_1_), custom_call_target="tpu_custom_call" | custom-call | flops 1024 | bytes 1024 | tf_op jit(solution)/shard_map/ints_2/pallas_call | solution.py:521
  140.3 20.8 %early.1 = f32[2048,768]{1,0:T(8,128)} custom-call(s32[4]{0:T(128)S(1)} %pad_add_fusion.meta, bf16[4,256,1024]{2,1,0:T(8,128)(2,1)} %get-tuple-element.130.refs_0_, bf16[4,256,1024]{2,1,0:T(8,128)(2,1)} %get-tuple-element.131.refs_1_, bf16[4,256,1024]{2,1,0:T(8,128)(2,1)} %get-tuple-element.134.refs_2_, ...), custom_call_target="tpu_custom_call" | custom-call | flops 1024 | bytes 1024 | tf_op jit(solution)/shard_map/early/pallas_call | solution.py:625
  162.4 11.8 %collective-permute-done.14.refs_0_ = bf16[160,32,128]{2,1,0:T(8,128)(2,1)} collective-permute-done((bf16[160,32,128]{2,1,0:T(8,128)(2,1)}, bf16[160,32,128]{2,1,0:T(8,128)(2,1)}, u32[]{:S(2)}, u32[]{:S(2)}) %collective-permute-start.14) | collective-permute-done | bytes 1310752 | tf_op jit(solution)/shard_map/ppermute | solution.py:610
  174.2 8.0 %ints_3.1 = (bf16[4,256,1024]{2,1,0:T(8,128)(2,1)}, bf16[4,1024,256]{2,1,0:T(8,128)(2,1)}) custom-call(s32[4]{0:T(128)S(1)} %pad_add_fusion.meta, s32[4,4,16,16]{3,2,1,0:T(8,128)S(1)} %copy-done.3, bf16[160,32,128]{2,1,0:T(8,128)(2,1)} %collective-permute-done.14.refs_0_, bf16[160,32,128]{2,1,0:T(8,128)(2,1)} %collective-permute-done.1.refs_0_.refs_1_, ...), custom_call_target="tpu_custom_call" | custom-call | flops 1024 | bytes 1024 | tf_op jit(solution)/shard_map/ints_3/pallas_call | solution.py:521
  182.2 13.0 %late.1 = (bf16[1024,1024]{1,0:T(8,128)(2,1)}, f32[2048,256]{1,0:T(8,128)}) custom-call(s32[4]{0:T(128)S(1)} %pad_add_fusion.meta, bf16[4,256,1024]{2,1,0:T(8,128)(2,1)} %get-tuple-element.130.refs_0_, bf16[4,256,1024]{2,1,0:T(8,128)(2,1)} %get-tuple-element.131.refs_1_, bf16[4,256,1024]{2,1,0:T(8,128)(2,1)} %get-tuple-element.134.refs_2_, ...), custom_call_target="tpu_custom_call" | custom-call | flops 1024 | bytes 1024 | tf_op jit(solution)/shard_map/late/pallas_call | solution.py:647
  195.2 4.3 %combine_3_0.1 = (bf16[1,2,2,256,512]{4,3,2,1,0:T(8,128)(2,1)S(1)}, s32[1]{0:T(128)}) custom-call(s32[4]{0:T(128)S(1)} %pad_add_fusion.meta, s32[4,16,16]{2,1,0:T(8,128)} %mask.21, bf16[2,2,2,2,256,1024]{5,4,3,2,1,0:T(8,128)(2,1)} %bitcast.65, bf16[2,2,2,2,256,1024]{5,4,3,2,1,0:T(8,128)(2,1)} %collective-permute-done.3.oth_ref, ...), custom_call_target="tpu_custom_call" | custom-call | flops 1024 | bytes 1024 | tf_op jit(solution)/shard_map/combine_3_0/pallas_call | solution.py:548
  199.5 5.2 %combine_3_2.1 = (bf16[1,2,2,256,512]{4,3,2,1,0:T(8,128)(2,1)}, s32[1]{0:T(128)}) custom-call(s32[4]{0:T(128)S(1)} %pad_add_fusion.meta, s32[4,16,16]{2,1,0:T(8,128)} %mask.21, bf16[2,2,2,2,256,1024]{5,4,3,2,1,0:T(8,128)(2,1)} %bitcast.66, bf16[2,2,2,2,256,1024]{5,4,3,2,1,0:T(8,128)(2,1)} %collective-permute-done.3.oth_ref, bf16[46,64,128]{2,1,0:T(8,128)(2,1)} %copy-done.5, ...), custom_call_target="tpu_custom_call" | custom-call | flops 1024 | bytes 1024 | tf_op jit(solution)/shard_map/combine_3_2/pallas_call | solution.py:548
  205.2 3.7 %collective-permute-done.17 = bf16[1,2,2,256,512]{4,3,2,1,0:T(8,128)(2,1)S(1)} collective-permute-done((bf16[1,2,2,256,512]{4,3,2,1,0:T(8,128)(2,1)}, bf16[1,2,2,256,512]{4,3,2,1,0:T(8,128)(2,1)S(1)}, u32[]{:S(2)}, u32[]{:S(2)}) %collective-permute-start.17) | collective-permute-done | bytes 1048608 | tf_op jit(solution)/shard_map/ppermute | solution.py:676
  209.0 35.7 %conditional.1 = (f32[8,256,1,1024]{3,2,1,0:T(1,128)}) conditional(s32[]{:T(128)} %bitcast.27, (s32[]{:T(128)}, f32[1024]{0:T(1024)S(1)}, s32[4]{0:T(128)S(1)}, f32[8]{0:T(128)S(1)}, f32[1]{0:T(128)}, /*index=5*/f32[2048,768]{1,0:T(8,128)}, f32[2048,256]{1,0:T(8,128)}, bf16[1024,1024]{1,0:T(8,128)(2,1)}, bf16[1,2,2,256,512]{4,3,2,1,0:T(8,128)(2,1)S(1)}, ...), branch_computations={%region_6.7_spmd, %region_7.9_spmd} | conditional | flops 34424766464 | bytes 426019776 | solution.py:709
  227.5 17.2 %tail.1 = f32[8,256,1,1024]{3,2,1,0:T(1,128)} custom-call(s32[4]{0:T(128)S(1)} %get-tuple-element.59.meta, f32[8]{0:T(128)S(1)} %get-tuple-element.60.eps_slab, f32[1]{0:T(128)} %get-tuple-element.61.eps_pair, f32[256,1]{1,0:T(8,128)} %copy.53.eps_rows, f32[1,1024]{1,0:T(1,128)S(1)} %bitcast.70, f32[2048,768]{1,0:T(8,128)} %get-tuple-element.64.part_ref, ...), custom_call_target="tpu_custom_call" | custom-call | flops 1024 | bytes 1024 | tf_op jit(solution)/shard_map/cond/branch_0_fun/tail/pallas_call | solution.py:682
  (48 shorter events, 15.2 us)
Async XLA Ops:
  6.5 4.7 %collective-permute-start = (bf16[2,2,256,1024]{3,2,1,0:T(8,128)(2,1)}, bf16[2,2,256,1024]{3,2,1,0:T(8,128)(2,1)S(1)}, u32[]{:S(2)}, u32[]{:S(2)}) collective-permute-start(bf16[2,2,256,1024]{3,2,1,0:T(8,128)(2,1)} %own_ref.3), channel_id=1, source_target_pairs={{0,1},{1,0},{2,3},{3,2},{4,5},{5,4},{6,7},{7,6},{8,9},{9,8},{10,11... | collective-permute-start | bytes 6291464 | tf_op jit(solution)/shard_map/ppermute | solution.py:461
  11.2 1.3 copy-start.2
  11.2 13.5 %collective-permute-start.3 = (bf16[2,2,2,2,256,1024]{5,4,3,2,1,0:T(8,128)(2,1)}, bf16[2,2,2,2,256,1024]{5,4,3,2,1,0:T(8,128)(2,1)}, u32[]{:S(2)}, u32[]{:S(2)}) collective-permute-start(bf16[2,2,2,2,256,1024]{5,4,3,2,1,0:T(8,128)(2,1)} %bitcast.60), channel_id=1, source_target_pairs={{0,1},{1,0},{2,3},{3,2},{4,5},{5,4},{6,7},{7,6},{8,9},{9,8},{10,11... | collective-permute-start | bytes 25165832 | tf_op jit(solution)/shard_map/ppermute | solution.py:464
  17.6 39.3 %copy-start.3 = (s32[4,4,16,16]{3,2,1,0:T(8,128)S(1)}, s32[4,4,16,16]{3,2,1,0:T(8,128)}, u32[]{:S(2)}) copy-start(s32[4,4,16,16]{3,2,1,0:T(8,128)} %mask.19) | copy-start | bytes 49156
  17.6 45.0 %copy-start = (bf16[2,2,256,1024]{3,2,1,0:T(8,128)(2,1)S(1)}, bf16[2,2,256,1024]{3,2,1,0:T(8,128)(2,1)}, u32[]{:S(2)}) copy-start(bf16[2,2,256,1024]{3,2,1,0:T(8,128)(2,1)} %own_ref.3) | copy-start | bytes 6291460
  17.6 32.3 %collective-permute-start.2 = (bf16[160,32,128]{2,1,0:T(8,128)(2,1)}, bf16[160,32,128]{2,1,0:T(8,128)(2,1)S(1)}, u32[]{:S(2)}, u32[]{:S(2)}) collective-permute-start(bf16[160,32,128]{2,1,0:T(8,128)(2,1)} %pack_int.1), channel_id=1, source_target_pairs={{0,4},{4,8},{8,12},{1,5},{5,9},{9,13},{2,6},{6,10},{10,14},{3,7},{... | collective-permute-start | bytes 3932168 | tf_op jit(solution)/shard_map/ppermute | solution.py:476
  21.0 33.3 %collective-permute-start.1 = (bf16[160,32,128]{2,1,0:T(8,128)(2,1)}, bf16[160,32,128]{2,1,0:T(8,128)(2,1)}, u32[]{:S(2)}, u32[]{:S(2)}) collective-permute-start(bf16[160,32,128]{2,1,0:T(8,128)(2,1)} %pack_int.1), channel_id=1, source_target_pairs={{4,0},{8,4},{12,8},{5,1},{9,5},{13,9},{6,2},{10,6},{14,10},{7,3},{... | collective-permute-start | bytes 3932168 | tf_op jit(solution)/shard_map/ppermute | solution.py:477
  31.2 52.0 %collective-permute-start.4 = (bf16[46,64,128]{2,1,0:T(8,128)(2,1)}, bf16[46,64,128]{2,1,0:T(8,128)(2,1)}, u32[]{:S(2)}, u32[]{:S(2)}) collective-permute-start(bf16[46,64,128]{2,1,0:T(8,128)(2,1)} %get-tuple-element.118), channel_id=1, source_target_pairs={{0,4},{4,0},{8,12},{12,8},{1,5},{5,1},{9,13},{13,9},{2,6},{6,2},{1... | collective-permute-start | bytes 2261000 | tf_op jit(solution)/shard_map/ppermute | solution.py:497
  31.2 55.0 %collective-permute-start.6 = (bf16[46,64,128]{2,1,0:T(8,128)(2,1)}, bf16[46,64,128]{2,1,0:T(8,128)(2,1)}, u32[]{:S(2)}, u32[]{:S(2)}) collective-permute-start(bf16[46,64,128]{2,1,0:T(8,128)(2,1)} %get-tuple-element.122), channel_id=1, source_target_pairs={{0,8},{4,12},{8,0},{12,4},{1,9},{5,13},{9,1},{13,5},{2,10},{6,14},... | collective-permute-start | bytes 2261000 | tf_op jit(solution)/shard_map/ppermute | solution.py:497
  50.0 25.9 %copy-start.4 = (bf16[160,32,128]{2,1,0:T(8,128)(2,1)}, bf16[160,32,128]{2,1,0:T(8,128)(2,1)S(1)}, u32[]{:S(2)}) copy-start(bf16[160,32,128]{2,1,0:T(8,128)(2,1)S(1)} %collective-permute-done.2.refs_1_.refs_2_) | copy-start | bytes 3932164
  50.0 64.5 %collective-permute-start.8 = (bf16[160,32,128]{2,1,0:T(8,128)(2,1)S(1)}, bf16[160,32,128]{2,1,0:T(8,128)(2,1)}, u32[]{:S(2)}, u32[]{:S(2)}) collective-permute-start(bf16[160,32,128]{2,1,0:T(8,128)(2,1)S(1)} %collective-permute-done.2.refs_1_.refs_2_), channel_id=1, source_target_pairs={{4,8},{8,12},{5,9},{9,13},{6,10},{10,14},{7,11},{11,15},{20,24},{2... | collective-permute-start | bytes 3932168 | tf_op jit(solution)/shard_map/ppermute | solution.py:499
  54.3 60.2 %collective-permute-start.9 = (bf16[160,32,128]{2,1,0:T(8,128)(2,1)}, bf16[160,32,128]{2,1,0:T(8,128)(2,1)}, u32[]{:S(2)}, u32[]{:S(2)}) collective-permute-start(bf16[160,32,128]{2,1,0:T(8,128)(2,1)} %collective-permute-done.1.refs_0_.refs_1_), channel_id=1, source_target_pairs={{4,0},{8,4},{5,1},{9,5},{6,2},{10,6},{7,3},{11,7},{20,16},{24,20},... | collective-permute-start | bytes 3932168 | tf_op jit(solution)/shard_map/ppermute | solution.py:500
  83.2 15.6 %collective-permute-start.5 = (bf16[46,64,128]{2,1,0:T(8,128)(2,1)}, bf16[46,64,128]{2,1,0:T(8,128)(2,1)}, u32[]{:S(2)}, u32[]{:S(2)}) collective-permute-start(bf16[46,64,128]{2,1,0:T(8,128)(2,1)} %collective-permute-done.4.near_ref), channel_id=1, source_target_pairs={{0,2},{2,0},{1,3},{3,1},{4,6},{6,4},{5,7},{7,5},{8,10},{10,8},{9,1... | collective-permute-start | bytes 2261000 | tf_op jit(solution)/shard_map/ppermute | solution.py:602
  86.2 22.0 %collective-permute-start.10 = (bf16[46,64,128]{2,1,0:T(8,128)(2,1)}, bf16[46,64,128]{2,1,0:T(8,128)(2,1)}, u32[]{:S(2)}, u32[]{:S(2)}) collective-permute-start(bf16[46,64,128]{2,1,0:T(8,128)(2,1)} %collective-permute-done.6.near_ref), channel_id=1, source_target_pairs={{0,2},{2,0},{1,3},{3,1},{4,6},{6,4},{5,7},{7,5},{8,10},{10,8},{9,1... | collective-permute-start | bytes 2261000 | tf_op jit(solution)/shard_map/ppermute | solution.py:602
  95.3 2.8 %collective-permute-start.7 = (s32[1]{0:T(128)}, s32[1]{0:T(128)}, u32[]{:S(2)}, u32[]{:S(2)}) collective-permute-start(s32[1]{0:T(128)} %bitcast.26), channel_id=1, source_target_pairs={{0,16},{16,0},{1,17},{17,1},{2,18},{18,2},{3,19},{19,3},{4,20},{20... | collective-permute-start | bytes 20 | tf_op jit(solution)/shard_map/ppermute | solution.py:604
  114.5 25.8 %collective-permute-start.12 = (bf16[3,2,2,256,1024]{4,3,2,1,0:T(8,128)(2,1)}, bf16[3,2,2,256,1024]{4,3,2,1,0:T(8,128)(2,1)}, u32[]{:S(2)}, u32[]{:S(2)}) collective-permute-start(bf16[3,2,2,256,1024]{4,3,2,1,0:T(8,128)(2,1)} %combine_2_0.1.refs_6_.refs_7_.refs_8_.refs_9_.refs_10_), channel_id=1, source_target_pairs={{0,1},{1,0},{2,3},{3,2},{4,5},{5,4},{6,7},{7,6},{8,9},{9,8},{10,11... | collective-permute-start | bytes 18874376 | tf_op jit(solution)/shard_map/ppermute | solution.py:613
  125.2 35.9 %collective-permute-start.11 = (bf16[46,64,128]{2,1,0:T(8,128)(2,1)}, bf16[46,64,128]{2,1,0:T(8,128)(2,1)S(1)}, u32[]{:S(2)}, u32[]{:S(2)}) collective-permute-start(bf16[46,64,128]{2,1,0:T(8,128)(2,1)} %get-tuple-element.129), channel_id=1, source_target_pairs={{0,12},{4,8},{8,4},{12,0},{1,13},{5,9},{9,5},{13,1},{2,14},{6,10},... | collective-permute-start | bytes 2261000 | tf_op jit(solution)/shard_map/ppermute | solution.py:497
  125.2 49.0 %collective-permute-start.14 = (bf16[160,32,128]{2,1,0:T(8,128)(2,1)}, bf16[160,32,128]{2,1,0:T(8,128)(2,1)}, u32[]{:S(2)}, u32[]{:S(2)}) collective-permute-start(bf16[160,32,128]{2,1,0:T(8,128)(2,1)} %collective-permute-done.9.refs_0_), channel_id=1, source_target_pairs={{4,0},{5,1},{6,2},{7,3},{20,16},{21,17},{22,18},{23,19}} | collective-permute-start | bytes 3932168 | tf_op jit(solution)/shard_map/ppermute | solution.py:610
  130.4 43.8 %collective-permute-start.15 = (bf16[160,32,128]{2,1,0:T(8,128)(2,1)}, bf16[160,32,128]{2,1,0:T(8,128)(2,1)}, u32[]{:S(2)}, u32[]{:S(2)}) collective-permute-start(bf16[160,32,128]{2,1,0:T(8,128)(2,1)} %collective-permute-done.8.refs_1_), channel_id=1, source_target_pairs={{8,12},{9,13},{10,14},{11,15},{24,28},{25,29},{26,30},{27,31}} | collective-permute-start | bytes 3932168 | tf_op jit(solution)/shard_map/ppermute | solution.py:611
  161.1 34.0 %copy-start.5 = (bf16[46,64,128]{2,1,0:T(8,128)(2,1)}, bf16[46,64,128]{2,1,0:T(8,128)(2,1)S(1)}, u32[]{:S(2)}) copy-start(bf16[46,64,128]{2,1,0:T(8,128)(2,1)S(1)} %collective-permute-done.11.near_ref) | copy-start | bytes 2260996
  161.1 34.0 %collective-permute-start.13 = (bf16[46,64,128]{2,1,0:T(8,128)(2,1)S(1)}, bf16[46,64,128]{2,1,0:T(8,128)(2,1)}, u32[]{:S(2)}, u32[]{:S(2)}) collective-permute-start(bf16[46,64,128]{2,1,0:T(8,128)(2,1)S(1)} %collective-permute-done.11.near_ref), channel_id=1, source_target_pairs={{0,2},{2,0},{1,3},{3,1},{4,6},{6,4},{5,7},{7,5},{8,10},{10,8},{9,1... | collective-permute-start | bytes 2261000 | tf_op jit(solution)/shard_map/ppermute | solution.py:644
  199.5 9.5 %copy-start.8 = (f32[1024]{0:T(1024)S(1)}, f32[1024]{0:T(1024)}, u32[]{:S(2)}) copy-start(f32[1024]{0:T(1024)} %param.15) | copy-start | bytes 12292
  199.5 9.5 %copy-start.9 = (f32[8]{0:T(128)S(1)}, f32[8]{0:T(128)}, u32[]{:S(2)}) copy-start(f32[8]{0:T(128)} %param.13) | copy-start | bytes 100
  204.7 4.3 %collective-permute-start.17 = (bf16[1,2,2,256,512]{4,3,2,1,0:T(8,128)(2,1)}, bf16[1,2,2,256,512]{4,3,2,1,0:T(8,128)(2,1)S(1)}, u32[]{:S(2)}, u32[]{:S(2)}) collective-permute-start(bf16[1,2,2,256,512]{4,3,2,1,0:T(8,128)(2,1)} %get-tuple-element.149), channel_id=1, source_target_pairs={{0,1},{1,0},{2,3},{3,2},{4,5},{5,4},{6,7},{7,6},{8,9},{9,8},{10,11... | collective-permute-start | bytes 3145736 | tf_op jit(solution)/shard_map/ppermute | solution.py:676
  205.2 3.8 %collective-permute-start.16 = (bf16[1,2,2,256,512]{4,3,2,1,0:T(8,128)(2,1)S(1)}, bf16[1,2,2,256,512]{4,3,2,1,0:T(8,128)(2,1)S(1)}, u32[]{:S(2)}, u32[]{:S(2)}) collective-permute-start(bf16[1,2,2,256,512]{4,3,2,1,0:T(8,128)(2,1)S(1)} %get-tuple-element.147), channel_id=1, source_target_pairs={{0,1},{1,0},{2,3},{3,2},{4,5},{5,4},{6,7},{7,6},{8,9},{9,8},{10,11... | collective-permute-start | bytes 3145736 | tf_op jit(solution)/shard_map/ppermute | solution.py:676
  224.7 1.0 copy-start.6
  225.7 1.0 copy-start.7

commit v5 on v4

--- a/solution.py
+++ b/solution.py
@@ -442,6 +442,19 @@
     return pltpu.CompilerParams(vmem_limit_bytes=VMEM_LIMIT)
 
 
+def as_is(array):
+    def kernel(from_ref, to_ref):
+        pltpu.sync_copy(from_ref, to_ref)
+
+    return pl.pallas_call(
+        kernel,
+        out_shape=jax.ShapeDtypeStruct(array.shape, array.dtype),
+        in_specs=[anywhere()],
+        out_specs=anywhere(),
+        name="as_is",
+    )(array)
+
+
 def k_place(kk, r):
     return lax.rem(kk + 2 * r, 4)
 
@@ -496,6 +509,9 @@
     def across(d, packed):
         return lax.ppermute(packed, "vir", [(s, s ^ d) for s in range(4)])
 
+    packed3, over = lax.optimization_barrier((packed_amp[2], over))
+    over = over + lax.ppermute(over, "frag", swap)
+    up1, down1, over = lax.optimization_barrier((up1, down1, over))
     up2 = lax.ppermute(up1, "vir", [(1, 2), (2, 3)])
     down2 = lax.ppermute(down1, "vir", [(1, 0), (2, 1)])
 
@@ -598,15 +614,13 @@
     first = combine_first(0, None, None, None)
     near1, near2 = across(1, packed_amp[0]), across(2, packed_amp[1])
     near1, ints[0], first = ready((near1, ints[0], first))
-    near2, over = ready((near2, over))
     far1, far2 = lax.ppermute(near1, "occ", swap), lax.ppermute(near2, "occ", swap)
     ints.append(unpack(1, down1, up1))
-    over = over + lax.ppermute(over, "frag", swap)
-    ints[1], far1, over = ready((ints[1], far1, over))
+    ints[1], far1 = ready((ints[1], far1))
     first = combine_first(1, near1, far1, first)
     first = combine_first(2, near2, far2, first)
-    up2, down2, first, packed3 = ready((up2, down2, first, packed_amp[2]))
     near3 = across(3, packed3)
+    up2, down2, near3, first = ready((up2, down2, near3, first))
     end_down = lax.ppermute(down2, "vir", [(1, 0)])
     end_up = lax.ppermute(up2, "vir", [(2, 3)])
     ints.append(unpack(2, down2, up2))
@@ -640,8 +654,13 @@
         name="early",
     )(meta, *[d for d, _ in ints], *[t for _, t in ints], *[first] * 3, *[first_oth] * 3)
 
-    near3, part = ready((near3, part))
     far3 = lax.ppermute(near3, "occ", swap)
+    far3, part = ready((far3, part))
+    half0, count = combine_half(0, near3, far3)
+    half1, _ = combine_half(2, near3, far3, count)
+    halves = (half0, half1)
+    halves_oth = tuple(lax.ppermute(h, "rep", swap) for h in halves)
+    end_down, end_up, half1 = ready((end_down, end_up, half1))
     ints.append(unpack(3, end_down, down1, up1, end_up))
     rows, cols = [d for d, _ in ints], [t for _, t in ints]
     last_row, late = pl.pallas_call(
@@ -669,11 +688,6 @@
         cost_estimate=NO_COST,
         name="late",
     )(meta, *rows, *cols, *[first] * 3, *[first_oth] * 3)
-    far3, late = ready((far3, late))
-    half0, count = combine_half(0, near3, far3)
-    half1, _ = combine_half(2, near3, far3, count)
-    halves = (half0, half1)
-    halves_oth = tuple(lax.ppermute(h, "rep", swap) for h in halves)
     row_energy = lax.dynamic_slice_in_dim(eps_vir, v * 256, 256, 0).reshape(256, 1)
     col_energy = eps_vir.reshape(1, 1024)
 
@@ -701,17 +715,14 @@
             name="tail",
         )(meta, eps_slab, eps_pair, row_energy, col_energy, part, late, last_row, *own, *oth)
 
-    def dense(ops):
-        return dense_shards(
-            amplitudes, integrals, amp_mask, int_mask, eps_slab, eps_pair, eps_vir
+    def dense(state):
+        out = dense_shards(
+            as_is(amplitudes), as_is(integrals), amp_mask, int_mask, eps_slab, eps_pair, eps_vir
         )
-
-    return lax.cond(
-        over[0] > 0,
-        dense,
-        finish,
-        (part, late, last_row, halves, halves_oth),
-    )
+        return as_is(out), jnp.zeros((), jnp.int32)
+
+    out = finish((part, late, last_row, halves, halves_oth))
+    return lax.while_loop(lambda state: state[1] > 0, dense, (out, over[0]))[0]
 
 
 def shards(sizes, *args):

time: 253 us -> 240 us (0.949)
  waiting for transfers between devices: 50.6 us -> 67.1 us
  loops' own time: 15.7 us -> 0.01 us
  starting transfers between devices: 39.3 us -> 27 us
    ppermute x3, waiting for transfers between devices: 9.1 us -> 39.3 us  [across(): return lax.ppermute(packed, 'vir', [(s, s ^ d) for s in range(4)])]
    another operation x1, loops' own time: 15.7 us -> 0.01 us  [packed_shards(): return lax.while_loop(lambda state: state[1] > 0, dense, (out, over[0]))[0]]
    ppermute x1, waiting for transfers between devices: 11.8 us -> 0.01 us  [packed_shards(): end_down = lax.ppermute(down2, 'vir', [(1, 0)])]
    ppermute x1, starting transfers between devices: 10.7 us -> 1.53 us  [packed_shards(): first_oth = lax.ppermute(first, 'rep', swap)]
    ppermute x1, waiting for transfers between devices: 16.3 us -> 7.18 us  [packed_shards(): up1 = lax.ppermute(packed_int, 'vir', [(0, 1), (1, 2), (2, 3)])]
    ppermute x1, waiting for transfers between devices: 3.17 us -> 10 us  [packed_shards(): lax.ppermute(near2, 'occ', swap)]
    ppermute x2, waiting for transfers between devices: 3.76 us -> 0.01 us  [packed_shards(): halves_oth = tuple((lax.ppermute(h, 'rep', swap) for h in halves))]
    ppermute x1, waiting for transfers between devices: 0.01 us -> 2.89 us  [packed_shards(): down1 = lax.ppermute(packed_int, 'vir', [(1, 0), (2, 1), (3, 2)])]
  transfers between devices with their start and end apart: 18 -> 18, of which waited for: 9 -> 10; matrix products, arithmetic and copies ran while one was open for 2% -> 2% of each run, Pallas kernels for 38% -> 44%
where the time goes in v5:
time: 240 us; the launch traced here: 239 us
  Pallas kernels  122 us (51%)
  waiting for transfers between devices  67.1 us (28%)
  starting transfers between devices  27 us (11%)
  between operations  16.1 us (7%)
  other arithmetic  4.24 us (2%)
  local copies, waits for them, and re-layouts  2.67 us (1%)
    ppermute x3, waiting for transfers between devices, across(): return lax.ppermute(packed, 'vir', [(s, s ^ d) for s in range(4)])  39.3 us
    pallas_call x4, Pallas kernels, unpack(): pl.pallas_call(kernel, grid_spec=pltpu.PrefetchScalarGridSpec(num_scalar_...  31.2 us
    pallas_call x5, Pallas kernels, combine(): pl.pallas_call(kernel, grid_spec=pltpu.PrefetchScalarGridSpec(num_scalar_...  27.7 us
    pallas_call x1, Pallas kernels, packed_shards(): pl.pallas_call(early_kernel, grid_spec=pltpu.PrefetchScalarGridSpec(num_s...  20.9 us
    pallas_call x1, Pallas kernels, finish(): pl.pallas_call(tail_kernel, grid_spec=pltpu.PrefetchScalarGridSpec(num_sc...  17.2 us
    pallas_call x1, Pallas kernels, packed_shards(): pl.pallas_call(late_kernel, grid_spec=pltpu.PrefetchScalarGridSpec(num_sc...  13.2 us
    ppermute x1, waiting for transfers between devices, packed_shards(): lax.ppermute(near2, 'occ', swap)  10 us
    ppermute x1, waiting for transfers between devices, packed_shards(): up1 = lax.ppermute(packed_int, 'vir', [(0, 1), (1, 2), (2, 3)])  7.18 us
  transfers between devices with their start and end apart: 18, of which 10 were waited for; matrix products, arithmetic and copies ran while one was open for 2% of the time, Pallas kernels for 44%

profile of v5, /device:TPU:9, one launch (start us, length us, event | category | flops | bytes accessed | tf_op | source)
XLA Modules:
  0.0 239.1 jit_solution(15672893196520143586)
XLA Ops:
  7.2 4.0 %collective-permute-done.oth_ref = bf16[2,2,256,1024]{3,2,1,0:T(8,128)(2,1)S(1)} collective-permute-done((bf16[2,2,256,1024]{3,2,1,0:T(8,128)(2,1)}, bf16[2,2,256,1024]{3,2,1,0:T(8,128)(2,1)S(1)}, u32[]{:S(2)}, u32[]{:S(2)}) %collective-permute-start) | collective-permute-done | bytes 2097184 | tf_op jit(solution)/shard_map/ppermute | solution.py:474
  12.5 5.1 %pack_int.1 = bf16[160,32,128]{2,1,0:T(8,128)(2,1)} custom-call(s32[4]{0:T(128)} %pad_add_fusion.meta, s32[4,4,16,16]{3,2,1,0:T(8,128)} %mask.21, bf16[2,2,256,1024]{3,2,1,0:T(8,128)(2,1)} %own_ref.3, bf16[2,2,256,1024]{3,2,1,0:T(8,128)(2,1)} %copy-done.3), custom_call_target="tpu_custom_call" | custom-call | flops 1024 | bytes 1024 | tf_op jit(solution)/shard_map/pack_int/pallas_call | solution.py:479
  17.6 3.3 %collective-permute-start.1 = (bf16[160,32,128]{2,1,0:T(8,128)(2,1)}, bf16[160,32,128]{2,1,0:T(8,128)(2,1)S(1)}, u32[]{:S(2)}, u32[]{:S(2)}) collective-permute-start(bf16[160,32,128]{2,1,0:T(8,128)(2,1)} %pack_int.1), channel_id=1, source_target_pairs={{0,4},{4,8},{8,12},{1,5},{5,9},{9,13},{2,6},{6,10},{10,14},{3,7},{... | collective-permute-start | bytes 3932168 | tf_op jit(solution)/shard_map/ppermute | solution.py:489
  20.9 2.2 collective-permute-start.2
  23.1 1.6 collective-permute-done.3.oth_ref
  24.7 6.5 %pack_amp.1 = (bf16[46,64,128]{2,1,0:T(8,128)(2,1)}, bf16[46,64,128]{2,1,0:T(8,128)(2,1)}, bf16[46,64,128]{2,1,0:T(8,128)(2,1)}) custom-call(s32[4]{0:T(128)} %pad_add_fusion.meta, s32[4,16,16]{2,1,0:T(8,128)} %mask.20, bf16[2,2,2,2,256,1024]{5,4,3,2,1,0:T(8,128)(2,1)} %bitcast.61, bf16[2,2,2,2,256,1024]{5,4,3,2,1,0:T(8,128)(2,1)} %collective-permute-done.3.oth_ref), custom_call_target="tpu_custom_call" | custom-call | flops 1024 | bytes 1024 | tf_op jit(solution)/shard_map/pack_amp/pallas_call | solution.py:492
  31.3 2.5 %collective-permute-start.8 = (bf16[46,64,128]{2,1,0:T(8,128)(2,1)}, bf16[46,64,128]{2,1,0:T(8,128)(2,1)}, u32[]{:S(2)}, u32[]{:S(2)}) collective-permute-start(bf16[46,64,128]{2,1,0:T(8,128)(2,1)} %get-tuple-element.95), channel_id=1, source_target_pairs={{0,8},{4,12},{8,0},{12,4},{1,9},{5,13},{9,1},{13,5},{2,10},{6,14},... | collective-permute-start | bytes 2261000 | tf_op jit(solution)/shard_map/ppermute | solution.py:510
  39.3 2.0 collective-permute-start.4
  42.7 7.2 %collective-permute-done.1.refs_1_.refs_2_ = bf16[160,32,128]{2,1,0:T(8,128)(2,1)S(1)} collective-permute-done((bf16[160,32,128]{2,1,0:T(8,128)(2,1)}, bf16[160,32,128]{2,1,0:T(8,128)(2,1)S(1)}, u32[]{:S(2)}, u32[]{:S(2)}) %collective-permute-start.1) | collective-permute-done | bytes 1310752 | tf_op jit(solution)/shard_map/ppermute | solution.py:489
  49.9 2.9 %collective-permute-done.2.refs_0_.refs_1_ = bf16[160,32,128]{2,1,0:T(8,128)(2,1)} collective-permute-done((bf16[160,32,128]{2,1,0:T(8,128)(2,1)}, bf16[160,32,128]{2,1,0:T(8,128)(2,1)}, u32[]{:S(2)}, u32[]{:S(2)}) %collective-permute-start.2) | collective-permute-done | bytes 1310752 | tf_op jit(solution)/shard_map/ppermute | solution.py:490
  52.8 4.3 %collective-permute-start.5 = (bf16[160,32,128]{2,1,0:T(8,128)(2,1)S(1)}, bf16[160,32,128]{2,1,0:T(8,128)(2,1)}, u32[]{:S(2)}, u32[]{:S(2)}) collective-permute-start(bf16[160,32,128]{2,1,0:T(8,128)(2,1)S(1)} %collective-permute-done.1.refs_1_.refs_2_), channel_id=1, source_target_pairs={{4,8},{8,12},{5,9},{9,13},{6,10},{10,14},{7,11},{11,15},{20,24},{2... | collective-permute-start | bytes 3932168 | tf_op jit(solution)/shard_map/ppermute | solution.py:515
  57.1 1.9 collective-permute-start.6
  59.1 7.4 %ints_0.1 = (bf16[4,256,1024]{2,1,0:T(8,128)(2,1)}, bf16[4,1024,256]{2,1,0:T(8,128)(2,1)}) custom-call(s32[4]{0:T(128)} %pad_add_fusion.meta, s32[4,4,16,16]{3,2,1,0:T(8,128)S(1)} %copy-done.4, bf16[2,2,256,1024]{3,2,1,0:T(8,128)(2,1)S(1)} %copy-done, bf16[2,2,256,1024]{3,2,1,0:T(8,128)(2,1)} %copy-done.3), custom_call_target="tpu_custom_call" | custom-call | flops 1024 | bytes 1024 | tf_op jit(solution)/shard_map/ints_0/pallas_call | solution.py:537
  66.5 5.9 %combine_0_0.1.refs_0_ = bf16[3,2,2,256,1024]{4,3,2,1,0:T(8,128)(2,1)} custom-call(s32[4]{0:T(128)} %pad_add_fusion.meta, s32[4,16,16]{2,1,0:T(8,128)} %mask.20, bf16[2,2,2,2,256,1024]{5,4,3,2,1,0:T(8,128)(2,1)} %bitcast.62, bf16[2,2,2,2,256,1024]{5,4,3,2,1,0:T(8,128)(2,1)} %collective-permute-done.3.oth_ref), custom_call_target="tpu_custom_call" | custom-call | flops 1024 | bytes 1024 | tf_op jit(solution)/shard_map/combine_0_0/pallas_call | solution.py:564
  72.5 10.7 %collective-permute-done.10.near_ref = bf16[46,64,128]{2,1,0:T(8,128)(2,1)} collective-permute-done((bf16[46,64,128]{2,1,0:T(8,128)(2,1)}, bf16[46,64,128]{2,1,0:T(8,128)(2,1)}, u32[]{:S(2)}, u32[]{:S(2)}) %collective-permute-start.10) | collective-permute-done | bytes 753696 | tf_op jit(solution)/shard_map/ppermute | solution.py:510
  84.3 1.8 collective-permute-done.8.near_ref
  86.2 1.2 collective-permute-start.9
  87.4 7.9 %ints_1.1 = (bf16[4,256,1024]{2,1,0:T(8,128)(2,1)}, bf16[4,1024,256]{2,1,0:T(8,128)(2,1)}) custom-call(s32[4]{0:T(128)} %pad_add_fusion.meta, s32[4,4,16,16]{3,2,1,0:T(8,128)S(1)} %copy-done.4, bf16[160,32,128]{2,1,0:T(8,128)(2,1)} %collective-permute-done.2.refs_0_.refs_1_, bf16[160,32,128]{2,1,0:T(8,128)(2,1)} %copy-done.5), custom_call_target="tpu_custom_call" | custom-call | flops 1024 | bytes 1024 | tf_op jit(solution)/shard_map/ints_1/pallas_call | solution.py:537
  96.5 6.1 %combine_1_0.1.refs_0_ = bf16[3,2,2,256,1024]{4,3,2,1,0:T(8,128)(2,1)} custom-call(s32[4]{0:T(128)} %pad_add_fusion.meta, s32[4,16,16]{2,1,0:T(8,128)S(1)} %copy-done.7, bf16[2,2,2,2,256,1024]{5,4,3,2,1,0:T(8,128)(2,1)} %bitcast.63, bf16[2,2,2,2,256,1024]{5,4,3,2,1,0:T(8,128)(2,1)} %collective-permute-done.3.oth_ref, ...), custom_call_target="tpu_custom_call", output_to_operand_aliasing={{}: (6, {})} | custom-call | flops 1024 | bytes 1024 | tf_op jit(solution)/shard_map/combine_1_0/pallas_call | solution.py:564
  102.6 10.0 %collective-permute-done.9.far_ref = bf16[46,64,128]{2,1,0:T(8,128)(2,1)} collective-permute-done((bf16[46,64,128]{2,1,0:T(8,128)(2,1)}, bf16[46,64,128]{2,1,0:T(8,128)(2,1)}, u32[]{:S(2)}, u32[]{:S(2)}) %collective-permute-start.9) | collective-permute-done | bytes 753696 | tf_op jit(solution)/shard_map/ppermute | solution.py:617
  112.6 6.1 %combine_2_0.1.refs_6_.refs_7_.refs_8_.refs_9_.refs_10_ = bf16[3,2,2,256,1024]{4,3,2,1,0:T(8,128)(2,1)} custom-call(s32[4]{0:T(128)} %pad_add_fusion.meta, s32[4,16,16]{2,1,0:T(8,128)S(1)} %copy-done.7, bf16[2,2,2,2,256,1024]{5,4,3,2,1,0:T(8,128)(2,1)} %bitcast.64, ...), custom_call_target="tpu_custom_call", output_to_operand_aliasing={{}: (6, {})} | custom-call | flops 1024 | bytes 1024 | tf_op jit(solution)/shard_map/combine_2_0/pallas_call | solution.py:564
  118.7 26.8 %collective-permute-done.7.near_ref = bf16[46,64,128]{2,1,0:T(8,128)(2,1)} collective-permute-done((bf16[46,64,128]{2,1,0:T(8,128)(2,1)}, bf16[46,64,128]{2,1,0:T(8,128)(2,1)}, u32[]{:S(2)}, u32[]{:S(2)}) %collective-permute-start.7) | collective-permute-done | bytes 753696 | tf_op jit(solution)/shard_map/ppermute | solution.py:510
  145.6 1.5 collective-permute-start.13
  148.3 2.4 collective-permute-start.14
  150.7 1.7 collective-permute-start.15
  152.4 7.9 %ints_2.1 = (bf16[4,256,1024]{2,1,0:T(8,128)(2,1)}, bf16[4,1024,256]{2,1,0:T(8,128)(2,1)}) custom-call(s32[4]{0:T(128)} %pad_add_fusion.meta, s32[4,4,16,16]{3,2,1,0:T(8,128)S(1)} %copy-done.4, bf16[160,32,128]{2,1,0:T(8,128)(2,1)} %collective-permute-done.6.refs_0_, bf16[160,32,128]{2,1,0:T(8,128)(2,1)} %collective-permute-done.5.refs_1_), custom_call_target="tpu_custom_call" | custom-call | flops 1024 | bytes 1024 | tf_op jit(solution)/shard_map/ints_2/pallas_call | solution.py:537
  160.3 20.9 %early.1.part_ref = f32[2048,768]{1,0:T(8,128)} custom-call(s32[4]{0:T(128)} %pad_add_fusion.meta, bf16[4,256,1024]{2,1,0:T(8,128)(2,1)} %get-tuple-element.105.refs_0_, bf16[4,256,1024]{2,1,0:T(8,128)(2,1)} %get-tuple-element.106.refs_1_, bf16[4,256,1024]{2,1,0:T(8,128)(2,1)} %get-tuple-element.109.refs_2_, ...), custom_call_target="tpu_custom_call" | custom-call | flops 1024 | bytes 1024 | tf_op jit(solution)/shard_map/early/pallas_call | solution.py:639
  182.1 4.4 %combine_3_0.1 = (bf16[1,2,2,256,512]{4,3,2,1,0:T(8,128)(2,1)}, s32[1]{0:T(128)}) custom-call(s32[4]{0:T(128)} %pad_add_fusion.meta, s32[4,16,16]{2,1,0:T(8,128)S(1)} %copy-done.7, bf16[2,2,2,2,256,1024]{5,4,3,2,1,0:T(8,128)(2,1)} %bitcast.65, bf16[2,2,2,2,256,1024]{5,4,3,2,1,0:T(8,128)(2,1)} %collective-permute-done.3.oth_ref, ...), custom_call_target="tpu_custom_call" | custom-call | flops 1024 | bytes 1024 | tf_op jit(solution)/shard_map/combine_3_0/pallas_call | solution.py:564
  186.5 5.1 %combine_3_2.1 = (bf16[1,2,2,256,512]{4,3,2,1,0:T(8,128)(2,1)}, s32[1]{0:T(128)}) custom-call(s32[4]{0:T(128)} %pad_add_fusion.meta, s32[4,16,16]{2,1,0:T(8,128)S(1)} %copy-done.7, bf16[2,2,2,2,256,1024]{5,4,3,2,1,0:T(8,128)(2,1)} %bitcast.66, bf16[2,2,2,2,256,1024]{5,4,3,2,1,0:T(8,128)(2,1)} %collective-permute-done.3.oth_ref, ...), custom_call_target="tpu_custom_call" | custom-call | flops 1024 | bytes 1024 | tf_op jit(solution)/shard_map/combine_3_2/pallas_call | solution.py:564
  193.7 8.0 %ints_3.1 = (bf16[4,256,1024]{2,1,0:T(8,128)(2,1)}, bf16[4,1024,256]{2,1,0:T(8,128)(2,1)}) custom-call(s32[4]{0:T(128)} %pad_add_fusion.meta, s32[4,4,16,16]{3,2,1,0:T(8,128)S(1)} %copy-done.4, bf16[160,32,128]{2,1,0:T(8,128)(2,1)} %collective-permute-done.14.refs_0_, bf16[160,32,128]{2,1,0:T(8,128)(2,1)} %collective-permute-done.2.refs_0_.refs_1_, ...), custom_call_target="tpu_custom_call" | custom-call | flops 1024 | bytes 1024 | tf_op jit(solution)/shard_map/ints_3/pallas_call | solution.py:537
  201.7 13.2 %late.1 = (bf16[1024,1024]{1,0:T(8,128)(2,1)}, f32[2048,256]{1,0:T(8,128)}) custom-call(s32[4]{0:T(128)} %pad_add_fusion.meta, bf16[4,256,1024]{2,1,0:T(8,128)(2,1)} %get-tuple-element.105.refs_0_, bf16[4,256,1024]{2,1,0:T(8,128)(2,1)} %get-tuple-element.106.refs_1_, bf16[4,256,1024]{2,1,0:T(8,128)(2,1)} %get-tuple-element.109.refs_2_, ...), custom_call_target="tpu_custom_call" | custom-call | flops 1024 | bytes 1024 | tf_op jit(solution)/shard_map/late/pallas_call | solution.py:666
  215.0 17.2 %tail.1 = f32[8,256,1,1024]{3,2,1,0:T(1,128)} custom-call(s32[4]{0:T(128)} %pad_add_fusion.meta, f32[8]{0:T(128)S(1)} %copy-done.12, f32[1]{0:T(128)S(6)} %copy.90.eps_pair, f32[256,1]{1,0:T(8,128)} %copy.60.eps_rows, f32[1,1024]{1,0:T(1,128)S(1)} %bitcast.69, f32[2048,768]{1,0:T(8,128)} %early.1.part_ref, f32[2048,256]{1,0:T(8,128)} %get-tuple-element.122.late_ref, ...), custom_call_target="tpu_custom_call" | custom-call | flops 1024 | bytes 1024 | tf_op jit(solution)/shard_map/tail/pallas_call | solution.py:696
  (50 shorter events, 13.0 us)
Async XLA Ops:
  6.5 4.7 %collective-permute-start = (bf16[2,2,256,1024]{3,2,1,0:T(8,128)(2,1)}, bf16[2,2,256,1024]{3,2,1,0:T(8,128)(2,1)S(1)}, u32[]{:S(2)}, u32[]{:S(2)}) collective-permute-start(bf16[2,2,256,1024]{3,2,1,0:T(8,128)(2,1)} %own_ref.3), channel_id=1, source_target_pairs={{0,1},{1,0},{2,3},{3,2},{4,5},{5,4},{6,7},{7,6},{8,9},{9,8},{10,11... | collective-permute-start | bytes 6291464 | tf_op jit(solution)/shard_map/ppermute | solution.py:474
  11.2 1.3 copy-start.3
  11.2 13.5 %collective-permute-start.3 = (bf16[2,2,2,2,256,1024]{5,4,3,2,1,0:T(8,128)(2,1)}, bf16[2,2,2,2,256,1024]{5,4,3,2,1,0:T(8,128)(2,1)}, u32[]{:S(2)}, u32[]{:S(2)}) collective-permute-start(bf16[2,2,2,2,256,1024]{5,4,3,2,1,0:T(8,128)(2,1)} %bitcast.60), channel_id=1, source_target_pairs={{0,1},{1,0},{2,3},{3,2},{4,5},{5,4},{6,7},{7,6},{8,9},{9,8},{10,11... | collective-permute-start | bytes 25165832 | tf_op jit(solution)/shard_map/ppermute | solution.py:477
  17.6 16.9 %copy-start.4 = (s32[4,4,16,16]{3,2,1,0:T(8,128)S(1)}, s32[4,4,16,16]{3,2,1,0:T(8,128)}, u32[]{:S(2)}) copy-start(s32[4,4,16,16]{3,2,1,0:T(8,128)} %mask.21) | copy-start | bytes 49156
  17.6 41.4 %copy-start = (bf16[2,2,256,1024]{3,2,1,0:T(8,128)(2,1)S(1)}, bf16[2,2,256,1024]{3,2,1,0:T(8,128)(2,1)}, u32[]{:S(2)}) copy-start(bf16[2,2,256,1024]{3,2,1,0:T(8,128)(2,1)} %own_ref.3) | copy-start | bytes 6291460
  17.6 32.3 %collective-permute-start.1 = (bf16[160,32,128]{2,1,0:T(8,128)(2,1)}, bf16[160,32,128]{2,1,0:T(8,128)(2,1)S(1)}, u32[]{:S(2)}, u32[]{:S(2)}) collective-permute-start(bf16[160,32,128]{2,1,0:T(8,128)(2,1)} %pack_int.1), channel_id=1, source_target_pairs={{0,4},{4,8},{8,12},{1,5},{5,9},{9,13},{2,6},{6,10},{10,14},{3,7},{... | collective-permute-start | bytes 3932168 | tf_op jit(solution)/shard_map/ppermute | solution.py:489
  20.9 31.9 %collective-permute-start.2 = (bf16[160,32,128]{2,1,0:T(8,128)(2,1)}, bf16[160,32,128]{2,1,0:T(8,128)(2,1)}, u32[]{:S(2)}, u32[]{:S(2)}) collective-permute-start(bf16[160,32,128]{2,1,0:T(8,128)(2,1)} %pack_int.1), channel_id=1, source_target_pairs={{4,0},{8,4},{12,8},{5,1},{9,5},{13,9},{6,2},{10,6},{14,10},{7,3},{... | collective-permute-start | bytes 3932168 | tf_op jit(solution)/shard_map/ppermute | solution.py:490
  31.3 51.9 %collective-permute-start.10 = (bf16[46,64,128]{2,1,0:T(8,128)(2,1)}, bf16[46,64,128]{2,1,0:T(8,128)(2,1)}, u32[]{:S(2)}, u32[]{:S(2)}) collective-permute-start(bf16[46,64,128]{2,1,0:T(8,128)(2,1)} %get-tuple-element.96), channel_id=1, source_target_pairs={{0,4},{4,0},{8,12},{12,8},{1,5},{5,1},{9,13},{13,9},{2,6},{6,2},{1... | collective-permute-start | bytes 2261000 | tf_op jit(solution)/shard_map/ppermute | solution.py:510
  31.3 54.9 %collective-permute-start.8 = (bf16[46,64,128]{2,1,0:T(8,128)(2,1)}, bf16[46,64,128]{2,1,0:T(8,128)(2,1)}, u32[]{:S(2)}, u32[]{:S(2)}) collective-permute-start(bf16[46,64,128]{2,1,0:T(8,128)(2,1)} %get-tuple-element.95), channel_id=1, source_target_pairs={{0,8},{4,12},{8,0},{12,4},{1,9},{5,13},{9,1},{13,5},{2,10},{6,14},... | collective-permute-start | bytes 2261000 | tf_op jit(solution)/shard_map/ppermute | solution.py:510
  39.3 2.9 %collective-permute-start.4 = (s32[1]{0:T(128)}, s32[1]{0:T(128)}, u32[]{:S(2)}, u32[]{:S(2)}) collective-permute-start(s32[1]{0:T(128)} %bitcast.27), channel_id=1, source_target_pairs={{0,16},{16,0},{1,17},{17,1},{2,18},{18,2},{3,19},{19,3},{4,20},{20... | collective-permute-start | bytes 20 | tf_op jit(solution)/shard_map/ppermute | solution.py:513
  49.9 22.5 %copy-start.5 = (bf16[160,32,128]{2,1,0:T(8,128)(2,1)}, bf16[160,32,128]{2,1,0:T(8,128)(2,1)S(1)}, u32[]{:S(2)}) copy-start(bf16[160,32,128]{2,1,0:T(8,128)(2,1)S(1)} %collective-permute-done.1.refs_1_.refs_2_) | copy-start | bytes 3932164
  52.8 92.7 %collective-permute-start.5 = (bf16[160,32,128]{2,1,0:T(8,128)(2,1)S(1)}, bf16[160,32,128]{2,1,0:T(8,128)(2,1)}, u32[]{:S(2)}, u32[]{:S(2)}) collective-permute-start(bf16[160,32,128]{2,1,0:T(8,128)(2,1)S(1)} %collective-permute-done.1.refs_1_.refs_2_), channel_id=1, source_target_pairs={{4,8},{8,12},{5,9},{9,13},{6,10},{10,14},{7,11},{11,15},{20,24},{2... | collective-permute-start | bytes 3932168 | tf_op jit(solution)/shard_map/ppermute | solution.py:515
  57.1 88.4 %collective-permute-start.6 = (bf16[160,32,128]{2,1,0:T(8,128)(2,1)}, bf16[160,32,128]{2,1,0:T(8,128)(2,1)}, u32[]{:S(2)}, u32[]{:S(2)}) collective-permute-start(bf16[160,32,128]{2,1,0:T(8,128)(2,1)} %collective-permute-done.2.refs_0_.refs_1_), channel_id=1, source_target_pairs={{4,0},{8,4},{5,1},{9,5},{6,2},{10,6},{7,3},{11,7},{20,16},{24,20},... | collective-permute-start | bytes 3932168 | tf_op jit(solution)/shard_map/ppermute | solution.py:516
  66.5 30.0 %copy-start.7 = (s32[4,16,16]{2,1,0:T(8,128)S(1)}, s32[4,16,16]{2,1,0:T(8,128)}, u32[]{:S(2)}) copy-start(s32[4,16,16]{2,1,0:T(8,128)} %mask.20) | copy-start | bytes 12292
  83.1 13.3 %collective-permute-start.11 = (bf16[46,64,128]{2,1,0:T(8,128)(2,1)}, bf16[46,64,128]{2,1,0:T(8,128)(2,1)}, u32[]{:S(2)}, u32[]{:S(2)}) collective-permute-start(bf16[46,64,128]{2,1,0:T(8,128)(2,1)} %collective-permute-done.10.near_ref), channel_id=1, source_target_pairs={{0,2},{2,0},{1,3},{3,1},{4,6},{6,4},{5,7},{7,5},{8,10},{10,8},{9,1... | collective-permute-start | bytes 2261000 | tf_op jit(solution)/shard_map/ppermute | solution.py:617
  86.2 26.4 %collective-permute-start.9 = (bf16[46,64,128]{2,1,0:T(8,128)(2,1)}, bf16[46,64,128]{2,1,0:T(8,128)(2,1)}, u32[]{:S(2)}, u32[]{:S(2)}) collective-permute-start(bf16[46,64,128]{2,1,0:T(8,128)(2,1)} %collective-permute-done.8.near_ref), channel_id=1, source_target_pairs={{0,2},{2,0},{1,3},{3,1},{4,6},{6,4},{5,7},{7,5},{8,10},{10,8},{9,1... | collective-permute-start | bytes 2261000 | tf_op jit(solution)/shard_map/ppermute | solution.py:617
  87.4 58.2 %collective-permute-start.7 = (bf16[46,64,128]{2,1,0:T(8,128)(2,1)}, bf16[46,64,128]{2,1,0:T(8,128)(2,1)}, u32[]{:S(2)}, u32[]{:S(2)}) collective-permute-start(bf16[46,64,128]{2,1,0:T(8,128)(2,1)} %get-tuple-element.94), channel_id=1, source_target_pairs={{0,12},{4,8},{8,4},{12,0},{1,13},{5,9},{9,5},{13,1},{2,14},{6,10},... | collective-permute-start | bytes 2261000 | tf_op jit(solution)/shard_map/ppermute | solution.py:510
  145.6 14.8 %collective-permute-start.13 = (bf16[3,2,2,256,1024]{4,3,2,1,0:T(8,128)(2,1)}, bf16[3,2,2,256,1024]{4,3,2,1,0:T(8,128)(2,1)}, u32[]{:S(2)}, u32[]{:S(2)}) collective-permute-start(bf16[3,2,2,256,1024]{4,3,2,1,0:T(8,128)(2,1)} %combine_2_0.1.refs_6_.refs_7_.refs_8_.refs_9_.refs_10_), channel_id=1, source_target_pairs={{0,1},{1,0},{2,3},{3,2},{4,5},{5,4},{6,7},{7,6},{8,9},{9,8},{10,11... | collective-permute-start | bytes 18874376 | tf_op jit(solution)/shard_map/ppermute | solution.py:627
  147.1 34.1 %collective-permute-start.12 = (bf16[46,64,128]{2,1,0:T(8,128)(2,1)}, bf16[46,64,128]{2,1,0:T(8,128)(2,1)S(1)}, u32[]{:S(2)}, u32[]{:S(2)}) collective-permute-start(bf16[46,64,128]{2,1,0:T(8,128)(2,1)} %collective-permute-done.7.near_ref), channel_id=1, source_target_pairs={{0,2},{2,0},{1,3},{3,1},{4,6},{6,4},{5,7},{7,5},{8,10},{10,8},{9,1... | collective-permute-start | bytes 2261000 | tf_op jit(solution)/shard_map/ppermute | solution.py:657
  148.3 45.4 %collective-permute-start.14 = (bf16[160,32,128]{2,1,0:T(8,128)(2,1)}, bf16[160,32,128]{2,1,0:T(8,128)(2,1)}, u32[]{:S(2)}, u32[]{:S(2)}) collective-permute-start(bf16[160,32,128]{2,1,0:T(8,128)(2,1)} %collective-permute-done.6.refs_0_), channel_id=1, source_target_pairs={{4,0},{5,1},{6,2},{7,3},{20,16},{21,17},{22,18},{23,19}} | collective-permute-start | bytes 3932168 | tf_op jit(solution)/shard_map/ppermute | solution.py:624
  150.7 43.0 %collective-permute-start.15 = (bf16[160,32,128]{2,1,0:T(8,128)(2,1)}, bf16[160,32,128]{2,1,0:T(8,128)(2,1)}, u32[]{:S(2)}, u32[]{:S(2)}) collective-permute-start(bf16[160,32,128]{2,1,0:T(8,128)(2,1)} %collective-permute-done.5.refs_1_), channel_id=1, source_target_pairs={{8,12},{9,13},{10,14},{11,15},{24,28},{25,29},{26,30},{27,31}} | collective-permute-start | bytes 3932168 | tf_op jit(solution)/shard_map/ppermute | solution.py:625
  181.2 0.9 copy-start.6
  186.5 5.5 %copy-start.9 = (bf16[1,2,2,256,512]{4,3,2,1,0:T(8,128)(2,1)S(1)}, bf16[1,2,2,256,512]{4,3,2,1,0:T(8,128)(2,1)}, u32[]{:S(2)}) copy-start(bf16[1,2,2,256,512]{4,3,2,1,0:T(8,128)(2,1)} %get-tuple-element.124.refs_0_) | copy-start | bytes 3145732
  186.5 5.7 %copy-start.10 = (f32[1024]{0:T(1024)S(1)}, f32[1024]{0:T(1024)}, u32[]{:S(2)}) copy-start(f32[1024]{0:T(1024)} %param.15) | copy-start | bytes 12292
  191.6 23.3 %collective-permute-start.17 = (bf16[1,2,2,256,512]{4,3,2,1,0:T(8,128)(2,1)}, bf16[1,2,2,256,512]{4,3,2,1,0:T(8,128)(2,1)}, u32[]{:S(2)}, u32[]{:S(2)}) collective-permute-start(bf16[1,2,2,256,512]{4,3,2,1,0:T(8,128)(2,1)} %get-tuple-element.117.refs_1_), channel_id=1, source_target_pairs={{0,1},{1,0},{2,3},{3,2},{4,5},{5,4},{6,7},{7,6},{8,9},{9,8},{10,11... | collective-permute-start | bytes 3145736 | tf_op jit(solution)/shard_map/ppermute | solution.py:662
  191.9 23.0 %collective-permute-start.16 = (bf16[1,2,2,256,512]{4,3,2,1,0:T(8,128)(2,1)S(1)}, bf16[1,2,2,256,512]{4,3,2,1,0:T(8,128)(2,1)}, u32[]{:S(2)}, u32[]{:S(2)}) collective-permute-start(bf16[1,2,2,256,512]{4,3,2,1,0:T(8,128)(2,1)S(1)} %copy-done.9), channel_id=1, source_target_pairs={{0,1},{1,0},{2,3},{3,2},{4,5},{5,4},{6,7},{7,6},{8,9},{9,8},{10,11... | collective-permute-start | bytes 3145736 | tf_op jit(solution)/shard_map/ppermute | solution.py:662
  201.7 13.3 %copy-start.12 = (f32[8]{0:T(128)S(1)}, f32[8]{0:T(128)}, u32[]{:S(2)}) copy-start(f32[8]{0:T(128)} %eps_slab.1) | copy-start | bytes 100
  214.9 17.2 %copy-start.8 = (s32[4,16,16]{2,1,0:T(8,128)S(1)}, s32[4,16,16]{2,1,0:T(8,128)}, u32[]{:S(2)}) copy-start(s32[4,16,16]{2,1,0:T(8,128)} %mask.20) | copy-start | bytes 12292

commit v6 on v5

--- a/solution.py
+++ b/solution.py
@@ -312,41 +312,28 @@
     return (2.0 * direct.astype(jnp.float32) - swapped.astype(jnp.float32)).astype(jnp.bfloat16)
 
 
-def early_kernel(meta, *refs):
-    direct, swapped, own, oth, out_ref, w_ref = (
-        refs[:3], refs[3:6], refs[6:9], refs[9:12], refs[12], refs[13]
-    )
+def fold_kernel(meta, *refs):
+    direct, swapped, w_ref = refs[:3], refs[3:6], refs[6]
     v = meta[0]
-    g = pl.program_id(0)
-
-    @pl.when(g == 0)
-    def _():
-        for q in range(3):
-            for p in range(3):
-                col = pl.multiple_of((v ^ p) * 256, 256)
-                row = pl.multiple_of((v ^ q) * 256, 256)
-                for k in range(4):
-                    w_ref[q, k * 256 : (k + 1) * 256, p * 256 : (p + 1) * 256] = folded(
-                        direct[q][k, :, pl.ds(col, 256)], swapped[p][k, pl.ds(row, 256), :]
-                    )
-
-    def work(blocks):
-        total = jnp.dot(
-            blocks[0][...].reshape(512, 1024), w_ref[0], preferred_element_type=jnp.float32
+    for q in range(3):
+        for p in range(3):
+            col = pl.multiple_of((v ^ p) * 256, 256)
+            row = pl.multiple_of((v ^ q) * 256, 256)
+            w_ref[q, :, p * 256 : (p + 1) * 256] = folded(
+                direct[q][0, :, pl.ds(col, 256)], swapped[p][0, pl.ds(row, 256), :]
+            )
+
+
+def early_kernel(meta, w_ref, *refs):
+    blocks, out_ref = refs[:3], refs[-1]
+    total = jnp.dot(
+        blocks[0][...].reshape(512, 1024), w_ref[0], preferred_element_type=jnp.float32
+    )
+    for q in range(1, 3):
+        total += jnp.dot(
+            blocks[q][...].reshape(512, 1024), w_ref[q], preferred_element_type=jnp.float32
         )
-        for q in range(1, 3):
-            total += jnp.dot(
-                blocks[q][...].reshape(512, 1024), w_ref[q], preferred_element_type=jnp.float32
-            )
-        out_ref[...] = total
-
-    @pl.when(g < 2)
-    def _():
-        work(own)
-
-    @pl.when(g >= 2)
-    def _():
-        work(oth)
+    out_ref[...] = total
 
 
 def late_kernel(meta, *refs):
@@ -620,39 +607,59 @@
     first = combine_first(1, near1, far1, first)
     first = combine_first(2, near2, far2, first)
     near3 = across(3, packed3)
-    up2, down2, near3, first = ready((up2, down2, near3, first))
-    end_down = lax.ppermute(down2, "vir", [(1, 0)])
-    end_up = lax.ppermute(up2, "vir", [(2, 3)])
+    up2, down2, first = ready((up2, down2, first))
     ints.append(unpack(2, down2, up2))
-    first_oth = lax.ppermute(first, "rep", swap)
-
-    def own_at(d, width=1024):
-        return pl.BlockSpec((1, 1, 2, 256, width), lambda g, *_: (d % 3, jnp.minimum(g, 1), 0, 0, 0))
-
-    def oth_at(d, width=1024):
-        return pl.BlockSpec((1, 1, 2, 256, width), lambda g, *_: (d % 3, jnp.maximum(g - 2, 0), 0, 0, 0))
-
-    def place(g, meta, *_):
-        return (2 * (g % 2) + jnp.where(g < 2, meta[2], 1 - meta[2]), 0)
-
-    once = pl.Buffered(1)
-    part = pl.pallas_call(
-        early_kernel,
+    folded_w = pl.pallas_call(
+        fold_kernel,
         grid_spec=pltpu.PrefetchScalarGridSpec(
             num_scalar_prefetch=1,
             grid=(4,),
-            in_specs=[pl.BlockSpec((4, 256, 1024), lambda g, *_: (0, 0, 0), pipeline_mode=once)] * 3
-            + [pl.BlockSpec((4, 1024, 256), lambda g, *_: (0, 0, 0), pipeline_mode=once)] * 3
-            + [own_at(d) for d in range(3)]
-            + [oth_at(d) for d in range(3)],
-            out_specs=pl.BlockSpec((512, 768), place),
-            scratch_shapes=[pltpu.VMEM((3, 1024, 768), bf16)],
+            in_specs=[pl.BlockSpec((1, 256, 1024), lambda k, meta: (k, 0, 0))] * 3
+            + [pl.BlockSpec((1, 1024, 256), lambda k, meta: (k, 0, 0))] * 3,
+            out_specs=pl.BlockSpec((3, 256, 768), lambda k, meta: (0, k, 0)),
         ),
-        out_shape=jax.ShapeDtypeStruct((2048, 768), jnp.float32),
+        out_shape=jax.ShapeDtypeStruct((3, 1024, 768), bf16),
         compiler_params=params(),
         cost_estimate=NO_COST,
-        name="early",
-    )(meta, *[d for d, _ in ints], *[t for _, t in ints], *[first] * 3, *[first_oth] * 3)
+        name="fold",
+    )(meta, *[d for d, _ in ints], *[t for _, t in ints])
+    up2, down2, near3, first, folded_w = ready((up2, down2, near3, first, folded_w))
+    end_down = lax.ppermute(down2, "vir", [(1, 0)])
+    end_up = lax.ppermute(up2, "vir", [(2, 3)])
+    first_oth = lax.ppermute(first, "rep", swap)
+
+    def own_at(d, width=1024):
+        return pl.BlockSpec((1, 1, 2, 256, width), lambda g, *_: (d % 3, jnp.minimum(g, 1), 0, 0, 0))
+
+    def oth_at(d, width=1024):
+        return pl.BlockSpec((1, 1, 2, 256, width), lambda g, *_: (d % 3, jnp.maximum(g - 2, 0), 0, 0, 0))
+
+    def place(g, meta, *_):
+        return (2 * (g % 2) + jnp.where(g < 2, meta[2], 1 - meta[2]), 0)
+
+    once = pl.Buffered(1)
+    def early(c, other, *sofar):
+        def at(d):
+            return pl.BlockSpec((1, 1, 2, 256, 1024), lambda g, *_: (d, g, 0, 0, 0))
+
+        return pl.pallas_call(
+            early_kernel,
+            grid_spec=pltpu.PrefetchScalarGridSpec(
+                num_scalar_prefetch=1,
+                grid=(2,),
+                in_specs=[pl.BlockSpec((3, 1024, 768), lambda g, *_: (0, 0, 0), pipeline_mode=once)]
+                + [at(d) for d in range(3)]
+                + [anywhere() for _ in sofar],
+                out_specs=pl.BlockSpec((512, 768), lambda g, meta: place(g + 2 * other, meta)),
+            ),
+            out_shape=jax.ShapeDtypeStruct((2048, 768), jnp.float32),
+            input_output_aliases={5: 0} if sofar else {},
+            compiler_params=params(),
+            cost_estimate=NO_COST,
+            name=f"early_{other}",
+        )(meta, folded_w, c, c, c, *sofar)
+
+    part = early(first_oth, 1, early(first, 0))
 
     far3 = lax.ppermute(near3, "occ", swap)
     far3, part = ready((far3, part))

time: 240 us -> 234 us (0.975)
  waiting for transfers between devices: 67.1 us -> 50.8 us
  Pallas kernels: 122 us -> 131 us
    ppermute x3, waiting for transfers between devices: 39.3 us -> 12.7 us  [across(): return lax.ppermute(packed, 'vir', [(s, s ^ d) for s in range(4)])]
    pallas_call x1 -> x3, Pallas kernels: 20.9 us -> 29.5 us  [the longest x2 21.4 us: early(): pl.pallas_call(early_kernel, grid_spec=pltpu.PrefetchScalarGridSpec(num_s...]
    ppermute x1, waiting for transfers between devices: 0.01 us -> 6.57 us  [packed_shards(): up2 = lax.ppermute(up1, 'vir', [(1, 2), (2, 3)])]
    ppermute x1, waiting for transfers between devices: 0.01 us -> 3.9 us  [packed_shards(): down2 = lax.ppermute(down1, 'vir', [(1, 0), (2, 1)])]
  transfers between devices with their start and end apart: 18 -> 18, of which waited for: 10 -> 12; matrix products, arithmetic and copies ran while one was open for 2% -> 3% of each run, Pallas kernels for 44% -> 49%
where the time goes in v6:
time: 234 us; the launch traced here: 233 us
  Pallas kernels  131 us (56%)
  waiting for transfers between devices  50.8 us (22%)
  starting transfers between devices  28 us (12%)
  between operations  16.3 us (7%)
  other arithmetic  4.25 us (2%)
  local copies, waits for them, and re-layouts  2.67 us (1%)
    pallas_call x4, Pallas kernels, unpack(): pl.pallas_call(kernel, grid_spec=pltpu.PrefetchScalarGridSpec(num_scalar_...  31.3 us
    pallas_call x5, Pallas kernels, combine(): pl.pallas_call(kernel, grid_spec=pltpu.PrefetchScalarGridSpec(num_scalar_...  27.7 us
    pallas_call x2, Pallas kernels, early(): pl.pallas_call(early_kernel, grid_spec=pltpu.PrefetchScalarGridSpec(num_s...  21.4 us
    pallas_call x1, Pallas kernels, finish(): pl.pallas_call(tail_kernel, grid_spec=pltpu.PrefetchScalarGridSpec(num_sc...  17.2 us
    pallas_call x1, Pallas kernels, packed_shards(): pl.pallas_call(late_kernel, grid_spec=pltpu.PrefetchScalarGridSpec(num_sc...  13.2 us
    ppermute x3, waiting for transfers between devices, across(): return lax.ppermute(packed, 'vir', [(s, s ^ d) for s in range(4)])  12.7 us
    ppermute x1, waiting for transfers between devices, packed_shards(): lax.ppermute(near2, 'occ', swap)  10 us
    pallas_call x1, Pallas kernels, packed_shards(): pl.pallas_call(fold_kernel, grid_spec=pltpu.PrefetchScalarGridSpec(num_sc...  8.02 us
  transfers between devices with their start and end apart: 18, of which 12 were waited for; matrix products, arithmetic and copies ran while one was open for 3% of the time, Pallas kernels for 49%

profile of v6, /device:TPU:9, one launch (start us, length us, event | category | flops | bytes accessed | tf_op | source)
XLA Modules:
  0.0 232.5 jit_solution(8691502395350079084)
XLA Ops:
  7.2 4.0 %collective-permute-done.oth_ref = bf16[2,2,256,1024]{3,2,1,0:T(8,128)(2,1)S(1)} collective-permute-done((bf16[2,2,256,1024]{3,2,1,0:T(8,128)(2,1)}, bf16[2,2,256,1024]{3,2,1,0:T(8,128)(2,1)S(1)}, u32[]{:S(2)}, u32[]{:S(2)}) %collective-permute-start) | collective-permute-done | bytes 2097184 | tf_op jit(solution)/shard_map/ppermute | solution.py:461
  12.5 5.1 %pack_int.1 = bf16[160,32,128]{2,1,0:T(8,128)(2,1)} custom-call(s32[4]{0:T(128)} %pad_add_fusion.meta, s32[4,4,16,16]{3,2,1,0:T(8,128)} %mask.21, bf16[2,2,256,1024]{3,2,1,0:T(8,128)(2,1)} %own_ref.3, bf16[2,2,256,1024]{3,2,1,0:T(8,128)(2,1)} %copy-done.3), custom_call_target="tpu_custom_call" | custom-call | flops 1024 | bytes 1024 | tf_op jit(solution)/shard_map/pack_int/pallas_call | solution.py:466
  17.6 3.3 %collective-permute-start.1 = (bf16[160,32,128]{2,1,0:T(8,128)(2,1)}, bf16[160,32,128]{2,1,0:T(8,128)(2,1)S(1)}, u32[]{:S(2)}, u32[]{:S(2)}) collective-permute-start(bf16[160,32,128]{2,1,0:T(8,128)(2,1)} %pack_int.1), channel_id=1, source_target_pairs={{0,4},{4,8},{8,12},{1,5},{5,9},{9,13},{2,6},{6,10},{10,14},{3,7},{... | collective-permute-start | bytes 3932168 | tf_op jit(solution)/shard_map/ppermute | solution.py:476
  20.9 2.2 collective-permute-start.2
  24.7 6.5 %pack_amp.1 = (bf16[46,64,128]{2,1,0:T(8,128)(2,1)}, bf16[46,64,128]{2,1,0:T(8,128)(2,1)}, bf16[46,64,128]{2,1,0:T(8,128)(2,1)}) custom-call(s32[4]{0:T(128)} %pad_add_fusion.meta, s32[4,16,16]{2,1,0:T(8,128)} %mask.20, bf16[2,2,2,2,256,1024]{5,4,3,2,1,0:T(8,128)(2,1)} %bitcast.61, bf16[2,2,2,2,256,1024]{5,4,3,2,1,0:T(8,128)(2,1)} %collective-permute-done.3.oth_ref), custom_call_target="tpu_custom_call" | custom-call | flops 1024 | bytes 1024 | tf_op jit(solution)/shard_map/pack_amp/pallas_call | solution.py:479
  31.2 2.5 %collective-permute-start.7 = (bf16[46,64,128]{2,1,0:T(8,128)(2,1)}, bf16[46,64,128]{2,1,0:T(8,128)(2,1)}, u32[]{:S(2)}, u32[]{:S(2)}) collective-permute-start(bf16[46,64,128]{2,1,0:T(8,128)(2,1)} %get-tuple-element.98), channel_id=1, source_target_pairs={{0,8},{4,12},{8,0},{12,4},{1,9},{5,13},{9,1},{13,5},{2,10},{6,14},... | collective-permute-start | bytes 2261000 | tf_op jit(solution)/shard_map/ppermute | solution.py:497
  39.3 2.0 collective-permute-start.4
  42.9 7.1 %collective-permute-done.1.refs_1_.refs_2_ = bf16[160,32,128]{2,1,0:T(8,128)(2,1)S(1)} collective-permute-done((bf16[160,32,128]{2,1,0:T(8,128)(2,1)}, bf16[160,32,128]{2,1,0:T(8,128)(2,1)S(1)}, u32[]{:S(2)}, u32[]{:S(2)}) %collective-permute-start.1) | collective-permute-done | bytes 1310752 | tf_op jit(solution)/shard_map/ppermute | solution.py:476
  49.9 2.9 %collective-permute-done.2.refs_0_.refs_1_ = bf16[160,32,128]{2,1,0:T(8,128)(2,1)} collective-permute-done((bf16[160,32,128]{2,1,0:T(8,128)(2,1)}, bf16[160,32,128]{2,1,0:T(8,128)(2,1)}, u32[]{:S(2)}, u32[]{:S(2)}) %collective-permute-start.2) | collective-permute-done | bytes 1310752 | tf_op jit(solution)/shard_map/ppermute | solution.py:477
  52.8 4.3 %collective-permute-start.5 = (bf16[160,32,128]{2,1,0:T(8,128)(2,1)S(1)}, bf16[160,32,128]{2,1,0:T(8,128)(2,1)}, u32[]{:S(2)}, u32[]{:S(2)}) collective-permute-start(bf16[160,32,128]{2,1,0:T(8,128)(2,1)S(1)} %collective-permute-done.1.refs_1_.refs_2_), channel_id=1, source_target_pairs={{4,8},{8,12},{5,9},{9,13},{6,10},{10,14},{7,11},{11,15},{20,24},{2... | collective-permute-start | bytes 3932168 | tf_op jit(solution)/shard_map/ppermute | solution.py:502
  57.1 1.9 collective-permute-start.6
  59.1 7.4 %ints_0.1 = (bf16[4,256,1024]{2,1,0:T(8,128)(2,1)}, bf16[4,1024,256]{2,1,0:T(8,128)(2,1)}) custom-call(s32[4]{0:T(128)} %pad_add_fusion.meta, s32[4,4,16,16]{3,2,1,0:T(8,128)S(1)} %copy-done.4, bf16[2,2,256,1024]{3,2,1,0:T(8,128)(2,1)S(1)} %copy-done, bf16[2,2,256,1024]{3,2,1,0:T(8,128)(2,1)} %copy-done.3), custom_call_target="tpu_custom_call" | custom-call | flops 1024 | bytes 1024 | tf_op jit(solution)/shard_map/ints_0/pallas_call | solution.py:524
  66.5 5.9 %combine_0_0.1.refs_0_ = bf16[3,2,2,256,1024]{4,3,2,1,0:T(8,128)(2,1)} custom-call(s32[4]{0:T(128)} %pad_add_fusion.meta, s32[4,16,16]{2,1,0:T(8,128)} %mask.20, bf16[2,2,2,2,256,1024]{5,4,3,2,1,0:T(8,128)(2,1)} %bitcast.62, bf16[2,2,2,2,256,1024]{5,4,3,2,1,0:T(8,128)(2,1)} %collective-permute-done.3.oth_ref), custom_call_target="tpu_custom_call" | custom-call | flops 1024 | bytes 1024 | tf_op jit(solution)/shard_map/combine_0_0/pallas_call | solution.py:551
  72.5 10.7 %collective-permute-done.9.near_ref = bf16[46,64,128]{2,1,0:T(8,128)(2,1)} collective-permute-done((bf16[46,64,128]{2,1,0:T(8,128)(2,1)}, bf16[46,64,128]{2,1,0:T(8,128)(2,1)}, u32[]{:S(2)}, u32[]{:S(2)}) %collective-permute-start.9) | collective-permute-done | bytes 753696 | tf_op jit(solution)/shard_map/ppermute | solution.py:497
  84.3 1.8 collective-permute-done.7.near_ref
  87.4 8.0 %ints_1.1 = (bf16[4,256,1024]{2,1,0:T(8,128)(2,1)}, bf16[4,1024,256]{2,1,0:T(8,128)(2,1)}) custom-call(s32[4]{0:T(128)} %pad_add_fusion.meta, s32[4,4,16,16]{3,2,1,0:T(8,128)S(1)} %copy-done.4, bf16[160,32,128]{2,1,0:T(8,128)(2,1)} %collective-permute-done.2.refs_0_.refs_1_, bf16[160,32,128]{2,1,0:T(8,128)(2,1)} %copy-done.5), custom_call_target="tpu_custom_call" | custom-call | flops 1024 | bytes 1024 | tf_op jit(solution)/shard_map/ints_1/pallas_call | solution.py:524
  96.6 6.1 %combine_1_0.1.refs_0_ = bf16[3,2,2,256,1024]{4,3,2,1,0:T(8,128)(2,1)} custom-call(s32[4]{0:T(128)} %pad_add_fusion.meta, s32[4,16,16]{2,1,0:T(8,128)S(1)} %copy-done.7, bf16[2,2,2,2,256,1024]{5,4,3,2,1,0:T(8,128)(2,1)} %bitcast.63, bf16[2,2,2,2,256,1024]{5,4,3,2,1,0:T(8,128)(2,1)} %collective-permute-done.3.oth_ref, ...), custom_call_target="tpu_custom_call", output_to_operand_aliasing={{}: (6, {})} | custom-call | flops 1024 | bytes 1024 | tf_op jit(solution)/shard_map/combine_1_0/pallas_call | solution.py:551
  102.7 10.0 %collective-permute-done.8.far_ref = bf16[46,64,128]{2,1,0:T(8,128)(2,1)} collective-permute-done((bf16[46,64,128]{2,1,0:T(8,128)(2,1)}, bf16[46,64,128]{2,1,0:T(8,128)(2,1)}, u32[]{:S(2)}, u32[]{:S(2)}) %collective-permute-start.8) | collective-permute-done | bytes 753696 | tf_op jit(solution)/shard_map/ppermute | solution.py:604
  112.7 6.2 %combine_2_0.1.refs_0_.refs_1_.refs_2_.refs_8_.refs_9_.refs_10_ = bf16[3,2,2,256,1024]{4,3,2,1,0:T(8,128)(2,1)} custom-call(s32[4]{0:T(128)} %pad_add_fusion.meta, s32[4,16,16]{2,1,0:T(8,128)S(1)} %copy-done.7, bf16[2,2,2,2,256,1024]{5,4,3,2,1,0:T(8,128)(2,1)} %bitcast.64, ...), custom_call_target="tpu_custom_call", output_to_operand_aliasing={{}: (6, {})} | custom-call | flops 1024 | bytes 1024 | tf_op jit(solution)/shard_map/combine_2_0/pallas_call | solution.py:551
  118.9 6.6 %collective-permute-done.5.refs_1_ = bf16[160,32,128]{2,1,0:T(8,128)(2,1)} collective-permute-done((bf16[160,32,128]{2,1,0:T(8,128)(2,1)S(1)}, bf16[160,32,128]{2,1,0:T(8,128)(2,1)}, u32[]{:S(2)}, u32[]{:S(2)}) %collective-permute-start.5) | collective-permute-done | bytes 1310752 | tf_op jit(solution)/shard_map/ppermute | solution.py:502
  125.5 3.9 %collective-permute-done.6.refs_0_ = bf16[160,32,128]{2,1,0:T(8,128)(2,1)} collective-permute-done((bf16[160,32,128]{2,1,0:T(8,128)(2,1)}, bf16[160,32,128]{2,1,0:T(8,128)(2,1)}, u32[]{:S(2)}, u32[]{:S(2)}) %collective-permute-start.6) | collective-permute-done | bytes 1310752 | tf_op jit(solution)/shard_map/ppermute | solution.py:503
  129.4 8.0 %ints_2.1 = (bf16[4,256,1024]{2,1,0:T(8,128)(2,1)}, bf16[4,1024,256]{2,1,0:T(8,128)(2,1)}) custom-call(s32[4]{0:T(128)} %pad_add_fusion.meta, s32[4,4,16,16]{3,2,1,0:T(8,128)S(1)} %copy-done.4, bf16[160,32,128]{2,1,0:T(8,128)(2,1)} %collective-permute-done.6.refs_0_, bf16[160,32,128]{2,1,0:T(8,128)(2,1)} %collective-permute-done.5.refs_1_), custom_call_target="tpu_custom_call" | custom-call | flops 1024 | bytes 1024 | tf_op jit(solution)/shard_map/ints_2/pallas_call | solution.py:524
  137.4 8.0 %fold.1.w_ref = bf16[3,1024,768]{2,1,0:T(8,128)(2,1)} custom-call(s32[4]{0:T(128)} %pad_add_fusion.meta, bf16[4,256,1024]{2,1,0:T(8,128)(2,1)} %get-tuple-element.111.refs_0_, bf16[4,256,1024]{2,1,0:T(8,128)(2,1)} %get-tuple-element.112.refs_1_, bf16[4,256,1024]{2,1,0:T(8,128)(2,1)} %get-tuple-element.113.refs_2_, ...), custom_call_target="tpu_custom_call" | custom-call | flops 1024 | bytes 1024 | tf_op jit(solution)/shard_map/fold/pallas_call | solution.py:612
  145.6 2.5 %collective-permute-start.13 = (bf16[3,2,2,256,1024]{4,3,2,1,0:T(8,128)(2,1)}, bf16[3,2,2,256,1024]{4,3,2,1,0:T(8,128)(2,1)}, u32[]{:S(2)}, u32[]{:S(2)}) collective-permute-start(bf16[3,2,2,256,1024]{4,3,2,1,0:T(8,128)(2,1)} %combine_2_0.1.refs_0_.refs_1_.refs_2_.refs_8_.refs_9_.refs_10_), channel_id=1, source_target_pairs={{0,1},{1,0},{2,3},{3,2},{4,5},{5,4},{6,7},{7,6},{8,9},{9,8},{10,11... | collective-permute-start | bytes 18874376 | tf_op jit(solution)/shard_map/ppermute | solution.py:629
  149.3 2.3 %collective-permute-start.14 = (bf16[160,32,128]{2,1,0:T(8,128)(2,1)}, bf16[160,32,128]{2,1,0:T(8,128)(2,1)}, u32[]{:S(2)}, u32[]{:S(2)}) collective-permute-start(bf16[160,32,128]{2,1,0:T(8,128)(2,1)} %collective-permute-done.6.refs_0_), channel_id=1, source_target_pairs={{4,0},{5,1},{6,2},{7,3},{20,16},{21,17},{22,18},{23,19}} | collective-permute-start | bytes 3932168 | tf_op jit(solution)/shard_map/ppermute | solution.py:627
  153.4 10.7 %early_0.1.refs_3_ = f32[2048,768]{1,0:T(8,128)} custom-call(s32[4]{0:T(128)} %pad_add_fusion.meta, bf16[3,1024,768]{2,1,0:T(8,128)(2,1)} %fold.1.w_ref, bf16[3,2,2,256,1024]{4,3,2,1,0:T(8,128)(2,1)} %combine_2_0.1.refs_0_.refs_1_.refs_2_.refs_8_.refs_9_.refs_10_, bf16[3,2,2,256,1024]{4,3,2,1,0:T(8,128)(2,1)} %combine_2_0.1.refs_0_.refs_1_.refs_2_.refs_8_.refs_9_.refs_10_, ...), custom_call_target="tpu_custom_call" | custom-call | flops 1024 | bytes 1024 | tf_op jit(solution)/shard_map/early_0/pallas_call | solution.py:645
  164.1 10.7 %early_1.1.part_ref = f32[2048,768]{1,0:T(8,128)} custom-call(s32[4]{0:T(128)} %pad_add_fusion.meta, bf16[3,1024,768]{2,1,0:T(8,128)(2,1)} %fold.1.w_ref, bf16[3,2,2,256,1024]{4,3,2,1,0:T(8,128)(2,1)} %collective-permute-done.13.refs_0_.refs_1_.refs_2_.refs_11_.refs_12_.refs_13_, ...), custom_call_target="tpu_custom_call", output_to_operand_aliasing={{}: (5, {})} | custom-call | flops 1024 | bytes 1024 | tf_op jit(solution)/shard_map/early_1/pallas_call | solution.py:645
  175.7 4.4 %combine_3_0.1 = (bf16[1,2,2,256,512]{4,3,2,1,0:T(8,128)(2,1)}, s32[1]{0:T(128)}) custom-call(s32[4]{0:T(128)} %pad_add_fusion.meta, s32[4,16,16]{2,1,0:T(8,128)S(1)} %copy-done.7, bf16[2,2,2,2,256,1024]{5,4,3,2,1,0:T(8,128)(2,1)} %bitcast.65, bf16[2,2,2,2,256,1024]{5,4,3,2,1,0:T(8,128)(2,1)} %collective-permute-done.3.oth_ref, ...), custom_call_target="tpu_custom_call" | custom-call | flops 1024 | bytes 1024 | tf_op jit(solution)/shard_map/combine_3_0/pallas_call | solution.py:551
  180.1 5.0 %combine_3_2.1 = (bf16[1,2,2,256,512]{4,3,2,1,0:T(8,128)(2,1)}, s32[1]{0:T(128)}) custom-call(s32[4]{0:T(128)} %pad_add_fusion.meta, s32[4,16,16]{2,1,0:T(8,128)S(1)} %copy-done.7, bf16[2,2,2,2,256,1024]{5,4,3,2,1,0:T(8,128)(2,1)} %bitcast.66, bf16[2,2,2,2,256,1024]{5,4,3,2,1,0:T(8,128)(2,1)} %collective-permute-done.3.oth_ref, ...), custom_call_target="tpu_custom_call" | custom-call | flops 1024 | bytes 1024 | tf_op jit(solution)/shard_map/combine_3_2/pallas_call | solution.py:551
  187.2 7.9 %ints_3.1 = (bf16[4,256,1024]{2,1,0:T(8,128)(2,1)}, bf16[4,1024,256]{2,1,0:T(8,128)(2,1)}) custom-call(s32[4]{0:T(128)} %pad_add_fusion.meta, s32[4,4,16,16]{3,2,1,0:T(8,128)S(1)} %copy-done.4, bf16[160,32,128]{2,1,0:T(8,128)(2,1)} %collective-permute-done.14.refs_0_, bf16[160,32,128]{2,1,0:T(8,128)(2,1)} %collective-permute-done.2.refs_0_.refs_1_, ...), custom_call_target="tpu_custom_call" | custom-call | flops 1024 | bytes 1024 | tf_op jit(solution)/shard_map/ints_3/pallas_call | solution.py:524
  195.1 13.2 %late.1 = (bf16[1024,1024]{1,0:T(8,128)(2,1)}, f32[2048,256]{1,0:T(8,128)}) custom-call(s32[4]{0:T(128)} %pad_add_fusion.meta, bf16[4,256,1024]{2,1,0:T(8,128)(2,1)} %get-tuple-element.111.refs_0_, bf16[4,256,1024]{2,1,0:T(8,128)(2,1)} %get-tuple-element.112.refs_1_, bf16[4,256,1024]{2,1,0:T(8,128)(2,1)} %get-tuple-element.113.refs_2_, ...), custom_call_target="tpu_custom_call" | custom-call | flops 1024 | bytes 1024 | tf_op jit(solution)/shard_map/late/pallas_call | solution.py:673
  208.4 17.2 %tail.1 = f32[8,256,1,1024]{3,2,1,0:T(1,128)} custom-call(s32[4]{0:T(128)} %pad_add_fusion.meta, f32[8]{0:T(128)S(1)} %copy-done.12, f32[1]{0:T(128)S(6)} %copy.92.eps_pair, f32[256,1]{1,0:T(8,128)} %copy.61.eps_rows, f32[1,1024]{1,0:T(1,128)S(1)} %bitcast.69, f32[2048,768]{1,0:T(8,128)} %early_1.1.part_ref, f32[2048,256]{1,0:T(8,128)} %get-tuple-element.130.late_ref, ...), custom_call_target="tpu_custom_call" | custom-call | flops 1024 | bytes 1024 | tf_op jit(solution)/shard_map/tail/pallas_call | solution.py:703
  (52 shorter events, 17.7 us)
Async XLA Ops:
  6.5 4.7 %collective-permute-start = (bf16[2,2,256,1024]{3,2,1,0:T(8,128)(2,1)}, bf16[2,2,256,1024]{3,2,1,0:T(8,128)(2,1)S(1)}, u32[]{:S(2)}, u32[]{:S(2)}) collective-permute-start(bf16[2,2,256,1024]{3,2,1,0:T(8,128)(2,1)} %own_ref.3), channel_id=1, source_target_pairs={{0,1},{1,0},{2,3},{3,2},{4,5},{5,4},{6,7},{7,6},{8,9},{9,8},{10,11... | collective-permute-start | bytes 6291464 | tf_op jit(solution)/shard_map/ppermute | solution.py:461
  11.2 1.3 copy-start.3
  11.2 13.5 %collective-permute-start.3 = (bf16[2,2,2,2,256,1024]{5,4,3,2,1,0:T(8,128)(2,1)}, bf16[2,2,2,2,256,1024]{5,4,3,2,1,0:T(8,128)(2,1)}, u32[]{:S(2)}, u32[]{:S(2)}) collective-permute-start(bf16[2,2,2,2,256,1024]{5,4,3,2,1,0:T(8,128)(2,1)} %bitcast.60), channel_id=1, source_target_pairs={{0,1},{1,0},{2,3},{3,2},{4,5},{5,4},{6,7},{7,6},{8,9},{9,8},{10,11... | collective-permute-start | bytes 25165832 | tf_op jit(solution)/shard_map/ppermute | solution.py:464
  17.6 16.9 %copy-start.4 = (s32[4,4,16,16]{3,2,1,0:T(8,128)S(1)}, s32[4,4,16,16]{3,2,1,0:T(8,128)}, u32[]{:S(2)}) copy-start(s32[4,4,16,16]{3,2,1,0:T(8,128)} %mask.21) | copy-start | bytes 49156
  17.6 41.5 %copy-start = (bf16[2,2,256,1024]{3,2,1,0:T(8,128)(2,1)S(1)}, bf16[2,2,256,1024]{3,2,1,0:T(8,128)(2,1)}, u32[]{:S(2)}) copy-start(bf16[2,2,256,1024]{3,2,1,0:T(8,128)(2,1)} %own_ref.3) | copy-start | bytes 6291460
  17.6 32.3 %collective-permute-start.1 = (bf16[160,32,128]{2,1,0:T(8,128)(2,1)}, bf16[160,32,128]{2,1,0:T(8,128)(2,1)S(1)}, u32[]{:S(2)}, u32[]{:S(2)}) collective-permute-start(bf16[160,32,128]{2,1,0:T(8,128)(2,1)} %pack_int.1), channel_id=1, source_target_pairs={{0,4},{4,8},{8,12},{1,5},{5,9},{9,13},{2,6},{6,10},{10,14},{3,7},{... | collective-permute-start | bytes 3932168 | tf_op jit(solution)/shard_map/ppermute | solution.py:476
  20.9 31.9 %collective-permute-start.2 = (bf16[160,32,128]{2,1,0:T(8,128)(2,1)}, bf16[160,32,128]{2,1,0:T(8,128)(2,1)}, u32[]{:S(2)}, u32[]{:S(2)}) collective-permute-start(bf16[160,32,128]{2,1,0:T(8,128)(2,1)} %pack_int.1), channel_id=1, source_target_pairs={{4,0},{8,4},{12,8},{5,1},{9,5},{13,9},{6,2},{10,6},{14,10},{7,3},{... | collective-permute-start | bytes 3932168 | tf_op jit(solution)/shard_map/ppermute | solution.py:477
  31.2 51.9 %collective-permute-start.9 = (bf16[46,64,128]{2,1,0:T(8,128)(2,1)}, bf16[46,64,128]{2,1,0:T(8,128)(2,1)}, u32[]{:S(2)}, u32[]{:S(2)}) collective-permute-start(bf16[46,64,128]{2,1,0:T(8,128)(2,1)} %get-tuple-element.99), channel_id=1, source_target_pairs={{0,4},{4,0},{8,12},{12,8},{1,5},{5,1},{9,13},{13,9},{2,6},{6,2},{1... | collective-permute-start | bytes 2261000 | tf_op jit(solution)/shard_map/ppermute | solution.py:497
  31.2 54.9 %collective-permute-start.7 = (bf16[46,64,128]{2,1,0:T(8,128)(2,1)}, bf16[46,64,128]{2,1,0:T(8,128)(2,1)}, u32[]{:S(2)}, u32[]{:S(2)}) collective-permute-start(bf16[46,64,128]{2,1,0:T(8,128)(2,1)} %get-tuple-element.98), channel_id=1, source_target_pairs={{0,8},{4,12},{8,0},{12,4},{1,9},{5,13},{9,1},{13,5},{2,10},{6,14},... | collective-permute-start | bytes 2261000 | tf_op jit(solution)/shard_map/ppermute | solution.py:497
  39.3 2.9 %collective-permute-start.4 = (s32[1]{0:T(128)}, s32[1]{0:T(128)}, u32[]{:S(2)}, u32[]{:S(2)}) collective-permute-start(s32[1]{0:T(128)} %bitcast.27), channel_id=1, source_target_pairs={{0,16},{16,0},{1,17},{17,1},{2,18},{18,2},{3,19},{19,3},{4,20},{20... | collective-permute-start | bytes 20 | tf_op jit(solution)/shard_map/ppermute | solution.py:500
  49.9 22.5 %copy-start.5 = (bf16[160,32,128]{2,1,0:T(8,128)(2,1)}, bf16[160,32,128]{2,1,0:T(8,128)(2,1)S(1)}, u32[]{:S(2)}) copy-start(bf16[160,32,128]{2,1,0:T(8,128)(2,1)S(1)} %collective-permute-done.1.refs_1_.refs_2_) | copy-start | bytes 3932164
  52.8 72.7 %collective-permute-start.5 = (bf16[160,32,128]{2,1,0:T(8,128)(2,1)S(1)}, bf16[160,32,128]{2,1,0:T(8,128)(2,1)}, u32[]{:S(2)}, u32[]{:S(2)}) collective-permute-start(bf16[160,32,128]{2,1,0:T(8,128)(2,1)S(1)} %collective-permute-done.1.refs_1_.refs_2_), channel_id=1, source_target_pairs={{4,8},{8,12},{5,9},{9,13},{6,10},{10,14},{7,11},{11,15},{20,24},{2... | collective-permute-start | bytes 3932168 | tf_op jit(solution)/shard_map/ppermute | solution.py:502
  57.1 72.3 %collective-permute-start.6 = (bf16[160,32,128]{2,1,0:T(8,128)(2,1)}, bf16[160,32,128]{2,1,0:T(8,128)(2,1)}, u32[]{:S(2)}, u32[]{:S(2)}) collective-permute-start(bf16[160,32,128]{2,1,0:T(8,128)(2,1)} %collective-permute-done.2.refs_0_.refs_1_), channel_id=1, source_target_pairs={{4,0},{8,4},{5,1},{9,5},{6,2},{10,6},{7,3},{11,7},{20,16},{24,20},... | collective-permute-start | bytes 3932168 | tf_op jit(solution)/shard_map/ppermute | solution.py:503
  66.5 30.1 %copy-start.7 = (s32[4,16,16]{2,1,0:T(8,128)S(1)}, s32[4,16,16]{2,1,0:T(8,128)}, u32[]{:S(2)}) copy-start(s32[4,16,16]{2,1,0:T(8,128)} %mask.20) | copy-start | bytes 12292
  83.1 13.4 %collective-permute-start.10 = (bf16[46,64,128]{2,1,0:T(8,128)(2,1)}, bf16[46,64,128]{2,1,0:T(8,128)(2,1)}, u32[]{:S(2)}, u32[]{:S(2)}) collective-permute-start(bf16[46,64,128]{2,1,0:T(8,128)(2,1)} %collective-permute-done.9.near_ref), channel_id=1, source_target_pairs={{0,2},{2,0},{1,3},{3,1},{4,6},{6,4},{5,7},{7,5},{8,10},{10,8},{9,1... | collective-permute-start | bytes 2261000 | tf_op jit(solution)/shard_map/ppermute | solution.py:604
  86.2 26.5 %collective-permute-start.8 = (bf16[46,64,128]{2,1,0:T(8,128)(2,1)}, bf16[46,64,128]{2,1,0:T(8,128)(2,1)}, u32[]{:S(2)}, u32[]{:S(2)}) collective-permute-start(bf16[46,64,128]{2,1,0:T(8,128)(2,1)} %collective-permute-done.7.near_ref), channel_id=1, source_target_pairs={{0,2},{2,0},{1,3},{3,1},{4,6},{6,4},{5,7},{7,5},{8,10},{10,8},{9,1... | collective-permute-start | bytes 2261000 | tf_op jit(solution)/shard_map/ppermute | solution.py:604
  87.4 58.2 %collective-permute-start.11 = (bf16[46,64,128]{2,1,0:T(8,128)(2,1)}, bf16[46,64,128]{2,1,0:T(8,128)(2,1)}, u32[]{:S(2)}, u32[]{:S(2)}) collective-permute-start(bf16[46,64,128]{2,1,0:T(8,128)(2,1)} %get-tuple-element.109), channel_id=1, source_target_pairs={{0,12},{4,8},{8,4},{12,0},{1,13},{5,9},{9,5},{13,1},{2,14},{6,10},... | collective-permute-start | bytes 2261000 | tf_op jit(solution)/shard_map/ppermute | solution.py:497
  145.6 18.6 %collective-permute-start.13 = (bf16[3,2,2,256,1024]{4,3,2,1,0:T(8,128)(2,1)}, bf16[3,2,2,256,1024]{4,3,2,1,0:T(8,128)(2,1)}, u32[]{:S(2)}, u32[]{:S(2)}) collective-permute-start(bf16[3,2,2,256,1024]{4,3,2,1,0:T(8,128)(2,1)} %combine_2_0.1.refs_0_.refs_1_.refs_2_.refs_8_.refs_9_.refs_10_), channel_id=1, source_target_pairs={{0,1},{1,0},{2,3},{3,2},{4,5},{5,4},{6,7},{7,6},{8,9},{9,8},{10,11... | collective-permute-start | bytes 18874376 | tf_op jit(solution)/shard_map/ppermute | solution.py:629
  148.1 26.7 %collective-permute-start.12 = (bf16[46,64,128]{2,1,0:T(8,128)(2,1)}, bf16[46,64,128]{2,1,0:T(8,128)(2,1)S(1)}, u32[]{:S(2)}, u32[]{:S(2)}) collective-permute-start(bf16[46,64,128]{2,1,0:T(8,128)(2,1)} %collective-permute-done.11.near_ref), channel_id=1, source_target_pairs={{0,2},{2,0},{1,3},{3,1},{4,6},{6,4},{5,7},{7,5},{8,10},{10,8},{9,1... | collective-permute-start | bytes 2261000 | tf_op jit(solution)/shard_map/ppermute | solution.py:664
  149.3 37.8 %collective-permute-start.14 = (bf16[160,32,128]{2,1,0:T(8,128)(2,1)}, bf16[160,32,128]{2,1,0:T(8,128)(2,1)}, u32[]{:S(2)}, u32[]{:S(2)}) collective-permute-start(bf16[160,32,128]{2,1,0:T(8,128)(2,1)} %collective-permute-done.6.refs_0_), channel_id=1, source_target_pairs={{4,0},{5,1},{6,2},{7,3},{20,16},{21,17},{22,18},{23,19}} | collective-permute-start | bytes 3932168 | tf_op jit(solution)/shard_map/ppermute | solution.py:627
  151.7 35.5 %collective-permute-start.15 = (bf16[160,32,128]{2,1,0:T(8,128)(2,1)}, bf16[160,32,128]{2,1,0:T(8,128)(2,1)}, u32[]{:S(2)}, u32[]{:S(2)}) collective-permute-start(bf16[160,32,128]{2,1,0:T(8,128)(2,1)} %collective-permute-done.5.refs_1_), channel_id=1, source_target_pairs={{8,12},{9,13},{10,14},{11,15},{24,28},{25,29},{26,30},{27,31}} | collective-permute-start | bytes 3932168 | tf_op jit(solution)/shard_map/ppermute | solution.py:628
  174.8 0.9 copy-start.6
  180.1 5.4 %copy-start.9 = (bf16[1,2,2,256,512]{4,3,2,1,0:T(8,128)(2,1)S(1)}, bf16[1,2,2,256,512]{4,3,2,1,0:T(8,128)(2,1)}, u32[]{:S(2)}) copy-start(bf16[1,2,2,256,512]{4,3,2,1,0:T(8,128)(2,1)} %get-tuple-element.132.refs_0_) | copy-start | bytes 3145732
  180.1 5.5 %copy-start.10 = (f32[1024]{0:T(1024)S(1)}, f32[1024]{0:T(1024)}, u32[]{:S(2)}) copy-start(f32[1024]{0:T(1024)} %param.15) | copy-start | bytes 12292
  185.1 23.2 %collective-permute-start.17 = (bf16[1,2,2,256,512]{4,3,2,1,0:T(8,128)(2,1)}, bf16[1,2,2,256,512]{4,3,2,1,0:T(8,128)(2,1)}, u32[]{:S(2)}, u32[]{:S(2)}) collective-permute-start(bf16[1,2,2,256,512]{4,3,2,1,0:T(8,128)(2,1)} %get-tuple-element.125.refs_1_), channel_id=1, source_target_pairs={{0,1},{1,0},{2,3},{3,2},{4,5},{5,4},{6,7},{7,6},{8,9},{9,8},{10,11... | collective-permute-start | bytes 3145736 | tf_op jit(solution)/shard_map/ppermute | solution.py:669
  185.5 22.9 %collective-permute-start.16 = (bf16[1,2,2,256,512]{4,3,2,1,0:T(8,128)(2,1)S(1)}, bf16[1,2,2,256,512]{4,3,2,1,0:T(8,128)(2,1)}, u32[]{:S(2)}, u32[]{:S(2)}) collective-permute-start(bf16[1,2,2,256,512]{4,3,2,1,0:T(8,128)(2,1)S(1)} %copy-done.9), channel_id=1, source_target_pairs={{0,1},{1,0},{2,3},{3,2},{4,5},{5,4},{6,7},{7,6},{8,9},{9,8},{10,11... | collective-permute-start | bytes 3145736 | tf_op jit(solution)/shard_map/ppermute | solution.py:669
  195.1 13.3 %copy-start.12 = (f32[8]{0:T(128)S(1)}, f32[8]{0:T(128)}, u32[]{:S(2)}) copy-start(f32[8]{0:T(128)} %eps_slab.1) | copy-start | bytes 100
  208.4 17.2 %copy-start.8 = (s32[4,16,16]{2,1,0:T(8,128)S(1)}, s32[4,16,16]{2,1,0:T(8,128)}, u32[]{:S(2)}) copy-start(s32[4,16,16]{2,1,0:T(8,128)} %mask.20) | copy-start | bytes 12292

commit v7 on v6

--- a/solution.py
+++ b/solution.py
@@ -380,6 +380,7 @@
 
 def tail_kernel(meta, eps_slab, eps_pair, eps_rows, eps_cols, part_ref, late_ref, row_ref, *refs):
     own, oth, out_ref = refs[:2], refs[2:4], refs[4]
+    flat_ref = out_ref.reshape(4096, 128)
     v, r = meta[0], meta[2]
     g = pl.program_id(0)
 
@@ -401,8 +402,9 @@
                 energy = (eps_rows[...] + cols) - eps_slab[i + ii] - eps_pair[0]
                 done = value[ii * 256 : (ii + 1) * 256] / energy
                 for n in range(2):
-                    at = pl.multiple_of(s * 256 + n * 128, 128)
-                    out_ref[ii, :, 0, pl.ds(at, 128)] = done[:, n * 128 : (n + 1) * 128]
+                    flat_ref[pl.ds(ii * 2048 + 2 * s + n, 256, stride=8), :] = done[
+                        :, n * 128 : (n + 1) * 128
+                    ]
 
     @pl.when(g < 2)
     def _():

time: 234 us -> 229 us (0.979)
  Pallas kernels: 131 us -> 126 us
    pallas_call x1, Pallas kernels: 17.2 us -> 12.9 us  [finish(): pl.pallas_call(tail_kernel, grid_spec=pltpu.PrefetchScalarGridSpec(num_sc...]
  transfers between devices with their start and end apart: 18 -> 18, of which waited for: 12 -> 12; matrix products, arithmetic and copies ran while one was open for 3% -> 3% of each run, Pallas kernels for 49% -> 50%
where the time goes in v7:
time: 229 us; the launch traced here: 228 us
  Pallas kernels  126 us (55%)
  waiting for transfers between devices  50.8 us (22%)
  starting transfers between devices  28 us (12%)
  between operations  16.3 us (7%)
  other arithmetic  4.25 us (2%)
  local copies, waits for them, and re-layouts  2.67 us (1%)
    pallas_call x4, Pallas kernels, unpack(): pl.pallas_call(kernel, grid_spec=pltpu.PrefetchScalarGridSpec(num_scalar_...  31.3 us
    pallas_call x5, Pallas kernels, combine(): pl.pallas_call(kernel, grid_spec=pltpu.PrefetchScalarGridSpec(num_scalar_...  27.7 us
    pallas_call x2, Pallas kernels, early(): pl.pallas_call(early_kernel, grid_spec=pltpu.PrefetchScalarGridSpec(num_s...  21.4 us
    pallas_call x1, Pallas kernels, packed_shards(): pl.pallas_call(late_kernel, grid_spec=pltpu.PrefetchScalarGridSpec(num_sc...  13.2 us
    pallas_call x1, Pallas kernels, finish(): pl.pallas_call(tail_kernel, grid_spec=pltpu.PrefetchScalarGridSpec(num_sc...  12.9 us
    ppermute x3, waiting for transfers between devices, across(): return lax.ppermute(packed, 'vir', [(s, s ^ d) for s in range(4)])  12.7 us
    ppermute x1, waiting for transfers between devices, packed_shards(): lax.ppermute(near2, 'occ', swap)  10 us
    pallas_call x1, Pallas kernels, packed_shards(): pl.pallas_call(fold_kernel, grid_spec=pltpu.PrefetchScalarGridSpec(num_sc...  8.02 us
  transfers between devices with their start and end apart: 18, of which 12 were waited for; matrix products, arithmetic and copies ran while one was open for 3% of the time, Pallas kernels for 50%

profile of v7, /device:TPU:9, one launch (start us, length us, event | category | flops | bytes accessed | tf_op | source)
XLA Modules:
  0.0 228.2 jit_solution(5230813257652245780)
XLA Ops:
  7.2 4.0 %collective-permute-done.oth_ref = bf16[2,2,256,1024]{3,2,1,0:T(8,128)(2,1)S(1)} collective-permute-done((bf16[2,2,256,1024]{3,2,1,0:T(8,128)(2,1)}, bf16[2,2,256,1024]{3,2,1,0:T(8,128)(2,1)S(1)}, u32[]{:S(2)}, u32[]{:S(2)}) %collective-permute-start) | collective-permute-done | bytes 2097184 | tf_op jit(solution)/shard_map/ppermute | solution.py:463
  12.5 5.1 %pack_int.1 = bf16[160,32,128]{2,1,0:T(8,128)(2,1)} custom-call(s32[4]{0:T(128)} %pad_add_fusion.meta, s32[4,4,16,16]{3,2,1,0:T(8,128)} %mask.21, bf16[2,2,256,1024]{3,2,1,0:T(8,128)(2,1)} %own_ref.3, bf16[2,2,256,1024]{3,2,1,0:T(8,128)(2,1)} %copy-done.3), custom_call_target="tpu_custom_call" | custom-call | flops 1024 | bytes 1024 | tf_op jit(solution)/shard_map/pack_int/pallas_call | solution.py:468
  17.6 3.3 %collective-permute-start.1 = (bf16[160,32,128]{2,1,0:T(8,128)(2,1)}, bf16[160,32,128]{2,1,0:T(8,128)(2,1)S(1)}, u32[]{:S(2)}, u32[]{:S(2)}) collective-permute-start(bf16[160,32,128]{2,1,0:T(8,128)(2,1)} %pack_int.1), channel_id=1, source_target_pairs={{0,4},{4,8},{8,12},{1,5},{5,9},{9,13},{2,6},{6,10},{10,14},{3,7},{... | collective-permute-start | bytes 3932168 | tf_op jit(solution)/shard_map/ppermute | solution.py:478
  20.9 2.2 collective-permute-start.2
  24.7 6.5 %pack_amp.1 = (bf16[46,64,128]{2,1,0:T(8,128)(2,1)}, bf16[46,64,128]{2,1,0:T(8,128)(2,1)}, bf16[46,64,128]{2,1,0:T(8,128)(2,1)}) custom-call(s32[4]{0:T(128)} %pad_add_fusion.meta, s32[4,16,16]{2,1,0:T(8,128)} %mask.20, bf16[2,2,2,2,256,1024]{5,4,3,2,1,0:T(8,128)(2,1)} %bitcast.61, bf16[2,2,2,2,256,1024]{5,4,3,2,1,0:T(8,128)(2,1)} %collective-permute-done.3.oth_ref), custom_call_target="tpu_custom_call" | custom-call | flops 1024 | bytes 1024 | tf_op jit(solution)/shard_map/pack_amp/pallas_call | solution.py:481
  31.2 2.5 %collective-permute-start.7 = (bf16[46,64,128]{2,1,0:T(8,128)(2,1)}, bf16[46,64,128]{2,1,0:T(8,128)(2,1)}, u32[]{:S(2)}, u32[]{:S(2)}) collective-permute-start(bf16[46,64,128]{2,1,0:T(8,128)(2,1)} %get-tuple-element.98), channel_id=1, source_target_pairs={{0,8},{4,12},{8,0},{12,4},{1,9},{5,13},{9,1},{13,5},{2,10},{6,14},... | collective-permute-start | bytes 2261000 | tf_op jit(solution)/shard_map/ppermute | solution.py:499
  39.3 2.0 collective-permute-start.4
  42.9 7.1 %collective-permute-done.1.refs_1_.refs_2_ = bf16[160,32,128]{2,1,0:T(8,128)(2,1)S(1)} collective-permute-done((bf16[160,32,128]{2,1,0:T(8,128)(2,1)}, bf16[160,32,128]{2,1,0:T(8,128)(2,1)S(1)}, u32[]{:S(2)}, u32[]{:S(2)}) %collective-permute-start.1) | collective-permute-done | bytes 1310752 | tf_op jit(solution)/shard_map/ppermute | solution.py:478
  49.9 2.9 %collective-permute-done.2.refs_0_.refs_1_ = bf16[160,32,128]{2,1,0:T(8,128)(2,1)} collective-permute-done((bf16[160,32,128]{2,1,0:T(8,128)(2,1)}, bf16[160,32,128]{2,1,0:T(8,128)(2,1)}, u32[]{:S(2)}, u32[]{:S(2)}) %collective-permute-start.2) | collective-permute-done | bytes 1310752 | tf_op jit(solution)/shard_map/ppermute | solution.py:479
  52.8 4.3 %collective-permute-start.5 = (bf16[160,32,128]{2,1,0:T(8,128)(2,1)S(1)}, bf16[160,32,128]{2,1,0:T(8,128)(2,1)}, u32[]{:S(2)}, u32[]{:S(2)}) collective-permute-start(bf16[160,32,128]{2,1,0:T(8,128)(2,1)S(1)} %collective-permute-done.1.refs_1_.refs_2_), channel_id=1, source_target_pairs={{4,8},{8,12},{5,9},{9,13},{6,10},{10,14},{7,11},{11,15},{20,24},{2... | collective-permute-start | bytes 3932168 | tf_op jit(solution)/shard_map/ppermute | solution.py:504
  57.1 1.9 collective-permute-start.6
  59.1 7.4 %ints_0.1 = (bf16[4,256,1024]{2,1,0:T(8,128)(2,1)}, bf16[4,1024,256]{2,1,0:T(8,128)(2,1)}) custom-call(s32[4]{0:T(128)} %pad_add_fusion.meta, s32[4,4,16,16]{3,2,1,0:T(8,128)S(1)} %copy-done.4, bf16[2,2,256,1024]{3,2,1,0:T(8,128)(2,1)S(1)} %copy-done, bf16[2,2,256,1024]{3,2,1,0:T(8,128)(2,1)} %copy-done.3), custom_call_target="tpu_custom_call" | custom-call | flops 1024 | bytes 1024 | tf_op jit(solution)/shard_map/ints_0/pallas_call | solution.py:526
  66.5 5.9 %combine_0_0.1.refs_0_ = bf16[3,2,2,256,1024]{4,3,2,1,0:T(8,128)(2,1)} custom-call(s32[4]{0:T(128)} %pad_add_fusion.meta, s32[4,16,16]{2,1,0:T(8,128)} %mask.20, bf16[2,2,2,2,256,1024]{5,4,3,2,1,0:T(8,128)(2,1)} %bitcast.62, bf16[2,2,2,2,256,1024]{5,4,3,2,1,0:T(8,128)(2,1)} %collective-permute-done.3.oth_ref), custom_call_target="tpu_custom_call" | custom-call | flops 1024 | bytes 1024 | tf_op jit(solution)/shard_map/combine_0_0/pallas_call | solution.py:553
  72.5 10.7 %collective-permute-done.9.near_ref = bf16[46,64,128]{2,1,0:T(8,128)(2,1)} collective-permute-done((bf16[46,64,128]{2,1,0:T(8,128)(2,1)}, bf16[46,64,128]{2,1,0:T(8,128)(2,1)}, u32[]{:S(2)}, u32[]{:S(2)}) %collective-permute-start.9) | collective-permute-done | bytes 753696 | tf_op jit(solution)/shard_map/ppermute | solution.py:499
  84.3 1.8 collective-permute-done.7.near_ref
  87.4 8.0 %ints_1.1 = (bf16[4,256,1024]{2,1,0:T(8,128)(2,1)}, bf16[4,1024,256]{2,1,0:T(8,128)(2,1)}) custom-call(s32[4]{0:T(128)} %pad_add_fusion.meta, s32[4,4,16,16]{3,2,1,0:T(8,128)S(1)} %copy-done.4, bf16[160,32,128]{2,1,0:T(8,128)(2,1)} %collective-permute-done.2.refs_0_.refs_1_, bf16[160,32,128]{2,1,0:T(8,128)(2,1)} %copy-done.5), custom_call_target="tpu_custom_call" | custom-call | flops 1024 | bytes 1024 | tf_op jit(solution)/shard_map/ints_1/pallas_call | solution.py:526
  96.6 6.1 %combine_1_0.1.refs_0_ = bf16[3,2,2,256,1024]{4,3,2,1,0:T(8,128)(2,1)} custom-call(s32[4]{0:T(128)} %pad_add_fusion.meta, s32[4,16,16]{2,1,0:T(8,128)S(1)} %copy-done.7, bf16[2,2,2,2,256,1024]{5,4,3,2,1,0:T(8,128)(2,1)} %bitcast.63, bf16[2,2,2,2,256,1024]{5,4,3,2,1,0:T(8,128)(2,1)} %collective-permute-done.3.oth_ref, ...), custom_call_target="tpu_custom_call", output_to_operand_aliasing={{}: (6, {})} | custom-call | flops 1024 | bytes 1024 | tf_op jit(solution)/shard_map/combine_1_0/pallas_call | solution.py:553
  102.7 10.0 %collective-permute-done.8.far_ref = bf16[46,64,128]{2,1,0:T(8,128)(2,1)} collective-permute-done((bf16[46,64,128]{2,1,0:T(8,128)(2,1)}, bf16[46,64,128]{2,1,0:T(8,128)(2,1)}, u32[]{:S(2)}, u32[]{:S(2)}) %collective-permute-start.8) | collective-permute-done | bytes 753696 | tf_op jit(solution)/shard_map/ppermute | solution.py:606
  112.7 6.2 %combine_2_0.1.refs_0_.refs_1_.refs_2_.refs_8_.refs_9_.refs_10_ = bf16[3,2,2,256,1024]{4,3,2,1,0:T(8,128)(2,1)} custom-call(s32[4]{0:T(128)} %pad_add_fusion.meta, s32[4,16,16]{2,1,0:T(8,128)S(1)} %copy-done.7, bf16[2,2,2,2,256,1024]{5,4,3,2,1,0:T(8,128)(2,1)} %bitcast.64, ...), custom_call_target="tpu_custom_call", output_to_operand_aliasing={{}: (6, {})} | custom-call | flops 1024 | bytes 1024 | tf_op jit(solution)/shard_map/combine_2_0/pallas_call | solution.py:553
  118.9 6.6 %collective-permute-done.5.refs_1_ = bf16[160,32,128]{2,1,0:T(8,128)(2,1)} collective-permute-done((bf16[160,32,128]{2,1,0:T(8,128)(2,1)S(1)}, bf16[160,32,128]{2,1,0:T(8,128)(2,1)}, u32[]{:S(2)}, u32[]{:S(2)}) %collective-permute-start.5) | collective-permute-done | bytes 1310752 | tf_op jit(solution)/shard_map/ppermute | solution.py:504
  125.5 3.9 %collective-permute-done.6.refs_0_ = bf16[160,32,128]{2,1,0:T(8,128)(2,1)} collective-permute-done((bf16[160,32,128]{2,1,0:T(8,128)(2,1)}, bf16[160,32,128]{2,1,0:T(8,128)(2,1)}, u32[]{:S(2)}, u32[]{:S(2)}) %collective-permute-start.6) | collective-permute-done | bytes 1310752 | tf_op jit(solution)/shard_map/ppermute | solution.py:505
  129.4 8.0 %ints_2.1 = (bf16[4,256,1024]{2,1,0:T(8,128)(2,1)}, bf16[4,1024,256]{2,1,0:T(8,128)(2,1)}) custom-call(s32[4]{0:T(128)} %pad_add_fusion.meta, s32[4,4,16,16]{3,2,1,0:T(8,128)S(1)} %copy-done.4, bf16[160,32,128]{2,1,0:T(8,128)(2,1)} %collective-permute-done.6.refs_0_, bf16[160,32,128]{2,1,0:T(8,128)(2,1)} %collective-permute-done.5.refs_1_), custom_call_target="tpu_custom_call" | custom-call | flops 1024 | bytes 1024 | tf_op jit(solution)/shard_map/ints_2/pallas_call | solution.py:526
  137.4 8.0 %fold.1.w_ref = bf16[3,1024,768]{2,1,0:T(8,128)(2,1)} custom-call(s32[4]{0:T(128)} %pad_add_fusion.meta, bf16[4,256,1024]{2,1,0:T(8,128)(2,1)} %get-tuple-element.111.refs_0_, bf16[4,256,1024]{2,1,0:T(8,128)(2,1)} %get-tuple-element.112.refs_1_, bf16[4,256,1024]{2,1,0:T(8,128)(2,1)} %get-tuple-element.113.refs_2_, ...), custom_call_target="tpu_custom_call" | custom-call | flops 1024 | bytes 1024 | tf_op jit(solution)/shard_map/fold/pallas_call | solution.py:614
  145.6 2.5 %collective-permute-start.13 = (bf16[3,2,2,256,1024]{4,3,2,1,0:T(8,128)(2,1)}, bf16[3,2,2,256,1024]{4,3,2,1,0:T(8,128)(2,1)}, u32[]{:S(2)}, u32[]{:S(2)}) collective-permute-start(bf16[3,2,2,256,1024]{4,3,2,1,0:T(8,128)(2,1)} %combine_2_0.1.refs_0_.refs_1_.refs_2_.refs_8_.refs_9_.refs_10_), channel_id=1, source_target_pairs={{0,1},{1,0},{2,3},{3,2},{4,5},{5,4},{6,7},{7,6},{8,9},{9,8},{10,11... | collective-permute-start | bytes 18874376 | tf_op jit(solution)/shard_map/ppermute | solution.py:631
  149.3 2.3 %collective-permute-start.14 = (bf16[160,32,128]{2,1,0:T(8,128)(2,1)}, bf16[160,32,128]{2,1,0:T(8,128)(2,1)}, u32[]{:S(2)}, u32[]{:S(2)}) collective-permute-start(bf16[160,32,128]{2,1,0:T(8,128)(2,1)} %collective-permute-done.6.refs_0_), channel_id=1, source_target_pairs={{4,0},{5,1},{6,2},{7,3},{20,16},{21,17},{22,18},{23,19}} | collective-permute-start | bytes 3932168 | tf_op jit(solution)/shard_map/ppermute | solution.py:629
  153.4 10.7 %early_0.1.refs_3_ = f32[2048,768]{1,0:T(8,128)} custom-call(s32[4]{0:T(128)} %pad_add_fusion.meta, bf16[3,1024,768]{2,1,0:T(8,128)(2,1)} %fold.1.w_ref, bf16[3,2,2,256,1024]{4,3,2,1,0:T(8,128)(2,1)} %combine_2_0.1.refs_0_.refs_1_.refs_2_.refs_8_.refs_9_.refs_10_, bf16[3,2,2,256,1024]{4,3,2,1,0:T(8,128)(2,1)} %combine_2_0.1.refs_0_.refs_1_.refs_2_.refs_8_.refs_9_.refs_10_, ...), custom_call_target="tpu_custom_call" | custom-call | flops 1024 | bytes 1024 | tf_op jit(solution)/shard_map/early_0/pallas_call | solution.py:647
  164.1 10.7 %early_1.1.part_ref = f32[2048,768]{1,0:T(8,128)} custom-call(s32[4]{0:T(128)} %pad_add_fusion.meta, bf16[3,1024,768]{2,1,0:T(8,128)(2,1)} %fold.1.w_ref, bf16[3,2,2,256,1024]{4,3,2,1,0:T(8,128)(2,1)} %collective-permute-done.13.refs_0_.refs_1_.refs_2_.refs_11_.refs_12_.refs_13_, ...), custom_call_target="tpu_custom_call", output_to_operand_aliasing={{}: (5, {})} | custom-call | flops 1024 | bytes 1024 | tf_op jit(solution)/shard_map/early_1/pallas_call | solution.py:647
  175.7 4.4 %combine_3_0.1 = (bf16[1,2,2,256,512]{4,3,2,1,0:T(8,128)(2,1)}, s32[1]{0:T(128)}) custom-call(s32[4]{0:T(128)} %pad_add_fusion.meta, s32[4,16,16]{2,1,0:T(8,128)S(1)} %copy-done.7, bf16[2,2,2,2,256,1024]{5,4,3,2,1,0:T(8,128)(2,1)} %bitcast.65, bf16[2,2,2,2,256,1024]{5,4,3,2,1,0:T(8,128)(2,1)} %collective-permute-done.3.oth_ref, ...), custom_call_target="tpu_custom_call" | custom-call | flops 1024 | bytes 1024 | tf_op jit(solution)/shard_map/combine_3_0/pallas_call | solution.py:553
  180.1 5.0 %combine_3_2.1 = (bf16[1,2,2,256,512]{4,3,2,1,0:T(8,128)(2,1)}, s32[1]{0:T(128)}) custom-call(s32[4]{0:T(128)} %pad_add_fusion.meta, s32[4,16,16]{2,1,0:T(8,128)S(1)} %copy-done.7, bf16[2,2,2,2,256,1024]{5,4,3,2,1,0:T(8,128)(2,1)} %bitcast.66, bf16[2,2,2,2,256,1024]{5,4,3,2,1,0:T(8,128)(2,1)} %collective-permute-done.3.oth_ref, ...), custom_call_target="tpu_custom_call" | custom-call | flops 1024 | bytes 1024 | tf_op jit(solution)/shard_map/combine_3_2/pallas_call | solution.py:553
  187.2 7.9 %ints_3.1 = (bf16[4,256,1024]{2,1,0:T(8,128)(2,1)}, bf16[4,1024,256]{2,1,0:T(8,128)(2,1)}) custom-call(s32[4]{0:T(128)} %pad_add_fusion.meta, s32[4,4,16,16]{3,2,1,0:T(8,128)S(1)} %copy-done.4, bf16[160,32,128]{2,1,0:T(8,128)(2,1)} %collective-permute-done.14.refs_0_, bf16[160,32,128]{2,1,0:T(8,128)(2,1)} %collective-permute-done.2.refs_0_.refs_1_, ...), custom_call_target="tpu_custom_call" | custom-call | flops 1024 | bytes 1024 | tf_op jit(solution)/shard_map/ints_3/pallas_call | solution.py:526
  195.1 13.2 %late.1 = (bf16[1024,1024]{1,0:T(8,128)(2,1)}, f32[2048,256]{1,0:T(8,128)}) custom-call(s32[4]{0:T(128)} %pad_add_fusion.meta, bf16[4,256,1024]{2,1,0:T(8,128)(2,1)} %get-tuple-element.111.refs_0_, bf16[4,256,1024]{2,1,0:T(8,128)(2,1)} %get-tuple-element.112.refs_1_, bf16[4,256,1024]{2,1,0:T(8,128)(2,1)} %get-tuple-element.113.refs_2_, ...), custom_call_target="tpu_custom_call" | custom-call | flops 1024 | bytes 1024 | tf_op jit(solution)/shard_map/late/pallas_call | solution.py:675
  208.4 12.9 %tail.1 = f32[8,256,1,1024]{3,2,1,0:T(1,128)} custom-call(s32[4]{0:T(128)} %pad_add_fusion.meta, f32[8]{0:T(128)S(1)} %copy-done.12, f32[1]{0:T(128)S(6)} %copy.92.eps_pair, f32[256,1]{1,0:T(8,128)} %copy.61.eps_rows, f32[1,1024]{1,0:T(1,128)S(1)} %bitcast.69, f32[2048,768]{1,0:T(8,128)} %early_1.1.part_ref, f32[2048,256]{1,0:T(8,128)} %get-tuple-element.130.late_ref, ...), custom_call_target="tpu_custom_call" | custom-call | flops 1024 | bytes 1024 | tf_op jit(solution)/shard_map/tail/pallas_call | solution.py:705
  (52 shorter events, 17.7 us)
Async XLA Ops:
  6.5 4.7 %collective-permute-start = (bf16[2,2,256,1024]{3,2,1,0:T(8,128)(2,1)}, bf16[2,2,256,1024]{3,2,1,0:T(8,128)(2,1)S(1)}, u32[]{:S(2)}, u32[]{:S(2)}) collective-permute-start(bf16[2,2,256,1024]{3,2,1,0:T(8,128)(2,1)} %own_ref.3), channel_id=1, source_target_pairs={{0,1},{1,0},{2,3},{3,2},{4,5},{5,4},{6,7},{7,6},{8,9},{9,8},{10,11... | collective-permute-start | bytes 6291464 | tf_op jit(solution)/shard_map/ppermute | solution.py:463
  11.2 1.3 copy-start.3
  11.2 13.5 %collective-permute-start.3 = (bf16[2,2,2,2,256,1024]{5,4,3,2,1,0:T(8,128)(2,1)}, bf16[2,2,2,2,256,1024]{5,4,3,2,1,0:T(8,128)(2,1)}, u32[]{:S(2)}, u32[]{:S(2)}) collective-permute-start(bf16[2,2,2,2,256,1024]{5,4,3,2,1,0:T(8,128)(2,1)} %bitcast.60), channel_id=1, source_target_pairs={{0,1},{1,0},{2,3},{3,2},{4,5},{5,4},{6,7},{7,6},{8,9},{9,8},{10,11... | collective-permute-start | bytes 25165832 | tf_op jit(solution)/shard_map/ppermute | solution.py:466
  17.6 16.9 %copy-start.4 = (s32[4,4,16,16]{3,2,1,0:T(8,128)S(1)}, s32[4,4,16,16]{3,2,1,0:T(8,128)}, u32[]{:S(2)}) copy-start(s32[4,4,16,16]{3,2,1,0:T(8,128)} %mask.21) | copy-start | bytes 49156
  17.6 41.5 %copy-start = (bf16[2,2,256,1024]{3,2,1,0:T(8,128)(2,1)S(1)}, bf16[2,2,256,1024]{3,2,1,0:T(8,128)(2,1)}, u32[]{:S(2)}) copy-start(bf16[2,2,256,1024]{3,2,1,0:T(8,128)(2,1)} %own_ref.3) | copy-start | bytes 6291460
  17.6 32.3 %collective-permute-start.1 = (bf16[160,32,128]{2,1,0:T(8,128)(2,1)}, bf16[160,32,128]{2,1,0:T(8,128)(2,1)S(1)}, u32[]{:S(2)}, u32[]{:S(2)}) collective-permute-start(bf16[160,32,128]{2,1,0:T(8,128)(2,1)} %pack_int.1), channel_id=1, source_target_pairs={{0,4},{4,8},{8,12},{1,5},{5,9},{9,13},{2,6},{6,10},{10,14},{3,7},{... | collective-permute-start | bytes 3932168 | tf_op jit(solution)/shard_map/ppermute | solution.py:478
  20.9 31.9 %collective-permute-start.2 = (bf16[160,32,128]{2,1,0:T(8,128)(2,1)}, bf16[160,32,128]{2,1,0:T(8,128)(2,1)}, u32[]{:S(2)}, u32[]{:S(2)}) collective-permute-start(bf16[160,32,128]{2,1,0:T(8,128)(2,1)} %pack_int.1), channel_id=1, source_target_pairs={{4,0},{8,4},{12,8},{5,1},{9,5},{13,9},{6,2},{10,6},{14,10},{7,3},{... | collective-permute-start | bytes 3932168 | tf_op jit(solution)/shard_map/ppermute | solution.py:479
  31.2 51.9 %collective-permute-start.9 = (bf16[46,64,128]{2,1,0:T(8,128)(2,1)}, bf16[46,64,128]{2,1,0:T(8,128)(2,1)}, u32[]{:S(2)}, u32[]{:S(2)}) collective-permute-start(bf16[46,64,128]{2,1,0:T(8,128)(2,1)} %get-tuple-element.99), channel_id=1, source_target_pairs={{0,4},{4,0},{8,12},{12,8},{1,5},{5,1},{9,13},{13,9},{2,6},{6,2},{1... | collective-permute-start | bytes 2261000 | tf_op jit(solution)/shard_map/ppermute | solution.py:499
  31.2 54.9 %collective-permute-start.7 = (bf16[46,64,128]{2,1,0:T(8,128)(2,1)}, bf16[46,64,128]{2,1,0:T(8,128)(2,1)}, u32[]{:S(2)}, u32[]{:S(2)}) collective-permute-start(bf16[46,64,128]{2,1,0:T(8,128)(2,1)} %get-tuple-element.98), channel_id=1, source_target_pairs={{0,8},{4,12},{8,0},{12,4},{1,9},{5,13},{9,1},{13,5},{2,10},{6,14},... | collective-permute-start | bytes 2261000 | tf_op jit(solution)/shard_map/ppermute | solution.py:499
  39.3 2.9 %collective-permute-start.4 = (s32[1]{0:T(128)}, s32[1]{0:T(128)}, u32[]{:S(2)}, u32[]{:S(2)}) collective-permute-start(s32[1]{0:T(128)} %bitcast.27), channel_id=1, source_target_pairs={{0,16},{16,0},{1,17},{17,1},{2,18},{18,2},{3,19},{19,3},{4,20},{20... | collective-permute-start | bytes 20 | tf_op jit(solution)/shard_map/ppermute | solution.py:502
  49.9 22.5 %copy-start.5 = (bf16[160,32,128]{2,1,0:T(8,128)(2,1)}, bf16[160,32,128]{2,1,0:T(8,128)(2,1)S(1)}, u32[]{:S(2)}) copy-start(bf16[160,32,128]{2,1,0:T(8,128)(2,1)S(1)} %collective-permute-done.1.refs_1_.refs_2_) | copy-start | bytes 3932164
  52.8 72.7 %collective-permute-start.5 = (bf16[160,32,128]{2,1,0:T(8,128)(2,1)S(1)}, bf16[160,32,128]{2,1,0:T(8,128)(2,1)}, u32[]{:S(2)}, u32[]{:S(2)}) collective-permute-start(bf16[160,32,128]{2,1,0:T(8,128)(2,1)S(1)} %collective-permute-done.1.refs_1_.refs_2_), channel_id=1, source_target_pairs={{4,8},{8,12},{5,9},{9,13},{6,10},{10,14},{7,11},{11,15},{20,24},{2... | collective-permute-start | bytes 3932168 | tf_op jit(solution)/shard_map/ppermute | solution.py:504
  57.1 72.3 %collective-permute-start.6 = (bf16[160,32,128]{2,1,0:T(8,128)(2,1)}, bf16[160,32,128]{2,1,0:T(8,128)(2,1)}, u32[]{:S(2)}, u32[]{:S(2)}) collective-permute-start(bf16[160,32,128]{2,1,0:T(8,128)(2,1)} %collective-permute-done.2.refs_0_.refs_1_), channel_id=1, source_target_pairs={{4,0},{8,4},{5,1},{9,5},{6,2},{10,6},{7,3},{11,7},{20,16},{24,20},... | collective-permute-start | bytes 3932168 | tf_op jit(solution)/shard_map/ppermute | solution.py:505
  66.5 30.1 %copy-start.7 = (s32[4,16,16]{2,1,0:T(8,128)S(1)}, s32[4,16,16]{2,1,0:T(8,128)}, u32[]{:S(2)}) copy-start(s32[4,16,16]{2,1,0:T(8,128)} %mask.20) | copy-start | bytes 12292
  83.1 13.4 %collective-permute-start.10 = (bf16[46,64,128]{2,1,0:T(8,128)(2,1)}, bf16[46,64,128]{2,1,0:T(8,128)(2,1)}, u32[]{:S(2)}, u32[]{:S(2)}) collective-permute-start(bf16[46,64,128]{2,1,0:T(8,128)(2,1)} %collective-permute-done.9.near_ref), channel_id=1, source_target_pairs={{0,2},{2,0},{1,3},{3,1},{4,6},{6,4},{5,7},{7,5},{8,10},{10,8},{9,1... | collective-permute-start | bytes 2261000 | tf_op jit(solution)/shard_map/ppermute | solution.py:606
  86.2 26.5 %collective-permute-start.8 = (bf16[46,64,128]{2,1,0:T(8,128)(2,1)}, bf16[46,64,128]{2,1,0:T(8,128)(2,1)}, u32[]{:S(2)}, u32[]{:S(2)}) collective-permute-start(bf16[46,64,128]{2,1,0:T(8,128)(2,1)} %collective-permute-done.7.near_ref), channel_id=1, source_target_pairs={{0,2},{2,0},{1,3},{3,1},{4,6},{6,4},{5,7},{7,5},{8,10},{10,8},{9,1... | collective-permute-start | bytes 2261000 | tf_op jit(solution)/shard_map/ppermute | solution.py:606
  87.4 58.2 %collective-permute-start.11 = (bf16[46,64,128]{2,1,0:T(8,128)(2,1)}, bf16[46,64,128]{2,1,0:T(8,128)(2,1)}, u32[]{:S(2)}, u32[]{:S(2)}) collective-permute-start(bf16[46,64,128]{2,1,0:T(8,128)(2,1)} %get-tuple-element.109), channel_id=1, source_target_pairs={{0,12},{4,8},{8,4},{12,0},{1,13},{5,9},{9,5},{13,1},{2,14},{6,10},... | collective-permute-start | bytes 2261000 | tf_op jit(solution)/shard_map/ppermute | solution.py:499
  145.6 18.6 %collective-permute-start.13 = (bf16[3,2,2,256,1024]{4,3,2,1,0:T(8,128)(2,1)}, bf16[3,2,2,256,1024]{4,3,2,1,0:T(8,128)(2,1)}, u32[]{:S(2)}, u32[]{:S(2)}) collective-permute-start(bf16[3,2,2,256,1024]{4,3,2,1,0:T(8,128)(2,1)} %combine_2_0.1.refs_0_.refs_1_.refs_2_.refs_8_.refs_9_.refs_10_), channel_id=1, source_target_pairs={{0,1},{1,0},{2,3},{3,2},{4,5},{5,4},{6,7},{7,6},{8,9},{9,8},{10,11... | collective-permute-start | bytes 18874376 | tf_op jit(solution)/shard_map/ppermute | solution.py:631
  148.1 26.7 %collective-permute-start.12 = (bf16[46,64,128]{2,1,0:T(8,128)(2,1)}, bf16[46,64,128]{2,1,0:T(8,128)(2,1)S(1)}, u32[]{:S(2)}, u32[]{:S(2)}) collective-permute-start(bf16[46,64,128]{2,1,0:T(8,128)(2,1)} %collective-permute-done.11.near_ref), channel_id=1, source_target_pairs={{0,2},{2,0},{1,3},{3,1},{4,6},{6,4},{5,7},{7,5},{8,10},{10,8},{9,1... | collective-permute-start | bytes 2261000 | tf_op jit(solution)/shard_map/ppermute | solution.py:666
  149.3 37.8 %collective-permute-start.14 = (bf16[160,32,128]{2,1,0:T(8,128)(2,1)}, bf16[160,32,128]{2,1,0:T(8,128)(2,1)}, u32[]{:S(2)}, u32[]{:S(2)}) collective-permute-start(bf16[160,32,128]{2,1,0:T(8,128)(2,1)} %collective-permute-done.6.refs_0_), channel_id=1, source_target_pairs={{4,0},{5,1},{6,2},{7,3},{20,16},{21,17},{22,18},{23,19}} | collective-permute-start | bytes 3932168 | tf_op jit(solution)/shard_map/ppermute | solution.py:629
  151.7 35.5 %collective-permute-start.15 = (bf16[160,32,128]{2,1,0:T(8,128)(2,1)}, bf16[160,32,128]{2,1,0:T(8,128)(2,1)}, u32[]{:S(2)}, u32[]{:S(2)}) collective-permute-start(bf16[160,32,128]{2,1,0:T(8,128)(2,1)} %collective-permute-done.5.refs_1_), channel_id=1, source_target_pairs={{8,12},{9,13},{10,14},{11,15},{24,28},{25,29},{26,30},{27,31}} | collective-permute-start | bytes 3932168 | tf_op jit(solution)/shard_map/ppermute | solution.py:630
  174.8 0.9 copy-start.6
  180.1 5.4 %copy-start.9 = (bf16[1,2,2,256,512]{4,3,2,1,0:T(8,128)(2,1)S(1)}, bf16[1,2,2,256,512]{4,3,2,1,0:T(8,128)(2,1)}, u32[]{:S(2)}) copy-start(bf16[1,2,2,256,512]{4,3,2,1,0:T(8,128)(2,1)} %get-tuple-element.132.refs_0_) | copy-start | bytes 3145732
  180.1 5.5 %copy-start.10 = (f32[1024]{0:T(1024)S(1)}, f32[1024]{0:T(1024)}, u32[]{:S(2)}) copy-start(f32[1024]{0:T(1024)} %param.15) | copy-start | bytes 12292
  185.1 23.2 %collective-permute-start.17 = (bf16[1,2,2,256,512]{4,3,2,1,0:T(8,128)(2,1)}, bf16[1,2,2,256,512]{4,3,2,1,0:T(8,128)(2,1)}, u32[]{:S(2)}, u32[]{:S(2)}) collective-permute-start(bf16[1,2,2,256,512]{4,3,2,1,0:T(8,128)(2,1)} %get-tuple-element.125.refs_1_), channel_id=1, source_target_pairs={{0,1},{1,0},{2,3},{3,2},{4,5},{5,4},{6,7},{7,6},{8,9},{9,8},{10,11... | collective-permute-start | bytes 3145736 | tf_op jit(solution)/shard_map/ppermute | solution.py:671
  185.5 22.9 %collective-permute-start.16 = (bf16[1,2,2,256,512]{4,3,2,1,0:T(8,128)(2,1)S(1)}, bf16[1,2,2,256,512]{4,3,2,1,0:T(8,128)(2,1)}, u32[]{:S(2)}, u32[]{:S(2)}) collective-permute-start(bf16[1,2,2,256,512]{4,3,2,1,0:T(8,128)(2,1)S(1)} %copy-done.9), channel_id=1, source_target_pairs={{0,1},{1,0},{2,3},{3,2},{4,5},{5,4},{6,7},{7,6},{8,9},{9,8},{10,11... | collective-permute-start | bytes 3145736 | tf_op jit(solution)/shard_map/ppermute | solution.py:671
  195.1 13.3 %copy-start.12 = (f32[8]{0:T(128)S(1)}, f32[8]{0:T(128)}, u32[]{:S(2)}) copy-start(f32[8]{0:T(128)} %eps_slab.1) | copy-start | bytes 100
  208.4 12.9 %copy-start.8 = (s32[4,16,16]{2,1,0:T(8,128)S(1)}, s32[4,16,16]{2,1,0:T(8,128)}, u32[]{:S(2)}) copy-start(s32[4,16,16]{2,1,0:T(8,128)} %mask.20) | copy-start | bytes 12292

commit v8 on v7

--- a/solution.py
+++ b/solution.py
@@ -500,9 +500,6 @@
 
     packed3, over = lax.optimization_barrier((packed_amp[2], over))
     over = over + lax.ppermute(over, "frag", swap)
-    up1, down1, over = lax.optimization_barrier((up1, down1, over))
-    up2 = lax.ppermute(up1, "vir", [(1, 2), (2, 3)])
-    down2 = lax.ppermute(down1, "vir", [(1, 0), (2, 1)])
 
     int_shapes = [
         jax.ShapeDtypeStruct((4, 256, 1024), bf16),
@@ -602,7 +599,9 @@
     ints = [unpack(0, integrals, int_oth)]
     first = combine_first(0, None, None, None)
     near1, near2 = across(1, packed_amp[0]), across(2, packed_amp[1])
-    near1, ints[0], first = ready((near1, ints[0], first))
+    up1, down1, over, ints[0], first = ready((up1, down1, over, ints[0], first))
+    up2 = lax.ppermute(up1, "vir", [(1, 2), (2, 3)])
+    down2 = lax.ppermute(down1, "vir", [(1, 0), (2, 1)])
     far1, far2 = lax.ppermute(near1, "occ", swap), lax.ppermute(near2, "occ", swap)
     ints.append(unpack(1, down1, up1))
     ints[1], far1 = ready((ints[1], far1))

time: 229 us -> 229 us (level)
    ppermute x3, waiting for transfers between devices: 12.7 us -> 24.5 us  [across(): return lax.ppermute(packed, 'vir', [(s, s ^ d) for s in range(4)])]
    ppermute x1, waiting for transfers between devices: 7.07 us -> 0.01 us  [packed_shards(): up1 = lax.ppermute(packed_int, 'vir', [(0, 1), (1, 2), (2, 3)])]
    ppermute x1, waiting for transfers between devices: 2.89 us -> 0.01 us  [packed_shards(): down1 = lax.ppermute(packed_int, 'vir', [(1, 0), (2, 1), (3, 2)])]
    ppermute x1, waiting for transfers between devices: 1.19 us -> 3.74 us  [packed_shards(): lax.ppermute(near1, 'occ', swap)]
    ppermute x1, waiting for transfers between devices: 6.57 us -> 4.11 us  [packed_shards(): up2 = lax.ppermute(up1, 'vir', [(1, 2), (2, 3)])]
  transfers between devices with their start and end apart: 18 -> 18, of which waited for: 12 -> 9; matrix products, arithmetic and copies ran while one was open for 3% -> 3% of each run, Pallas kernels for 50% -> 50%
where the time goes in v8:
time: 229 us; the launch traced here: 228 us
  Pallas kernels  126 us (55%)
  waiting for transfers between devices  52 us (23%)
  starting transfers between devices  26.9 us (12%)
  between operations  16.3 us (7%)
  other arithmetic  4.25 us (2%)
  local copies, waits for them, and re-layouts  2.67 us (1%)
    pallas_call x4, Pallas kernels, unpack(): pl.pallas_call(kernel, grid_spec=pltpu.PrefetchScalarGridSpec(num_scalar_...  31.3 us
    pallas_call x5, Pallas kernels, combine(): pl.pallas_call(kernel, grid_spec=pltpu.PrefetchScalarGridSpec(num_scalar_...  27.4 us
    ppermute x3, waiting for transfers between devices, across(): return lax.ppermute(packed, 'vir', [(s, s ^ d) for s in range(4)])  24.5 us
    pallas_call x2, Pallas kernels, early(): pl.pallas_call(early_kernel, grid_spec=pltpu.PrefetchScalarGridSpec(num_s...  21.4 us
    pallas_call x1, Pallas kernels, packed_shards(): pl.pallas_call(late_kernel, grid_spec=pltpu.PrefetchScalarGridSpec(num_sc...  13.2 us
    pallas_call x1, Pallas kernels, finish(): pl.pallas_call(tail_kernel, grid_spec=pltpu.PrefetchScalarGridSpec(num_sc...  12.9 us
    ppermute x1, waiting for transfers between devices, packed_shards(): lax.ppermute(near2, 'occ', swap)  10 us
    pallas_call x1, Pallas kernels, packed_shards(): pl.pallas_call(fold_kernel, grid_spec=pltpu.PrefetchScalarGridSpec(num_sc...  8.02 us
  transfers between devices with their start and end apart: 18, of which 9 were waited for; matrix products, arithmetic and copies ran while one was open for 3% of the time, Pallas kernels for 50%

profile of v8, /device:TPU:9, one launch (start us, length us, event | category | flops | bytes accessed | tf_op | source)
XLA Modules:
  0.0 228.2 jit_solution(12310177853686962668)
XLA Ops:
  7.2 4.0 %collective-permute-done.oth_ref = bf16[2,2,256,1024]{3,2,1,0:T(8,128)(2,1)S(1)} collective-permute-done((bf16[2,2,256,1024]{3,2,1,0:T(8,128)(2,1)}, bf16[2,2,256,1024]{3,2,1,0:T(8,128)(2,1)S(1)}, u32[]{:S(2)}, u32[]{:S(2)}) %collective-permute-start) | collective-permute-done | bytes 2097184 | tf_op jit(solution)/shard_map/ppermute | solution.py:463
  12.5 5.0 %pack_int.1 = bf16[160,32,128]{2,1,0:T(8,128)(2,1)} custom-call(s32[4]{0:T(128)} %pad_add_fusion.meta, s32[4,4,16,16]{3,2,1,0:T(8,128)} %mask.21, bf16[2,2,256,1024]{3,2,1,0:T(8,128)(2,1)} %own_ref.3, bf16[2,2,256,1024]{3,2,1,0:T(8,128)(2,1)} %copy-done.3), custom_call_target="tpu_custom_call" | custom-call | flops 1024 | bytes 1024 | tf_op jit(solution)/shard_map/pack_int/pallas_call | solution.py:468
  17.6 3.3 %collective-permute-start.1 = (bf16[160,32,128]{2,1,0:T(8,128)(2,1)}, bf16[160,32,128]{2,1,0:T(8,128)(2,1)S(1)}, u32[]{:S(2)}, u32[]{:S(2)}) collective-permute-start(bf16[160,32,128]{2,1,0:T(8,128)(2,1)} %pack_int.1), channel_id=1, source_target_pairs={{0,4},{4,8},{8,12},{1,5},{5,9},{9,13},{2,6},{6,10},{10,14},{3,7},{... | collective-permute-start | bytes 3932168 | tf_op jit(solution)/shard_map/ppermute | solution.py:478
  20.9 2.2 collective-permute-start.2
  24.7 6.7 %pack_amp.1 = (bf16[46,64,128]{2,1,0:T(8,128)(2,1)}, bf16[46,64,128]{2,1,0:T(8,128)(2,1)}, bf16[46,64,128]{2,1,0:T(8,128)(2,1)}) custom-call(s32[4]{0:T(128)} %pad_add_fusion.meta, s32[4,16,16]{2,1,0:T(8,128)} %mask.20, bf16[2,2,2,2,256,1024]{5,4,3,2,1,0:T(8,128)(2,1)} %bitcast.61, bf16[2,2,2,2,256,1024]{5,4,3,2,1,0:T(8,128)(2,1)} %collective-permute-done.3.oth_ref), custom_call_target="tpu_custom_call" | custom-call | flops 1024 | bytes 1024 | tf_op jit(solution)/shard_map/pack_amp/pallas_call | solution.py:481
  31.4 2.5 %collective-permute-start.7 = (bf16[46,64,128]{2,1,0:T(8,128)(2,1)}, bf16[46,64,128]{2,1,0:T(8,128)(2,1)}, u32[]{:S(2)}, u32[]{:S(2)}) collective-permute-start(bf16[46,64,128]{2,1,0:T(8,128)(2,1)} %get-tuple-element.99), channel_id=1, source_target_pairs={{0,8},{4,12},{8,0},{12,4},{1,9},{5,13},{9,1},{13,5},{2,10},{6,14},... | collective-permute-start | bytes 2261000 | tf_op jit(solution)/shard_map/ppermute | solution.py:499
  39.5 7.4 %ints_0.1 = (bf16[4,256,1024]{2,1,0:T(8,128)(2,1)}, bf16[4,1024,256]{2,1,0:T(8,128)(2,1)}) custom-call(s32[4]{0:T(128)} %pad_add_fusion.meta, s32[4,4,16,16]{3,2,1,0:T(8,128)S(1)} %copy-done.4, bf16[2,2,256,1024]{3,2,1,0:T(8,128)(2,1)S(1)} %copy-done, bf16[2,2,256,1024]{3,2,1,0:T(8,128)(2,1)} %copy-done.3), custom_call_target="tpu_custom_call" | custom-call | flops 1024 | bytes 1024 | tf_op jit(solution)/shard_map/ints_0/pallas_call | solution.py:523
  46.9 2.0 collective-permute-start.4
  48.9 5.8 %combine_0_0.1.refs_0_ = bf16[3,2,2,256,1024]{4,3,2,1,0:T(8,128)(2,1)} custom-call(s32[4]{0:T(128)} %pad_add_fusion.meta, s32[4,16,16]{2,1,0:T(8,128)} %mask.20, bf16[2,2,2,2,256,1024]{5,4,3,2,1,0:T(8,128)(2,1)} %bitcast.62, bf16[2,2,2,2,256,1024]{5,4,3,2,1,0:T(8,128)(2,1)} %collective-permute-done.3.oth_ref), custom_call_target="tpu_custom_call" | custom-call | flops 1024 | bytes 1024 | tf_op jit(solution)/shard_map/combine_0_0/pallas_call | solution.py:550
  55.4 3.2 %collective-permute-start.5 = (bf16[160,32,128]{2,1,0:T(8,128)(2,1)S(1)}, bf16[160,32,128]{2,1,0:T(8,128)(2,1)}, u32[]{:S(2)}, u32[]{:S(2)}) collective-permute-start(bf16[160,32,128]{2,1,0:T(8,128)(2,1)S(1)} %collective-permute-done.1.refs_1_.refs_2_), channel_id=1, source_target_pairs={{4,8},{8,12},{5,9},{9,13},{6,10},{10,14},{7,11},{11,15},{20,24},{2... | collective-permute-start | bytes 3932168 | tf_op jit(solution)/shard_map/ppermute | solution.py:603
  58.6 1.9 collective-permute-start.6
  60.6 22.5 %collective-permute-done.9.near_ref = bf16[46,64,128]{2,1,0:T(8,128)(2,1)} collective-permute-done((bf16[46,64,128]{2,1,0:T(8,128)(2,1)}, bf16[46,64,128]{2,1,0:T(8,128)(2,1)}, u32[]{:S(2)}, u32[]{:S(2)}) %collective-permute-start.9) | collective-permute-done | bytes 753696 | tf_op jit(solution)/shard_map/ppermute | solution.py:499
  84.3 1.8 collective-permute-done.7.near_ref
  87.3 8.0 %ints_1.1 = (bf16[4,256,1024]{2,1,0:T(8,128)(2,1)}, bf16[4,1024,256]{2,1,0:T(8,128)(2,1)}) custom-call(s32[4]{0:T(128)} %pad_add_fusion.meta, s32[4,4,16,16]{3,2,1,0:T(8,128)S(1)} %copy-done.4, bf16[160,32,128]{2,1,0:T(8,128)(2,1)} %collective-permute-done.2.refs_0_.refs_1_, bf16[160,32,128]{2,1,0:T(8,128)(2,1)} %copy-done.5), custom_call_target="tpu_custom_call" | custom-call | flops 1024 | bytes 1024 | tf_op jit(solution)/shard_map/ints_1/pallas_call | solution.py:523
  95.3 3.7 %collective-permute-done.10.far_ref = bf16[46,64,128]{2,1,0:T(8,128)(2,1)} collective-permute-done((bf16[46,64,128]{2,1,0:T(8,128)(2,1)}, bf16[46,64,128]{2,1,0:T(8,128)(2,1)}, u32[]{:S(2)}, u32[]{:S(2)}) %collective-permute-start.10) | collective-permute-done | bytes 753696 | tf_op jit(solution)/shard_map/ppermute | solution.py:605
  99.1 6.1 %combine_1_0.1.refs_0_ = bf16[3,2,2,256,1024]{4,3,2,1,0:T(8,128)(2,1)} custom-call(s32[4]{0:T(128)} %pad_add_fusion.meta, s32[4,16,16]{2,1,0:T(8,128)S(1)} %copy-done.7, bf16[2,2,2,2,256,1024]{5,4,3,2,1,0:T(8,128)(2,1)} %bitcast.63, bf16[2,2,2,2,256,1024]{5,4,3,2,1,0:T(8,128)(2,1)} %collective-permute-done.3.oth_ref, ...), custom_call_target="tpu_custom_call", output_to_operand_aliasing={{}: (6, {})} | custom-call | flops 1024 | bytes 1024 | tf_op jit(solution)/shard_map/combine_1_0/pallas_call | solution.py:550
  105.2 10.0 %collective-permute-done.8.far_ref = bf16[46,64,128]{2,1,0:T(8,128)(2,1)} collective-permute-done((bf16[46,64,128]{2,1,0:T(8,128)(2,1)}, bf16[46,64,128]{2,1,0:T(8,128)(2,1)}, u32[]{:S(2)}, u32[]{:S(2)}) %collective-permute-start.8) | collective-permute-done | bytes 753696 | tf_op jit(solution)/shard_map/ppermute | solution.py:605
  115.2 6.1 %combine_2_0.1.refs_0_.refs_1_.refs_2_.refs_8_.refs_9_.refs_10_ = bf16[3,2,2,256,1024]{4,3,2,1,0:T(8,128)(2,1)} custom-call(s32[4]{0:T(128)} %pad_add_fusion.meta, s32[4,16,16]{2,1,0:T(8,128)S(1)} %copy-done.7, bf16[2,2,2,2,256,1024]{5,4,3,2,1,0:T(8,128)(2,1)} %bitcast.64, ...), custom_call_target="tpu_custom_call", output_to_operand_aliasing={{}: (6, {})} | custom-call | flops 1024 | bytes 1024 | tf_op jit(solution)/shard_map/combine_2_0/pallas_call | solution.py:550
  121.3 4.1 %collective-permute-done.5.refs_1_ = bf16[160,32,128]{2,1,0:T(8,128)(2,1)} collective-permute-done((bf16[160,32,128]{2,1,0:T(8,128)(2,1)S(1)}, bf16[160,32,128]{2,1,0:T(8,128)(2,1)}, u32[]{:S(2)}, u32[]{:S(2)}) %collective-permute-start.5) | collective-permute-done | bytes 1310752 | tf_op jit(solution)/shard_map/ppermute | solution.py:603
  125.5 3.9 %collective-permute-done.6.refs_0_ = bf16[160,32,128]{2,1,0:T(8,128)(2,1)} collective-permute-done((bf16[160,32,128]{2,1,0:T(8,128)(2,1)}, bf16[160,32,128]{2,1,0:T(8,128)(2,1)}, u32[]{:S(2)}, u32[]{:S(2)}) %collective-permute-start.6) | collective-permute-done | bytes 1310752 | tf_op jit(solution)/shard_map/ppermute | solution.py:604
  129.4 8.0 %ints_2.1 = (bf16[4,256,1024]{2,1,0:T(8,128)(2,1)}, bf16[4,1024,256]{2,1,0:T(8,128)(2,1)}) custom-call(s32[4]{0:T(128)} %pad_add_fusion.meta, s32[4,4,16,16]{3,2,1,0:T(8,128)S(1)} %copy-done.4, bf16[160,32,128]{2,1,0:T(8,128)(2,1)} %collective-permute-done.6.refs_0_, bf16[160,32,128]{2,1,0:T(8,128)(2,1)} %collective-permute-done.5.refs_1_), custom_call_target="tpu_custom_call" | custom-call | flops 1024 | bytes 1024 | tf_op jit(solution)/shard_map/ints_2/pallas_call | solution.py:523
  137.3 8.0 %fold.1.w_ref = bf16[3,1024,768]{2,1,0:T(8,128)(2,1)} custom-call(s32[4]{0:T(128)} %pad_add_fusion.meta, bf16[4,256,1024]{2,1,0:T(8,128)(2,1)} %get-tuple-element.109.refs_0_, bf16[4,256,1024]{2,1,0:T(8,128)(2,1)} %get-tuple-element.110.refs_1_, bf16[4,256,1024]{2,1,0:T(8,128)(2,1)} %get-tuple-element.111.refs_2_, ...), custom_call_target="tpu_custom_call" | custom-call | flops 1024 | bytes 1024 | tf_op jit(solution)/shard_map/fold/pallas_call | solution.py:613
  145.5 2.5 %collective-permute-start.13 = (bf16[3,2,2,256,1024]{4,3,2,1,0:T(8,128)(2,1)}, bf16[3,2,2,256,1024]{4,3,2,1,0:T(8,128)(2,1)}, u32[]{:S(2)}, u32[]{:S(2)}) collective-permute-start(bf16[3,2,2,256,1024]{4,3,2,1,0:T(8,128)(2,1)} %combine_2_0.1.refs_0_.refs_1_.refs_2_.refs_8_.refs_9_.refs_10_), channel_id=1, source_target_pairs={{0,1},{1,0},{2,3},{3,2},{4,5},{5,4},{6,7},{7,6},{8,9},{9,8},{10,11... | collective-permute-start | bytes 18874376 | tf_op jit(solution)/shard_map/ppermute | solution.py:630
  149.3 2.3 %collective-permute-start.14 = (bf16[160,32,128]{2,1,0:T(8,128)(2,1)}, bf16[160,32,128]{2,1,0:T(8,128)(2,1)}, u32[]{:S(2)}, u32[]{:S(2)}) collective-permute-start(bf16[160,32,128]{2,1,0:T(8,128)(2,1)} %collective-permute-done.6.refs_0_), channel_id=1, source_target_pairs={{4,0},{5,1},{6,2},{7,3},{20,16},{21,17},{22,18},{23,19}} | collective-permute-start | bytes 3932168 | tf_op jit(solution)/shard_map/ppermute | solution.py:628
  151.6 1.7 collective-permute-start.15
  153.3 10.7 %early_0.1.refs_3_ = f32[2048,768]{1,0:T(8,128)} custom-call(s32[4]{0:T(128)} %pad_add_fusion.meta, bf16[3,1024,768]{2,1,0:T(8,128)(2,1)} %fold.1.w_ref, bf16[3,2,2,256,1024]{4,3,2,1,0:T(8,128)(2,1)} %combine_2_0.1.refs_0_.refs_1_.refs_2_.refs_8_.refs_9_.refs_10_, bf16[3,2,2,256,1024]{4,3,2,1,0:T(8,128)(2,1)} %combine_2_0.1.refs_0_.refs_1_.refs_2_.refs_8_.refs_9_.refs_10_, ...), custom_call_target="tpu_custom_call" | custom-call | flops 1024 | bytes 1024 | tf_op jit(solution)/shard_map/early_0/pallas_call | solution.py:646
  164.1 10.7 %early_1.1.part_ref = f32[2048,768]{1,0:T(8,128)} custom-call(s32[4]{0:T(128)} %pad_add_fusion.meta, bf16[3,1024,768]{2,1,0:T(8,128)(2,1)} %fold.1.w_ref, bf16[3,2,2,256,1024]{4,3,2,1,0:T(8,128)(2,1)} %collective-permute-done.13.refs_0_.refs_1_.refs_2_.refs_11_.refs_12_.refs_13_, ...), custom_call_target="tpu_custom_call", output_to_operand_aliasing={{}: (5, {})} | custom-call | flops 1024 | bytes 1024 | tf_op jit(solution)/shard_map/early_1/pallas_call | solution.py:646
  175.7 4.4 %combine_3_0.1 = (bf16[1,2,2,256,512]{4,3,2,1,0:T(8,128)(2,1)}, s32[1]{0:T(128)}) custom-call(s32[4]{0:T(128)} %pad_add_fusion.meta, s32[4,16,16]{2,1,0:T(8,128)S(1)} %copy-done.7, bf16[2,2,2,2,256,1024]{5,4,3,2,1,0:T(8,128)(2,1)} %bitcast.65, bf16[2,2,2,2,256,1024]{5,4,3,2,1,0:T(8,128)(2,1)} %collective-permute-done.3.oth_ref, ...), custom_call_target="tpu_custom_call" | custom-call | flops 1024 | bytes 1024 | tf_op jit(solution)/shard_map/combine_3_0/pallas_call | solution.py:550
  180.0 5.0 %combine_3_2.1 = (bf16[1,2,2,256,512]{4,3,2,1,0:T(8,128)(2,1)}, s32[1]{0:T(128)}) custom-call(s32[4]{0:T(128)} %pad_add_fusion.meta, s32[4,16,16]{2,1,0:T(8,128)S(1)} %copy-done.7, bf16[2,2,2,2,256,1024]{5,4,3,2,1,0:T(8,128)(2,1)} %bitcast.66, bf16[2,2,2,2,256,1024]{5,4,3,2,1,0:T(8,128)(2,1)} %collective-permute-done.3.oth_ref, ...), custom_call_target="tpu_custom_call" | custom-call | flops 1024 | bytes 1024 | tf_op jit(solution)/shard_map/combine_3_2/pallas_call | solution.py:550
  187.1 7.9 %ints_3.1 = (bf16[4,256,1024]{2,1,0:T(8,128)(2,1)}, bf16[4,1024,256]{2,1,0:T(8,128)(2,1)}) custom-call(s32[4]{0:T(128)} %pad_add_fusion.meta, s32[4,4,16,16]{3,2,1,0:T(8,128)S(1)} %copy-done.4, bf16[160,32,128]{2,1,0:T(8,128)(2,1)} %collective-permute-done.14.refs_0_, bf16[160,32,128]{2,1,0:T(8,128)(2,1)} %collective-permute-done.2.refs_0_.refs_1_, ...), custom_call_target="tpu_custom_call" | custom-call | flops 1024 | bytes 1024 | tf_op jit(solution)/shard_map/ints_3/pallas_call | solution.py:523
  195.1 13.2 %late.1 = (bf16[1024,1024]{1,0:T(8,128)(2,1)}, f32[2048,256]{1,0:T(8,128)}) custom-call(s32[4]{0:T(128)} %pad_add_fusion.meta, bf16[4,256,1024]{2,1,0:T(8,128)(2,1)} %get-tuple-element.109.refs_0_, bf16[4,256,1024]{2,1,0:T(8,128)(2,1)} %get-tuple-element.110.refs_1_, bf16[4,256,1024]{2,1,0:T(8,128)(2,1)} %get-tuple-element.111.refs_2_, ...), custom_call_target="tpu_custom_call" | custom-call | flops 1024 | bytes 1024 | tf_op jit(solution)/shard_map/late/pallas_call | solution.py:674
  208.3 12.9 %tail.1 = f32[8,256,1,1024]{3,2,1,0:T(1,128)} custom-call(s32[4]{0:T(128)} %pad_add_fusion.meta, f32[8]{0:T(128)S(1)} %copy-done.12, f32[1]{0:T(128)S(6)} %copy.92.eps_pair, f32[256,1]{1,0:T(8,128)} %copy.61.eps_rows, f32[1,1024]{1,0:T(1,128)S(1)} %bitcast.69, f32[2048,768]{1,0:T(8,128)} %early_1.1.part_ref, f32[2048,256]{1,0:T(8,128)} %get-tuple-element.128.late_ref, ...), custom_call_target="tpu_custom_call" | custom-call | flops 1024 | bytes 1024 | tf_op jit(solution)/shard_map/tail/pallas_call | solution.py:704
  (52 shorter events, 14.0 us)
Async XLA Ops:
  6.5 4.7 %collective-permute-start = (bf16[2,2,256,1024]{3,2,1,0:T(8,128)(2,1)}, bf16[2,2,256,1024]{3,2,1,0:T(8,128)(2,1)S(1)}, u32[]{:S(2)}, u32[]{:S(2)}) collective-permute-start(bf16[2,2,256,1024]{3,2,1,0:T(8,128)(2,1)} %own_ref.3), channel_id=1, source_target_pairs={{0,1},{1,0},{2,3},{3,2},{4,5},{5,4},{6,7},{7,6},{8,9},{9,8},{10,11... | collective-permute-start | bytes 6291464 | tf_op jit(solution)/shard_map/ppermute | solution.py:463
  11.2 1.3 copy-start.3
  11.2 13.5 %collective-permute-start.3 = (bf16[2,2,2,2,256,1024]{5,4,3,2,1,0:T(8,128)(2,1)}, bf16[2,2,2,2,256,1024]{5,4,3,2,1,0:T(8,128)(2,1)}, u32[]{:S(2)}, u32[]{:S(2)}) collective-permute-start(bf16[2,2,2,2,256,1024]{5,4,3,2,1,0:T(8,128)(2,1)} %bitcast.60), channel_id=1, source_target_pairs={{0,1},{1,0},{2,3},{3,2},{4,5},{5,4},{6,7},{7,6},{8,9},{9,8},{10,11... | collective-permute-start | bytes 25165832 | tf_op jit(solution)/shard_map/ppermute | solution.py:466
  17.6 17.1 %copy-start.4 = (s32[4,4,16,16]{3,2,1,0:T(8,128)S(1)}, s32[4,4,16,16]{3,2,1,0:T(8,128)}, u32[]{:S(2)}) copy-start(s32[4,4,16,16]{3,2,1,0:T(8,128)} %mask.21) | copy-start | bytes 49156
  17.6 21.9 %copy-start = (bf16[2,2,256,1024]{3,2,1,0:T(8,128)(2,1)S(1)}, bf16[2,2,256,1024]{3,2,1,0:T(8,128)(2,1)}, u32[]{:S(2)}) copy-start(bf16[2,2,256,1024]{3,2,1,0:T(8,128)(2,1)} %own_ref.3) | copy-start | bytes 6291460
  17.6 37.8 %collective-permute-start.1 = (bf16[160,32,128]{2,1,0:T(8,128)(2,1)}, bf16[160,32,128]{2,1,0:T(8,128)(2,1)S(1)}, u32[]{:S(2)}, u32[]{:S(2)}) collective-permute-start(bf16[160,32,128]{2,1,0:T(8,128)(2,1)} %pack_int.1), channel_id=1, source_target_pairs={{0,4},{4,8},{8,12},{1,5},{5,9},{9,13},{2,6},{6,10},{10,14},{3,7},{... | collective-permute-start | bytes 3932168 | tf_op jit(solution)/shard_map/ppermute | solution.py:478
  20.9 34.5 %collective-permute-start.2 = (bf16[160,32,128]{2,1,0:T(8,128)(2,1)}, bf16[160,32,128]{2,1,0:T(8,128)(2,1)}, u32[]{:S(2)}, u32[]{:S(2)}) collective-permute-start(bf16[160,32,128]{2,1,0:T(8,128)(2,1)} %pack_int.1), channel_id=1, source_target_pairs={{4,0},{8,4},{12,8},{5,1},{9,5},{13,9},{6,2},{10,6},{14,10},{7,3},{... | collective-permute-start | bytes 3932168 | tf_op jit(solution)/shard_map/ppermute | solution.py:479
  31.4 51.7 %collective-permute-start.9 = (bf16[46,64,128]{2,1,0:T(8,128)(2,1)}, bf16[46,64,128]{2,1,0:T(8,128)(2,1)}, u32[]{:S(2)}, u32[]{:S(2)}) collective-permute-start(bf16[46,64,128]{2,1,0:T(8,128)(2,1)} %get-tuple-element.100), channel_id=1, source_target_pairs={{0,4},{4,0},{8,12},{12,8},{1,5},{5,1},{9,13},{13,9},{2,6},{6,2},{1... | collective-permute-start | bytes 2261000 | tf_op jit(solution)/shard_map/ppermute | solution.py:499
  31.4 54.7 %collective-permute-start.7 = (bf16[46,64,128]{2,1,0:T(8,128)(2,1)}, bf16[46,64,128]{2,1,0:T(8,128)(2,1)}, u32[]{:S(2)}, u32[]{:S(2)}) collective-permute-start(bf16[46,64,128]{2,1,0:T(8,128)(2,1)} %get-tuple-element.99), channel_id=1, source_target_pairs={{0,8},{4,12},{8,0},{12,4},{1,9},{5,13},{9,1},{13,5},{2,10},{6,14},... | collective-permute-start | bytes 2261000 | tf_op jit(solution)/shard_map/ppermute | solution.py:499
  46.9 52.1 %copy-start.7 = (s32[4,16,16]{2,1,0:T(8,128)S(1)}, s32[4,16,16]{2,1,0:T(8,128)}, u32[]{:S(2)}) copy-start(s32[4,16,16]{2,1,0:T(8,128)} %mask.20) | copy-start | bytes 12292
  46.9 7.8 %collective-permute-start.4 = (s32[1]{0:T(128)}, s32[1]{0:T(128)}, u32[]{:S(2)}, u32[]{:S(2)}) collective-permute-start(s32[1]{0:T(128)} %bitcast.27), channel_id=1, source_target_pairs={{0,16},{16,0},{1,17},{17,1},{2,18},{18,2},{3,19},{19,3},{4,20},{20... | collective-permute-start | bytes 20 | tf_op jit(solution)/shard_map/ppermute | solution.py:502
  55.4 31.9 %copy-start.5 = (bf16[160,32,128]{2,1,0:T(8,128)(2,1)}, bf16[160,32,128]{2,1,0:T(8,128)(2,1)S(1)}, u32[]{:S(2)}) copy-start(bf16[160,32,128]{2,1,0:T(8,128)(2,1)S(1)} %collective-permute-done.1.refs_1_.refs_2_) | copy-start | bytes 3932164
  55.4 70.0 %collective-permute-start.5 = (bf16[160,32,128]{2,1,0:T(8,128)(2,1)S(1)}, bf16[160,32,128]{2,1,0:T(8,128)(2,1)}, u32[]{:S(2)}, u32[]{:S(2)}) collective-permute-start(bf16[160,32,128]{2,1,0:T(8,128)(2,1)S(1)} %collective-permute-done.1.refs_1_.refs_2_), channel_id=1, source_target_pairs={{4,8},{8,12},{5,9},{9,13},{6,10},{10,14},{7,11},{11,15},{20,24},{2... | collective-permute-start | bytes 3932168 | tf_op jit(solution)/shard_map/ppermute | solution.py:603
  58.6 70.7 %collective-permute-start.6 = (bf16[160,32,128]{2,1,0:T(8,128)(2,1)}, bf16[160,32,128]{2,1,0:T(8,128)(2,1)}, u32[]{:S(2)}, u32[]{:S(2)}) collective-permute-start(bf16[160,32,128]{2,1,0:T(8,128)(2,1)} %collective-permute-done.2.refs_0_.refs_1_), channel_id=1, source_target_pairs={{4,0},{8,4},{5,1},{9,5},{6,2},{10,6},{7,3},{11,7},{20,16},{24,20},... | collective-permute-start | bytes 3932168 | tf_op jit(solution)/shard_map/ppermute | solution.py:604
  83.1 16.0 %collective-permute-start.10 = (bf16[46,64,128]{2,1,0:T(8,128)(2,1)}, bf16[46,64,128]{2,1,0:T(8,128)(2,1)}, u32[]{:S(2)}, u32[]{:S(2)}) collective-permute-start(bf16[46,64,128]{2,1,0:T(8,128)(2,1)} %collective-permute-done.9.near_ref), channel_id=1, source_target_pairs={{0,2},{2,0},{1,3},{3,1},{4,6},{6,4},{5,7},{7,5},{8,10},{10,8},{9,1... | collective-permute-start | bytes 2261000 | tf_op jit(solution)/shard_map/ppermute | solution.py:605
  86.1 29.1 %collective-permute-start.8 = (bf16[46,64,128]{2,1,0:T(8,128)(2,1)}, bf16[46,64,128]{2,1,0:T(8,128)(2,1)}, u32[]{:S(2)}, u32[]{:S(2)}) collective-permute-start(bf16[46,64,128]{2,1,0:T(8,128)(2,1)} %collective-permute-done.7.near_ref), channel_id=1, source_target_pairs={{0,2},{2,0},{1,3},{3,1},{4,6},{6,4},{5,7},{7,5},{8,10},{10,8},{9,1... | collective-permute-start | bytes 2261000 | tf_op jit(solution)/shard_map/ppermute | solution.py:605
  87.3 58.2 %collective-permute-start.11 = (bf16[46,64,128]{2,1,0:T(8,128)(2,1)}, bf16[46,64,128]{2,1,0:T(8,128)(2,1)}, u32[]{:S(2)}, u32[]{:S(2)}) collective-permute-start(bf16[46,64,128]{2,1,0:T(8,128)(2,1)} %get-tuple-element.107), channel_id=1, source_target_pairs={{0,12},{4,8},{8,4},{12,0},{1,13},{5,9},{9,5},{13,1},{2,14},{6,10},... | collective-permute-start | bytes 2261000 | tf_op jit(solution)/shard_map/ppermute | solution.py:499
  145.5 18.6 %collective-permute-start.13 = (bf16[3,2,2,256,1024]{4,3,2,1,0:T(8,128)(2,1)}, bf16[3,2,2,256,1024]{4,3,2,1,0:T(8,128)(2,1)}, u32[]{:S(2)}, u32[]{:S(2)}) collective-permute-start(bf16[3,2,2,256,1024]{4,3,2,1,0:T(8,128)(2,1)} %combine_2_0.1.refs_0_.refs_1_.refs_2_.refs_8_.refs_9_.refs_10_), channel_id=1, source_target_pairs={{0,1},{1,0},{2,3},{3,2},{4,5},{5,4},{6,7},{7,6},{8,9},{9,8},{10,11... | collective-permute-start | bytes 18874376 | tf_op jit(solution)/shard_map/ppermute | solution.py:630
  148.1 26.7 %collective-permute-start.12 = (bf16[46,64,128]{2,1,0:T(8,128)(2,1)}, bf16[46,64,128]{2,1,0:T(8,128)(2,1)S(1)}, u32[]{:S(2)}, u32[]{:S(2)}) collective-permute-start(bf16[46,64,128]{2,1,0:T(8,128)(2,1)} %collective-permute-done.11.near_ref), channel_id=1, source_target_pairs={{0,2},{2,0},{1,3},{3,1},{4,6},{6,4},{5,7},{7,5},{8,10},{10,8},{9,1... | collective-permute-start | bytes 2261000 | tf_op jit(solution)/shard_map/ppermute | solution.py:665
  149.3 37.8 %collective-permute-start.14 = (bf16[160,32,128]{2,1,0:T(8,128)(2,1)}, bf16[160,32,128]{2,1,0:T(8,128)(2,1)}, u32[]{:S(2)}, u32[]{:S(2)}) collective-permute-start(bf16[160,32,128]{2,1,0:T(8,128)(2,1)} %collective-permute-done.6.refs_0_), channel_id=1, source_target_pairs={{4,0},{5,1},{6,2},{7,3},{20,16},{21,17},{22,18},{23,19}} | collective-permute-start | bytes 3932168 | tf_op jit(solution)/shard_map/ppermute | solution.py:628
  151.6 35.5 %collective-permute-start.15 = (bf16[160,32,128]{2,1,0:T(8,128)(2,1)}, bf16[160,32,128]{2,1,0:T(8,128)(2,1)}, u32[]{:S(2)}, u32[]{:S(2)}) collective-permute-start(bf16[160,32,128]{2,1,0:T(8,128)(2,1)} %collective-permute-done.5.refs_1_), channel_id=1, source_target_pairs={{8,12},{9,13},{10,14},{11,15},{24,28},{25,29},{26,30},{27,31}} | collective-permute-start | bytes 3932168 | tf_op jit(solution)/shard_map/ppermute | solution.py:629
  174.8 0.9 copy-start.6
  180.0 5.4 %copy-start.9 = (bf16[1,2,2,256,512]{4,3,2,1,0:T(8,128)(2,1)S(1)}, bf16[1,2,2,256,512]{4,3,2,1,0:T(8,128)(2,1)}, u32[]{:S(2)}) copy-start(bf16[1,2,2,256,512]{4,3,2,1,0:T(8,128)(2,1)} %get-tuple-element.130.refs_0_) | copy-start | bytes 3145732
  180.0 5.5 %copy-start.10 = (f32[1024]{0:T(1024)S(1)}, f32[1024]{0:T(1024)}, u32[]{:S(2)}) copy-start(f32[1024]{0:T(1024)} %param.15) | copy-start | bytes 12292
  185.1 23.3 %collective-permute-start.17 = (bf16[1,2,2,256,512]{4,3,2,1,0:T(8,128)(2,1)}, bf16[1,2,2,256,512]{4,3,2,1,0:T(8,128)(2,1)}, u32[]{:S(2)}, u32[]{:S(2)}) collective-permute-start(bf16[1,2,2,256,512]{4,3,2,1,0:T(8,128)(2,1)} %get-tuple-element.123.refs_1_), channel_id=1, source_target_pairs={{0,1},{1,0},{2,3},{3,2},{4,5},{5,4},{6,7},{7,6},{8,9},{9,8},{10,11... | collective-permute-start | bytes 3145736 | tf_op jit(solution)/shard_map/ppermute | solution.py:670
  185.4 22.9 %collective-permute-start.16 = (bf16[1,2,2,256,512]{4,3,2,1,0:T(8,128)(2,1)S(1)}, bf16[1,2,2,256,512]{4,3,2,1,0:T(8,128)(2,1)}, u32[]{:S(2)}, u32[]{:S(2)}) collective-permute-start(bf16[1,2,2,256,512]{4,3,2,1,0:T(8,128)(2,1)S(1)} %copy-done.9), channel_id=1, source_target_pairs={{0,1},{1,0},{2,3},{3,2},{4,5},{5,4},{6,7},{7,6},{8,9},{9,8},{10,11... | collective-permute-start | bytes 3145736 | tf_op jit(solution)/shard_map/ppermute | solution.py:670
  195.1 13.3 %copy-start.12 = (f32[8]{0:T(128)S(1)}, f32[8]{0:T(128)}, u32[]{:S(2)}) copy-start(f32[8]{0:T(128)} %eps_slab.1) | copy-start | bytes 100
  208.3 12.9 %copy-start.8 = (s32[4,16,16]{2,1,0:T(8,128)S(1)}, s32[4,16,16]{2,1,0:T(8,128)}, u32[]{:S(2)}) copy-start(s32[4,16,16]{2,1,0:T(8,128)} %mask.20) | copy-start | bytes 12292

commit v9 on v8

--- a/solution.py
+++ b/solution.py
@@ -9,7 +9,7 @@
 
 TILE = 64
 LANES = 128
-AMP_SLOTS = 46
+AMP_SLOTS = 48
 INT_SLOTS = 160
 VMEM_LIMIT = 60 * 1024 * 1024
 NO_COST = pl.CostEstimate(flops=1024, bytes_accessed=1024, transcendentals=0)

time: 229 us -> 231 us (level)
  waiting for transfers between devices: 52 us -> 55.2 us
    ppermute x3, waiting for transfers between devices: 24.5 us -> 27.1 us  [across(): return lax.ppermute(packed, 'vir', [(s, s ^ d) for s in range(4)])]
  transfers between devices with their start and end apart: 18 -> 18, of which waited for: 9 -> 9; matrix products, arithmetic and copies ran while one was open for 3% -> 2% of each run, Pallas kernels for 50% -> 49%
where the time goes in v9:
time: 231 us; the launch traced here: 230 us
  Pallas kernels  126 us (55%)
  waiting for transfers between devices  55.2 us (24%)
  starting transfers between devices  26.2 us (11%)
  between operations  16 us (7%)
  other arithmetic  4.07 us (2%)
  local copies, waits for them, and re-layouts  2.72 us (1%)
    pallas_call x4, Pallas kernels, unpack(): pl.pallas_call(kernel, grid_spec=pltpu.PrefetchScalarGridSpec(num_scalar_...  31.3 us
    pallas_call x5, Pallas kernels, combine(): pl.pallas_call(kernel, grid_spec=pltpu.PrefetchScalarGridSpec(num_scalar_...  27.6 us
    ppermute x3, waiting for transfers between devices, across(): return lax.ppermute(packed, 'vir', [(s, s ^ d) for s in range(4)])  27.1 us
    pallas_call x2, Pallas kernels, early(): pl.pallas_call(early_kernel, grid_spec=pltpu.PrefetchScalarGridSpec(num_s...  21.4 us
    pallas_call x1, Pallas kernels, packed_shards(): pl.pallas_call(late_kernel, grid_spec=pltpu.PrefetchScalarGridSpec(num_sc...  13.2 us
    pallas_call x1, Pallas kernels, finish(): pl.pallas_call(tail_kernel, grid_spec=pltpu.PrefetchScalarGridSpec(num_sc...  12.9 us
    ppermute x1, waiting for transfers between devices, packed_shards(): lax.ppermute(near2, 'occ', swap)  10.7 us
    pallas_call x1, Pallas kernels, packed_shards(): pl.pallas_call(fold_kernel, grid_spec=pltpu.PrefetchScalarGridSpec(num_sc...  8.02 us
  transfers between devices with their start and end apart: 18, of which 9 were waited for; matrix products, arithmetic and copies ran while one was open for 2% of the time, Pallas kernels for 49%

profile of v9, /device:TPU:9, one launch (start us, length us, event | category | flops | bytes accessed | tf_op | source)
XLA Modules:
  0.0 230.4 jit_solution(11058691968661175180)
XLA Ops:
  7.2 4.0 %collective-permute-done.oth_ref = bf16[2,2,256,1024]{3,2,1,0:T(8,128)(2,1)S(1)} collective-permute-done((bf16[2,2,256,1024]{3,2,1,0:T(8,128)(2,1)}, bf16[2,2,256,1024]{3,2,1,0:T(8,128)(2,1)S(1)}, u32[]{:S(2)}, u32[]{:S(2)}) %collective-permute-start) | collective-permute-done | bytes 2097184 | tf_op jit(solution)/shard_map/ppermute | solution.py:463
  12.5 5.0 %pack_int.1 = bf16[160,32,128]{2,1,0:T(8,128)(2,1)} custom-call(s32[4]{0:T(128)} %pad_add_fusion.meta, s32[4,4,16,16]{3,2,1,0:T(8,128)} %mask.21, bf16[2,2,256,1024]{3,2,1,0:T(8,128)(2,1)} %own_ref.3, bf16[2,2,256,1024]{3,2,1,0:T(8,128)(2,1)} %copy-done.3), custom_call_target="tpu_custom_call" | custom-call | flops 1024 | bytes 1024 | tf_op jit(solution)/shard_map/pack_int/pallas_call | solution.py:468
  17.6 3.3 %collective-permute-start.1 = (bf16[160,32,128]{2,1,0:T(8,128)(2,1)}, bf16[160,32,128]{2,1,0:T(8,128)(2,1)S(1)}, u32[]{:S(2)}, u32[]{:S(2)}) collective-permute-start(bf16[160,32,128]{2,1,0:T(8,128)(2,1)} %pack_int.1), channel_id=1, source_target_pairs={{0,4},{4,8},{8,12},{1,5},{5,9},{9,13},{2,6},{6,10},{10,14},{3,7},{... | collective-permute-start | bytes 3932168 | tf_op jit(solution)/shard_map/ppermute | solution.py:478
  20.9 2.2 collective-permute-start.2
  24.7 6.7 %pack_amp.1 = (bf16[48,64,128]{2,1,0:T(8,128)(2,1)}, bf16[48,64,128]{2,1,0:T(8,128)(2,1)}, bf16[48,64,128]{2,1,0:T(8,128)(2,1)}) custom-call(s32[4]{0:T(128)} %pad_add_fusion.meta, s32[4,16,16]{2,1,0:T(8,128)} %mask.20, bf16[2,2,2,2,256,1024]{5,4,3,2,1,0:T(8,128)(2,1)} %bitcast.61, bf16[2,2,2,2,256,1024]{5,4,3,2,1,0:T(8,128)(2,1)} %collective-permute-done.3.oth_ref), custom_call_target="tpu_custom_call" | custom-call | flops 1024 | bytes 1024 | tf_op jit(solution)/shard_map/pack_amp/pallas_call | solution.py:481
  31.4 2.5 %collective-permute-start.7 = (bf16[48,64,128]{2,1,0:T(8,128)(2,1)}, bf16[48,64,128]{2,1,0:T(8,128)(2,1)}, u32[]{:S(2)}, u32[]{:S(2)}) collective-permute-start(bf16[48,64,128]{2,1,0:T(8,128)(2,1)} %get-tuple-element.99), channel_id=1, source_target_pairs={{0,8},{4,12},{8,0},{12,4},{1,9},{5,13},{9,1},{13,5},{2,10},{6,14},... | collective-permute-start | bytes 2359304 | tf_op jit(solution)/shard_map/ppermute | solution.py:499
  39.1 7.4 %ints_0.1 = (bf16[4,256,1024]{2,1,0:T(8,128)(2,1)}, bf16[4,1024,256]{2,1,0:T(8,128)(2,1)}) custom-call(s32[4]{0:T(128)} %pad_add_fusion.meta, s32[4,4,16,16]{3,2,1,0:T(8,128)S(1)} %copy-done.4, bf16[2,2,256,1024]{3,2,1,0:T(8,128)(2,1)S(1)} %copy-done, bf16[2,2,256,1024]{3,2,1,0:T(8,128)(2,1)} %copy-done.3), custom_call_target="tpu_custom_call" | custom-call | flops 1024 | bytes 1024 | tf_op jit(solution)/shard_map/ints_0/pallas_call | solution.py:523
  46.6 2.0 collective-permute-start.4
  48.5 5.8 %combine_0_0.1.refs_0_ = bf16[3,2,2,256,1024]{4,3,2,1,0:T(8,128)(2,1)} custom-call(s32[4]{0:T(128)} %pad_add_fusion.meta, s32[4,16,16]{2,1,0:T(8,128)} %mask.20, bf16[2,2,2,2,256,1024]{5,4,3,2,1,0:T(8,128)(2,1)} %bitcast.62, bf16[2,2,2,2,256,1024]{5,4,3,2,1,0:T(8,128)(2,1)} %collective-permute-done.3.oth_ref), custom_call_target="tpu_custom_call" | custom-call | flops 1024 | bytes 1024 | tf_op jit(solution)/shard_map/combine_0_0/pallas_call | solution.py:550
  55.0 3.2 %collective-permute-start.5 = (bf16[160,32,128]{2,1,0:T(8,128)(2,1)S(1)}, bf16[160,32,128]{2,1,0:T(8,128)(2,1)}, u32[]{:S(2)}, u32[]{:S(2)}) collective-permute-start(bf16[160,32,128]{2,1,0:T(8,128)(2,1)S(1)} %collective-permute-done.1.refs_1_.refs_2_), channel_id=1, source_target_pairs={{4,8},{8,12},{5,9},{9,13},{6,10},{10,14},{7,11},{11,15},{20,24},{2... | collective-permute-start | bytes 3932168 | tf_op jit(solution)/shard_map/ppermute | solution.py:603
  58.2 1.9 collective-permute-start.6
  60.1 24.4 %collective-permute-done.9.near_ref = bf16[48,64,128]{2,1,0:T(8,128)(2,1)} collective-permute-done((bf16[48,64,128]{2,1,0:T(8,128)(2,1)}, bf16[48,64,128]{2,1,0:T(8,128)(2,1)}, u32[]{:S(2)}, u32[]{:S(2)}) %collective-permute-start.9) | collective-permute-done | bytes 786464 | tf_op jit(solution)/shard_map/ppermute | solution.py:499
  85.7 1.8 collective-permute-done.7.near_ref
  88.7 8.0 %ints_1.1 = (bf16[4,256,1024]{2,1,0:T(8,128)(2,1)}, bf16[4,1024,256]{2,1,0:T(8,128)(2,1)}) custom-call(s32[4]{0:T(128)} %pad_add_fusion.meta, s32[4,4,16,16]{3,2,1,0:T(8,128)S(1)} %copy-done.4, bf16[160,32,128]{2,1,0:T(8,128)(2,1)} %collective-permute-done.2.refs_0_.refs_1_, bf16[160,32,128]{2,1,0:T(8,128)(2,1)} %copy-done.5), custom_call_target="tpu_custom_call" | custom-call | flops 1024 | bytes 1024 | tf_op jit(solution)/shard_map/ints_1/pallas_call | solution.py:523
  96.7 4.4 %collective-permute-done.10.far_ref = bf16[48,64,128]{2,1,0:T(8,128)(2,1)} collective-permute-done((bf16[48,64,128]{2,1,0:T(8,128)(2,1)}, bf16[48,64,128]{2,1,0:T(8,128)(2,1)}, u32[]{:S(2)}, u32[]{:S(2)}) %collective-permute-start.10) | collective-permute-done | bytes 786464 | tf_op jit(solution)/shard_map/ppermute | solution.py:605
  101.2 6.1 %combine_1_0.1.refs_0_ = bf16[3,2,2,256,1024]{4,3,2,1,0:T(8,128)(2,1)} custom-call(s32[4]{0:T(128)} %pad_add_fusion.meta, s32[4,16,16]{2,1,0:T(8,128)S(1)} %copy-done.7, bf16[2,2,2,2,256,1024]{5,4,3,2,1,0:T(8,128)(2,1)} %bitcast.63, bf16[2,2,2,2,256,1024]{5,4,3,2,1,0:T(8,128)(2,1)} %collective-permute-done.3.oth_ref, ...), custom_call_target="tpu_custom_call", output_to_operand_aliasing={{}: (6, {})} | custom-call | flops 1024 | bytes 1024 | tf_op jit(solution)/shard_map/combine_1_0/pallas_call | solution.py:550
  107.3 10.7 %collective-permute-done.8.far_ref = bf16[48,64,128]{2,1,0:T(8,128)(2,1)} collective-permute-done((bf16[48,64,128]{2,1,0:T(8,128)(2,1)}, bf16[48,64,128]{2,1,0:T(8,128)(2,1)}, u32[]{:S(2)}, u32[]{:S(2)}) %collective-permute-start.8) | collective-permute-done | bytes 786464 | tf_op jit(solution)/shard_map/ppermute | solution.py:605
  118.0 6.1 %combine_2_0.1.refs_0_.refs_1_.refs_2_.refs_8_.refs_9_.refs_10_ = bf16[3,2,2,256,1024]{4,3,2,1,0:T(8,128)(2,1)} custom-call(s32[4]{0:T(128)} %pad_add_fusion.meta, s32[4,16,16]{2,1,0:T(8,128)S(1)} %copy-done.7, bf16[2,2,2,2,256,1024]{5,4,3,2,1,0:T(8,128)(2,1)} %bitcast.64, ...), custom_call_target="tpu_custom_call", output_to_operand_aliasing={{}: (6, {})} | custom-call | flops 1024 | bytes 1024 | tf_op jit(solution)/shard_map/combine_2_0/pallas_call | solution.py:550
  124.2 3.4 %collective-permute-done.5.refs_1_ = bf16[160,32,128]{2,1,0:T(8,128)(2,1)} collective-permute-done((bf16[160,32,128]{2,1,0:T(8,128)(2,1)S(1)}, bf16[160,32,128]{2,1,0:T(8,128)(2,1)}, u32[]{:S(2)}, u32[]{:S(2)}) %collective-permute-start.5) | collective-permute-done | bytes 1310752 | tf_op jit(solution)/shard_map/ppermute | solution.py:603
  127.6 3.9 %collective-permute-done.6.refs_0_ = bf16[160,32,128]{2,1,0:T(8,128)(2,1)} collective-permute-done((bf16[160,32,128]{2,1,0:T(8,128)(2,1)}, bf16[160,32,128]{2,1,0:T(8,128)(2,1)}, u32[]{:S(2)}, u32[]{:S(2)}) %collective-permute-start.6) | collective-permute-done | bytes 1310752 | tf_op jit(solution)/shard_map/ppermute | solution.py:604
  131.5 8.0 %ints_2.1 = (bf16[4,256,1024]{2,1,0:T(8,128)(2,1)}, bf16[4,1024,256]{2,1,0:T(8,128)(2,1)}) custom-call(s32[4]{0:T(128)} %pad_add_fusion.meta, s32[4,4,16,16]{3,2,1,0:T(8,128)S(1)} %copy-done.4, bf16[160,32,128]{2,1,0:T(8,128)(2,1)} %collective-permute-done.6.refs_0_, bf16[160,32,128]{2,1,0:T(8,128)(2,1)} %collective-permute-done.5.refs_1_), custom_call_target="tpu_custom_call" | custom-call | flops 1024 | bytes 1024 | tf_op jit(solution)/shard_map/ints_2/pallas_call | solution.py:523
  139.4 8.0 %fold.1.w_ref = bf16[3,1024,768]{2,1,0:T(8,128)(2,1)} custom-call(s32[4]{0:T(128)} %pad_add_fusion.meta, bf16[4,256,1024]{2,1,0:T(8,128)(2,1)} %get-tuple-element.109.refs_0_, bf16[4,256,1024]{2,1,0:T(8,128)(2,1)} %get-tuple-element.110.refs_1_, bf16[4,256,1024]{2,1,0:T(8,128)(2,1)} %get-tuple-element.111.refs_2_, ...), custom_call_target="tpu_custom_call" | custom-call | flops 1024 | bytes 1024 | tf_op jit(solution)/shard_map/fold/pallas_call | solution.py:613
  148.3 1.8 collective-permute-start.13
  151.4 2.3 %collective-permute-start.14 = (bf16[160,32,128]{2,1,0:T(8,128)(2,1)}, bf16[160,32,128]{2,1,0:T(8,128)(2,1)}, u32[]{:S(2)}, u32[]{:S(2)}) collective-permute-start(bf16[160,32,128]{2,1,0:T(8,128)(2,1)} %collective-permute-done.6.refs_0_), channel_id=1, source_target_pairs={{4,0},{5,1},{6,2},{7,3},{20,16},{21,17},{22,18},{23,19}} | collective-permute-start | bytes 3932168 | tf_op jit(solution)/shard_map/ppermute | solution.py:628
  153.7 1.7 collective-permute-start.15
  155.4 10.7 %early_0.1.refs_3_ = f32[2048,768]{1,0:T(8,128)} custom-call(s32[4]{0:T(128)} %pad_add_fusion.meta, bf16[3,1024,768]{2,1,0:T(8,128)(2,1)} %fold.1.w_ref, bf16[3,2,2,256,1024]{4,3,2,1,0:T(8,128)(2,1)} %combine_2_0.1.refs_0_.refs_1_.refs_2_.refs_8_.refs_9_.refs_10_, bf16[3,2,2,256,1024]{4,3,2,1,0:T(8,128)(2,1)} %combine_2_0.1.refs_0_.refs_1_.refs_2_.refs_8_.refs_9_.refs_10_, ...), custom_call_target="tpu_custom_call" | custom-call | flops 1024 | bytes 1024 | tf_op jit(solution)/shard_map/early_0/pallas_call | solution.py:646
  166.2 10.7 %early_1.1.part_ref = f32[2048,768]{1,0:T(8,128)} custom-call(s32[4]{0:T(128)} %pad_add_fusion.meta, bf16[3,1024,768]{2,1,0:T(8,128)(2,1)} %fold.1.w_ref, bf16[3,2,2,256,1024]{4,3,2,1,0:T(8,128)(2,1)} %collective-permute-done.13.refs_0_.refs_1_.refs_2_.refs_11_.refs_12_.refs_13_, ...), custom_call_target="tpu_custom_call", output_to_operand_aliasing={{}: (5, {})} | custom-call | flops 1024 | bytes 1024 | tf_op jit(solution)/shard_map/early_1/pallas_call | solution.py:646
  177.8 4.4 %combine_3_0.1 = (bf16[1,2,2,256,512]{4,3,2,1,0:T(8,128)(2,1)}, s32[1]{0:T(128)}) custom-call(s32[4]{0:T(128)} %pad_add_fusion.meta, s32[4,16,16]{2,1,0:T(8,128)S(1)} %copy-done.7, bf16[2,2,2,2,256,1024]{5,4,3,2,1,0:T(8,128)(2,1)} %bitcast.65, bf16[2,2,2,2,256,1024]{5,4,3,2,1,0:T(8,128)(2,1)} %collective-permute-done.3.oth_ref, ...), custom_call_target="tpu_custom_call" | custom-call | flops 1024 | bytes 1024 | tf_op jit(solution)/shard_map/combine_3_0/pallas_call | solution.py:550
  182.2 5.1 %combine_3_2.1 = (bf16[1,2,2,256,512]{4,3,2,1,0:T(8,128)(2,1)}, s32[1]{0:T(128)}) custom-call(s32[4]{0:T(128)} %pad_add_fusion.meta, s32[4,16,16]{2,1,0:T(8,128)S(1)} %copy-done.7, bf16[2,2,2,2,256,1024]{5,4,3,2,1,0:T(8,128)(2,1)} %bitcast.66, bf16[2,2,2,2,256,1024]{5,4,3,2,1,0:T(8,128)(2,1)} %collective-permute-done.3.oth_ref, ...), custom_call_target="tpu_custom_call" | custom-call | flops 1024 | bytes 1024 | tf_op jit(solution)/shard_map/combine_3_2/pallas_call | solution.py:550
  189.4 7.9 %ints_3.1 = (bf16[4,256,1024]{2,1,0:T(8,128)(2,1)}, bf16[4,1024,256]{2,1,0:T(8,128)(2,1)}) custom-call(s32[4]{0:T(128)} %pad_add_fusion.meta, s32[4,4,16,16]{3,2,1,0:T(8,128)S(1)} %copy-done.4, bf16[160,32,128]{2,1,0:T(8,128)(2,1)} %collective-permute-done.14.refs_0_, bf16[160,32,128]{2,1,0:T(8,128)(2,1)} %collective-permute-done.2.refs_0_.refs_1_, ...), custom_call_target="tpu_custom_call" | custom-call | flops 1024 | bytes 1024 | tf_op jit(solution)/shard_map/ints_3/pallas_call | solution.py:523
  197.3 13.2 %late.1 = (bf16[1024,1024]{1,0:T(8,128)(2,1)}, f32[2048,256]{1,0:T(8,128)}) custom-call(s32[4]{0:T(128)} %pad_add_fusion.meta, bf16[4,256,1024]{2,1,0:T(8,128)(2,1)} %get-tuple-element.109.refs_0_, bf16[4,256,1024]{2,1,0:T(8,128)(2,1)} %get-tuple-element.110.refs_1_, bf16[4,256,1024]{2,1,0:T(8,128)(2,1)} %get-tuple-element.111.refs_2_, ...), custom_call_target="tpu_custom_call" | custom-call | flops 1024 | bytes 1024 | tf_op jit(solution)/shard_map/late/pallas_call | solution.py:674
  210.6 12.9 %tail.1 = f32[8,256,1,1024]{3,2,1,0:T(1,128)} custom-call(s32[4]{0:T(128)} %pad_add_fusion.meta, f32[8]{0:T(128)S(1)} %copy-done.12, f32[1]{0:T(128)S(6)} %copy.92.eps_pair, f32[256,1]{1,0:T(8,128)} %copy.61.eps_rows, f32[1,1024]{1,0:T(1,128)S(1)} %bitcast.69, f32[2048,768]{1,0:T(8,128)} %early_1.1.part_ref, f32[2048,256]{1,0:T(8,128)} %get-tuple-element.128.late_ref, ...), custom_call_target="tpu_custom_call" | custom-call | flops 1024 | bytes 1024 | tf_op jit(solution)/shard_map/tail/pallas_call | solution.py:704
  (52 shorter events, 14.6 us)
Async XLA Ops:
  6.5 4.7 %collective-permute-start = (bf16[2,2,256,1024]{3,2,1,0:T(8,128)(2,1)}, bf16[2,2,256,1024]{3,2,1,0:T(8,128)(2,1)S(1)}, u32[]{:S(2)}, u32[]{:S(2)}) collective-permute-start(bf16[2,2,256,1024]{3,2,1,0:T(8,128)(2,1)} %own_ref.3), channel_id=1, source_target_pairs={{0,1},{1,0},{2,3},{3,2},{4,5},{5,4},{6,7},{7,6},{8,9},{9,8},{10,11... | collective-permute-start | bytes 6291464 | tf_op jit(solution)/shard_map/ppermute | solution.py:463
  11.2 1.3 copy-start.3
  11.2 13.5 %collective-permute-start.3 = (bf16[2,2,2,2,256,1024]{5,4,3,2,1,0:T(8,128)(2,1)}, bf16[2,2,2,2,256,1024]{5,4,3,2,1,0:T(8,128)(2,1)}, u32[]{:S(2)}, u32[]{:S(2)}) collective-permute-start(bf16[2,2,2,2,256,1024]{5,4,3,2,1,0:T(8,128)(2,1)} %bitcast.60), channel_id=1, source_target_pairs={{0,1},{1,0},{2,3},{3,2},{4,5},{5,4},{6,7},{7,6},{8,9},{9,8},{10,11... | collective-permute-start | bytes 25165832 | tf_op jit(solution)/shard_map/ppermute | solution.py:466
  17.6 17.1 %copy-start.4 = (s32[4,4,16,16]{3,2,1,0:T(8,128)S(1)}, s32[4,4,16,16]{3,2,1,0:T(8,128)}, u32[]{:S(2)}) copy-start(s32[4,4,16,16]{3,2,1,0:T(8,128)} %mask.21) | copy-start | bytes 49156
  17.6 21.5 %copy-start = (bf16[2,2,256,1024]{3,2,1,0:T(8,128)(2,1)S(1)}, bf16[2,2,256,1024]{3,2,1,0:T(8,128)(2,1)}, u32[]{:S(2)}) copy-start(bf16[2,2,256,1024]{3,2,1,0:T(8,128)(2,1)} %own_ref.3) | copy-start | bytes 6291460
  17.6 37.4 %collective-permute-start.1 = (bf16[160,32,128]{2,1,0:T(8,128)(2,1)}, bf16[160,32,128]{2,1,0:T(8,128)(2,1)S(1)}, u32[]{:S(2)}, u32[]{:S(2)}) collective-permute-start(bf16[160,32,128]{2,1,0:T(8,128)(2,1)} %pack_int.1), channel_id=1, source_target_pairs={{0,4},{4,8},{8,12},{1,5},{5,9},{9,13},{2,6},{6,10},{10,14},{3,7},{... | collective-permute-start | bytes 3932168 | tf_op jit(solution)/shard_map/ppermute | solution.py:478
  20.9 34.1 %collective-permute-start.2 = (bf16[160,32,128]{2,1,0:T(8,128)(2,1)}, bf16[160,32,128]{2,1,0:T(8,128)(2,1)}, u32[]{:S(2)}, u32[]{:S(2)}) collective-permute-start(bf16[160,32,128]{2,1,0:T(8,128)(2,1)} %pack_int.1), channel_id=1, source_target_pairs={{4,0},{8,4},{12,8},{5,1},{9,5},{13,9},{6,2},{10,6},{14,10},{7,3},{... | collective-permute-start | bytes 3932168 | tf_op jit(solution)/shard_map/ppermute | solution.py:479
  31.4 53.1 %collective-permute-start.9 = (bf16[48,64,128]{2,1,0:T(8,128)(2,1)}, bf16[48,64,128]{2,1,0:T(8,128)(2,1)}, u32[]{:S(2)}, u32[]{:S(2)}) collective-permute-start(bf16[48,64,128]{2,1,0:T(8,128)(2,1)} %get-tuple-element.100), channel_id=1, source_target_pairs={{0,4},{4,0},{8,12},{12,8},{1,5},{5,1},{9,13},{13,9},{2,6},{6,2},{1... | collective-permute-start | bytes 2359304 | tf_op jit(solution)/shard_map/ppermute | solution.py:499
  31.4 56.1 %collective-permute-start.7 = (bf16[48,64,128]{2,1,0:T(8,128)(2,1)}, bf16[48,64,128]{2,1,0:T(8,128)(2,1)}, u32[]{:S(2)}, u32[]{:S(2)}) collective-permute-start(bf16[48,64,128]{2,1,0:T(8,128)(2,1)} %get-tuple-element.99), channel_id=1, source_target_pairs={{0,8},{4,12},{8,0},{12,4},{1,9},{5,13},{9,1},{13,5},{2,10},{6,14},... | collective-permute-start | bytes 2359304 | tf_op jit(solution)/shard_map/ppermute | solution.py:499
  46.6 54.6 %copy-start.7 = (s32[4,16,16]{2,1,0:T(8,128)S(1)}, s32[4,16,16]{2,1,0:T(8,128)}, u32[]{:S(2)}) copy-start(s32[4,16,16]{2,1,0:T(8,128)} %mask.20) | copy-start | bytes 12292
  46.6 7.8 %collective-permute-start.4 = (s32[1]{0:T(128)}, s32[1]{0:T(128)}, u32[]{:S(2)}, u32[]{:S(2)}) collective-permute-start(s32[1]{0:T(128)} %bitcast.27), channel_id=1, source_target_pairs={{0,16},{16,0},{1,17},{17,1},{2,18},{18,2},{3,19},{19,3},{4,20},{20... | collective-permute-start | bytes 20 | tf_op jit(solution)/shard_map/ppermute | solution.py:502
  55.0 33.8 %copy-start.5 = (bf16[160,32,128]{2,1,0:T(8,128)(2,1)}, bf16[160,32,128]{2,1,0:T(8,128)(2,1)S(1)}, u32[]{:S(2)}) copy-start(bf16[160,32,128]{2,1,0:T(8,128)(2,1)S(1)} %collective-permute-done.1.refs_1_.refs_2_) | copy-start | bytes 3932164
  55.0 72.6 %collective-permute-start.5 = (bf16[160,32,128]{2,1,0:T(8,128)(2,1)S(1)}, bf16[160,32,128]{2,1,0:T(8,128)(2,1)}, u32[]{:S(2)}, u32[]{:S(2)}) collective-permute-start(bf16[160,32,128]{2,1,0:T(8,128)(2,1)S(1)} %collective-permute-done.1.refs_1_.refs_2_), channel_id=1, source_target_pairs={{4,8},{8,12},{5,9},{9,13},{6,10},{10,14},{7,11},{11,15},{20,24},{2... | collective-permute-start | bytes 3932168 | tf_op jit(solution)/shard_map/ppermute | solution.py:603
  58.2 73.2 %collective-permute-start.6 = (bf16[160,32,128]{2,1,0:T(8,128)(2,1)}, bf16[160,32,128]{2,1,0:T(8,128)(2,1)}, u32[]{:S(2)}, u32[]{:S(2)}) collective-permute-start(bf16[160,32,128]{2,1,0:T(8,128)(2,1)} %collective-permute-done.2.refs_0_.refs_1_), channel_id=1, source_target_pairs={{4,0},{8,4},{5,1},{9,5},{6,2},{10,6},{7,3},{11,7},{20,16},{24,20},... | collective-permute-start | bytes 3932168 | tf_op jit(solution)/shard_map/ppermute | solution.py:604
  84.5 16.7 %collective-permute-start.10 = (bf16[48,64,128]{2,1,0:T(8,128)(2,1)}, bf16[48,64,128]{2,1,0:T(8,128)(2,1)}, u32[]{:S(2)}, u32[]{:S(2)}) collective-permute-start(bf16[48,64,128]{2,1,0:T(8,128)(2,1)} %collective-permute-done.9.near_ref), channel_id=1, source_target_pairs={{0,2},{2,0},{1,3},{3,1},{4,6},{6,4},{5,7},{7,5},{8,10},{10,8},{9,1... | collective-permute-start | bytes 2359304 | tf_op jit(solution)/shard_map/ppermute | solution.py:605
  87.5 30.5 %collective-permute-start.8 = (bf16[48,64,128]{2,1,0:T(8,128)(2,1)}, bf16[48,64,128]{2,1,0:T(8,128)(2,1)}, u32[]{:S(2)}, u32[]{:S(2)}) collective-permute-start(bf16[48,64,128]{2,1,0:T(8,128)(2,1)} %collective-permute-done.7.near_ref), channel_id=1, source_target_pairs={{0,2},{2,0},{1,3},{3,1},{4,6},{6,4},{5,7},{7,5},{8,10},{10,8},{9,1... | collective-permute-start | bytes 2359304 | tf_op jit(solution)/shard_map/ppermute | solution.py:605
  88.7 59.6 %collective-permute-start.11 = (bf16[48,64,128]{2,1,0:T(8,128)(2,1)}, bf16[48,64,128]{2,1,0:T(8,128)(2,1)}, u32[]{:S(2)}, u32[]{:S(2)}) collective-permute-start(bf16[48,64,128]{2,1,0:T(8,128)(2,1)} %get-tuple-element.107), channel_id=1, source_target_pairs={{0,12},{4,8},{8,4},{12,0},{1,13},{5,9},{9,5},{13,1},{2,14},{6,10},... | collective-permute-start | bytes 2359304 | tf_op jit(solution)/shard_map/ppermute | solution.py:499
  148.3 17.9 %collective-permute-start.13 = (bf16[3,2,2,256,1024]{4,3,2,1,0:T(8,128)(2,1)}, bf16[3,2,2,256,1024]{4,3,2,1,0:T(8,128)(2,1)}, u32[]{:S(2)}, u32[]{:S(2)}) collective-permute-start(bf16[3,2,2,256,1024]{4,3,2,1,0:T(8,128)(2,1)} %combine_2_0.1.refs_0_.refs_1_.refs_2_.refs_8_.refs_9_.refs_10_), channel_id=1, source_target_pairs={{0,1},{1,0},{2,3},{3,2},{4,5},{5,4},{6,7},{7,6},{8,9},{9,8},{10,11... | collective-permute-start | bytes 18874376 | tf_op jit(solution)/shard_map/ppermute | solution.py:630
  150.2 26.7 %collective-permute-start.12 = (bf16[48,64,128]{2,1,0:T(8,128)(2,1)}, bf16[48,64,128]{2,1,0:T(8,128)(2,1)S(1)}, u32[]{:S(2)}, u32[]{:S(2)}) collective-permute-start(bf16[48,64,128]{2,1,0:T(8,128)(2,1)} %collective-permute-done.11.near_ref), channel_id=1, source_target_pairs={{0,2},{2,0},{1,3},{3,1},{4,6},{6,4},{5,7},{7,5},{8,10},{10,8},{9,1... | collective-permute-start | bytes 2359304 | tf_op jit(solution)/shard_map/ppermute | solution.py:665
  151.4 38.0 %collective-permute-start.14 = (bf16[160,32,128]{2,1,0:T(8,128)(2,1)}, bf16[160,32,128]{2,1,0:T(8,128)(2,1)}, u32[]{:S(2)}, u32[]{:S(2)}) collective-permute-start(bf16[160,32,128]{2,1,0:T(8,128)(2,1)} %collective-permute-done.6.refs_0_), channel_id=1, source_target_pairs={{4,0},{5,1},{6,2},{7,3},{20,16},{21,17},{22,18},{23,19}} | collective-permute-start | bytes 3932168 | tf_op jit(solution)/shard_map/ppermute | solution.py:628
  153.7 35.6 %collective-permute-start.15 = (bf16[160,32,128]{2,1,0:T(8,128)(2,1)}, bf16[160,32,128]{2,1,0:T(8,128)(2,1)}, u32[]{:S(2)}, u32[]{:S(2)}) collective-permute-start(bf16[160,32,128]{2,1,0:T(8,128)(2,1)} %collective-permute-done.5.refs_1_), channel_id=1, source_target_pairs={{8,12},{9,13},{10,14},{11,15},{24,28},{25,29},{26,30},{27,31}} | collective-permute-start | bytes 3932168 | tf_op jit(solution)/shard_map/ppermute | solution.py:629
  176.9 0.9 copy-start.6
  182.2 5.5 %copy-start.9 = (bf16[1,2,2,256,512]{4,3,2,1,0:T(8,128)(2,1)S(1)}, bf16[1,2,2,256,512]{4,3,2,1,0:T(8,128)(2,1)}, u32[]{:S(2)}) copy-start(bf16[1,2,2,256,512]{4,3,2,1,0:T(8,128)(2,1)} %get-tuple-element.130.refs_0_) | copy-start | bytes 3145732
  182.2 5.6 %copy-start.10 = (f32[1024]{0:T(1024)S(1)}, f32[1024]{0:T(1024)}, u32[]{:S(2)}) copy-start(f32[1024]{0:T(1024)} %param.15) | copy-start | bytes 12292
  187.3 23.3 %collective-permute-start.17 = (bf16[1,2,2,256,512]{4,3,2,1,0:T(8,128)(2,1)}, bf16[1,2,2,256,512]{4,3,2,1,0:T(8,128)(2,1)}, u32[]{:S(2)}, u32[]{:S(2)}) collective-permute-start(bf16[1,2,2,256,512]{4,3,2,1,0:T(8,128)(2,1)} %get-tuple-element.123.refs_1_), channel_id=1, source_target_pairs={{0,1},{1,0},{2,3},{3,2},{4,5},{5,4},{6,7},{7,6},{8,9},{9,8},{10,11... | collective-permute-start | bytes 3145736 | tf_op jit(solution)/shard_map/ppermute | solution.py:670
  187.6 22.9 %collective-permute-start.16 = (bf16[1,2,2,256,512]{4,3,2,1,0:T(8,128)(2,1)S(1)}, bf16[1,2,2,256,512]{4,3,2,1,0:T(8,128)(2,1)}, u32[]{:S(2)}, u32[]{:S(2)}) collective-permute-start(bf16[1,2,2,256,512]{4,3,2,1,0:T(8,128)(2,1)S(1)} %copy-done.9), channel_id=1, source_target_pairs={{0,1},{1,0},{2,3},{3,2},{4,5},{5,4},{6,7},{7,6},{8,9},{9,8},{10,11... | collective-permute-start | bytes 3145736 | tf_op jit(solution)/shard_map/ppermute | solution.py:670
  197.3 13.3 %copy-start.12 = (f32[8]{0:T(128)S(1)}, f32[8]{0:T(128)}, u32[]{:S(2)}) copy-start(f32[8]{0:T(128)} %eps_slab.1) | copy-start | bytes 100
  210.6 12.9 %copy-start.8 = (s32[4,16,16]{2,1,0:T(8,128)S(1)}, s32[4,16,16]{2,1,0:T(8,128)}, u32[]{:S(2)}) copy-start(s32[4,16,16]{2,1,0:T(8,128)} %mask.20) | copy-start | bytes 12292
